TPU v7x, 32 devices: a whole 2x2x4 slice. The times are simulated.
32 devices in a mesh: dp: 8 (over y, x, core), mp: 4 (over z).
Axes of the slice: x: 2, y: 2, z: 4, core: 2. Of those that a mesh axis runs over, the one named last changes fastest.
Arguments:
- tokens: bfloat16 [4096, 6144], P(('dp', 'mp')), may hold values from -40 to 40
- norm_gain: float32 [6144], replicated, may hold values from 0.1 to 1.9
- q_gain: float32 [128], replicated, may hold values from 0.5 to 8
- k_gain: float32 [128], replicated, may hold values from 0.5 to 8
- w_query: bfloat16 [6144, 4096], P('dp', 'mp'), may hold values from -0.078125 to 0.078125
- w_key: bfloat16 [6144, 4096], P('dp', 'mp'), may hold values from -0.078125 to 0.078125
- w_value: bfloat16 [6144, 4096], P('dp', 'mp'), may hold values from -0.078125 to 0.078125
- grad_heads: bfloat16 [4096, 4096], P('dp', 'mp'), may hold values from -6 to 6
Outputs:
- grad_tokens: bfloat16 [4096, 6144], P(('dp', 'mp'))
- grad_query_weight: bfloat16 [6144, 4096], P('dp', 'mp')
- grad_key_weight: bfloat16 [6144, 4096], P('dp', 'mp')
- grad_value_weight: bfloat16 [6144, 4096], P('dp', 'mp')
All inputs are finite; a program needn't handle non-finite values.
Results may differ from a plain program's by a relative error of at most 0.03.
The roundings to bfloat16 on the way count: a program that leaves them out, or rounds other values in their place, can miss the bound.
Values may be sent and summed in bfloat16 or wider, within the bound.
No kernel may reach another device: no remote copies, remote signals or barrier semaphores. Data moves between devices by JAX's collectives and lax.ppermute only.
A program may use at most 192 MiB of HBM per device.

v0:
```python
import jax
import jax.numpy as jnp
from jax import lax
from jax.sharding import PartitionSpec as P

PATCH = 256


def normalize(row_data, gain_vector):
    average = jnp.mean(row_data, axis=-1, keepdims=True)
    centred = row_data - average
    inv_spread = lax.rsqrt(jnp.mean(centred * centred, axis=-1, keepdims=True) + 1e-06)
    unit_data = centred * inv_spread
    return (unit_data * gain_vector, unit_data, inv_spread)


def normalize_back(grad_out, unit_data, inv_spread, gain_vector):
    scaled = grad_out * gain_vector
    inner_term = jnp.mean(scaled * unit_data, axis=-1, keepdims=True)
    return (scaled - jnp.mean(scaled, axis=-1, keepdims=True) - unit_data * inner_term) * inv_spread


def attend_first(query_bf, key_bf, grad_out):
    factor = query_bf.shape[-1] ** (-0.5)
    scores = (
        jnp.einsum("bqhd,bkhd->bhqk", query_bf, key_bf, preferred_element_type=jnp.float32) * factor
    )
    attention = jax.nn.softmax(scores, axis=-1)
    attention_bf = attention.astype(jnp.bfloat16)
    grad_value = jnp.einsum(
        "bhqk,bqhd->bkhd", attention_bf, grad_out, preferred_element_type=jnp.float32
    ).astype(jnp.bfloat16)
    return (attention, grad_value)


def attend_rest(attention, query_bf, key_bf, value_bf, grad_out):
    factor = query_bf.shape[-1] ** (-0.5)
    grad_probs = jnp.einsum(
        "bqhd,bkhd->bhqk", grad_out, value_bf, preferred_element_type=jnp.float32
    )
    row_delta = jnp.sum(attention * grad_probs, axis=-1, keepdims=True)
    grad_scores = (attention * (grad_probs - row_delta) * factor).astype(jnp.bfloat16)
    grad_query = jnp.einsum(
        "bhqk,bkhd->bqhd", grad_scores, key_bf, preferred_element_type=jnp.float32
    )
    grad_key = jnp.einsum(
        "bhqk,bqhd->bkhd", grad_scores, query_bf, preferred_element_type=jnp.float32
    )
    return (grad_query, grad_key)


def weight_term(normed_all, grad_list):
    products = [
        lax.dot_general(
            normed_all, grad_item, (((0,), (0,)), ((), ())), preferred_element_type=jnp.float32
        )
        for grad_item in grad_list
    ]
    return jnp.concatenate(products, axis=1)


def per_device(tokens, norm_gain, q_gain, k_gain, w_query, w_key, w_value, grad_heads):
    model_width = tokens.shape[1]
    head_size = q_gain.shape[0]
    local_cols = w_query.shape[1]
    local_heads = local_cols // head_size
    normed_own, unit_rows, row_spread = normalize(tokens.astype(jnp.float32), norm_gain)
    normed_all = lax.all_gather(normed_own.astype(jnp.bfloat16), "mp", axis=0, tiled=True)
    group_tokens = normed_all.shape[0]
    image_count = group_tokens // PATCH
    full_query, full_key, full_value = (
        lax.all_gather(w_query, "dp", axis=0, tiled=True),
        lax.all_gather(w_key, "dp", axis=0, tiled=True),
        lax.all_gather(w_value, "dp", axis=0, tiled=True),
    )
    queries = jnp.dot(normed_all, full_query, preferred_element_type=jnp.float32)
    key_proj = jnp.dot(normed_all, full_key, preferred_element_type=jnp.float32)
    values = jnp.dot(normed_all, full_value, preferred_element_type=jnp.float32).astype(
        jnp.bfloat16
    )
    layout = (image_count, PATCH, local_heads, head_size)
    query_normed, query_unit, query_spread = normalize(queries.reshape(layout), q_gain)
    key_normed, key_unit, key_spread = normalize(key_proj.reshape(layout), k_gain)
    query_bf = query_normed.astype(jnp.bfloat16)
    key_bf = key_normed.astype(jnp.bfloat16)
    grad_out = grad_heads.reshape(layout)
    attention, grad_value = attend_first(query_bf, key_bf, grad_out)
    grad_value = grad_value.reshape(group_tokens, local_cols)
    grad_qn, grad_kn = attend_rest(attention, query_bf, key_bf, values.reshape(layout), grad_out)
    grad_query = (
        normalize_back(grad_qn, query_unit, query_spread, q_gain)
        .astype(jnp.bfloat16)
        .reshape(group_tokens, local_cols)
    )
    grad_key = (
        normalize_back(grad_kn, key_unit, key_spread, k_gain)
        .astype(jnp.bfloat16)
        .reshape(group_tokens, local_cols)
    )
    grad_list = (grad_query, grad_key, grad_value)
    full_weights = (full_query, full_key, full_value)
    running = jnp.zeros((tokens.shape[0] * lax.axis_size("mp"), model_width), jnp.float32)
    for grad_item, weight_item in zip(grad_list, full_weights):
        running = running + lax.dot_general(
            grad_item, weight_item, (((1,), (1,)), ((), ())), preferred_element_type=jnp.float32
        )
    grad_normed = lax.psum_scatter(
        running.astype(jnp.bfloat16), "mp", scatter_dimension=0, tiled=True
    ).astype(jnp.float32)
    grad_tokens = normalize_back(grad_normed, unit_rows, row_spread, norm_gain).astype(jnp.bfloat16)
    stacked = lax.psum_scatter(
        weight_term(normed_all, grad_list).astype(jnp.bfloat16),
        "dp",
        scatter_dimension=0,
        tiled=True,
    ).astype(jnp.float32)
    pieces = (
        stacked[:, :local_cols],
        stacked[:, local_cols : 2 * local_cols],
        stacked[:, 2 * local_cols :],
    )
    return (
        grad_tokens,
        pieces[0].astype(jnp.bfloat16),
        pieces[1].astype(jnp.bfloat16),
        pieces[2].astype(jnp.bfloat16),
    )


def solution(mesh):
    placed = (
        P(("dp", "mp"), None),
        P(),
        P(),
        P(),
        P("dp", "mp"),
        P("dp", "mp"),
        P("dp", "mp"),
        P("dp", "mp"),
    )
    return jax.shard_map(
        per_device,
        mesh=mesh,
        in_specs=placed,
        out_specs=(P(("dp", "mp"), None), P("dp", "mp"), P("dp", "mp"), P("dp", "mp")),
        check_vma=False,
    )
```

profile of v0, /device:TPU:1, one launch (start us, length us, event | category | flops | bytes accessed | tf_op | source)
XLA Modules:
  0.0 820.0 jit_solution(17891819990779151045)
XLA Ops:
  7.2 1.8 convert_reduce_fusion
  9.1 2.0 fusion.18
  15.7 115.4 %all-gather.5.cloned.1.call-done = bf16[512,6144]{1,0:T(8,128)(2,1)} async-done(((bf16[128,6144]{1,0:T(8,128)(2,1)}), bf16[512,6144]{1,0:T(8,128)(2,1)}) %all-gather.5.cloned.1.call-update) | async-done | bytes 6291472 | tf_op jit(solution)/shard_map/all_gather | solution.py:68
  131.1 72.5 %all-gather.11.cloned.1.call-done = bf16[6144,1024]{1,0:T(8,128)(2,1)} async-done(((bf16[768,1024]{1,0:T(8,128)(2,1)}), bf16[6144,1024]{1,0:T(8,128)(2,1)}) %all-gather.11.cloned.1.call-update) | async-done | bytes 12582928 | tf_op jit(solution)/shard_map/all_gather | solution.py:74
  203.6 11.4 %fusion.40 = bf16[64,8,8,128]{3,1,2,0:T(8,128)(2,1)S(1)} fusion(bf16[512,6144]{1,0:T(8,128)(2,1)} %all-gather.5.cloned.1.call-done, bf16[6144,1024]{1,0:T(8,128)(2,1)} %all-gather.11.cloned.1.call-done), kind=kOutput, calls=%fused_computation.62 | convolution fusion | flops 6442975232 | bytes 19922944 | tf_op jit(solution)/shard_map/dot_general | solution.py:78
  216.3 61.3 %all-gather.9.cloned.1.call-done = bf16[6144,1024]{1,0:T(8,128)(2,1)} async-done(((bf16[768,1024]{1,0:T(8,128)(2,1)}), bf16[6144,1024]{1,0:T(8,128)(2,1)}) %all-gather.9.cloned.1.call-update) | async-done | bytes 12582928 | tf_op jit(solution)/shard_map/all_gather | solution.py:72
  277.6 11.4 %convolution_bitcast_fusion = f32[64,8,8,128]{3,1,2,0:T(8,128)S(1)} fusion(bf16[512,6144]{1,0:T(8,128)(2,1)} %all-gather.5.cloned.1.call-done, bf16[6144,1024]{1,0:T(8,128)(2,1)} %all-gather.9.cloned.1.call-done), kind=kOutput, calls=%fused_computation.57 | convolution fusion | flops 6442450944 | bytes 20971520 | tf_op jit(solution)/shard_map/dot_general | solution.py:76
  290.9 1.9 copy.90
  292.8 58.8 %all-gather.7.cloned.1.call-done = bf16[6144,1024]{1,0:T(8,128)(2,1)} async-done(((bf16[768,1024]{1,0:T(8,128)(2,1)}), bf16[6144,1024]{1,0:T(8,128)(2,1)}) %all-gather.7.cloned.1.call-update) | async-done | bytes 12582928 | tf_op jit(solution)/shard_map/all_gather | solution.py:73
  351.5 11.4 %convolution_bitcast_fusion.1 = f32[64,8,8,128]{3,1,2,0:T(8,128)S(1)} fusion(bf16[512,6144]{1,0:T(8,128)(2,1)} %all-gather.5.cloned.1.call-done, bf16[6144,1024]{1,0:T(8,128)(2,1)} %all-gather.7.cloned.1.call-done), kind=kOutput, calls=%fused_computation.58 | convolution fusion | flops 6442450944 | bytes 20971520 | tf_op jit(solution)/shard_map/dot_general | solution.py:77
  367.3 3.1 copy.88
  370.7 1.8 multiply_reduce_fusion.2
  372.6 3.9 fusion.49
  376.5 5.3 fusion.67
  381.9 3.9 fusion.37
  385.7 9.7 %bitcast_reduce_fusion = (f32[2,256,8]{1,2,0:T(8,128)S(1)}, f32[2,256,8]{1,2,0:T(8,128)S(1)}, f32[2,8,128,256]{3,2,1,0:T(8,128)}) fusion(f32[128]{0:T(128)S(1)} %copy-done.16, f32[2,256,8]{1,2,0:T(8,128)S(1)} %add_rsqrt_fusion.1, f32[2,256,8,128]{1,3,2,0:T(8,128)} %copy.88, f32[2,256,8]{1,2,0:T(8,128)S(1)} %broadcast_multiply_fusion.5, ...), kind=kOutput, calls=%fused_computation.32 | convolution fusion | flops 281014528 | bytes 14795776 | tf_op jit(solution)/shard_map/bhqk,bqhd->bkhd/dot_general | solution.py:46
  395.4 9.6 %bitcast_reduce_fusion.1 = (f32[2,256,8]{1,2,0:T(8,128)S(1)}, f32[2,256,8]{1,2,0:T(8,128)S(1)}, f32[2,8,128,256]{3,2,1,0:T(8,128)}) fusion(f32[128]{0:T(128)S(1)} %copy-done.17, f32[2,256,8]{1,2,0:T(8,128)S(1)} %add_rsqrt_fusion, f32[2,256,8,128]{1,3,2,0:T(8,128)S(1)} %copy.90, f32[2,256,8]{1,2,0:T(8,128)S(1)} %broadcast_multiply_fusion.4, ...), kind=kOutput, calls=%fused_computation.39 | convolution fusion | flops 281014528 | bytes 14795776 | tf_op jit(solution)/shard_map/bhqk,bkhd->bqhd/dot_general | solution.py:43
  406.7 2.3 fusion.22
  410.4 2.2 fusion.26
  413.4 12.8 %fusion.44 = f32[512,6144]{1,0:T(8,128)} fusion(bf16[6144,1024]{1,0:T(8,128)(2,1)} %all-gather.7.cloned.1.call-done, bf16[64,8,8,128]{3,2,1,0:T(8,128)(2,1)} %bitcast.115), kind=kOutput, calls=%fused_computation.66 | convolution fusion | flops 6442450944 | bytes 26214400 | tf_op jit(solution)/shard_map/dot_general | solution.py:104
  426.3 19.6 %fusion.47 = f32[512,6144]{1,0:T(8,128)} fusion(bf16[6144,1024]{1,0:T(8,128)(2,1)} %all-gather.9.cloned.1.call-done, bf16[64,8,8,128]{3,2,1,0:T(8,128)(2,1)S(1)} %bitcast.117), kind=kOutput, calls=%fused_computation.69 | convolution fusion | flops 6442450944 | bytes 26214400 | tf_op jit(solution)/shard_map/dot_general | solution.py:104
  445.9 17.3 %add_convert_fusion = bf16[512,6144]{1,0:T(8,128)(2,1)} fusion(f32[512,6144]{1,0:T(8,128)} %fusion.47, f32[512,6144]{1,0:T(8,128)} %fusion.44, bf16[6144,1024]{1,0:T(8,128)(2,1)} %all-gather.11.cloned.1.call-done, bf16[64,8,8,128]{3,2,1,0:T(8,128)(2,1)S(1)} %bitcast.113), kind=kOutput, calls=%fused_computation.3 | convolution fusion | flops 6451888128 | bytes 45088768 | tf_op jit(solution)/shard_map/dot_general | solution.py:104
  463.3 12.8 %convolution_convert_fusion = bf16[6144,1024]{0,1:T(8,128)(2,1)} fusion(bf16[512,6144]{1,0:T(8,128)(2,1)} %all-gather.5.cloned.1.call-done, bf16[64,8,8,128]{3,2,1,0:T(8,128)(2,1)S(1)} %bitcast.114), kind=kOutput, calls=%fused_computation.4 | convolution fusion | flops 6448742400 | bytes 19922944 | tf_op jit(solution)/shard_map/dot_general | solution.py:54
  476.1 12.5 %convolution_convert_fusion.2 = bf16[6144,1024]{0,1:T(8,128)(2,1)} fusion(bf16[512,6144]{1,0:T(8,128)(2,1)} %all-gather.5.cloned.1.call-done, bf16[64,8,8,128]{3,2,1,0:T(8,128)(2,1)S(1)} %bitcast.118), kind=kOutput, calls=%fused_computation.6 | convolution fusion | flops 6448742400 | bytes 19922944 | tf_op jit(solution)/shard_map/dot_general | solution.py:54
  488.6 9.9 %convolution_convert_fusion.1 = bf16[6144,1024]{0,1:T(8,128)(2,1)} fusion(bf16[512,6144]{1,0:T(8,128)(2,1)S(1)} %bitcast.120, bf16[64,8,8,128]{3,2,1,0:T(8,128)(2,1)S(1)} %bitcast.116), kind=kOutput, calls=%fused_computation.5 | convolution fusion | flops 6448742400 | bytes 19922944 | tf_op jit(solution)/shard_map/dot_general | solution.py:54
  498.5 26.1 %pad_maximum_fusion = bf16[6144,3072]{0,1:T(8,128)(2,1)} fusion(bf16[6144,1024]{0,1:T(8,128)(2,1)} %convolution_convert_fusion, bf16[6144,1024]{0,1:T(8,128)(2,1)} %convolution_convert_fusion.1, bf16[6144,1024]{0,1:T(8,128)(2,1)} %convolution_convert_fusion.2), kind=kLoop, calls=%fused_computation.2 | loop fusion | flops 113246208 | bytes 75497472 | tf_op jit(solution)/shard_map/concatenate | solution.py:59
  524.7 49.1 %reduce-scatter.3.cloned.1.call-done = bf16[128,6144]{1,0:T(8,128)(2,1)} async-done(((bf16[512,6144]{1,0:T(8,128)(2,1)}), bf16[128,6144]{1,0:T(8,128)(2,1)}) %reduce-scatter.3.cloned.1.call-update) | async-done | bytes 1572880 | tf_op jit(solution)/shard_map/reduce_scatter | solution.py:107
  573.8 2.5 fusion.19
  576.4 2.4 fusion.17
  578.8 224.3 %reduce-scatter.5.cloned.1.call-done = bf16[768,3072]{0,1:T(8,128)(2,1)} async-done(((bf16[6144,3072]{0,1:T(8,128)(2,1)}), bf16[768,3072]{0,1:T(8,128)(2,1)}) %reduce-scatter.5.cloned.1.call-update) | async-done | bytes 4718608 | tf_op jit(solution)/shard_map/reduce_scatter | solution.py:111
  803.0 3.8 fusion.66
  806.8 2.6 copy.103
  (79 shorter events, 19.5 us)
Async XLA Ops:
  7.2 4.4 copy-start
  7.2 4.4 copy-start.10
  7.2 123.9 %all-gather.5.cloned.1.call-start = ((), (), s32[]{:S(2)}) async-start(), calls=%async_computation.2 | async-start | bytes 7864320 | tf_op jit(solution)/shard_map/all_gather | solution.py:68
  9.0 2.0 copy-start.12
  11.1 0.5 copy-start.14
  13.3 2.1 copy-start.6
  13.3 190.3 %all-gather.11.cloned.1.call-start = ((), (), s32[]{:S(2)}) async-start(), calls=%async_computation.5 | async-start | bytes 14155776 | tf_op jit(solution)/shard_map/all_gather | solution.py:74
  14.0 263.6 %all-gather.9.cloned.1.call-start = ((), (), s32[]{:S(2)}) async-start(), calls=%async_computation.4 | async-start | bytes 14155776 | tf_op jit(solution)/shard_map/all_gather | solution.py:72
  14.8 336.8 %all-gather.7.cloned.1.call-start = ((), (), s32[]{:S(2)}) async-start(), calls=%async_computation.3 | async-start | bytes 14155776 | tf_op jit(solution)/shard_map/all_gather | solution.py:73
  15.4 558.4 %reduce-scatter.3.cloned.1.call-start = ((), (), s32[]{:S(2)}) async-start(), calls=%async_computation.6 | async-start | bytes 7864320 | tf_op jit(solution)/shard_map/reduce_scatter | solution.py:107
  363.0 1.9 copy-start.3
  363.5 2.7 copy-start.4
  372.6 3.9 copy-start.16
  372.6 3.9 copy-start.17
  395.4 9.6 %copy-start.9 = (bf16[2,256,8,128]{3,1,2,0:T(8,128)(2,1)S(1)}, bf16[2,256,8,128]{3,1,2,0:T(8,128)(2,1)}, u32[]{:S(2)}) copy-start(bf16[2,256,8,128]{3,1,2,0:T(8,128)(2,1)} %fusion.37) | copy-start | bytes 3145732
  405.0 1.7 copy-start.2
  426.2 19.6 %copy-start.7 = (bf16[2,256,8,128]{3,2,1,0:T(8,128)(2,1)S(1)}, bf16[2,256,8,128]{3,2,1,0:T(8,128)(2,1)}, u32[]{:S(2)}) copy-start(bf16[2,256,8,128]{3,2,1,0:T(8,128)(2,1)} %copy.100) | copy-start | bytes 3145732
  463.2 339.8 %reduce-scatter.5.cloned.1.call-start = ((), (), s32[]{:S(2)}) async-start(), calls=%async_computation.7 | async-start | bytes 42467328 | tf_op jit(solution)/shard_map/reduce_scatter | solution.py:111
  463.3 25.3 %slice-start = ((s8[6291456]{0:T(1024)(128)(4,1)}), s8[4194304]{0:T(1024)(128)(4,1)S(1)}, s32[]{:S(2)}) async-start(s8[6291456]{0:T(1024)(128)(4,1)} %bitcast.119), calls=%async_computation.8 | async-start | bytes 8388608
  476.1 12.5 %copy-start.8 = (bf16[2,256,8,128]{3,2,1,0:T(8,128)(2,1)S(1)}, bf16[2,256,8,128]{3,2,1,0:T(8,128)(2,1)}, u32[]{:S(2)}) copy-start(bf16[2,256,8,128]{3,2,1,0:T(8,128)(2,1)} %copy.98) | copy-start | bytes 3145732
  476.1 12.5 %slice-start.1 = ((s8[6291456]{0:T(1024)(128)(4,1)}), s8[2097152]{0:T(1024)(128)(4,1)S(1)}, s32[]{:S(2)}) async-start(s8[6291456]{0:T(1024)(128)(4,1)} %bitcast.119), calls=%async_computation.9 | async-start | bytes 4194304
  524.6 49.1 %copy-start.1 = (bf16[128,6144]{1,0:T(8,128)(2,1)S(1)}, bf16[128,6144]{1,0:T(8,128)(2,1)}, u32[]{:S(2)}) copy-start(bf16[128,6144]{1,0:T(8,128)(2,1)} %param.8) | copy-start | bytes 4718596
  524.7 49.1 %copy-start.11 = (f32[6144]{0:T(1024)S(1)}, f32[6144]{0:T(1024)}, u32[]{:S(2)}) copy-start(f32[6144]{0:T(1024)} %param.9) | copy-start | bytes 73732
  524.7 49.1 %copy-start.13 = (f32[128]{0:T(128)S(1)}, f32[128]{0:T(128)}, u32[]{:S(2)}) copy-start(f32[128]{0:T(128)} %copy-done.12) | copy-start | bytes 1540
  524.7 49.1 %copy-start.15 = (f32[128]{0:T(128)S(1)}, f32[128]{0:T(128)}, u32[]{:S(2)}) copy-start(f32[128]{0:T(128)} %copy-done.14) | copy-start | bytes 1540
  573.8 2.6 copy-start.5
Sparse Core Ops, SparseCore 0:
  13.4 117.6 all-gather.4
  133.0 70.5 all-gather.10
  205.5 72.1 all-gather.8
  279.4 72.1 all-gather.6
  463.4 110.3 reduce-scatter.2
  577.3 225.7 reduce-scatter.4
where the time goes:
time: 829 us; the launch traced here: 820 us
  waiting for transfers between devices  583 us (70%)
  matrix products  152 us (18%)
  other arithmetic  44.5 us (5%)
  local copies, waits for them, and re-layouts  25.4 us (3%)
  between operations  14.9 us (2%)
    reduce_scatter x1, waiting for transfers between devices, per_device(): lax.psum_scatter(weight_term(normed_all, grad_list).astype(jnp.bfloat16),...  224 us
    all_gather x1, waiting for transfers between devices, per_device(): lax.all_gather(normed_own.astype(jnp.bfloat16), 'mp', axis=0, tiled=True)  115 us
    all_gather x1, waiting for transfers between devices, per_device(): lax.all_gather(w_value, 'dp', axis=0, tiled=True)  72.5 us
    all_gather x1, waiting for transfers between devices, per_device(): lax.all_gather(w_query, 'dp', axis=0, tiled=True)  61.3 us
    all_gather x1, waiting for transfers between devices, per_device(): lax.all_gather(w_key, 'dp', axis=0, tiled=True)  58.8 us
    dot_general x3, matrix products, per_device(): lax.dot_general(grad_item, weight_item, (((1,), (1,)), ((), ())), preferr...  49.8 us
    reduce_scatter x1, waiting for transfers between devices, per_device(): lax.psum_scatter(running.astype(jnp.bfloat16), 'mp', scatter_dimension=0,...  49.1 us
    dot_general x3, matrix products, weight_term(): lax.dot_general(normed_all, grad_item, (((0,), (0,)), ((), ())), preferre...  35.2 us
  transfers between devices with their start and end apart: 6, of which 6 were waited for; matrix products, arithmetic and copies ran while one was open for 12% of the time, Pallas kernels for 0%

commit v1 on v0

v1 whole, which is shorter than its diff:
```python
import functools

import jax
import jax.numpy as jnp
from jax import lax
from jax.experimental import pallas as pl
from jax.experimental.pallas import tpu as pltpu
from jax.sharding import PartitionSpec as P

PATCH = 256
BF = jnp.bfloat16
F32 = jnp.float32


def normalize(row_data, gain_vector):
    average = jnp.mean(row_data, axis=-1, keepdims=True)
    centred = row_data - average
    inv_spread = lax.rsqrt(jnp.mean(centred * centred, axis=-1, keepdims=True) + 1e-06)
    unit_data = centred * inv_spread
    return (unit_data * gain_vector, unit_data, inv_spread)


def normalize_back(grad_out, unit_data, inv_spread, gain_vector):
    scaled = grad_out * gain_vector
    inner_term = jnp.mean(scaled * unit_data, axis=-1, keepdims=True)
    return (scaled - jnp.mean(scaled, axis=-1, keepdims=True) - unit_data * inner_term) * inv_spread


def dot_nt(a, b):
    return lax.dot_general(a, b, (((1,), (1,)), ((), ())), preferred_element_type=F32)


def dot_tn(a, b):
    return lax.dot_general(a, b, (((0,), (0,)), ((), ())), preferred_element_type=F32)


def attention_of(query_bf, key_bf):
    scores = dot_nt(key_bf, query_bf) * query_bf.shape[-1] ** (-0.5)
    raised = jnp.exp(scores - jnp.max(scores, axis=0, keepdims=True))
    return raised * (1.0 / jnp.sum(raised, axis=0, keepdims=True))


def rows_of(ref):
    block = ref[...]
    return block.reshape(-1, block.shape[-1])


def first_kernel(q_ref, k_ref, g_ref, q_gain_ref, k_gain_ref, grad_value_ref):
    query_bf = normalize(rows_of(q_ref), q_gain_ref[...])[0].astype(BF)
    key_bf = normalize(rows_of(k_ref), k_gain_ref[...])[0].astype(BF)
    attention = attention_of(query_bf, key_bf).astype(BF)
    grad_value = jnp.dot(attention, rows_of(g_ref), preferred_element_type=F32)
    grad_value_ref[...] = grad_value.astype(BF).reshape(grad_value_ref.shape)


def rest_kernel(q_ref, k_ref, v_ref, g_ref, q_gain_ref, k_gain_ref, grad_query_ref, grad_key_ref):
    q_gain, k_gain = q_gain_ref[...], k_gain_ref[...]
    query_normed, query_unit, query_spread = normalize(rows_of(q_ref), q_gain)
    key_normed, key_unit, key_spread = normalize(rows_of(k_ref), k_gain)
    query_bf, key_bf = query_normed.astype(BF), key_normed.astype(BF)
    attention = attention_of(query_bf, key_bf)
    grad_probs = dot_nt(rows_of(v_ref), rows_of(g_ref))
    delta = jnp.sum(attention * grad_probs, axis=0, keepdims=True)
    factor = query_bf.shape[-1] ** (-0.5)
    grad_scores = (attention * (grad_probs - delta) * factor).astype(BF)
    grad_kn = jnp.dot(grad_scores, query_bf, preferred_element_type=F32)
    grad_qn = dot_tn(grad_scores, key_bf)
    grad_query = normalize_back(grad_qn, query_unit, query_spread, q_gain)
    grad_key = normalize_back(grad_kn, key_unit, key_spread, k_gain)
    grad_query_ref[...] = grad_query.astype(BF).reshape(grad_query_ref.shape)
    grad_key_ref[...] = grad_key.astype(BF).reshape(grad_key_ref.shape)


def attention_call(kernel, arrays, gains, n_out):
    levels, groups, own, columns = arrays[0].shape
    head = gains[0].shape[-1]
    span = PATCH // own
    block = pl.BlockSpec((span, 1, own, head), lambda g, i, h: (i, g, 0, h))
    gain_block = pl.BlockSpec((1, head), lambda g, i, h: (0, 0))
    pairs = groups * (levels // span) * (columns // head)
    return pl.pallas_call(
        kernel,
        grid=(groups, levels // span, columns // head),
        in_specs=[block] * len(arrays) + [gain_block] * len(gains),
        out_specs=[block] * n_out,
        out_shape=[jax.ShapeDtypeStruct(arrays[0].shape, BF)] * n_out,
        cost_estimate=pl.CostEstimate(
            flops=pairs * 8 * PATCH * PATCH * head,
            bytes_accessed=4 * len(arrays) * arrays[0].size,
            transcendentals=pairs * PATCH * PATCH,
        ),
    )(*arrays, *[gain.reshape(1, head) for gain in gains])


def per_device(n_dp, n_mp, tokens, norm_gain, q_gain, k_gain, w_query, w_key, w_value, grad_heads):
    own, width = tokens.shape
    rows, cols = w_query.shape[0], w_query.shape[1] // 2
    n_chips = n_dp // 2
    place = lax.axis_index("dp")
    core = place & 1

    def swap(array, bit):
        return lax.ppermute(array, "dp", [(i, i ^ bit) for i in range(n_dp)])

    def half(array, which):
        return lax.dynamic_slice_in_dim(array, which * cols, cols, 1)

    def core_order(mine, other, axis):
        return jnp.where(
            core == 0,
            jnp.concatenate([mine, other], axis=axis),
            jnp.concatenate([other, mine], axis=axis),
        )

    def after(array, *others):
        return lax.optimization_barrier((array, *others))[0]

    ring = list(range(0, n_mp, 2)) + list(range(n_mp - 1, 0, -2))
    level = lax.axis_index("mp")
    spot = jnp.where(level % 2 == 0, level // 2, n_mp - 1 - level // 2)
    ring_pairs = [(ring[i], ring[(i + 1) % n_mp]) for i in range(n_mp)]

    def level_at(back):
        at = (spot + 2 * n_mp - back) % n_mp
        return jnp.where(at < n_mp // 2, 2 * at, 2 * (n_mp - 1 - at) + 1)

    def ring_on(array):
        return lax.ppermute(array, "mp", ring_pairs)

    def feature_block(array, r):
        return lax.dynamic_slice_in_dim(array, (place ^ r) * rows, rows, 1)

    normed_own, unit_rows, row_spread = normalize(tokens.astype(F32), norm_gain)
    normed_own = normed_own.astype(BF)
    even = jnp.concatenate([feature_block(normed_own, 2 * j) for j in range(n_chips)], axis=1)
    odd = jnp.concatenate([feature_block(normed_own, 2 * j + 1) for j in range(n_chips)], axis=1)
    block = core_order(even, swap(odd, 1), 0)

    def chip_shard(weight):
        return jnp.concatenate([half(weight, core), swap(half(weight, 1 - core), 1)], axis=0)

    def gather_start(shard):
        held = {0: shard}
        bit = 8
        while bit < n_dp:
            held.update({j ^ (bit // 2): swap(part, bit) for j, part in list(held.items())})
            bit *= 2
        for j, part in list(held.items()):
            held[j ^ 1] = swap(part, 2)
            held[j ^ 2] = swap(part, 4)
        return held

    def gather_rest(held):
        for j in range(0, n_chips, 4):
            upper = swap(held[j ^ 1][:rows], 4)
            lower = swap(held[j ^ 2][rows:], 2)
            held[j ^ 3] = jnp.concatenate([upper, lower], axis=0)
        return [held[j] for j in range(n_chips)]

    shard_query, shard_key, shard_value = (chip_shard(w) for w in (w_query, w_key, w_value))
    held_query, held_key = gather_start(shard_query), gather_start(shard_key)
    full_query = gather_rest(held_query)
    full_key = gather_rest(held_key)
    shard_value = after(shard_value, full_query[3], full_key[3])
    full_value = gather_rest(gather_start(shard_value))
    whole_query, whole_key, whole_value = (
        jnp.concatenate(parts, axis=0) for parts in (full_query, full_key, full_value)
    )

    step_rows = 2 * own
    normed = jnp.zeros((n_mp * step_rows, width), BF)
    for step in range(n_mp):
        beside = swap(block, 1)
        pieces = []
        for j in range(n_chips):
            pieces += [block[:, j * rows : (j + 1) * rows], beside[:, j * rows : (j + 1) * rows]]
        normed = lax.dynamic_update_slice_in_dim(
            normed, jnp.concatenate(pieces, axis=1), level_at(step) * step_rows, 0
        )
        if step < n_mp - 1:
            block = ring_on(block)

    grads_mine = half(grad_heads, core).reshape(n_mp, 1, own, cols)
    grads_other = swap(half(grad_heads, 1 - core), 1).reshape(n_mp, 1, own, cols)
    grad_out = core_order(grads_mine, grads_other, 1)

    layout = (n_mp, 2, own, cols)
    queries = jnp.dot(normed, whole_query, preferred_element_type=F32).reshape(layout)
    key_proj = jnp.dot(normed, whole_key, preferred_element_type=F32).reshape(layout)
    gains = (q_gain, k_gain)
    (grad_value,) = attention_call(first_kernel, (queries, key_proj, grad_out), gains, 1)

    def weight_product(grad, j):
        chip_rows = normed[:, j * 2 * rows : (j + 1) * 2 * rows]
        return dot_tn(chip_rows, grad)

    def scatter_weight(grad):
        totals = {}
        for j in range(0, n_chips, 4):
            far = weight_product(grad, j ^ 3).astype(BF)
            from_x = swap(far[:rows], 2)
            from_y = swap(far[rows:], 4)
            next_x = weight_product(grad, j ^ 1)
            next_y = weight_product(grad, j ^ 2)
            mine = weight_product(grad, j)
            next_x = jnp.concatenate([next_x[:rows], next_x[rows:] + from_y.astype(F32)], axis=0)
            next_y = jnp.concatenate([next_y[:rows] + from_x.astype(F32), next_y[rows:]], axis=0)
            from_x = swap(next_x.astype(BF), 2)
            from_y = swap(next_y.astype(BF), 4)
            totals[j] = mine + from_x.astype(F32) + from_y.astype(F32)
        bit = n_dp // 2
        while bit >= 8:
            for j in [j for j in totals if j < bit // 2]:
                totals[j] = totals[j] + swap(totals.pop(j ^ (bit // 2)).astype(BF), bit).astype(F32)
            bit //= 2
        total = totals[0].astype(BF)
        return core_order(total[:rows], swap(total[rows:], 1), 1)

    flat = (n_mp * step_rows, cols)
    grad_value = grad_value.reshape(flat)
    out_value = scatter_weight(grad_value)

    values = jnp.dot(normed, whole_value, preferred_element_type=F32).astype(BF).reshape(layout)
    grad_query, grad_key = attention_call(
        rest_kernel, (queries, key_proj, values, grad_out), gains, 2
    )
    grad_query, grad_key = grad_query.reshape(flat), grad_key.reshape(flat)

    arrived = None
    for step in range(n_mp):
        start = level_at(step + 1) * step_rows
        partial = None
        for grad, weight in (
            (grad_query, whole_query),
            (grad_key, whole_key),
            (grad_value, whole_value),
        ):
            term = dot_nt(lax.dynamic_slice_in_dim(grad, start, step_rows, 0), weight)
            partial = term if partial is None else partial + term
        pieces = [partial[:, r * rows : (r + 1) * rows] for r in range(n_dp)]
        sent = jnp.concatenate(pieces[1::2], axis=1).astype(BF)
        kept = jnp.concatenate(pieces[0::2], axis=1)
        kept = kept + swap(sent, 1).astype(F32)
        if arrived is not None:
            kept = kept + arrived.astype(F32)
        if step < n_mp - 1:
            arrived = ring_on(kept.astype(BF))

    out_query = scatter_weight(grad_query)
    out_key = scatter_weight(grad_key)

    mine = lax.dynamic_slice_in_dim(kept, core * own, own, 0)
    other = swap(lax.dynamic_slice_in_dim(kept, (1 - core) * own, own, 0).astype(BF), 1).astype(F32)
    pieces = []
    for j in range(n_chips):
        pieces += [mine[:, j * rows : (j + 1) * rows], other[:, j * rows : (j + 1) * rows]]
    relative = jnp.concatenate(pieces, axis=1)
    grad_normed = jnp.concatenate([feature_block(relative, b) for b in range(n_dp)], axis=1)
    grad_tokens = normalize_back(grad_normed, unit_rows, row_spread, norm_gain).astype(BF)
    return (grad_tokens, out_query, out_key, out_value)


def solution(mesh):
    matrix = P("dp", "mp")
    token_rows = P(("dp", "mp"), None)
    return jax.shard_map(
        functools.partial(per_device, mesh.shape["dp"], mesh.shape["mp"]),
        mesh=mesh,
        in_specs=(token_rows, P(), P(), P(), matrix, matrix, matrix, matrix),
        out_specs=(token_rows, matrix, matrix, matrix),
        check_vma=False,
    )
```

time: 829 us -> 612 us (0.74)
  waiting for transfers between devices: 583 us -> 197 us
  local copies, waits for them, and re-layouts: 25.4 us -> 100 us
  starting transfers between devices: 0.24 us -> 57 us
  Pallas kernels: 0 us -> 32.8 us
  other arithmetic: 44.5 us -> 66.1 us
  between operations: 14.9 us -> 2.15 us
    all_gather x4 -> x0, waiting for transfers between devices: 308 us -> none  [the longest x1 115 us: per_device(): lax.all_gather(normed_own.astype(jnp.bfloat16), 'mp', axis=0, tiled=True)]
    reduce_scatter x2 -> x0, waiting for transfers between devices: 273 us -> none  [the longest x1 224 us: per_device(): lax.psum_scatter(weight_term(normed_all, grad_list).astype(jnp.bfloat16),...]
    ppermute x0 -> x47, waiting for transfers between devices: none -> 197 us  [the longest x41 151 us: swap(): return lax.ppermute(array, 'dp', [(i, i ^ bit) for i in range(n_dp)])]
    ppermute x0 -> x47, starting transfers between devices: none -> 57 us  [the longest x41 43.3 us: swap(): return lax.ppermute(array, 'dp', [(i, i ^ bit) for i in range(n_dp)])]
    unnamed x47 -> x195, local copies, waits for them, and re-layouts: 11.6 us -> 46.4 us
    pallas_call x0 -> x2, Pallas kernels: none -> 32.8 us  [attention_call(): pl.pallas_call(kernel, grid=(groups, levels // span, columns // head), in...]
    slice x1 -> x26, local copies, waits for them, and re-layouts: 3.8 us -> 30.8 us  [the longest x8 14.3 us: per_device(): pieces = [partial[:, r * rows:(r + 1) * rows] for r in range(n_dp)]]
    select_n x0 -> x5, other arithmetic: none -> 21.4 us  [core_order(): jnp.where(core == 0, jnp.concatenate([mine, other], axis=axis), jnp.conca...]
  transfers between devices with their start and end apart: 6 -> 47, of which waited for: 6 -> 15; matrix products, arithmetic and copies ran while one was open for 12% -> 32% of each run, Pallas kernels for 0% -> 0%
where the time goes in v1:
time: 612 us; the launch traced here: 602 us
  waiting for transfers between devices  197 us (32%)
  matrix products  146 us (24%)
  local copies, waits for them, and re-layouts  100 us (16%)
  other arithmetic  66.1 us (11%)
  starting transfers between devices  57 us (9%)
  Pallas kernels  32.8 us (5%)
    ppermute x41, waiting for transfers between devices, swap(): return lax.ppermute(array, 'dp', [(i, i ^ bit) for i in range(n_dp)])  151 us
    dot_general x12, matrix products, dot_nt(): lax.dot_general(a, b, (((1,), (1,)), ((), ())), preferred_element_type=F32)  72.8 us
    ppermute x6, waiting for transfers between devices, ring_on(): return lax.ppermute(array, 'mp', ring_pairs)  46.8 us
    unnamed x195, local copies, waits for them, and re-layouts  46.4 us
    dot_general x12, matrix products, dot_tn(): lax.dot_general(a, b, (((0,), (0,)), ((), ())), preferred_element_type=F32)  45.3 us
    ppermute x41, starting transfers between devices, swap(): return lax.ppermute(array, 'dp', [(i, i ^ bit) for i in range(n_dp)])  43.3 us
    pallas_call x2, Pallas kernels, attention_call(): pl.pallas_call(kernel, grid=(groups, levels // span, columns // head), in...  32.8 us
    select_n x5, other arithmetic, core_order(): jnp.where(core == 0, jnp.concatenate([mine, other], axis=axis), jnp.conca...  21.4 us
  transfers between devices with their start and end apart: 47, of which 15 were waited for; matrix products, arithmetic and copies ran while one was open for 32% of the time, Pallas kernels for 0%

profile of v1, /device:TPU:1, one launch (start us, length us, event | category | flops | bytes accessed | tf_op | source)
XLA Modules:
  0.0 601.7 jit_solution(13913518484909680882)
XLA Ops:
  17.6 8.9 %maximum_select_fusion = bf16[256,3072]{1,0:T(8,128)(2,1)} fusion(bf16[128,3072]{1,0:T(8,128)(2,1)} %collective-permute-done, bf16[128,768]{1,0:T(8,128)(2,1)S(1)} %get-tuple-element.69, bf16[128,768]{1,0:T(8,128)(2,1)S(1)} %get-tuple-element.70, bf16[128,768]{1,0:T(8,128)(2,1)} %get-tuple-element.71, bf16[128,768]{1,0:T(8,128)(2,1)S(1)} %get-tuple-element.64, ...), kind=kLoop, calls=%fused_computation.80 | loop fusion | flops 16515072 | bytes 3145729 | tf_op jit(solution)/shard_map/jit(_where)/select_n | solution.py:109
  46.7 18.6 %collective-permute-done.20 = bf16[1536,512]{1,0:T(8,128)(2,1)S(1)} collective-permute-done((bf16[1536,512]{1,0:T(8,128)(2,1)S(1)}, bf16[1536,512]{1,0:T(8,128)(2,1)S(1)}, u32[]{:S(2)}, u32[]{:S(2)}) %collective-permute-start.20) | collective-permute-done | bytes 1572896 | tf_op jit(solution)/shard_map/ppermute | solution.py:103
  69.6 30.3 %collective-permute-done.9 = bf16[1536,512]{1,0:T(8,128)(2,1)S(1)} collective-permute-done((bf16[1536,512]{1,0:T(8,128)(2,1)}, bf16[1536,512]{1,0:T(8,128)(2,1)S(1)}, u32[]{:S(2)}, u32[]{:S(2)}) %collective-permute-start.9) | collective-permute-done | bytes 1572896 | tf_op jit(solution)/shard_map/ppermute | solution.py:103
  103.9 6.1 %broadcast_in_dim.2 = bf16[1024,6144]{1,0:T(8,128)(2,1)} broadcast(bf16[]{:T(256)} %constant.87.clone.1), dimensions={} | broadcast | bytes 12582914 | tf_op jit(solution)/shard_map/broadcast_in_dim | solution.py:171
  119.6 13.2 %collective-permute-done.15 = bf16[1536,512]{1,0:T(8,128)(2,1)} collective-permute-done((bf16[1536,512]{1,0:T(8,128)(2,1)}, bf16[1536,512]{1,0:T(8,128)(2,1)}, u32[]{:S(2)}, u32[]{:S(2)}) %collective-permute-start.15) | collective-permute-done | bytes 1572896 | tf_op jit(solution)/shard_map/ppermute | solution.py:103
  142.2 8.3 %collective-permute-done.22 = bf16[768,512]{1,0:T(8,128)(2,1)} collective-permute-done((bf16[768,512]{1,0:T(8,128)(2,1)}, bf16[768,512]{1,0:T(8,128)(2,1)}, u32[]{:S(2)}, u32[]{:S(2)}) %collective-permute-start.22) | collective-permute-done | bytes 786464 | tf_op jit(solution)/shard_map/ppermute | solution.py:103
  155.7 10.6 %collective-permute-done.11 = bf16[768,512]{1,0:T(8,128)(2,1)S(1)} collective-permute-done((bf16[768,512]{1,0:T(8,128)(2,1)S(1)}, bf16[768,512]{1,0:T(8,128)(2,1)S(1)}, u32[]{:S(2)}, u32[]{:S(2)}) %collective-permute-start.11) | collective-permute-done | bytes 786464 | tf_op jit(solution)/shard_map/ppermute | solution.py:103
  170.4 12.9 %collective-permute-done.16 = bf16[768,512]{1,0:T(8,128)(2,1)S(1)} collective-permute-done((bf16[768,512]{1,0:T(8,128)(2,1)S(1)}, bf16[768,512]{1,0:T(8,128)(2,1)S(1)}, u32[]{:S(2)}, u32[]{:S(2)}) %collective-permute-start.16) | collective-permute-done | bytes 786464 | tf_op jit(solution)/shard_map/ppermute | solution.py:103
  195.8 25.4 %collective-permute-done.6 = bf16[256,3072]{1,0:T(8,128)(2,1)S(1)} collective-permute-done((bf16[256,3072]{1,0:T(8,128)(2,1)S(1)}, bf16[256,3072]{1,0:T(8,128)(2,1)S(1)}, u32[]{:S(2)}, u32[]{:S(2)}) %collective-permute-start.6) | collective-permute-done | bytes 1572896 | tf_op jit(solution)/shard_map/ppermute | solution.py:128
  228.8 11.8 %convolution_convert_fusion.3 = bf16[1024,512]{1,0:T(8,128)(2,1)} fusion(bf16[1024,6144]{1,0:T(8,128)(2,1)} %constant_dynamic-update-slice_fusion.17, bf16[6144,512]{1,0:T(8,128)(2,1)S(1)} %constant_dynamic-update-slice_fusion.12), kind=kOutput, calls=%fused_computation.98 | convolution fusion | flops 6442975232 | bytes 19922944 | tf_op jit(solution)/shard_map/dot_general | solution.py:223
  240.6 8.0 %fusion.102 = f32[1024,512]{1,0:T(8,128)} fusion(bf16[1024,6144]{1,0:T(8,128)(2,1)S(1)} %copy-done.9, bf16[6144,512]{1,0:T(8,128)(2,1)S(1)} %constant_dynamic-update-slice_fusion.6), kind=kOutput, calls=%fused_computation.241 | convolution fusion | flops 6442450944 | bytes 20971520 | tf_op jit(solution)/shard_map/dot_general | solution.py:189
  248.7 8.0 %fusion.101 = f32[1024,512]{1,0:T(8,128)} fusion(bf16[1024,6144]{1,0:T(8,128)(2,1)S(1)} %copy-done.9, bf16[6144,512]{1,0:T(8,128)(2,1)S(1)} %constant_dynamic-update-slice_fusion), kind=kOutput, calls=%fused_computation.240 | convolution fusion | flops 6442450944 | bytes 20971520 | tf_op jit(solution)/shard_map/dot_general | solution.py:188
  256.6 15.2 %shard_map.112 = bf16[4,2,128,512]{3,2,1,0:T(8,128)(2,1)} custom-call(f32[4,2,128,512]{3,2,1,0:T(8,128)} %bitcast.52, f32[4,2,128,512]{3,2,1,0:T(8,128)} %bitcast.50, bf16[4,2,128,512]{3,2,1,0:T(8,128)(2,1)} %maximum_select_fusion.4.g_ref, f32[1,128]{1,0:T(1,128)} %bitcast.80, f32[1,128]{1,0:T(1,128)} %bitcast.82), custom_call_target="tpu_custom_call" | custom-call | flops 1073741824 | bytes 6291456 | tf_op jit(solution)/shard_map/pallas_call | solution.py:81
  271.9 17.6 %shard_map.111 = (bf16[4,2,128,512]{3,2,1,0:T(8,128)(2,1)}, bf16[4,2,128,512]{3,2,1,0:T(8,128)(2,1)}) custom-call(f32[4,2,128,512]{3,2,1,0:T(8,128)} %bitcast.53, f32[4,2,128,512]{3,2,1,0:T(8,128)} %bitcast.51, bf16[4,2,128,512]{3,2,1,0:T(8,128)(2,1)} %bitcast.79, bf16[4,2,128,512]{3,2,1,0:T(8,128)(2,1)} %maximum_select_fusion.4.g_ref, f32[1,128]{1,0:T(1,128)} %bitcast.81, ...), custom_call_target="tpu_custom_call" | custom-call | flops 1073741824 | bytes 8388608 | tf_op jit(solution)/shard_map/pallas_call | solution.py:81
  293.7 5.5 fusion.29
  322.5 4.5 fusion.53
  333.5 4.6 fusion.51
  338.1 4.5 fusion.56
  342.6 4.9 fusion.61
  347.6 4.5 fusion.68
  352.1 4.5 fusion.66
  362.2 10.2 %fusion.97 = (bf16[256,6144]{1,0:T(8,128)(2,1)}, f32[256,6144]{1,0:T(8,128)}) fusion(f32[256,6144]{1,0:T(8,128)} %fusion.51, f32[256,6144]{1,0:T(8,128)} %fusion.53, bf16[6144,512]{1,0:T(8,128)(2,1)S(1)} %bitcast.45, bf16[1024,512]{1,0:T(8,128)(2,1)} %bitcast.63, s32[]{:T(128)S(6)} %select_n.185), kind=kOutput, calls=%fused_computation.236 | convolution fusion | flops 1615331328 | bytes 28573700 | tf_op jit(solution)/shard_map/dot_general | solution.py:30
  378.3 10.1 %fusion.98 = (bf16[256,6144]{1,0:T(8,128)(2,1)}, f32[256,6144]{1,0:T(8,128)}) fusion(f32[256,6144]{1,0:T(8,128)} %fusion.56, f32[256,6144]{1,0:T(8,128)} %fusion.58, bf16[6144,512]{1,0:T(8,128)(2,1)S(1)} %bitcast.45, bf16[1024,512]{1,0:T(8,128)(2,1)} %bitcast.64, s32[]{:T(128)S(6)} %select_n.188), kind=kOutput, calls=%fused_computation.237 | convolution fusion | flops 1615331328 | bytes 28573700 | tf_op jit(solution)/shard_map/dot_general | solution.py:30
  394.5 10.1 %fusion.100 = (bf16[256,6144]{1,0:T(8,128)(2,1)}, f32[256,6144]{1,0:T(8,128)}) fusion(f32[256,6144]{1,0:T(8,128)} %fusion.66, f32[256,6144]{1,0:T(8,128)} %fusion.68, bf16[6144,512]{1,0:T(8,128)(2,1)S(1)} %bitcast.45, bf16[1024,512]{1,0:T(8,128)(2,1)} %bitcast.65, s32[]{:T(128)S(6)} %select_n.198), kind=kOutput, calls=%fused_computation.239 | convolution fusion | flops 1615331328 | bytes 28573700 | tf_op jit(solution)/shard_map/dot_general | solution.py:30
  407.2 8.3 %fusion.99 = (bf16[256,6144]{1,0:T(8,128)(2,1)}, f32[256,6144]{1,0:T(8,128)}) fusion(f32[256,6144]{1,0:T(8,128)} %fusion.61, f32[256,6144]{1,0:T(8,128)S(1)} %fusion.63, bf16[6144,512]{1,0:T(8,128)(2,1)S(1)} %bitcast.45, bf16[1024,512]{1,0:T(8,128)(2,1)} %bitcast.66, s32[]{:T(128)S(6)} %select_n.191), kind=kOutput, calls=%fused_computation.238 | convolution fusion | flops 1615331328 | bytes 28573700 | tf_op jit(solution)/shard_map/dot_general | solution.py:30
  450.9 11.8 %collective-permute-done.44 = bf16[768,512]{0,1:T(8,128)(2,1)S(1)} collective-permute-done((bf16[768,512]{0,1:T(8,128)(2,1)}, bf16[768,512]{0,1:T(8,128)(2,1)S(1)}, u32[]{:S(2)}, u32[]{:S(2)}) %collective-permute-start.44) | collective-permute-done | bytes 786464 | tf_op jit(solution)/shard_map/ppermute | solution.py:103
  465.9 10.2 %collective-permute-done.28 = bf16[256,3072]{1,0:T(8,128)(2,1)S(1)} collective-permute-done((bf16[256,3072]{1,0:T(8,128)(2,1)S(1)}, bf16[256,3072]{1,0:T(8,128)(2,1)S(1)}, u32[]{:S(2)}, u32[]{:S(2)}) %collective-permute-start.28) | collective-permute-done | bytes 1572896 | tf_op jit(solution)/shard_map/ppermute | solution.py:128
  489.8 8.6 %collective-permute-done.40 = bf16[1536,512]{0,1:T(8,128)(2,1)} collective-permute-done((bf16[1536,512]{0,1:T(8,128)(2,1)}, bf16[1536,512]{0,1:T(8,128)(2,1)}, u32[]{:S(2)}, u32[]{:S(2)}) %collective-permute-start.40) | collective-permute-done | bytes 1572896 | tf_op jit(solution)/shard_map/ppermute | solution.py:103
  506.4 11.2 %collective-permute-done.29 = bf16[256,3072]{1,0:T(8,128)(2,1)} collective-permute-done((bf16[256,3072]{1,0:T(8,128)(2,1)}, bf16[256,3072]{1,0:T(8,128)(2,1)}, u32[]{:S(2)}, u32[]{:S(2)}) %collective-permute-start.29) | collective-permute-done | bytes 1572896 | tf_op jit(solution)/shard_map/ppermute | solution.py:128
  522.6 10.1 %collective-permute-done.35 = bf16[1536,512]{0,1:T(8,128)(2,1)} collective-permute-done((bf16[1536,512]{0,1:T(8,128)(2,1)S(1)}, bf16[1536,512]{0,1:T(8,128)(2,1)}, u32[]{:S(2)}, u32[]{:S(2)}) %collective-permute-start.35) | collective-permute-done | bytes 1572896 | tf_op jit(solution)/shard_map/ppermute | solution.py:103
  532.6 4.9 collective-permute-start.41
  543.6 22.7 %collective-permute-done.45 = bf16[1536,512]{0,1:T(8,128)(2,1)} collective-permute-done((bf16[1536,512]{0,1:T(8,128)(2,1)}, bf16[1536,512]{0,1:T(8,128)(2,1)}, u32[]{:S(2)}, u32[]{:S(2)}) %collective-permute-start.45) | collective-permute-done | bytes 1572896 | tf_op jit(solution)/shard_map/ppermute | solution.py:103
  (373 shorter events, 253.2 us)
Async XLA Ops:
  28.0 37.4 %collective-permute-start.20 = (bf16[1536,512]{1,0:T(8,128)(2,1)S(1)}, bf16[1536,512]{1,0:T(8,128)(2,1)S(1)}, u32[]{:S(2)}, u32[]{:S(2)}) collective-permute-start(bf16[1536,512]{1,0:T(8,128)(2,1)S(1)} %pad_maximum_fusion.2), channel_id=1, source_target_pairs={{0,16},{4,20},{8,24},{12,28},{16,0},{20,4},{24,8},{28,12},{1,17},{... | collective-permute-start | bytes 4718600 | tf_op jit(solution)/shard_map/ppermute | solution.py:103
  30.6 36.8 %collective-permute-start.19 = (bf16[1536,512]{1,0:T(8,128)(2,1)S(1)}, bf16[1536,512]{1,0:T(8,128)(2,1)S(1)}, u32[]{:S(2)}, u32[]{:S(2)}) collective-permute-start(bf16[1536,512]{1,0:T(8,128)(2,1)S(1)} %pad_maximum_fusion.2), channel_id=1, source_target_pairs={{0,8},{4,12},{8,0},{12,4},{16,24},{20,28},{24,16},{28,20},{1,9},{5... | collective-permute-start | bytes 4718600 | tf_op jit(solution)/shard_map/ppermute | solution.py:103
  31.8 82.3 %collective-permute-start.2 = (bf16[256,3072]{1,0:T(8,128)(2,1)}, bf16[256,3072]{1,0:T(8,128)(2,1)}, u32[]{:S(2)}, u32[]{:S(2)}) collective-permute-start(bf16[256,3072]{1,0:T(8,128)(2,1)} %maximum_select_fusion), channel_id=1, source_target_pairs={{0,2},{2,3},{3,1},{1,0},{4,6},{6,7},{7,5},{5,4},{8,10},{10,11},{11... | collective-permute-start | bytes 4718600 | tf_op jit(solution)/shard_map/ppermute | solution.py:128
  38.5 61.4 %collective-permute-start.9 = (bf16[1536,512]{1,0:T(8,128)(2,1)}, bf16[1536,512]{1,0:T(8,128)(2,1)S(1)}, u32[]{:S(2)}, u32[]{:S(2)}) collective-permute-start(bf16[1536,512]{1,0:T(8,128)(2,1)} %pad_maximum_fusion), channel_id=1, source_target_pairs={{0,8},{4,12},{8,0},{12,4},{16,24},{20,28},{24,16},{28,20},{1,9},{5... | collective-permute-start | bytes 4718600 | tf_op jit(solution)/shard_map/ppermute | solution.py:103
  43.2 72.4 %collective-permute-start.10 = (bf16[1536,512]{1,0:T(8,128)(2,1)}, bf16[1536,512]{1,0:T(8,128)(2,1)}, u32[]{:S(2)}, u32[]{:S(2)}) collective-permute-start(bf16[1536,512]{1,0:T(8,128)(2,1)} %pad_maximum_fusion), channel_id=1, source_target_pairs={{0,16},{4,20},{8,24},{12,28},{16,0},{20,4},{24,8},{28,12},{1,17},{... | collective-permute-start | bytes 4718600 | tf_op jit(solution)/shard_map/ppermute | solution.py:103
  65.4 67.4 %collective-permute-start.15 = (bf16[1536,512]{1,0:T(8,128)(2,1)}, bf16[1536,512]{1,0:T(8,128)(2,1)}, u32[]{:S(2)}, u32[]{:S(2)}) collective-permute-start(bf16[1536,512]{1,0:T(8,128)(2,1)} %pad_maximum_fusion.1), channel_id=1, source_target_pairs={{0,16},{4,20},{8,24},{12,28},{16,0},{20,4},{24,8},{28,12},{1,17},{... | collective-permute-start | bytes 4718600 | tf_op jit(solution)/shard_map/ppermute | solution.py:103
  67.4 67.6 %collective-permute-start.14 = (bf16[1536,512]{1,0:T(8,128)(2,1)}, bf16[1536,512]{1,0:T(8,128)(2,1)}, u32[]{:S(2)}, u32[]{:S(2)}) collective-permute-start(bf16[1536,512]{1,0:T(8,128)(2,1)} %pad_maximum_fusion.1), channel_id=1, source_target_pairs={{0,8},{4,12},{8,0},{12,4},{16,24},{20,28},{24,16},{28,20},{1,9},{5... | collective-permute-start | bytes 4718600 | tf_op jit(solution)/shard_map/ppermute | solution.py:103
  99.9 50.6 %collective-permute-start.22 = (bf16[768,512]{1,0:T(8,128)(2,1)}, bf16[768,512]{1,0:T(8,128)(2,1)}, u32[]{:S(2)}, u32[]{:S(2)}) collective-permute-start(bf16[768,512]{1,0:T(8,128)(2,1)} %slice.491), channel_id=1, source_target_pairs={{0,8},{4,12},{8,0},{12,4},{16,24},{20,28},{24,16},{28,20},{1,9},{5... | collective-permute-start | bytes 2359304 | tf_op jit(solution)/shard_map/ppermute | solution.py:103
  114.1 37.6 %collective-permute-start.21 = (bf16[768,512]{1,0:T(8,128)(2,1)S(1)}, bf16[768,512]{1,0:T(8,128)(2,1)S(1)}, u32[]{:S(2)}, u32[]{:S(2)}) collective-permute-start(bf16[768,512]{1,0:T(8,128)(2,1)S(1)} %copy-done.49), channel_id=1, source_target_pairs={{0,16},{4,20},{8,24},{12,28},{16,0},{20,4},{24,8},{28,12},{1,17},{... | collective-permute-start | bytes 2359304 | tf_op jit(solution)/shard_map/ppermute | solution.py:103
  115.6 50.7 %collective-permute-start.11 = (bf16[768,512]{1,0:T(8,128)(2,1)S(1)}, bf16[768,512]{1,0:T(8,128)(2,1)S(1)}, u32[]{:S(2)}, u32[]{:S(2)}) collective-permute-start(bf16[768,512]{1,0:T(8,128)(2,1)S(1)} %copy-done.48), channel_id=1, source_target_pairs={{0,16},{4,20},{8,24},{12,28},{16,0},{20,4},{24,8},{28,12},{1,17},{... | collective-permute-start | bytes 2359304 | tf_op jit(solution)/shard_map/ppermute | solution.py:103
  132.8 53.3 %collective-permute-start.4 = (bf16[256,3072]{1,0:T(8,128)(2,1)}, bf16[256,3072]{1,0:T(8,128)(2,1)S(1)}, u32[]{:S(2)}, u32[]{:S(2)}) collective-permute-start(bf16[256,3072]{1,0:T(8,128)(2,1)} %collective-permute-done.2), channel_id=1, source_target_pairs={{0,2},{2,3},{3,1},{1,0},{4,6},{6,7},{7,5},{5,4},{8,10},{10,11},{11... | collective-permute-start | bytes 4718600 | tf_op jit(solution)/shard_map/ppermute | solution.py:128
  135.0 55.5 %collective-permute-start.3 = (bf16[256,3072]{1,0:T(8,128)(2,1)}, bf16[256,3072]{1,0:T(8,128)(2,1)S(1)}, u32[]{:S(2)}, u32[]{:S(2)}) collective-permute-start(bf16[256,3072]{1,0:T(8,128)(2,1)} %collective-permute-done.2), channel_id=1, source_target_pairs={{0,4},{4,0},{8,12},{12,8},{16,20},{20,16},{24,28},{28,24},{1,5},{5... | collective-permute-start | bytes 4718600 | tf_op jit(solution)/shard_map/ppermute | solution.py:103
  186.1 35.1 %collective-permute-start.6 = (bf16[256,3072]{1,0:T(8,128)(2,1)S(1)}, bf16[256,3072]{1,0:T(8,128)(2,1)S(1)}, u32[]{:S(2)}, u32[]{:S(2)}) collective-permute-start(bf16[256,3072]{1,0:T(8,128)(2,1)S(1)} %collective-permute-done.4), channel_id=1, source_target_pairs={{0,2},{2,3},{3,1},{1,0},{4,6},{6,7},{7,5},{5,4},{8,10},{10,11},{11... | collective-permute-start | bytes 4718600 | tf_op jit(solution)/shard_map/ppermute | solution.py:128
  188.6 34.8 %collective-permute-start.5 = (bf16[256,3072]{1,0:T(8,128)(2,1)S(1)}, bf16[256,3072]{1,0:T(8,128)(2,1)S(1)}, u32[]{:S(2)}, u32[]{:S(2)}) collective-permute-start(bf16[256,3072]{1,0:T(8,128)(2,1)S(1)} %collective-permute-done.4), channel_id=1, source_target_pairs={{0,4},{4,0},{8,12},{12,8},{16,20},{20,16},{24,28},{28,24},{1,5},{5... | collective-permute-start | bytes 4718600 | tf_op jit(solution)/shard_map/ppermute | solution.py:103
  357.9 77.1 %collective-permute-start.37 = (bf16[768,512]{0,1:T(8,128)(2,1)}, bf16[768,512]{0,1:T(8,128)(2,1)}, u32[]{:S(2)}, u32[]{:S(2)}) collective-permute-start(bf16[768,512]{0,1:T(8,128)(2,1)} %get-tuple-element.56), channel_id=1, source_target_pairs={{0,16},{4,20},{8,24},{12,28},{16,0},{20,4},{24,8},{28,12},{1,17},{... | collective-permute-start | bytes 2359304 | tf_op jit(solution)/shard_map/ppermute | solution.py:103
  358.0 74.4 %collective-permute-start.39 = (bf16[768,512]{0,1:T(8,128)(2,1)}, bf16[768,512]{0,1:T(8,128)(2,1)}, u32[]{:S(2)}, u32[]{:S(2)}) collective-permute-start(bf16[768,512]{0,1:T(8,128)(2,1)} %get-tuple-element.57), channel_id=1, source_target_pairs={{0,8},{4,12},{8,0},{12,4},{16,24},{20,28},{24,16},{28,20},{1,9},{5... | collective-permute-start | bytes 2359304 | tf_op jit(solution)/shard_map/ppermute | solution.py:103
  360.3 87.2 %collective-permute-start.32 = (bf16[768,512]{0,1:T(8,128)(2,1)}, bf16[768,512]{0,1:T(8,128)(2,1)}, u32[]{:S(2)}, u32[]{:S(2)}) collective-permute-start(bf16[768,512]{0,1:T(8,128)(2,1)} %get-tuple-element.60), channel_id=1, source_target_pairs={{0,16},{4,20},{8,24},{12,28},{16,0},{20,4},{24,8},{28,12},{1,17},{... | collective-permute-start | bytes 2359304 | tf_op jit(solution)/shard_map/ppermute | solution.py:103
  361.8 81.8 %collective-permute-start.34 = (bf16[768,512]{0,1:T(8,128)(2,1)}, bf16[768,512]{0,1:T(8,128)(2,1)}, u32[]{:S(2)}, u32[]{:S(2)}) collective-permute-start(bf16[768,512]{0,1:T(8,128)(2,1)} %get-tuple-element.61), channel_id=1, source_target_pairs={{0,8},{4,12},{8,0},{12,4},{16,24},{20,28},{24,16},{28,20},{1,9},{5... | collective-permute-start | bytes 2359304 | tf_op jit(solution)/shard_map/ppermute | solution.py:103
  375.3 62.1 %collective-permute-start.27 = (bf16[256,3072]{1,0:T(8,128)(2,1)}, bf16[256,3072]{1,0:T(8,128)(2,1)}, u32[]{:S(2)}, u32[]{:S(2)}) collective-permute-start(bf16[256,3072]{1,0:T(8,128)(2,1)} %pad_maximum_fusion.6), channel_id=1, source_target_pairs={{0,4},{4,0},{8,12},{12,8},{16,20},{20,16},{24,28},{28,24},{1,5},{5... | collective-permute-start | bytes 4718600 | tf_op jit(solution)/shard_map/ppermute | solution.py:103
  432.3 53.3 %collective-permute-start.42 = (bf16[768,512]{0,1:T(8,128)(2,1)}, bf16[768,512]{0,1:T(8,128)(2,1)}, u32[]{:S(2)}, u32[]{:S(2)}) collective-permute-start(bf16[768,512]{0,1:T(8,128)(2,1)} %get-tuple-element.52), channel_id=1, source_target_pairs={{0,16},{4,20},{8,24},{12,28},{16,0},{20,4},{24,8},{28,12},{1,17},{... | collective-permute-start | bytes 2359304 | tf_op jit(solution)/shard_map/ppermute | solution.py:103
  439.3 36.8 %collective-permute-start.28 = (bf16[256,3072]{1,0:T(8,128)(2,1)S(1)}, bf16[256,3072]{1,0:T(8,128)(2,1)S(1)}, u32[]{:S(2)}, u32[]{:S(2)}) collective-permute-start(bf16[256,3072]{1,0:T(8,128)(2,1)S(1)} %fusion.23), channel_id=1, source_target_pairs={{0,2},{2,3},{3,1},{1,0},{4,6},{6,7},{7,5},{5,4},{8,10},{10,11},{11... | collective-permute-start | bytes 4718600 | tf_op jit(solution)/shard_map/ppermute | solution.py:128
  447.5 58.6 %collective-permute-start.25 = (bf16[256,3072]{1,0:T(8,128)(2,1)}, bf16[256,3072]{1,0:T(8,128)(2,1)}, u32[]{:S(2)}, u32[]{:S(2)}) collective-permute-start(bf16[256,3072]{1,0:T(8,128)(2,1)} %pad_maximum_fusion.4), channel_id=1, source_target_pairs={{0,4},{4,0},{8,12},{12,8},{16,20},{20,16},{24,28},{28,24},{1,5},{5... | collective-permute-start | bytes 4718600 | tf_op jit(solution)/shard_map/ppermute | solution.py:103
  462.7 35.7 %collective-permute-start.40 = (bf16[1536,512]{0,1:T(8,128)(2,1)}, bf16[1536,512]{0,1:T(8,128)(2,1)}, u32[]{:S(2)}, u32[]{:S(2)}) collective-permute-start(bf16[1536,512]{0,1:T(8,128)(2,1)} %pad_maximum_fusion.10), channel_id=1, source_target_pairs={{0,16},{4,20},{8,24},{12,28},{16,0},{20,4},{24,8},{28,12},{1,17},{... | collective-permute-start | bytes 4718600 | tf_op jit(solution)/shard_map/ppermute | solution.py:103
  464.7 34.9 %collective-permute-start.38 = (bf16[1536,512]{0,1:T(8,128)(2,1)}, bf16[1536,512]{0,1:T(8,128)(2,1)}, u32[]{:S(2)}, u32[]{:S(2)}) collective-permute-start(bf16[1536,512]{0,1:T(8,128)(2,1)} %pad_maximum_fusion.9), channel_id=1, source_target_pairs={{0,8},{4,12},{8,0},{12,4},{16,24},{20,28},{24,16},{28,20},{1,9},{5... | collective-permute-start | bytes 4718600 | tf_op jit(solution)/shard_map/ppermute | solution.py:103
  481.2 36.4 %collective-permute-start.29 = (bf16[256,3072]{1,0:T(8,128)(2,1)}, bf16[256,3072]{1,0:T(8,128)(2,1)}, u32[]{:S(2)}, u32[]{:S(2)}) collective-permute-start(bf16[256,3072]{1,0:T(8,128)(2,1)} %fusion.22), channel_id=1, source_target_pairs={{0,2},{2,3},{3,1},{1,0},{4,6},{6,7},{7,5},{5,4},{8,10},{10,11},{11... | collective-permute-start | bytes 4718600 | tf_op jit(solution)/shard_map/ppermute | solution.py:128
  485.6 90.0 %collective-permute-start.24 = (bf16[256,3072]{1,0:T(8,128)(2,1)S(1)}, bf16[256,3072]{1,0:T(8,128)(2,1)S(1)}, u32[]{:S(2)}, u32[]{:S(2)}) collective-permute-start(bf16[256,3072]{1,0:T(8,128)(2,1)S(1)} %copy-done.40), channel_id=1, source_target_pairs={{0,4},{4,0},{8,12},{12,8},{16,20},{20,16},{24,28},{28,24},{1,5},{5... | collective-permute-start | bytes 4718600 | tf_op jit(solution)/shard_map/ppermute | solution.py:103
  498.4 34.3 %collective-permute-start.35 = (bf16[1536,512]{0,1:T(8,128)(2,1)S(1)}, bf16[1536,512]{0,1:T(8,128)(2,1)}, u32[]{:S(2)}, u32[]{:S(2)}) collective-permute-start(bf16[1536,512]{0,1:T(8,128)(2,1)S(1)} %copy-done.42), channel_id=1, source_target_pairs={{0,16},{4,20},{8,24},{12,28},{16,0},{20,4},{24,8},{28,12},{1,17},{... | collective-permute-start | bytes 4718600 | tf_op jit(solution)/shard_map/ppermute | solution.py:103
  499.5 38.0 %collective-permute-start.33 = (bf16[1536,512]{0,1:T(8,128)(2,1)}, bf16[1536,512]{0,1:T(8,128)(2,1)}, u32[]{:S(2)}, u32[]{:S(2)}) collective-permute-start(bf16[1536,512]{0,1:T(8,128)(2,1)} %pad_maximum_fusion.7), channel_id=1, source_target_pairs={{0,8},{4,12},{8,0},{12,4},{16,24},{20,28},{24,16},{28,20},{1,9},{5... | collective-permute-start | bytes 4718600 | tf_op jit(solution)/shard_map/ppermute | solution.py:103
  506.1 60.2 %collective-permute-start.45 = (bf16[1536,512]{0,1:T(8,128)(2,1)}, bf16[1536,512]{0,1:T(8,128)(2,1)}, u32[]{:S(2)}, u32[]{:S(2)}) collective-permute-start(bf16[1536,512]{0,1:T(8,128)(2,1)} %pad_maximum_fusion.12), channel_id=1, source_target_pairs={{0,16},{4,20},{8,24},{12,28},{16,0},{20,4},{24,8},{28,12},{1,17},{... | collective-permute-start | bytes 4718600 | tf_op jit(solution)/shard_map/ppermute | solution.py:103
  517.6 51.4 %collective-permute-start.43 = (bf16[1536,512]{0,1:T(8,128)(2,1)}, bf16[1536,512]{0,1:T(8,128)(2,1)}, u32[]{:S(2)}, u32[]{:S(2)}) collective-permute-start(bf16[1536,512]{0,1:T(8,128)(2,1)} %pad_maximum_fusion.11), channel_id=1, source_target_pairs={{0,8},{4,12},{8,0},{12,4},{16,24},{20,28},{24,16},{28,20},{1,9},{5... | collective-permute-start | bytes 4718600 | tf_op jit(solution)/shard_map/ppermute | solution.py:103
  532.6 44.7 %collective-permute-start.41 = (bf16[768,512]{0,1:T(8,128)(2,1)}, bf16[768,512]{0,1:T(8,128)(2,1)}, u32[]{:S(2)}, u32[]{:S(2)}) collective-permute-start(bf16[768,512]{0,1:T(8,128)(2,1)} %get-tuple-element.55), channel_id=1, source_target_pairs={{0,4},{4,0},{8,12},{12,8},{16,20},{20,16},{24,28},{28,24},{1,5},{5... | collective-permute-start | bytes 2359304 | tf_op jit(solution)/shard_map/ppermute | solution.py:103
  537.5 38.1 %collective-permute-start.30 = (bf16[256,3072]{1,0:T(8,128)(2,1)}, bf16[256,3072]{1,0:T(8,128)(2,1)S(1)}, u32[]{:S(2)}, u32[]{:S(2)}) collective-permute-start(bf16[256,3072]{1,0:T(8,128)(2,1)} %fusion.20), channel_id=1, source_target_pairs={{0,2},{2,3},{3,1},{1,0},{4,6},{6,7},{7,5},{5,4},{8,10},{10,11},{11... | collective-permute-start | bytes 4718600 | tf_op jit(solution)/shard_map/ppermute | solution.py:128
  (83 other events, 958.3 us)

commit v2 on v1

v2 whole, which is shorter than its diff:
```python
import functools

import jax
import jax.numpy as jnp
from jax import lax
from jax.experimental import pallas as pl
from jax.experimental.pallas import tpu as pltpu
from jax.sharding import PartitionSpec as P

PATCH = 256
BF = jnp.bfloat16
F32 = jnp.float32


def normalize(row_data, gain_vector):
    average = jnp.mean(row_data, axis=-1, keepdims=True)
    centred = row_data - average
    inv_spread = lax.rsqrt(jnp.mean(centred * centred, axis=-1, keepdims=True) + 1e-06)
    unit_data = centred * inv_spread
    return (unit_data * gain_vector, unit_data, inv_spread)


def normalize_back(grad_out, unit_data, inv_spread, gain_vector):
    scaled = grad_out * gain_vector
    inner_term = jnp.mean(scaled * unit_data, axis=-1, keepdims=True)
    return (scaled - jnp.mean(scaled, axis=-1, keepdims=True) - unit_data * inner_term) * inv_spread


def dot_nt(a, b):
    return lax.dot_general(a, b, (((1,), (1,)), ((), ())), preferred_element_type=F32)


def dot_tn(a, b):
    return lax.dot_general(a, b, (((0,), (0,)), ((), ())), preferred_element_type=F32)


def attention_of(query_bf, key_bf):
    scores = dot_nt(key_bf, query_bf) * query_bf.shape[-1] ** (-0.5)
    raised = jnp.exp(scores - jnp.max(scores, axis=0, keepdims=True))
    return raised * (1.0 / jnp.sum(raised, axis=0, keepdims=True))


def first_kernel(q_ref, k_ref, g_ref, q_gain_ref, k_gain_ref, grad_value_ref, turned_ref):
    query_bf = normalize(q_ref[...], q_gain_ref[...])[0].astype(BF)
    key_bf = normalize(k_ref[...], k_gain_ref[...])[0].astype(BF)
    attention = attention_of(query_bf, key_bf).astype(BF)
    grad_value = jnp.dot(attention, g_ref[...], preferred_element_type=F32)
    grad_value_ref[...] = grad_value.astype(BF)
    turned_ref[...] = grad_value.T.astype(BF)


def rest_kernel(
    q_ref, k_ref, v_ref, g_ref, q_gain_ref, k_gain_ref, grad_q_ref, turned_q_ref, grad_k_ref, turned_k_ref
):
    q_gain, k_gain = q_gain_ref[...], k_gain_ref[...]
    query_normed, query_unit, query_spread = normalize(q_ref[...], q_gain)
    key_normed, key_unit, key_spread = normalize(k_ref[...], k_gain)
    query_bf, key_bf = query_normed.astype(BF), key_normed.astype(BF)
    attention = attention_of(query_bf, key_bf)
    grad_probs = dot_nt(v_ref[...], g_ref[...])
    delta = jnp.sum(attention * grad_probs, axis=0, keepdims=True)
    factor = query_bf.shape[-1] ** (-0.5)
    grad_scores = (attention * (grad_probs - delta) * factor).astype(BF)
    grad_kn = jnp.dot(grad_scores, query_bf, preferred_element_type=F32)
    grad_qn = dot_tn(grad_scores, key_bf)
    grad_query = normalize_back(grad_qn, query_unit, query_spread, q_gain)
    grad_key = normalize_back(grad_kn, key_unit, key_spread, k_gain)
    grad_q_ref[...] = grad_query.astype(BF)
    turned_q_ref[...] = grad_query.T.astype(BF)
    grad_k_ref[...] = grad_key.astype(BF)
    turned_k_ref[...] = grad_key.T.astype(BF)


def attention_call(kernel, arrays, gains, n_out):
    tokens, columns = arrays[0].shape
    head = gains[0].shape[-1]
    block = pl.BlockSpec((PATCH, head), lambda i, h: (i, h))
    turned = pl.BlockSpec((head, PATCH), lambda i, h: (h, i))
    gain_block = pl.BlockSpec((1, head), lambda i, h: (0, 0))
    pairs = (tokens // PATCH) * (columns // head)
    return pl.pallas_call(
        kernel,
        grid=(tokens // PATCH, columns // head),
        in_specs=[block] * len(arrays) + [gain_block] * len(gains),
        out_specs=[block, turned] * n_out,
        out_shape=[
            jax.ShapeDtypeStruct((tokens, columns), BF),
            jax.ShapeDtypeStruct((columns, tokens), BF),
        ]
        * n_out,
        cost_estimate=pl.CostEstimate(
            flops=pairs * 8 * PATCH * PATCH * head,
            bytes_accessed=4 * len(arrays) * arrays[0].size,
            transcendentals=pairs * PATCH * PATCH,
        ),
    )(*arrays, *[gain.reshape(1, head) for gain in gains])


def per_device(n_dp, n_mp, tokens, norm_gain, q_gain, k_gain, w_query, w_key, w_value, grad_heads):
    own, width = tokens.shape
    rows, cols = w_query.shape[0], w_query.shape[1] // 2
    n_chips = n_dp // 2
    group = n_mp * own
    place = lax.axis_index("dp")
    core = place & 1

    def swap(array, bit):
        return lax.ppermute(array, "dp", [(i, i ^ bit) for i in range(n_dp)])

    def half(array, which):
        return lax.dynamic_slice_in_dim(array, which * cols, cols, 1)

    def after(arrays, *others):
        flat, tree = jax.tree.flatten(arrays)
        done = lax.optimization_barrier((*flat, *jax.tree.leaves(others)))
        return jax.tree.unflatten(tree, done[: len(flat)])

    def add(a, b):
        return a.astype(F32) + b.astype(F32)

    ring = list(range(0, n_mp, 2)) + list(range(n_mp - 1, 0, -2))
    level = lax.axis_index("mp")
    spot = jnp.where(level % 2 == 0, level // 2, n_mp - 1 - level // 2)
    ring_pairs = [(ring[i], ring[(i + 1) % n_mp]) for i in range(n_mp)]

    def level_at(back):
        at = (spot + 2 * n_mp - back) % n_mp
        return jnp.where(at < n_mp // 2, 2 * at, 2 * (n_mp - 1 - at) + 1)

    def ring_on(arrays):
        return [lax.ppermute(array, "mp", ring_pairs) for array in arrays]

    def feature_block(array, r):
        return lax.dynamic_slice_in_dim(array, (place ^ r) * rows, rows, 1)

    def pieces_of(weight):
        return {0: half(weight, core), 1: swap(half(weight, 1 - core), 1)}

    def gather_start(held):
        held = dict(held)
        bit = 8
        while bit < n_dp:
            held.update({r ^ bit: swap(part, bit) for r, part in list(held.items())})
            bit *= 2
        for r, part in list(held.items()):
            held[r ^ 2] = swap(part, 2)
            held[r ^ 4] = swap(part, 4)
        return held

    def gather_rest(held):
        held = dict(held)
        for r in range(0, n_dp, 8):
            held[r ^ 6] = swap(held[r ^ 2], 4)
            held[r ^ 7] = swap(held[r ^ 5], 2)
        return held

    def relayed(held):
        return [held[r ^ f] for r in range(0, n_dp, 8) for f in (6, 7)]

    def whole(held):
        return jnp.concatenate([held[r] for r in (*range(0, n_dp, 2), *range(1, n_dp, 2))], axis=0)

    held_query = gather_start(pieces_of(w_query))

    normed_own, unit_rows, row_spread = normalize(tokens.astype(F32), norm_gain)
    normed_own = normed_own.astype(BF)
    even = jnp.concatenate([feature_block(normed_own, r) for r in range(0, n_dp, 2)], axis=1)
    odd = jnp.concatenate([feature_block(normed_own, r) for r in range(1, n_dp, 2)], axis=1)
    blocks = [even, swap(odd, 1)]

    held_key = gather_start(after(pieces_of(w_key), even))
    value_pieces = pieces_of(w_value)
    grads_mine = half(grad_heads, core)
    grads_other = swap(half(grad_heads, 1 - core), 1)

    normed = jnp.zeros((2 * group, width), BF)

    def put(normed, blocks, step):
        start = level_at(step) * own
        mine, other = core * group + start, (1 - core) * group + start
        beside_other, beside_mine = (swap(block, 1) for block in blocks)
        for block, at, column in (
            (blocks[0], mine, 0),
            (blocks[1], other, 0),
            (beside_other, other, width // 2),
            (beside_mine, mine, width // 2),
        ):
            normed = lax.dynamic_update_slice(normed, block, (at, column))
        return normed

    grad_out = jnp.zeros((2 * group, cols), BF)
    grad_out = lax.dynamic_update_slice_in_dim(grad_out, grads_mine, core * group, 0)
    grad_out = lax.dynamic_update_slice_in_dim(grad_out, grads_other, (1 - core) * group, 0)

    normed = put(normed, blocks, 0)
    for step in range(1, n_mp):
        blocks = ring_on(blocks)
        if step == 1:
            held_query, blocks, normed = after((held_query, blocks, normed))
            held_query = gather_rest(held_query)
        elif step == 2:
            held_key, blocks = after((held_key, blocks))
            held_key = gather_rest(held_key)
            held_value = gather_start(after(value_pieces, relayed(held_query)))
        normed = put(normed, blocks, step)
    normed, held_query, held_key = after((normed, held_query, held_key))
    full_query, full_key = whole(held_query), whole(held_key)

    queries = jnp.dot(normed, full_query, preferred_element_type=F32)
    key_proj = jnp.dot(normed, full_key, preferred_element_type=F32)
    gains = (q_gain, k_gain)
    grad_value, turned_value = attention_call(first_kernel, (queries, key_proj, grad_out), gains, 1)

    def product(turned, r):
        unit = (r & 1) * n_chips + r // 2
        side = normed[:, unit * rows : (unit + 1) * rows]
        return jnp.dot(turned, side, preferred_element_type=F32)

    def scatter_start(turned):
        state = {}
        for r in range(0, n_dp, 8):
            far = [product(turned, r ^ f).astype(BF) for f in (6, 7)]
            state[r, "far"] = [swap(far[0], 2), swap(far[1], 4)]
            next_x, next_y = [product(turned, r ^ f).astype(BF) for f in (2, 5)]
            state[r, "sent"] = [swap(next_x, 2), swap(next_y, 4)]
            state[r, "next"] = [product(turned, r ^ f) for f in (3, 4)]
            state[r, "own"] = [product(turned, r ^ f) for f in (0, 1)]
        return state

    def scatter_rest(state):
        state = dict(state)
        for r in range(0, n_dp, 8):
            from_x, from_y = state[r, "far"]
            next_x, next_y = state[r, "next"]
            next_x, next_y = add(next_x, from_y).astype(BF), add(next_y, from_x).astype(BF)
            state[r, "late"] = [swap(next_x, 2), swap(next_y, 4)]
        return state

    def scatter_end(state):
        totals = {}
        for r in range(0, n_dp, 8):
            own_even, own_odd = state[r, "own"]
            even_x, odd_y = state[r, "sent"]
            odd_x, even_y = state[r, "late"]
            totals[r] = [add(own_even, even_x) + even_y, add(own_odd, odd_x) + odd_y]
        bit = n_dp // 2
        while bit >= 8:
            for r in [r for r in totals if r < bit]:
                passed = [swap(total.astype(BF), bit) for total in totals.pop(r ^ bit)]
                totals[r] = [add(a, b) for a, b in zip(totals[r], passed)]
            bit //= 2
        mine, other = [total.astype(BF) for total in totals[0]]
        result = jnp.zeros((2 * cols, rows), BF)
        result = lax.dynamic_update_slice_in_dim(result, mine, core * cols, 0)
        result = lax.dynamic_update_slice_in_dim(result, swap(other, 1), (1 - core) * cols, 0)
        return result.T

    def computed(state):
        return [state[key] for key in state if key[1] in ("next", "own")]

    held_value, turned_value = after((held_value, turned_value))
    held_value = gather_rest(held_value)
    state_value = scatter_start(turned_value)

    full_value = whole(after(held_value, computed(state_value)))
    values = jnp.dot(normed, full_value, preferred_element_type=F32).astype(BF)
    grad_query, turned_query, grad_key, turned_key = attention_call(
        rest_kernel, (queries, key_proj, values, grad_out), gains, 2
    )

    state_value, turned_query = after((state_value, turned_query), turned_key)
    state_value = scatter_rest(state_value)
    state_query = scatter_start(turned_query)

    grads = after([grad_query, grad_key, grad_value], computed(state_query))
    grads = [grad.reshape(2, n_mp, own, cols) for grad in grads]
    arrived = None
    for step in range(n_mp):
        at = level_at(step + 1)
        partial = None
        for grad, weight in zip(grads, (full_query, full_key, full_value)):
            chosen = lax.dynamic_slice_in_dim(grad, at, 1, 1).reshape(2 * own, cols)
            term = dot_nt(chosen, weight)
            partial = term if partial is None else partial + term
        sent = partial[:, width // 2 :].astype(BF)
        if step == 0:
            state_key = scatter_start(after(turned_key, sent))
            grads = after(grads, computed(state_key))
        elif step == 1:
            state_query = scatter_rest(after(state_query, sent))
        elif step == n_mp - 2:
            state_key = scatter_rest(after(state_key, sent))
        kept = add(partial[:, : width // 2], swap(sent, 1))
        if arrived is not None:
            kept = add(kept, arrived)
        if step < n_mp - 1:
            (arrived,) = ring_on([kept.astype(BF)])

    out_value, out_query, out_key = (
        scatter_end(state) for state in (state_value, state_query, state_key)
    )

    mine = lax.dynamic_slice_in_dim(kept, core * own, own, 0)
    other = swap(lax.dynamic_slice_in_dim(kept, (1 - core) * own, own, 0).astype(BF), 1).astype(F32)
    units = jnp.concatenate([mine, other], axis=1)
    ordered = []
    for b in range(n_dp):
        r = b ^ place
        unit = (r & 1) * n_chips + r // 2
        ordered.append(lax.dynamic_slice_in_dim(units, unit * rows, rows, 1))
    grad_normed = jnp.concatenate(ordered, axis=1)
    grad_tokens = normalize_back(grad_normed, unit_rows, row_spread, norm_gain).astype(BF)
    return (grad_tokens, out_query, out_key, out_value)


def solution(mesh):
    matrix = P("dp", "mp")
    token_rows = P(("dp", "mp"), None)
    return jax.shard_map(
        functools.partial(per_device, mesh.shape["dp"], mesh.shape["mp"]),
        mesh=mesh,
        in_specs=(token_rows, P(), P(), P(), matrix, matrix, matrix, matrix),
        out_specs=(token_rows, matrix, matrix, matrix),
        check_vma=False,
    )
```

time: 612 us -> 582 us (0.951)
  waiting for transfers between devices: 197 us -> 145 us
  matrix products: 146 us -> 170 us
  starting transfers between devices: 57 us -> 80.9 us
  other arithmetic: 66.1 us -> 49.5 us
  local copies, waits for them, and re-layouts: 100 us -> 91.8 us
    ppermute x41 -> x57, waiting for transfers between devices: 151 us -> 84 us  [swap(): return lax.ppermute(array, 'dp', [(i, i ^ bit) for i in range(n_dp)])]
    dot_general x15 -> x27, matrix products: 73.1 us -> 99.8 us  [the longest x24 76.2 us: product(): return jnp.dot(turned, side, preferred_element_type=F32)]
    unnamed x195 -> x159, local copies, waits for them, and re-layouts: 46.4 us -> 21.1 us
    convert_element_type x3 -> x15, other arithmetic: 9.54 us -> 34.5 us  [the longest x6 13.6 us: scatter_end(): mine, other = [total.astype(BF) for total in totals[0]]]
    select_n x5 -> x0, other arithmetic: 21.4 us -> none  [core_order(): jnp.where(core == 0, jnp.concatenate([mine, other], axis=axis), jnp.conca...]
    slice x26 -> x4, local copies, waits for them, and re-layouts: 30.8 us -> 10.1 us  [per_device(): sent = partial[:, width // 2:].astype(BF)]
    dynamic_update_slice x4 -> x22, local copies, waits for them, and re-layouts: 10.1 us -> 30.6 us  [the longest x15 22.4 us: put(): normed = lax.dynamic_update_slice(normed, block, (at, column))]
    ppermute x41 -> x57, starting transfers between devices: 43.3 us -> 61.9 us  [swap(): return lax.ppermute(array, 'dp', [(i, i ^ bit) for i in range(n_dp)])]
  transfers between devices with their start and end apart: 47 -> 66, of which waited for: 15 -> 20; matrix products, arithmetic and copies ran while one was open for 32% -> 35% of each run, Pallas kernels for 0% -> 6%
where the time goes in v2:
time: 582 us; the launch traced here: 574 us
  matrix products  170 us (29%)
  waiting for transfers between devices  145 us (25%)
  local copies, waits for them, and re-layouts  91.8 us (16%)
  starting transfers between devices  80.9 us (14%)
  other arithmetic  49.5 us (9%)
  Pallas kernels  34.3 us (6%)
    ppermute x57, waiting for transfers between devices, swap(): return lax.ppermute(array, 'dp', [(i, i ^ bit) for i in range(n_dp)])  84 us
    dot_general x24, matrix products, product(): return jnp.dot(turned, side, preferred_element_type=F32)  76.2 us
    dot_general x12, matrix products, dot_nt(): lax.dot_general(a, b, (((1,), (1,)), ((), ())), preferred_element_type=F32)  70.5 us
    ppermute x57, starting transfers between devices, swap(): return lax.ppermute(array, 'dp', [(i, i ^ bit) for i in range(n_dp)])  61.9 us
    ppermute x9, waiting for transfers between devices, ring_on(): return [lax.ppermute(array, 'mp', ring_pairs) for array in arrays]  61.4 us
    pallas_call x2, Pallas kernels, attention_call(): pl.pallas_call(kernel, grid=(tokens // PATCH, columns // head), in_specs=...  34.3 us
    dynamic_update_slice x15, local copies, waits for them, and re-layouts, put(): normed = lax.dynamic_update_slice(normed, block, (at, column))  22.4 us
    unnamed x159, local copies, waits for them, and re-layouts  21.1 us
  transfers between devices with their start and end apart: 66, of which 20 were waited for; matrix products, arithmetic and copies ran while one was open for 35% of the time, Pallas kernels for 6%

profile of v2, /device:TPU:1, one launch (start us, length us, event | category | flops | bytes accessed | tf_op | source)
XLA Modules:
  0.0 574.2 jit_solution(11237851237525634172)
XLA Ops:
  14.8 6.2 %broadcast_in_dim.4 = bf16[1024,6144]{1,0:T(8,128)(2,1)} broadcast(bf16[]{:T(256)} %constant.163.clone.1), dimensions={} | broadcast | bytes 12582914 | tf_op jit(solution)/shard_map/broadcast_in_dim | solution.py:176
  37.2 4.5 collective-permute-done.5
  47.4 11.2 %collective-permute-done.7 = bf16[128,3072]{1,0:T(8,128)(2,1)} collective-permute-done((bf16[128,3072]{1,0:T(8,128)(2,1)}, bf16[128,3072]{1,0:T(8,128)(2,1)}, u32[]{:S(2)}, u32[]{:S(2)}) %collective-permute-start.7) | collective-permute-done | bytes 786464 | tf_op jit(solution)/shard_map/ppermute | solution.py:131
  63.5 5.2 collective-permute-done.15
  72.4 4.6 collective-permute-done.13
  80.1 5.4 collective-permute-done.16
  86.6 7.2 %collective-permute-done.14 = bf16[768,512]{1,0:T(8,128)(2,1)} collective-permute-done((bf16[768,512]{1,0:T(8,128)(2,1)}, bf16[768,512]{1,0:T(8,128)(2,1)}, u32[]{:S(2)}, u32[]{:S(2)}) %collective-permute-start.14) | collective-permute-done | bytes 786464 | tf_op jit(solution)/shard_map/ppermute | solution.py:108
  105.7 5.7 collective-permute-done.25
  126.5 13.4 %collective-permute-done.22 = bf16[128,3072]{1,0:T(8,128)(2,1)S(1)} collective-permute-done((bf16[128,3072]{1,0:T(8,128)(2,1)}, bf16[128,3072]{1,0:T(8,128)(2,1)S(1)}, u32[]{:S(2)}, u32[]{:S(2)}) %collective-permute-start.22) | collective-permute-done | bytes 786464 | tf_op jit(solution)/shard_map/ppermute | solution.py:131
  147.0 7.5 %collective-permute-done.27 = bf16[768,512]{1,0:T(8,128)(2,1)S(1)} collective-permute-done((bf16[768,512]{1,0:T(8,128)(2,1)}, bf16[768,512]{1,0:T(8,128)(2,1)S(1)}, u32[]{:S(2)}, u32[]{:S(2)}) %collective-permute-start.27) | collective-permute-done | bytes 786464 | tf_op jit(solution)/shard_map/ppermute | solution.py:108
  164.6 7.9 %fusion.69.q_ref = f32[1024,512]{1,0:T(8,128)} fusion(bf16[1024,6144]{1,0:T(8,128)(2,1)S(1)} %bitcast.87, bf16[6144,512]{1,0:T(8,128)(2,1)S(1)} %get-tuple-element.215), kind=kOutput, calls=%fused_computation.212 | convolution fusion | flops 6442450944 | bytes 20971520 | tf_op jit(solution)/shard_map/dot_general | solution.py:209
  172.5 8.0 %fusion.70.k_ref = f32[1024,512]{1,0:T(8,128)} fusion(bf16[1024,6144]{1,0:T(8,128)(2,1)S(1)} %bitcast.87, bf16[6144,512]{1,0:T(8,128)(2,1)S(1)} %get-tuple-element.216), kind=kOutput, calls=%fused_computation.213 | convolution fusion | flops 6442450944 | bytes 20971520 | tf_op jit(solution)/shard_map/dot_general | solution.py:210
  180.6 16.2 %shard_map.111 = (bf16[1024,512]{1,0:T(8,128)(2,1)}, bf16[512,1024]{1,0:T(8,128)(2,1)}) custom-call(f32[1024,512]{1,0:T(8,128)} %fusion.69.q_ref, f32[1024,512]{1,0:T(8,128)} %fusion.70.k_ref, bf16[1024,512]{1,0:T(8,128)(2,1)} %copy-done.7, f32[1,128]{1,0:T(1,128)} %bitcast.109, f32[1,128]{1,0:T(1,128)} %bitcast.111), custom_call_target="tpu_custom_call" | custom-call | flops 1073741824 | bytes 6291456 | tf_op jit(solution)/shard_map/pallas_call | solution.py:81
  222.5 8.2 %collective-permute-done.35 = bf16[768,512]{1,0:T(8,128)(2,1)S(1)} collective-permute-done((bf16[768,512]{1,0:T(8,128)(2,1)}, bf16[768,512]{1,0:T(8,128)(2,1)S(1)}, u32[]{:S(2)}, u32[]{:S(2)}) %collective-permute-start.35) | collective-permute-done | bytes 786464 | tf_op jit(solution)/shard_map/ppermute | solution.py:108
  240.4 7.6 %convolution_convert_fusion.v_ref = bf16[1024,512]{1,0:T(8,128)(2,1)} fusion(bf16[1024,6144]{1,0:T(8,128)(2,1)S(1)} %bitcast.89, bf16[6144,512]{1,0:T(8,128)(2,1)S(1)} %constant_dynamic-update-slice_fusion.16), kind=kOutput, calls=%fused_computation.65 | convolution fusion | flops 6442975232 | bytes 19922944 | tf_op jit(solution)/shard_map/dot_general | solution.py:266
  248.0 18.1 %shard_map.112 = (bf16[1024,512]{1,0:T(8,128)(2,1)}, bf16[512,1024]{1,0:T(8,128)(2,1)}, bf16[1024,512]{1,0:T(8,128)(2,1)}, bf16[512,1024]{1,0:T(8,128)(2,1)}) custom-call(f32[1024,512]{1,0:T(8,128)} %fusion.69.q_ref, f32[1024,512]{1,0:T(8,128)} %fusion.70.k_ref, bf16[1024,512]{1,0:T(8,128)(2,1)} %convolution_convert_fusion.v_ref, ...), custom_call_target="tpu_custom_call" | custom-call | flops 1073741824 | bytes 8388608 | tf_op jit(solution)/shard_map/pallas_call | solution.py:81
  296.1 4.5 fusion.71
  300.7 7.8 %convolution_add_fusion.7 = f32[256,6144]{1,0:T(8,128)} fusion(f32[256,6144]{1,0:T(8,128)} %fusion.71, bf16[256,512]{1,0:T(8,128)(2,1)S(1)} %bitcast.98, bf16[6144,512]{1,0:T(8,128)(2,1)S(1)} %bitcast.77), kind=kOutput, calls=%fused_computation.7 | convolution fusion | flops 1612185600 | bytes 19136512 | tf_op jit(solution)/shard_map/dot_general | solution.py:30
  308.4 7.6 %convolution_add_fusion.6 = f32[256,6144]{1,0:T(8,128)} fusion(f32[256,6144]{1,0:T(8,128)} %convolution_add_fusion.7, bf16[256,512]{1,0:T(8,128)(2,1)S(1)} %bitcast.97, bf16[6144,512]{1,0:T(8,128)(2,1)S(1)} %bitcast.79), kind=kOutput, calls=%fused_computation.6 | convolution fusion | flops 1612185600 | bytes 19136512 | tf_op jit(solution)/shard_map/dot_general | solution.py:30
  346.1 4.5 collective-permute-start.44
  354.3 4.5 fusion.73
  363.2 4.5 fusion.72
  367.7 7.6 %convolution_add_fusion.1 = f32[256,6144]{1,0:T(8,128)} fusion(f32[256,6144]{1,0:T(8,128)} %fusion.74, bf16[256,512]{1,0:T(8,128)(2,1)} %bitcast.95, bf16[6144,512]{1,0:T(8,128)(2,1)S(1)} %bitcast.77), kind=kOutput, calls=%fused_computation.1 | convolution fusion | flops 1612185600 | bytes 19136512 | tf_op jit(solution)/shard_map/dot_general | solution.py:30
  375.3 8.1 %convolution_add_fusion = f32[256,6144]{1,0:T(8,128)} fusion(f32[256,6144]{1,0:T(8,128)} %convolution_add_fusion.1, bf16[256,512]{1,0:T(8,128)(2,1)} %bitcast.96, bf16[6144,512]{1,0:T(8,128)(2,1)S(1)} %bitcast.79), kind=kOutput, calls=%fused_computation | convolution fusion | flops 1612185600 | bytes 19136512 | tf_op jit(solution)/shard_map/dot_general | solution.py:30
  387.5 5.7 convolution_add_fusion.3
  393.3 7.8 %convolution_add_fusion.2 = f32[256,6144]{1,0:T(8,128)} fusion(f32[256,6144]{1,0:T(8,128)} %convolution_add_fusion.3, bf16[256,512]{1,0:T(8,128)(2,1)} %bitcast.94, bf16[6144,512]{1,0:T(8,128)(2,1)S(1)} %bitcast.79), kind=kOutput, calls=%fused_computation.2 | convolution fusion | flops 1612185600 | bytes 19136512 | tf_op jit(solution)/shard_map/dot_general | solution.py:30
  405.5 4.7 convolution_add_fusion.5
  422.0 19.3 %collective-permute-done.45 = bf16[256,3072]{1,0:T(8,128)(2,1)} collective-permute-done((bf16[256,3072]{1,0:T(8,128)(2,1)}, bf16[256,3072]{1,0:T(8,128)(2,1)}, u32[]{:S(2)}, u32[]{:S(2)}) %collective-permute-start.45) | collective-permute-done | bytes 1572896 | tf_op jit(solution)/shard_map/ppermute | solution.py:131
  445.9 9.6 %collective-permute-done.58 = bf16[512,768]{1,0:T(8,128)(2,1)S(1)} collective-permute-done((bf16[512,768]{1,0:T(8,128)(2,1)}, bf16[512,768]{1,0:T(8,128)(2,1)S(1)}, u32[]{:S(2)}, u32[]{:S(2)}) %collective-permute-start.58) | collective-permute-done | bytes 786464 | tf_op jit(solution)/shard_map/ppermute | solution.py:108
  456.9 14.9 %collective-permute-done.59 = bf16[512,768]{1,0:T(8,128)(2,1)S(1)} collective-permute-done((bf16[512,768]{1,0:T(8,128)(2,1)}, bf16[512,768]{1,0:T(8,128)(2,1)S(1)}, u32[]{:S(2)}, u32[]{:S(2)}) %collective-permute-start.59) | collective-permute-done | bytes 786464 | tf_op jit(solution)/shard_map/ppermute | solution.py:108
  485.8 7.6 %collective-permute-done.64 = bf16[512,768]{1,0:T(8,128)(2,1)S(1)} collective-permute-done((bf16[512,768]{1,0:T(8,128)(2,1)S(1)}, bf16[512,768]{1,0:T(8,128)(2,1)S(1)}, u32[]{:S(2)}, u32[]{:S(2)}) %collective-permute-start.64) | collective-permute-done | bytes 786464 | tf_op jit(solution)/shard_map/ppermute | solution.py:108
  499.7 7.2 %collective-permute-done.46 = bf16[256,3072]{1,0:T(8,128)(2,1)S(1)} collective-permute-done((bf16[256,3072]{1,0:T(8,128)(2,1)S(1)}, bf16[256,3072]{1,0:T(8,128)(2,1)S(1)}, u32[]{:S(2)}, u32[]{:S(2)}) %collective-permute-start.46) | collective-permute-done | bytes 1572896 | tf_op jit(solution)/shard_map/ppermute | solution.py:131
  (396 shorter events, 309.2 us)
Async XLA Ops:
  30.1 28.6 %collective-permute-start.7 = (bf16[128,3072]{1,0:T(8,128)(2,1)}, bf16[128,3072]{1,0:T(8,128)(2,1)}, u32[]{:S(2)}, u32[]{:S(2)}) collective-permute-start(bf16[128,3072]{1,0:T(8,128)(2,1)} %collective-permute-done.6), channel_id=1, source_target_pairs={{0,2},{2,3},{3,1},{1,0},{4,6},{6,7},{7,5},{5,4},{8,10},{10,11},{11... | collective-permute-start | bytes 2359304 | tf_op jit(solution)/shard_map/ppermute | solution.py:131
  59.2 34.7 %collective-permute-start.14 = (bf16[768,512]{1,0:T(8,128)(2,1)}, bf16[768,512]{1,0:T(8,128)(2,1)}, u32[]{:S(2)}, u32[]{:S(2)}) collective-permute-start(bf16[768,512]{1,0:T(8,128)(2,1)} %collective-permute-done.12), channel_id=1, source_target_pairs={{0,8},{4,12},{8,0},{12,4},{16,24},{20,28},{24,16},{28,20},{1,9},{5... | collective-permute-start | bytes 2359304 | tf_op jit(solution)/shard_map/ppermute | solution.py:108
  60.4 33.7 %collective-permute-start.17 = (bf16[128,3072]{1,0:T(8,128)(2,1)}, bf16[128,3072]{1,0:T(8,128)(2,1)}, u32[]{:S(2)}, u32[]{:S(2)}) collective-permute-start(bf16[128,3072]{1,0:T(8,128)(2,1)} %collective-permute-done.5), channel_id=1, source_target_pairs={{0,2},{2,3},{3,1},{1,0},{4,6},{6,7},{7,5},{5,4},{8,10},{10,11},{11... | collective-permute-start | bytes 2359304 | tf_op jit(solution)/shard_map/ppermute | solution.py:131
  85.5 31.8 %collective-permute-start.10 = (bf16[128,3072]{1,0:T(8,128)(2,1)}, bf16[128,3072]{1,0:T(8,128)(2,1)S(1)}, u32[]{:S(2)}, u32[]{:S(2)}) collective-permute-start(bf16[128,3072]{1,0:T(8,128)(2,1)} %collective-permute-done.5), channel_id=1, source_target_pairs={{0,4},{4,0},{8,12},{12,8},{16,20},{20,16},{24,28},{28,24},{1,5},{5... | collective-permute-start | bytes 2359304 | tf_op jit(solution)/shard_map/ppermute | solution.py:108
  118.6 78.2 %collective-permute-start.32 = (bf16[768,512]{1,0:T(8,128)(2,1)S(1)}, bf16[768,512]{1,0:T(8,128)(2,1)}, u32[]{:S(2)}, u32[]{:S(2)}) collective-permute-start(bf16[768,512]{1,0:T(8,128)(2,1)S(1)} %get-tuple-element.141), channel_id=1, source_target_pairs={{0,16},{4,20},{8,24},{12,28},{16,0},{20,4},{24,8},{28,12},{1,17},{... | collective-permute-start | bytes 2359304 | tf_op jit(solution)/shard_map/ppermute | solution.py:108
  125.0 29.5 %collective-permute-start.27 = (bf16[768,512]{1,0:T(8,128)(2,1)}, bf16[768,512]{1,0:T(8,128)(2,1)S(1)}, u32[]{:S(2)}, u32[]{:S(2)}) collective-permute-start(bf16[768,512]{1,0:T(8,128)(2,1)} %collective-permute-done.13), channel_id=1, source_target_pairs={{0,16},{4,20},{8,24},{12,28},{16,0},{20,4},{24,8},{28,12},{1,17},{... | collective-permute-start | bytes 2359304 | tf_op jit(solution)/shard_map/ppermute | solution.py:108
  126.2 28.5 %collective-permute-start.28 = (bf16[768,512]{1,0:T(8,128)(2,1)}, bf16[768,512]{1,0:T(8,128)(2,1)S(1)}, u32[]{:S(2)}, u32[]{:S(2)}) collective-permute-start(bf16[768,512]{1,0:T(8,128)(2,1)} %collective-permute-done.16), channel_id=1, source_target_pairs={{0,8},{4,12},{8,0},{12,4},{16,24},{20,28},{24,16},{28,20},{1,9},{5... | collective-permute-start | bytes 2359304 | tf_op jit(solution)/shard_map/ppermute | solution.py:108
  143.5 53.3 %collective-permute-start.30 = (bf16[768,512]{1,0:T(8,128)(2,1)S(1)}, bf16[768,512]{1,0:T(8,128)(2,1)}, u32[]{:S(2)}, u32[]{:S(2)}) collective-permute-start(bf16[768,512]{1,0:T(8,128)(2,1)S(1)} %get-tuple-element.141), channel_id=1, source_target_pairs={{0,8},{4,12},{8,0},{12,4},{16,24},{20,28},{24,16},{28,20},{1,9},{5... | collective-permute-start | bytes 2359304 | tf_op jit(solution)/shard_map/ppermute | solution.py:108
  144.7 52.0 %collective-permute-start.33 = (bf16[768,512]{1,0:T(8,128)(2,1)}, bf16[768,512]{1,0:T(8,128)(2,1)}, u32[]{:S(2)}, u32[]{:S(2)}) collective-permute-start(bf16[768,512]{1,0:T(8,128)(2,1)} %collective-permute-done.29), channel_id=1, source_target_pairs={{0,16},{4,20},{8,24},{12,28},{16,0},{20,4},{24,8},{28,12},{1,17},{... | collective-permute-start | bytes 2359304 | tf_op jit(solution)/shard_map/ppermute | solution.py:108
  154.5 42.3 %collective-permute-start.31 = (bf16[768,512]{1,0:T(8,128)(2,1)}, bf16[768,512]{1,0:T(8,128)(2,1)S(1)}, u32[]{:S(2)}, u32[]{:S(2)}) collective-permute-start(bf16[768,512]{1,0:T(8,128)(2,1)} %collective-permute-done.29), channel_id=1, source_target_pairs={{0,8},{4,12},{8,0},{12,4},{16,24},{20,28},{24,16},{28,20},{1,9},{5... | collective-permute-start | bytes 2359304 | tf_op jit(solution)/shard_map/ppermute | solution.py:108
  217.9 48.2 %collective-permute-start.37 = (bf16[512,768]{1,0:T(8,128)(2,1)}, bf16[512,768]{1,0:T(8,128)(2,1)}, u32[]{:S(2)}, u32[]{:S(2)}) collective-permute-start(bf16[512,768]{1,0:T(8,128)(2,1)} %convolution_convert_fusion.12), channel_id=1, source_target_pairs={{0,8},{4,12},{8,0},{12,4},{16,24},{20,28},{24,16},{28,20},{1,9},{5... | collective-permute-start | bytes 2359304 | tf_op jit(solution)/shard_map/ppermute | solution.py:108
  218.2 48.0 %collective-permute-start.38 = (bf16[512,768]{1,0:T(8,128)(2,1)}, bf16[512,768]{1,0:T(8,128)(2,1)}, u32[]{:S(2)}, u32[]{:S(2)}) collective-permute-start(bf16[512,768]{1,0:T(8,128)(2,1)} %convolution_convert_fusion.11), channel_id=1, source_target_pairs={{0,16},{4,20},{8,24},{12,28},{16,0},{20,4},{24,8},{28,12},{1,17},{... | collective-permute-start | bytes 2359304 | tf_op jit(solution)/shard_map/ppermute | solution.py:108
  218.2 48.0 %collective-permute-start.39 = (bf16[512,768]{1,0:T(8,128)(2,1)}, bf16[512,768]{1,0:T(8,128)(2,1)}, u32[]{:S(2)}, u32[]{:S(2)}) collective-permute-start(bf16[512,768]{1,0:T(8,128)(2,1)} %convolution_convert_fusion.10), channel_id=1, source_target_pairs={{0,8},{4,12},{8,0},{12,4},{16,24},{20,28},{24,16},{28,20},{1,9},{5... | collective-permute-start | bytes 2359304 | tf_op jit(solution)/shard_map/ppermute | solution.py:108
  230.8 35.4 %collective-permute-start.40 = (bf16[512,768]{1,0:T(8,128)(2,1)}, bf16[512,768]{1,0:T(8,128)(2,1)}, u32[]{:S(2)}, u32[]{:S(2)}) collective-permute-start(bf16[512,768]{1,0:T(8,128)(2,1)} %convolution_convert_fusion.9), channel_id=1, source_target_pairs={{0,16},{4,20},{8,24},{12,28},{16,0},{20,4},{24,8},{28,12},{1,17},{... | collective-permute-start | bytes 2359304 | tf_op jit(solution)/shard_map/ppermute | solution.py:108
  346.1 55.0 %collective-permute-start.44 = (bf16[256,3072]{1,0:T(8,128)(2,1)S(1)}, bf16[256,3072]{1,0:T(8,128)(2,1)}, u32[]{:S(2)}, u32[]{:S(2)}) collective-permute-start(bf16[256,3072]{1,0:T(8,128)(2,1)S(1)} %slice.163), channel_id=1, source_target_pairs={{0,4},{4,0},{8,12},{12,8},{16,20},{20,16},{24,28},{28,24},{1,5},{5... | collective-permute-start | bytes 4718600 | tf_op jit(solution)/shard_map/ppermute | solution.py:108
  350.6 68.5 %collective-permute-start.49 = (bf16[512,768]{1,0:T(8,128)(2,1)}, bf16[512,768]{1,0:T(8,128)(2,1)}, u32[]{:S(2)}, u32[]{:S(2)}) collective-permute-start(bf16[512,768]{1,0:T(8,128)(2,1)} %convolution_convert_fusion.8), channel_id=1, source_target_pairs={{0,8},{4,12},{8,0},{12,4},{16,24},{20,28},{24,16},{28,20},{1,9},{5... | collective-permute-start | bytes 2359304 | tf_op jit(solution)/shard_map/ppermute | solution.py:108
  351.8 68.3 %collective-permute-start.56 = (bf16[512,768]{1,0:T(8,128)(2,1)}, bf16[512,768]{1,0:T(8,128)(2,1)}, u32[]{:S(2)}, u32[]{:S(2)}) collective-permute-start(bf16[512,768]{1,0:T(8,128)(2,1)} %convolution_convert_fusion.4), channel_id=1, source_target_pairs={{0,8},{4,12},{8,0},{12,4},{16,24},{20,28},{24,16},{28,20},{1,9},{5... | collective-permute-start | bytes 2359304 | tf_op jit(solution)/shard_map/ppermute | solution.py:108
  352.0 69.3 %collective-permute-start.57 = (bf16[512,768]{1,0:T(8,128)(2,1)}, bf16[512,768]{1,0:T(8,128)(2,1)}, u32[]{:S(2)}, u32[]{:S(2)}) collective-permute-start(bf16[512,768]{1,0:T(8,128)(2,1)} %convolution_convert_fusion.3), channel_id=1, source_target_pairs={{0,16},{4,20},{8,24},{12,28},{16,0},{20,4},{24,8},{28,12},{1,17},{... | collective-permute-start | bytes 2359304 | tf_op jit(solution)/shard_map/ppermute | solution.py:108
  386.7 35.1 %collective-permute-start.43 = (bf16[256,3072]{1,0:T(8,128)(2,1)}, bf16[256,3072]{1,0:T(8,128)(2,1)}, u32[]{:S(2)}, u32[]{:S(2)}) collective-permute-start(bf16[256,3072]{1,0:T(8,128)(2,1)} %slice.160), channel_id=1, source_target_pairs={{0,4},{4,0},{8,12},{12,8},{16,20},{20,16},{24,28},{28,24},{1,5},{5... | collective-permute-start | bytes 4718600 | tf_op jit(solution)/shard_map/ppermute | solution.py:108
  405.1 36.3 %collective-permute-start.45 = (bf16[256,3072]{1,0:T(8,128)(2,1)}, bf16[256,3072]{1,0:T(8,128)(2,1)}, u32[]{:S(2)}, u32[]{:S(2)}) collective-permute-start(bf16[256,3072]{1,0:T(8,128)(2,1)} %fusion.11), channel_id=1, source_target_pairs={{0,2},{2,3},{3,1},{1,0},{4,6},{6,7},{7,5},{5,4},{8,10},{10,11},{11... | collective-permute-start | bytes 4718600 | tf_op jit(solution)/shard_map/ppermute | solution.py:131
  419.0 56.6 %collective-permute-start.50 = (bf16[512,768]{1,0:T(8,128)(2,1)}, bf16[512,768]{1,0:T(8,128)(2,1)S(1)}, u32[]{:S(2)}, u32[]{:S(2)}) collective-permute-start(bf16[512,768]{1,0:T(8,128)(2,1)} %convolution_convert_fusion.7), channel_id=1, source_target_pairs={{0,16},{4,20},{8,24},{12,28},{16,0},{20,4},{24,8},{28,12},{1,17},{... | collective-permute-start | bytes 2359304 | tf_op jit(solution)/shard_map/ppermute | solution.py:108
  420.1 56.8 %collective-permute-start.51 = (bf16[512,768]{1,0:T(8,128)(2,1)S(1)}, bf16[512,768]{1,0:T(8,128)(2,1)S(1)}, u32[]{:S(2)}, u32[]{:S(2)}) collective-permute-start(bf16[512,768]{1,0:T(8,128)(2,1)S(1)} %copy-done.50), channel_id=1, source_target_pairs={{0,8},{4,12},{8,0},{12,4},{16,24},{20,28},{24,16},{28,20},{1,9},{5... | collective-permute-start | bytes 2359304 | tf_op jit(solution)/shard_map/ppermute | solution.py:108
  421.3 56.7 %collective-permute-start.52 = (bf16[512,768]{1,0:T(8,128)(2,1)S(1)}, bf16[512,768]{1,0:T(8,128)(2,1)S(1)}, u32[]{:S(2)}, u32[]{:S(2)}) collective-permute-start(bf16[512,768]{1,0:T(8,128)(2,1)S(1)} %copy-done.49), channel_id=1, source_target_pairs={{0,16},{4,20},{8,24},{12,28},{16,0},{20,4},{24,8},{28,12},{1,17},{... | collective-permute-start | bytes 2359304 | tf_op jit(solution)/shard_map/ppermute | solution.py:108
  421.8 33.7 %collective-permute-start.58 = (bf16[512,768]{1,0:T(8,128)(2,1)}, bf16[512,768]{1,0:T(8,128)(2,1)S(1)}, u32[]{:S(2)}, u32[]{:S(2)}) collective-permute-start(bf16[512,768]{1,0:T(8,128)(2,1)} %convolution_convert_fusion.2), channel_id=1, source_target_pairs={{0,8},{4,12},{8,0},{12,4},{16,24},{20,28},{24,16},{28,20},{1,9},{5... | collective-permute-start | bytes 2359304 | tf_op jit(solution)/shard_map/ppermute | solution.py:108
  441.4 30.5 %collective-permute-start.59 = (bf16[512,768]{1,0:T(8,128)(2,1)}, bf16[512,768]{1,0:T(8,128)(2,1)S(1)}, u32[]{:S(2)}, u32[]{:S(2)}) collective-permute-start(bf16[512,768]{1,0:T(8,128)(2,1)} %convolution_convert_fusion.1), channel_id=1, source_target_pairs={{0,16},{4,20},{8,24},{12,28},{16,0},{20,4},{24,8},{28,12},{1,17},{... | collective-permute-start | bytes 2359304 | tf_op jit(solution)/shard_map/ppermute | solution.py:108
  455.5 43.8 %collective-permute-start.42 = (bf16[256,3072]{1,0:T(8,128)(2,1)}, bf16[256,3072]{1,0:T(8,128)(2,1)S(1)}, u32[]{:S(2)}, u32[]{:S(2)}) collective-permute-start(bf16[256,3072]{1,0:T(8,128)(2,1)} %slice.161), channel_id=1, source_target_pairs={{0,4},{4,0},{8,12},{12,8},{16,20},{20,16},{24,28},{28,24},{1,5},{5... | collective-permute-start | bytes 4718600 | tf_op jit(solution)/shard_map/ppermute | solution.py:108
  471.9 35.0 %collective-permute-start.46 = (bf16[256,3072]{1,0:T(8,128)(2,1)S(1)}, bf16[256,3072]{1,0:T(8,128)(2,1)S(1)}, u32[]{:S(2)}, u32[]{:S(2)}) collective-permute-start(bf16[256,3072]{1,0:T(8,128)(2,1)S(1)} %fusion.13), channel_id=1, source_target_pairs={{0,2},{2,3},{3,1},{1,0},{4,6},{6,7},{7,5},{5,4},{8,10},{10,11},{11... | collective-permute-start | bytes 4718600 | tf_op jit(solution)/shard_map/ppermute | solution.py:131
  478.0 60.1 %collective-permute-start.41 = (bf16[256,3072]{1,0:T(8,128)(2,1)}, bf16[256,3072]{1,0:T(8,128)(2,1)S(1)}, u32[]{:S(2)}, u32[]{:S(2)}) collective-permute-start(bf16[256,3072]{1,0:T(8,128)(2,1)} %slice.162), channel_id=1, source_target_pairs={{0,4},{4,0},{8,12},{12,8},{16,20},{20,16},{24,28},{28,24},{1,5},{5... | collective-permute-start | bytes 4718600 | tf_op jit(solution)/shard_map/ppermute | solution.py:108
  499.3 27.9 %collective-permute-start.54 = (bf16[512,768]{1,0:T(8,128)(2,1)}, bf16[512,768]{1,0:T(8,128)(2,1)}, u32[]{:S(2)}, u32[]{:S(2)}) collective-permute-start(bf16[512,768]{1,0:T(8,128)(2,1)} %add_convert_fusion.9), channel_id=1, source_target_pairs={{0,8},{4,12},{8,0},{12,4},{16,24},{20,28},{24,16},{28,20},{1,9},{5... | collective-permute-start | bytes 2359304 | tf_op jit(solution)/shard_map/ppermute | solution.py:108
  508.7 34.8 %collective-permute-start.47 = (bf16[256,3072]{1,0:T(8,128)(2,1)}, bf16[256,3072]{1,0:T(8,128)(2,1)}, u32[]{:S(2)}, u32[]{:S(2)}) collective-permute-start(bf16[256,3072]{1,0:T(8,128)(2,1)} %fusion.15), channel_id=1, source_target_pairs={{0,2},{2,3},{3,1},{1,0},{4,6},{6,7},{7,5},{5,4},{8,10},{10,11},{11... | collective-permute-start | bytes 4718600 | tf_op jit(solution)/shard_map/ppermute | solution.py:131
  527.2 31.4 %collective-permute-start.62 = (bf16[512,768]{1,0:T(8,128)(2,1)}, bf16[512,768]{1,0:T(8,128)(2,1)}, u32[]{:S(2)}, u32[]{:S(2)}) collective-permute-start(bf16[512,768]{1,0:T(8,128)(2,1)} %add_convert_fusion.4), channel_id=1, source_target_pairs={{0,4},{4,0},{8,12},{12,8},{16,20},{20,16},{24,28},{28,24},{1,5},{5... | collective-permute-start | bytes 2359304 | tf_op jit(solution)/shard_map/ppermute | solution.py:108
  532.8 28.1 %collective-permute-start.55 = (bf16[512,768]{1,0:T(8,128)(2,1)}, bf16[512,768]{1,0:T(8,128)(2,1)}, u32[]{:S(2)}, u32[]{:S(2)}) collective-permute-start(bf16[512,768]{1,0:T(8,128)(2,1)} %add_convert_fusion.8), channel_id=1, source_target_pairs={{0,4},{4,0},{8,12},{12,8},{16,20},{20,16},{24,28},{28,24},{1,5},{5... | collective-permute-start | bytes 2359304 | tf_op jit(solution)/shard_map/ppermute | solution.py:108
  (103 other events, 1296.6 us)

commit v3 on v2

v3 whole, which is shorter than its diff:
```python
import functools

import jax
import jax.numpy as jnp
from jax import lax
from jax.experimental import pallas as pl
from jax.experimental.pallas import tpu as pltpu
from jax.sharding import PartitionSpec as P

PATCH = 256
BF = jnp.bfloat16
F32 = jnp.float32


def normalize(row_data, gain_vector):
    average = jnp.mean(row_data, axis=-1, keepdims=True)
    centred = row_data - average
    inv_spread = lax.rsqrt(jnp.mean(centred * centred, axis=-1, keepdims=True) + 1e-06)
    unit_data = centred * inv_spread
    return (unit_data * gain_vector, unit_data, inv_spread)


def normalize_back(grad_out, unit_data, inv_spread, gain_vector):
    scaled = grad_out * gain_vector
    inner_term = jnp.mean(scaled * unit_data, axis=-1, keepdims=True)
    return (scaled - jnp.mean(scaled, axis=-1, keepdims=True) - unit_data * inner_term) * inv_spread


def dot_nt(a, b):
    return lax.dot_general(a, b, (((1,), (1,)), ((), ())), preferred_element_type=F32)


def dot_tn(a, b):
    return lax.dot_general(a, b, (((0,), (0,)), ((), ())), preferred_element_type=F32)


def params(mib):
    return pltpu.CompilerParams(vmem_limit_bytes=mib * 2**20)


def blank(shape, dtype):
    return pl.pallas_call(
        lambda out_ref: None,
        out_shape=jax.ShapeDtypeStruct(shape, dtype),
        out_specs=pl.BlockSpec(memory_space=pl.ANY),
    )()


def attention_of(query_bf, key_bf):
    scores = dot_nt(key_bf, query_bf) * query_bf.shape[-1] ** (-0.5)
    raised = jnp.exp(scores - jnp.max(scores, axis=0, keepdims=True))
    return raised * (1.0 / jnp.sum(raised, axis=0, keepdims=True))


def first_kernel(qk_ref, g_ref, gains_ref, turned_ref):
    head, cols = gains_ref.shape[1], g_ref.shape[1]
    for h in range(cols // head):
        at, key_at = pl.ds(h * head, head), pl.ds(cols + h * head, head)
        query_bf = normalize(qk_ref[:, at], gains_ref[0:1])[0].astype(BF)
        key_bf = normalize(qk_ref[:, key_at], gains_ref[1:2])[0].astype(BF)
        attention = attention_of(query_bf, key_bf).astype(BF)
        grad_value = jnp.dot(attention, g_ref[:, at], preferred_element_type=F32)
        turned_ref[at, :] = grad_value.T.astype(BF)


def rest_kernel(qk_ref, g_ref, v_ref, gains_ref, turned_ref):
    head, cols = gains_ref.shape[1], g_ref.shape[1]
    factor = head ** (-0.5)
    q_gain, k_gain = gains_ref[0:1], gains_ref[1:2]
    for h in range(cols // head):
        at, key_at = pl.ds(h * head, head), pl.ds(cols + h * head, head)
        query_normed, query_unit, query_spread = normalize(qk_ref[:, at], q_gain)
        key_normed, key_unit, key_spread = normalize(qk_ref[:, key_at], k_gain)
        query_bf, key_bf = query_normed.astype(BF), key_normed.astype(BF)
        attention = attention_of(query_bf, key_bf)
        grad_probs = dot_nt(v_ref[:, at], g_ref[:, at])
        delta = jnp.sum(attention * grad_probs, axis=0, keepdims=True)
        grad_scores = (attention * (grad_probs - delta) * factor).astype(BF)
        grad_kn = jnp.dot(grad_scores, query_bf, preferred_element_type=F32)
        grad_qn = dot_tn(grad_scores, key_bf)
        grad_query = normalize_back(grad_qn, query_unit, query_spread, q_gain)
        grad_key = normalize_back(grad_kn, key_unit, key_spread, k_gain)
        turned_ref[at, :] = grad_query.T.astype(BF)
        turned_ref[key_at, :] = grad_key.T.astype(BF)


def attention_call(kernel, arrays, gains, out_rows):
    tokens, columns = arrays[1].shape
    head = gains.shape[-1]
    pairs = (tokens // PATCH) * (columns // head)
    return pl.pallas_call(
        kernel,
        grid=(tokens // PATCH,),
        in_specs=[pl.BlockSpec((PATCH, array.shape[1]), lambda i: (i, 0)) for array in arrays]
        + [pl.BlockSpec(gains.shape, lambda i: (0, 0))],
        out_specs=pl.BlockSpec((out_rows, PATCH), lambda i: (0, i)),
        out_shape=jax.ShapeDtypeStruct((out_rows, tokens), BF),
        compiler_params=params(32),
        cost_estimate=pl.CostEstimate(
            flops=pairs * 8 * PATCH * PATCH * head,
            bytes_accessed=4 * len(arrays) * arrays[0].size,
            transcendentals=pairs * PATCH * PATCH,
        ),
    )(*arrays, gains)


def product_kernel(n_add, turn, turned_ref, *refs):
    turned = turned_ref[...]
    outs = refs[-2:]
    for side in range(2):
        total = jnp.dot(turned, refs[side][...], preferred_element_type=F32)
        for ref in refs[2 + side * n_add : 2 + (side + 1) * n_add]:
            total = total + ref[...].astype(F32)
        outs[side][...] = (total.T if turn else total).astype(BF)


def product_call(turned, normed, rows, units, addends=((), ()), turn=False):
    columns, tokens = turned.shape
    tile = 256 if rows % 256 == 0 else 128
    n_add, steps = len(addends[0]), rows // tile
    wide = pl.BlockSpec((columns, tile), lambda i: (0, i))
    tall = pl.BlockSpec((tile, columns), lambda i: (i, 0))

    def side(unit):
        return pl.BlockSpec((tokens, tile), lambda i: (0, unit * steps + i))

    shape = (rows, columns) if turn else (columns, rows)
    return pl.pallas_call(
        functools.partial(product_kernel, n_add, turn),
        grid=(steps,),
        in_specs=[pl.BlockSpec((columns, tokens), lambda i: (0, 0)), side(units[0]), side(units[1])]
        + [wide] * (2 * n_add),
        out_specs=[tall if turn else wide] * 2,
        out_shape=[jax.ShapeDtypeStruct(shape, BF)] * 2,
        compiler_params=params(24),
        cost_estimate=pl.CostEstimate(
            flops=4 * columns * tokens * rows,
            bytes_accessed=2 * (columns * tokens + 2 * tokens * rows + (2 + 2 * n_add) * columns * rows),
            transcendentals=0,
        ),
    )(turned, normed, normed, *addends[0], *addends[1])


def back_kernel(pair_ref, value_ref, w_pair_ref, w_value_ref, *refs):
    total = jnp.dot(w_pair_ref[...], pair_ref[...], preferred_element_type=F32)
    total = total + jnp.dot(w_value_ref[...], value_ref[...], preferred_element_type=F32)
    for ref in refs[:-1]:
        total = total + ref[...].astype(F32)
    refs[-1][...] = total.astype(refs[-1].dtype)


def back_call(pair, value, w_pair, w_value, rows, odd, addends, dtype):
    level_tokens = pair.shape[1]
    units = w_pair.shape[0] // rows // 2
    first = units if odd else 0
    block = pl.BlockSpec((rows, level_tokens), lambda i: (i, 0))
    return pl.pallas_call(
        back_kernel,
        grid=(units,),
        in_specs=[
            pl.BlockSpec(pair.shape, lambda i: (0, 0)),
            pl.BlockSpec(value.shape, lambda i: (0, 0)),
            pl.BlockSpec((rows, w_pair.shape[1]), lambda i: (first + i, 0)),
            pl.BlockSpec((rows, w_value.shape[1]), lambda i: (first + i, 0)),
        ]
        + [block] * len(addends),
        out_specs=block,
        out_shape=jax.ShapeDtypeStruct((units * rows, level_tokens), dtype),
        compiler_params=params(24),
        cost_estimate=pl.CostEstimate(
            flops=2 * units * rows * level_tokens * (pair.shape[0] + value.shape[0]),
            bytes_accessed=2 * units * rows * (pair.shape[0] + value.shape[0] + 3 * level_tokens),
            transcendentals=0,
        ),
    )(pair, value, w_pair, w_value, *addends)


def place_kernel(core_ref, mine_ref, other_ref, out_ref):
    here = pl.program_id(0) == core_ref[0]

    @pl.when(here)
    def _():
        out_ref[...] = mine_ref[...]

    @pl.when(jnp.logical_not(here))
    def _():
        out_ref[...] = other_ref[...]


def place_call(core, mine, other, cols, part):
    rows = mine.shape[0]
    block = pl.BlockSpec((rows, cols), lambda i, core_ref: (0, part))
    return pl.pallas_call(
        place_kernel,
        grid_spec=pltpu.PrefetchScalarGridSpec(
            num_scalar_prefetch=1,
            grid=(2,),
            in_specs=[block, block],
            out_specs=pl.BlockSpec((rows, cols), lambda i, core_ref: (0, i)),
        ),
        out_shape=jax.ShapeDtypeStruct((rows, 2 * cols), BF),
        compiler_params=params(16),
    )(core.reshape(1), mine, other)


def per_device(n_dp, n_mp, tokens, norm_gain, q_gain, k_gain, w_query, w_key, w_value, grad_heads):
    own, width = tokens.shape
    rows, cols = w_query.shape[0], w_query.shape[1] // 2
    n_chips = n_dp // 2
    group = n_mp * own
    place = lax.axis_index("dp")
    core = place & 1

    def swap(array, bit):
        return lax.ppermute(array, "dp", [(i, i ^ bit) for i in range(n_dp)])

    def half(array, which):
        return lax.dynamic_slice_in_dim(array, which * cols, cols, 1)

    def after(arrays, *others):
        flat, tree = jax.tree.flatten(arrays)
        done = lax.optimization_barrier((*flat, *jax.tree.leaves(others)))
        return jax.tree.unflatten(tree, done[: len(flat)])

    ring = list(range(0, n_mp, 2)) + list(range(n_mp - 1, 0, -2))
    level = lax.axis_index("mp")
    spot = jnp.where(level & 1 == 0, level >> 1, n_mp - 1 - (level >> 1))
    ring_pairs = [(ring[i], ring[(i + 1) % n_mp]) for i in range(n_mp)]

    def level_at(back):
        at = lax.rem(spot + 2 * n_mp - back, n_mp)
        return jnp.where(at < n_mp // 2, 2 * at, 2 * (n_mp - 1 - at) + 1)

    def ring_on(array):
        return lax.ppermute(array, "mp", ring_pairs)

    def unit_of(r):
        return (r & 1) * n_chips + (r >> 1)

    def feature_block(array, r):
        return lax.dynamic_slice_in_dim(array, (place ^ r) * rows, rows, 1)

    weights = (w_query, w_key, w_value)
    other_rows = swap(jnp.concatenate([half(w, 1 - core) for w in weights], axis=1), 1)
    own_rows = jnp.concatenate([half(w, core) for w in weights], axis=1)
    shard_pair, shard_value = (
        jnp.concatenate([own_rows[:, at], other_rows[:, at]], axis=0)
        for at in (slice(0, 2 * cols), slice(2 * cols, None))
    )

    def gather_start(shard):
        held = {0: shard}
        bit = 8
        while bit < n_dp:
            held.update({r ^ bit: swap(part, bit) for r, part in list(held.items())})
            bit *= 2
        for r, part in list(held.items()):
            held[r ^ 2] = swap(part, 2)
            held[r ^ 4] = swap(part, 4)
        return held

    def gather_rest(held):
        relays = {}
        for r in range(0, n_dp, 8):
            relays[r ^ 6] = swap(held[r ^ 2][:rows], 4)
            relays[r ^ 7] = swap(held[r ^ 4][rows:], 2)
        return relays

    def whole(held, relays):
        pieces = dict(relays)
        for r, part in held.items():
            pieces[r], pieces[r ^ 1] = part[:rows], part[rows:]
        return jnp.concatenate([pieces[r] for r in (*range(0, n_dp, 2), *range(1, n_dp, 2))], axis=0)

    held_pair = gather_start(shard_pair)

    normed_own, unit_rows, row_spread = normalize(tokens.astype(F32), norm_gain)
    normed_own = normed_own.astype(BF)
    even = jnp.concatenate([feature_block(normed_own, r) for r in range(0, n_dp, 2)], axis=1)
    odd = jnp.concatenate([feature_block(normed_own, r) for r in range(1, n_dp, 2)], axis=1)
    block = jnp.concatenate([even, swap(odd, 1)], axis=0)

    normed = blank((2 * group, width), BF)

    def put(normed, block, step):
        beside = swap(block, 1)
        start = level_at(step) * own
        mine, other = core * group + start, (1 - core) * group + start
        for piece, at, column in (
            (block[:own], mine, 0),
            (block[own:], other, 0),
            (beside[:own], other, width // 2),
            (beside[own:], mine, width // 2),
        ):
            normed = lax.dynamic_update_slice(normed, piece, (at, column))
        return normed

    normed = put(normed, block, 0)
    relays_pair = None
    for step in range(1, n_mp):
        block = ring_on(block)
        normed = put(normed, block, step)
        if step == 1:
            held_pair, normed = after((held_pair, normed))
            relays_pair = gather_rest(held_pair)
    held_value = gather_start(after(shard_value, relays_pair))

    grads_other = swap(half(grad_heads, 1 - core), 1)
    grad_out = blank((2 * group, cols), BF)
    grad_out = lax.dynamic_update_slice_in_dim(grad_out, half(grad_heads, core), core * group, 0)
    grad_out = lax.dynamic_update_slice_in_dim(grad_out, grads_other, (1 - core) * group, 0)
    gains = jnp.stack([q_gain, k_gain])

    full_pair = whole(held_pair, relays_pair)
    pair = jnp.dot(normed, full_pair, preferred_element_type=F32)
    turned_value = attention_call(first_kernel, (pair, grad_out), gains, cols)

    def products(turned, r, offsets, addends=((), ()), turn=False):
        return product_call(
            turned, normed, rows, [unit_of(r ^ f) for f in offsets], addends, turn
        )

    def scatter_far(turned):
        sent = {}
        for r in range(0, n_dp, 8):
            far_even, far_odd = products(turned, r, (6, 7))
            sent[r] = [swap(far_even, 2), swap(far_odd, 4)]
        return sent

    def scatter_early(turned):
        sent = {}
        for r in range(0, n_dp, 8):
            even_x, odd_y = products(turned, r, (2, 5))
            sent[r] = [swap(even_x, 2), swap(odd_y, 4)]
        return sent

    def scatter_late(turned, far):
        sent = {}
        for r in range(0, n_dp, 8):
            from_x, from_y = far[r]
            odd_x, even_y = products(turned, r, (3, 4), ((from_y,), (from_x,)))
            sent[r] = [swap(odd_x, 2), swap(even_y, 4)]
        return sent

    def scatter_end(turned, early, late):
        if n_dp == 8:
            (even_x, odd_y), (odd_x, even_y) = early[0], late[0]
            return products(turned, 0, (0, 1), ((even_x, even_y), (odd_x, odd_y)), True)
        totals = {}
        for r in range(0, n_dp, 8):
            (even_x, odd_y), (odd_x, even_y) = early[r], late[r]
            totals[r] = products(turned, r, (0, 1), ((even_x, even_y), (odd_x, odd_y)))
        bit = n_dp // 2
        while bit >= 8:
            for r in [r for r in totals if r < bit]:
                passed = [swap(total, bit) for total in totals.pop(r ^ bit)]
                totals[r] = [
                    (a.astype(F32) + b.astype(F32)).astype(BF) for a, b in zip(totals[r], passed)
                ]
            bit //= 2
        return [total.T for total in totals[0]]

    held_value, turned_value = after((held_value, turned_value))
    relays_value = gather_rest(held_value)
    far_value = scatter_far(turned_value)
    early_value = scatter_early(turned_value)
    full_value = whole(held_value, relays_value)
    values = jnp.dot(normed, full_value, preferred_element_type=F32).astype(BF)
    turned_pair = attention_call(rest_kernel, (pair, grad_out, values), gains, 2 * cols)

    turned_pair, turned_value, far_value = after((turned_pair, turned_value, far_value))
    late_value = scatter_late(turned_value, far_value)

    def back_odd(step):
        at = level_at(step + 1) * own
        chosen = [
            jnp.concatenate(
                [lax.dynamic_slice_in_dim(turned, g * group + at, own, 1) for g in range(2)], axis=1
            )
            for turned in (turned_pair, turned_value)
        ]
        sent = back_call(*chosen, full_pair, full_value, rows, True, (), BF)
        return chosen, swap(sent, 1)

    def back_even(chosen, passed, arrived, dtype):
        addends = (passed,) if arrived is None else (passed, arrived)
        return back_call(*chosen, full_pair, full_value, rows, False, addends, dtype)

    arrived = None
    for step in range(n_mp):
        last = step == n_mp - 1
        chosen, passed = back_odd(step)
        total = back_even(chosen, passed, arrived, F32 if last else BF)
        if not last:
            arrived = ring_on(total)
        if step == 0:
            far_pair = scatter_far(after(turned_pair, total))
            early_pair = scatter_early(turned_pair)
        elif step == 1:
            turned_late, far_pair = after((turned_pair, far_pair), total)
            late_pair = scatter_late(turned_late, far_pair)

    mine = lax.dynamic_slice_in_dim(total, core * own, own, 1)
    other = swap(lax.dynamic_slice_in_dim(total, (1 - core) * own, own, 1).astype(BF), 1).astype(F32)
    units = jnp.concatenate([mine, other], axis=0).T
    ordered = [
        lax.dynamic_slice_in_dim(units, unit_of(b ^ place) * rows, rows, 1) for b in range(n_dp)
    ]
    grad_normed = jnp.concatenate(ordered, axis=1)
    grad_tokens = normalize_back(grad_normed, unit_rows, row_spread, norm_gain).astype(BF)

    mine, other = scatter_end(turned_value, early_value, late_value)
    out_value = place_call(core, mine, swap(other, 1), cols, 0)
    mine, other = scatter_end(turned_pair, early_pair, late_pair)
    other = swap(other, 1)
    out_query, out_key = (place_call(core, mine, other, cols, part) for part in range(2))
    return (grad_tokens, out_query, out_key, out_value)


def solution(mesh):
    matrix = P("dp", "mp")
    token_rows = P(("dp", "mp"), None)
    return jax.shard_map(
        functools.partial(per_device, mesh.shape["dp"], mesh.shape["mp"]),
        mesh=mesh,
        in_specs=(token_rows, P(), P(), P(), matrix, matrix, matrix, matrix),
        out_specs=(token_rows, matrix, matrix, matrix),
        check_vma=False,
    )
```

time: 582 us -> 534 us (0.918)
  matrix products: 170 us -> 25.5 us
  waiting for transfers between devices: 145 us -> 231 us
  Pallas kernels: 34.3 us -> 107 us
  other arithmetic: 49.5 us -> 16.4 us
  starting transfers between devices: 80.9 us -> 54.6 us
    dot_general x38 -> x1, matrix products: 163 us -> 13.1 us  [per_device(): pair = jnp.dot(normed, full_pair, preferred_element_type=F32)]
    pallas_call x2 -> x23, Pallas kernels: 34.3 us -> 107 us  [the longest x8 44.3 us: back_call(): pl.pallas_call(back_kernel, grid=(units,), in_specs=[pl.BlockSpec(pair.sh...]
    ppermute x9 -> x6, waiting for transfers between devices: 61.4 us -> 108 us  [ring_on(): return lax.ppermute(array, 'mp', ring_pairs)]
    ppermute x57 -> x34, waiting for transfers between devices: 84 us -> 123 us  [swap(): return lax.ppermute(array, 'dp', [(i, i ^ bit) for i in range(n_dp)])]
    convert_element_type x16 -> x1, other arithmetic: 35.8 us -> 1.28 us  [per_device(): swap(lax.dynamic_slice_in_dim(total, (1 - core) * own, own, 1).astype(BF)...]
    unnamed x159 -> x126, local copies, waits for them, and re-layouts: 21.1 us -> 54 us
    ppermute x57 -> x34, starting transfers between devices: 61.9 us -> 37.3 us  [swap(): return lax.ppermute(array, 'dp', [(i, i ^ bit) for i in range(n_dp)])]
    dynamic_update_slice x21 -> x15, local copies, waits for them, and re-layouts: 30.5 us -> 16.3 us  [put(): normed = lax.dynamic_update_slice(normed, piece, (at, column))]
  transfers between devices with their start and end apart: 66 -> 40, of which waited for: 20 -> 16; matrix products, arithmetic and copies ran while one was open for 35% -> 13% of each run, Pallas kernels for 6% -> 19%
where the time goes in v3:
time: 534 us; the launch traced here: 528 us
  waiting for transfers between devices  231 us (43%)
  Pallas kernels  107 us (20%)
  local copies, waits for them, and re-layouts  92.7 us (17%)
  starting transfers between devices  54.6 us (10%)
  matrix products  25.5 us (5%)
  other arithmetic  16.4 us (3%)
    ppermute x34, waiting for transfers between devices, swap(): return lax.ppermute(array, 'dp', [(i, i ^ bit) for i in range(n_dp)])  123 us
    ppermute x6, waiting for transfers between devices, ring_on(): return lax.ppermute(array, 'mp', ring_pairs)  108 us
    unnamed x126, local copies, waits for them, and re-layouts  54 us
    pallas_call x8, Pallas kernels, back_call(): pl.pallas_call(back_kernel, grid=(units,), in_specs=[pl.BlockSpec(pair.sh...  44.3 us
    pallas_call x8, Pallas kernels, product_call(): pl.pallas_call(functools.partial(product_kernel, n_add, turn), grid=(step...  39.5 us
    ppermute x34, starting transfers between devices, swap(): return lax.ppermute(array, 'dp', [(i, i ^ bit) for i in range(n_dp)])  37.3 us
    ppermute x6, starting transfers between devices, ring_on(): return lax.ppermute(array, 'mp', ring_pairs)  17.3 us
    dynamic_update_slice x15, local copies, waits for them, and re-layouts, put(): normed = lax.dynamic_update_slice(normed, piece, (at, column))  16.3 us
  transfers between devices with their start and end apart: 40, of which 16 were waited for; matrix products, arithmetic and copies ran while one was open for 13% of the time, Pallas kernels for 19%

profile of v3, /device:TPU:1, one launch (start us, length us, event | category | flops | bytes accessed | tf_op | source)
XLA Modules:
  0.0 528.5 jit_solution(4643800455444218)
XLA Ops:
  30.8 21.8 %collective-permute-done.5 = bf16[256,3072]{1,0:T(8,128)(2,1)} collective-permute-done((bf16[256,3072]{1,0:T(8,128)(2,1)}, bf16[256,3072]{1,0:T(8,128)(2,1)}, u32[]{:S(2)}, u32[]{:S(2)}) %collective-permute-start.5) | collective-permute-done | bytes 1572896 | tf_op jit(solution)/shard_map/ppermute | solution.py:235
  67.8 23.3 %collective-permute-done.7 = bf16[256,3072]{1,0:T(8,128)(2,1)S(1)} collective-permute-done((bf16[256,3072]{1,0:T(8,128)(2,1)}, bf16[256,3072]{1,0:T(8,128)(2,1)S(1)}, u32[]{:S(2)}, u32[]{:S(2)}) %collective-permute-start.7) | collective-permute-done | bytes 1572896 | tf_op jit(solution)/shard_map/ppermute | solution.py:235
  100.7 28.5 %collective-permute-done.9 = bf16[256,3072]{1,0:T(8,128)(2,1)S(1)} collective-permute-done((bf16[256,3072]{1,0:T(8,128)(2,1)S(1)}, bf16[256,3072]{1,0:T(8,128)(2,1)S(1)}, u32[]{:S(2)}, u32[]{:S(2)}) %collective-permute-start.9) | collective-permute-done | bytes 1572896 | tf_op jit(solution)/shard_map/ppermute | solution.py:235
  139.6 30.5 %collective-permute-done.12 = bf16[768,1024]{1,0:T(8,128)(2,1)S(1)} collective-permute-done((bf16[768,1024]{1,0:T(8,128)(2,1)S(1)}, bf16[768,1024]{1,0:T(8,128)(2,1)S(1)}, u32[]{:S(2)}, u32[]{:S(2)}) %collective-permute-start.12) | collective-permute-done | bytes 1572896 | tf_op jit(solution)/shard_map/ppermute | solution.py:215
  173.8 13.1 %fusion.39.qk_ref = f32[1024,1024]{1,0:T(8,128)S(1)} fusion(bf16[1024,6144]{1,0:T(8,128)(2,1)S(1)} %slice_dynamic-update-slice_fusion.4.refs_0_.refs_1_, bf16[6144,1024]{1,0:T(8,128)(2,1)S(1)} %constant_dynamic-update-slice_fusion.w_pair_ref), kind=kOutput, calls=%fused_computation.144 | convolution fusion | flops 12884901888 | bytes 29360128 | tf_op jit(solution)/shard_map/dot_general | solution.py:315
  186.9 4.6 copy-done.1
  191.5 5.8 %shard_map.113.turned_ref = bf16[512,1024]{1,0:T(8,128)(2,1)S(1)} custom-call(f32[1024,1024]{1,0:T(8,128)S(1)} %fusion.39.qk_ref, bf16[1024,512]{1,0:T(8,128)(2,1)S(1)} %constant_dynamic-update-slice_fusion.8.g_ref, f32[2,128]{1,0:T(2,128)S(1)} %pad_maximum_fusion.13.gains_ref), custom_call_target="tpu_custom_call" | custom-call | flops 1073741824 | bytes 8388608 | tf_op jit(solution)/shard_map/pallas_call | solution.py:91
  197.3 8.2 %collective-permute-done.14 = bf16[1536,512]{1,0:T(8,128)(2,1)} collective-permute-done((bf16[1536,512]{1,0:T(8,128)(2,1)}, bf16[1536,512]{1,0:T(8,128)(2,1)}, u32[]{:S(2)}, u32[]{:S(2)}) %collective-permute-start.14) | collective-permute-done | bytes 1572896 | tf_op jit(solution)/shard_map/ppermute | solution.py:215
  214.5 13.2 %collective-permute-done.16 = bf16[768,512]{1,0:T(8,128)(2,1)S(1)} collective-permute-done((bf16[768,512]{1,0:T(8,128)(2,1)S(1)}, bf16[768,512]{1,0:T(8,128)(2,1)S(1)}, u32[]{:S(2)}, u32[]{:S(2)}) %collective-permute-start.16) | collective-permute-done | bytes 786464 | tf_op jit(solution)/shard_map/ppermute | solution.py:215
  235.8 4.6 copy-done.2
  245.3 5.7 %collective-permute-done.17 = bf16[768,512]{1,0:T(8,128)(2,1)S(1)} collective-permute-done((bf16[768,512]{1,0:T(8,128)(2,1)}, bf16[768,512]{1,0:T(8,128)(2,1)S(1)}, u32[]{:S(2)}, u32[]{:S(2)}) %collective-permute-start.17) | collective-permute-done | bytes 786464 | tf_op jit(solution)/shard_map/ppermute | solution.py:215
  252.0 12.4 %convolution_convert_fusion.v_ref = bf16[1024,512]{1,0:T(8,128)(2,1)S(1)} fusion(bf16[1024,6144]{1,0:T(8,128)(2,1)} %copy-done.1, bf16[6144,512]{1,0:T(8,128)(2,1)} %constant_dynamic-update-slice_fusion.4.w_value_ref), kind=kOutput, calls=%fused_computation.38 | convolution fusion | flops 6442975232 | bytes 19922944 | tf_op jit(solution)/shard_map/dot_general | solution.py:368
  264.5 10.1 %shard_map.114.turned_ref = bf16[1024,1024]{1,0:T(8,128)(2,1)S(1)} custom-call(f32[1024,1024]{1,0:T(8,128)S(1)} %copy-done.7, bf16[1024,512]{1,0:T(8,128)(2,1)S(1)} %constant_dynamic-update-slice_fusion.8.g_ref, bf16[1024,512]{1,0:T(8,128)(2,1)S(1)} %convolution_convert_fusion.v_ref, f32[2,128]{1,0:T(2,128)S(1)} %pad_maximum_fusion.13.gains_ref), custom_call_target="tpu_custom_call" | custom-call | flops 1073741824 | bytes 12582912 | tf_op jit(solution)/shard_map/pallas_call | solution.py:91
  277.0 6.6 %shard_map.119 = bf16[3072,256]{1,0:T(8,128)(2,1)} custom-call(bf16[1024,256]{1,0:T(8,128)(2,1)S(1)} %pad_maximum_fusion.8.pair_ref, bf16[512,256]{1,0:T(8,128)(2,1)S(1)} %pad_maximum_fusion.12.value_ref, bf16[6144,1024]{1,0:T(8,128)(2,1)S(1)} %bitcast.42, bf16[6144,512]{1,0:T(8,128)(2,1)} %constant_dynamic-update-slice_fusion.4.w_value_ref), custom_call_target="tpu_custom_call" | custom-call | flops 2415919104 | bytes 14155776 | tf_op jit(solution)/shard_map/pallas_call | solution.py:157
  283.6 8.3 %collective-permute-start.23 = (bf16[3072,256]{1,0:T(8,128)(2,1)}, bf16[3072,256]{1,0:T(8,128)(2,1)S(1)}, u32[]{:S(2)}, u32[]{:S(2)}) collective-permute-start(bf16[3072,256]{1,0:T(8,128)(2,1)} %shard_map.119), channel_id=1, source_target_pairs={{0,4},{4,0},{8,12},{12,8},{16,20},{20,16},{24,28},{28,24},{1,5},{5... | collective-permute-start | bytes 4718600 | tf_op jit(solution)/shard_map/ppermute | solution.py:215
  292.1 6.6 %shard_map.118 = bf16[3072,256]{1,0:T(8,128)(2,1)} custom-call(bf16[1024,256]{1,0:T(8,128)(2,1)S(1)} %pad_maximum_fusion.7.pair_ref, bf16[512,256]{1,0:T(8,128)(2,1)S(1)} %pad_maximum_fusion.11.value_ref, bf16[6144,1024]{1,0:T(8,128)(2,1)S(1)} %bitcast.44, bf16[6144,512]{1,0:T(8,128)(2,1)} %constant_dynamic-update-slice_fusion.4.w_value_ref), custom_call_target="tpu_custom_call" | custom-call | flops 2415919104 | bytes 14155776 | tf_op jit(solution)/shard_map/pallas_call | solution.py:157
  301.9 5.6 %shard_map.120 = bf16[3072,256]{1,0:T(8,128)(2,1)} custom-call(bf16[1024,256]{1,0:T(8,128)(2,1)S(1)} %pad_maximum_fusion.8.pair_ref, bf16[512,256]{1,0:T(8,128)(2,1)S(1)} %pad_maximum_fusion.12.value_ref, bf16[6144,1024]{1,0:T(8,128)(2,1)S(1)} %bitcast.44, bf16[6144,512]{1,0:T(8,128)(2,1)} %constant_dynamic-update-slice_fusion.4.w_value_ref, ...), custom_call_target="tpu_custom_call" | custom-call | flops 2415919104 | bytes 14155776 | tf_op jit(solution)/shard_map/pallas_call | solution.py:157
  311.8 5.6 %shard_map.125 = (bf16[1024,768]{1,0:T(8,128)(2,1)}, bf16[1024,768]{1,0:T(8,128)(2,1)}) custom-call(bf16[1024,1024]{1,0:T(8,128)(2,1)S(1)} %shard_map.114.turned_ref, bf16[1024,6144]{1,0:T(8,128)(2,1)S(1)} %bitcast.40, bf16[1024,6144]{1,0:T(8,128)(2,1)S(1)} %bitcast.40), custom_call_target="tpu_custom_call" | custom-call | flops 3221225472 | bytes 8388608 | tf_op jit(solution)/shard_map/pallas_call | solution.py:128
  319.0 5.6 %shard_map.117 = bf16[3072,256]{1,0:T(8,128)(2,1)} custom-call(bf16[1024,256]{1,0:T(8,128)(2,1)S(1)} %pad_maximum_fusion.6.pair_ref, bf16[512,256]{1,0:T(8,128)(2,1)S(1)} %pad_maximum_fusion.10.value_ref, bf16[6144,1024]{1,0:T(8,128)(2,1)S(1)} %bitcast.44, bf16[6144,512]{1,0:T(8,128)(2,1)} %constant_dynamic-update-slice_fusion.4.w_value_ref), custom_call_target="tpu_custom_call" | custom-call | flops 2415919104 | bytes 14155776 | tf_op jit(solution)/shard_map/pallas_call | solution.py:157
  326.6 19.2 %collective-permute-done.24.refs_1_ = bf16[3072,256]{1,0:T(8,128)(2,1)} collective-permute-done((bf16[3072,256]{1,0:T(8,128)(2,1)}, bf16[3072,256]{1,0:T(8,128)(2,1)}, u32[]{:S(2)}, u32[]{:S(2)}) %collective-permute-start.24) | collective-permute-done | bytes 1572896 | tf_op jit(solution)/shard_map/ppermute | solution.py:235
  347.2 4.9 shard_map.121
  355.3 5.2 shard_map.124
  362.1 6.5 %shard_map.126 = (bf16[1024,768]{1,0:T(8,128)(2,1)}, bf16[1024,768]{1,0:T(8,128)(2,1)}) custom-call(bf16[1024,1024]{1,0:T(8,128)(2,1)S(1)} %shard_map.114.turned_ref, bf16[1024,6144]{1,0:T(8,128)(2,1)S(1)} %bitcast.40, bf16[1024,6144]{1,0:T(8,128)(2,1)S(1)} %bitcast.40, bf16[1024,768]{1,0:T(8,128)(2,1)} %collective-permute-done.30.refs_2_, ...), custom_call_target="tpu_custom_call" | custom-call | flops 3221225472 | bytes 11534336 | tf_op jit(solution)/shard_map/pallas_call | solution.py:128
  373.4 15.0 %collective-permute-done.25.refs_1_ = bf16[3072,256]{1,0:T(8,128)(2,1)S(1)} collective-permute-done((bf16[3072,256]{1,0:T(8,128)(2,1)S(1)}, bf16[3072,256]{1,0:T(8,128)(2,1)S(1)}, u32[]{:S(2)}, u32[]{:S(2)}) %collective-permute-start.25) | collective-permute-done | bytes 1572896 | tf_op jit(solution)/shard_map/ppermute | solution.py:235
  390.0 4.8 shard_map.116
  396.8 4.9 shard_map.122
  401.7 44.5 %collective-permute-done.35.refs_2_ = bf16[512,768]{1,0:T(8,128)(2,1)} collective-permute-done((bf16[512,768]{1,0:T(8,128)(2,1)}, bf16[512,768]{1,0:T(8,128)(2,1)}, u32[]{:S(2)}, u32[]{:S(2)}) %collective-permute-start.35) | collective-permute-done | bytes 786464 | tf_op jit(solution)/shard_map/ppermute | solution.py:215
  456.2 7.3 %shard_map.127 = (bf16[768,1024]{1,0:T(8,128)(2,1)S(1)}, bf16[768,1024]{1,0:T(8,128)(2,1)}) custom-call(bf16[1024,1024]{1,0:T(8,128)(2,1)S(1)} %shard_map.114.turned_ref, bf16[1024,6144]{1,0:T(8,128)(2,1)S(1)} %bitcast.40, bf16[1024,6144]{1,0:T(8,128)(2,1)S(1)} %bitcast.40, bf16[1024,768]{1,0:T(8,128)(2,1)} %collective-permute-done.28.refs_2_, ...), custom_call_target="tpu_custom_call" | custom-call | flops 3221225472 | bytes 14680064 | tf_op jit(solution)/shard_map/pallas_call | solution.py:128
  470.1 14.3 %collective-permute-done.36.refs_3_ = bf16[512,768]{1,0:T(8,128)(2,1)} collective-permute-done((bf16[512,768]{1,0:T(8,128)(2,1)}, bf16[512,768]{1,0:T(8,128)(2,1)}, u32[]{:S(2)}, u32[]{:S(2)}) %collective-permute-start.36) | collective-permute-done | bytes 786464 | tf_op jit(solution)/shard_map/ppermute | solution.py:215
  484.4 4.6 copy-done.3
  490.1 5.0 shard_map.132
  501.7 5.2 shard_map.123
  (267 shorter events, 165.0 us)
Async XLA Ops:
  15.7 36.9 %collective-permute-start.5 = (bf16[256,3072]{1,0:T(8,128)(2,1)}, bf16[256,3072]{1,0:T(8,128)(2,1)}, u32[]{:S(2)}, u32[]{:S(2)}) collective-permute-start(bf16[256,3072]{1,0:T(8,128)(2,1)} %pad_maximum_fusion.2), channel_id=1, source_target_pairs={{0,2},{2,3},{3,1},{1,0},{4,6},{6,7},{7,5},{5,4},{8,10},{10,11},{11... | collective-permute-start | bytes 4718600 | tf_op jit(solution)/shard_map/ppermute | solution.py:235
  19.0 38.0 %collective-permute-start.4 = (bf16[256,3072]{1,0:T(8,128)(2,1)}, bf16[256,3072]{1,0:T(8,128)(2,1)}, u32[]{:S(2)}, u32[]{:S(2)}) collective-permute-start(bf16[256,3072]{1,0:T(8,128)(2,1)} %pad_maximum_fusion.2), channel_id=1, source_target_pairs={{0,4},{4,0},{8,12},{12,8},{16,20},{20,16},{24,28},{28,24},{1,5},{5... | collective-permute-start | bytes 4718600 | tf_op jit(solution)/shard_map/ppermute | solution.py:215
  28.3 69.6 %collective-permute-start.1 = (bf16[1536,1024]{1,0:T(8,128)(2,1)S(1)}, bf16[1536,1024]{1,0:T(8,128)(2,1)S(1)}, u32[]{:S(2)}, u32[]{:S(2)}) collective-permute-start(bf16[1536,1024]{1,0:T(8,128)(2,1)S(1)} %pad_maximum_fusion), channel_id=1, source_target_pairs={{0,8},{4,12},{8,0},{12,4},{16,24},{20,28},{24,16},{28,20},{1,9},{5... | collective-permute-start | bytes 9437192 | tf_op jit(solution)/shard_map/ppermute | solution.py:215
  29.6 69.2 %collective-permute-start.2 = (bf16[1536,1024]{1,0:T(8,128)(2,1)S(1)}, bf16[1536,1024]{1,0:T(8,128)(2,1)S(1)}, u32[]{:S(2)}, u32[]{:S(2)}) collective-permute-start(bf16[1536,1024]{1,0:T(8,128)(2,1)S(1)} %pad_maximum_fusion), channel_id=1, source_target_pairs={{0,16},{4,20},{8,24},{12,28},{16,0},{20,4},{24,8},{28,12},{1,17},{... | collective-permute-start | bytes 9437192 | tf_op jit(solution)/shard_map/ppermute | solution.py:215
  52.6 42.8 %collective-permute-start.6 = (bf16[256,3072]{1,0:T(8,128)(2,1)}, bf16[256,3072]{1,0:T(8,128)(2,1)S(1)}, u32[]{:S(2)}, u32[]{:S(2)}) collective-permute-start(bf16[256,3072]{1,0:T(8,128)(2,1)} %collective-permute-done.5), channel_id=1, source_target_pairs={{0,4},{4,0},{8,12},{12,8},{16,20},{20,16},{24,28},{28,24},{1,5},{5... | collective-permute-start | bytes 4718600 | tf_op jit(solution)/shard_map/ppermute | solution.py:215
  53.9 37.2 %collective-permute-start.7 = (bf16[256,3072]{1,0:T(8,128)(2,1)}, bf16[256,3072]{1,0:T(8,128)(2,1)S(1)}, u32[]{:S(2)}, u32[]{:S(2)}) collective-permute-start(bf16[256,3072]{1,0:T(8,128)(2,1)} %collective-permute-done.5), channel_id=1, source_target_pairs={{0,2},{2,3},{3,1},{1,0},{4,6},{6,7},{7,5},{5,4},{8,10},{10,11},{11... | collective-permute-start | bytes 4718600 | tf_op jit(solution)/shard_map/ppermute | solution.py:235
  91.1 40.8 %collective-permute-start.8 = (bf16[256,3072]{1,0:T(8,128)(2,1)S(1)}, bf16[256,3072]{1,0:T(8,128)(2,1)S(1)}, u32[]{:S(2)}, u32[]{:S(2)}) collective-permute-start(bf16[256,3072]{1,0:T(8,128)(2,1)S(1)} %collective-permute-done.7), channel_id=1, source_target_pairs={{0,4},{4,0},{8,12},{12,8},{16,20},{20,16},{24,28},{28,24},{1,5},{5... | collective-permute-start | bytes 4718600 | tf_op jit(solution)/shard_map/ppermute | solution.py:215
  91.9 37.3 %collective-permute-start.9 = (bf16[256,3072]{1,0:T(8,128)(2,1)S(1)}, bf16[256,3072]{1,0:T(8,128)(2,1)S(1)}, u32[]{:S(2)}, u32[]{:S(2)}) collective-permute-start(bf16[256,3072]{1,0:T(8,128)(2,1)S(1)} %collective-permute-done.7), channel_id=1, source_target_pairs={{0,2},{2,3},{3,1},{1,0},{4,6},{6,7},{7,5},{5,4},{8,10},{10,11},{11... | collective-permute-start | bytes 4718600 | tf_op jit(solution)/shard_map/ppermute | solution.py:235
  99.3 35.5 %collective-permute-start.11 = (bf16[768,1024]{1,0:T(8,128)(2,1)S(1)}, bf16[768,1024]{1,0:T(8,128)(2,1)S(1)}, u32[]{:S(2)}, u32[]{:S(2)}) collective-permute-start(bf16[768,1024]{1,0:T(8,128)(2,1)S(1)} %get-tuple-element.74), channel_id=1, source_target_pairs={{0,16},{4,20},{8,24},{12,28},{16,0},{20,4},{24,8},{28,12},{1,17},{... | collective-permute-start | bytes 4718600 | tf_op jit(solution)/shard_map/ppermute | solution.py:215
  135.6 34.6 %collective-permute-start.12 = (bf16[768,1024]{1,0:T(8,128)(2,1)S(1)}, bf16[768,1024]{1,0:T(8,128)(2,1)S(1)}, u32[]{:S(2)}, u32[]{:S(2)}) collective-permute-start(bf16[768,1024]{1,0:T(8,128)(2,1)S(1)} %get-tuple-element.72), channel_id=1, source_target_pairs={{0,8},{4,12},{8,0},{12,4},{16,24},{20,28},{24,16},{28,20},{1,9},{5... | collective-permute-start | bytes 4718600 | tf_op jit(solution)/shard_map/ppermute | solution.py:215
  170.2 35.4 %collective-permute-start.14 = (bf16[1536,512]{1,0:T(8,128)(2,1)}, bf16[1536,512]{1,0:T(8,128)(2,1)}, u32[]{:S(2)}, u32[]{:S(2)}) collective-permute-start(bf16[1536,512]{1,0:T(8,128)(2,1)} %pad_maximum_fusion.3), channel_id=1, source_target_pairs={{0,8},{4,12},{8,0},{12,4},{16,24},{20,28},{24,16},{28,20},{1,9},{5... | collective-permute-start | bytes 4718600 | tf_op jit(solution)/shard_map/ppermute | solution.py:215
  172.4 34.6 %collective-permute-start.15 = (bf16[1536,512]{1,0:T(8,128)(2,1)}, bf16[1536,512]{1,0:T(8,128)(2,1)}, u32[]{:S(2)}, u32[]{:S(2)}) collective-permute-start(bf16[1536,512]{1,0:T(8,128)(2,1)} %pad_maximum_fusion.3), channel_id=1, source_target_pairs={{0,16},{4,20},{8,24},{12,28},{16,0},{20,4},{24,8},{28,12},{1,17},{... | collective-permute-start | bytes 4718600 | tf_op jit(solution)/shard_map/ppermute | solution.py:215
  211.2 16.5 %collective-permute-start.16 = (bf16[768,512]{1,0:T(8,128)(2,1)S(1)}, bf16[768,512]{1,0:T(8,128)(2,1)S(1)}, u32[]{:S(2)}, u32[]{:S(2)}) collective-permute-start(bf16[768,512]{1,0:T(8,128)(2,1)S(1)} %get-tuple-element.86), channel_id=1, source_target_pairs={{0,16},{4,20},{8,24},{12,28},{16,0},{20,4},{24,8},{28,12},{1,17},{... | collective-permute-start | bytes 2359304 | tf_op jit(solution)/shard_map/ppermute | solution.py:215
  243.1 31.4 %collective-permute-start.18 = (bf16[512,768]{1,0:T(8,128)(2,1)S(1)}, bf16[512,768]{1,0:T(8,128)(2,1)S(1)}, u32[]{:S(2)}, u32[]{:S(2)}) collective-permute-start(bf16[512,768]{1,0:T(8,128)(2,1)S(1)} %get-tuple-element.46), channel_id=1, source_target_pairs={{0,8},{4,12},{8,0},{12,4},{16,24},{20,28},{24,16},{28,20},{1,9},{5... | collective-permute-start | bytes 2359304 | tf_op jit(solution)/shard_map/ppermute | solution.py:215
  244.1 30.5 %collective-permute-start.19 = (bf16[512,768]{1,0:T(8,128)(2,1)S(1)}, bf16[512,768]{1,0:T(8,128)(2,1)S(1)}, u32[]{:S(2)}, u32[]{:S(2)}) collective-permute-start(bf16[512,768]{1,0:T(8,128)(2,1)S(1)} %get-tuple-element.47), channel_id=1, source_target_pairs={{0,16},{4,20},{8,24},{12,28},{16,0},{20,4},{24,8},{28,12},{1,17},{... | collective-permute-start | bytes 2359304 | tf_op jit(solution)/shard_map/ppermute | solution.py:215
  298.6 26.8 %collective-permute-start.22 = (bf16[3072,256]{1,0:T(8,128)(2,1)}, bf16[3072,256]{1,0:T(8,128)(2,1)S(1)}, u32[]{:S(2)}, u32[]{:S(2)}) collective-permute-start(bf16[3072,256]{1,0:T(8,128)(2,1)} %shard_map.118), channel_id=1, source_target_pairs={{0,4},{4,0},{8,12},{12,8},{16,20},{20,16},{24,28},{28,24},{1,5},{5... | collective-permute-start | bytes 4718600 | tf_op jit(solution)/shard_map/ppermute | solution.py:215
  307.5 38.4 %collective-permute-start.24 = (bf16[3072,256]{1,0:T(8,128)(2,1)}, bf16[3072,256]{1,0:T(8,128)(2,1)}, u32[]{:S(2)}, u32[]{:S(2)}) collective-permute-start(bf16[3072,256]{1,0:T(8,128)(2,1)} %shard_map.120), channel_id=1, source_target_pairs={{0,2},{2,3},{3,1},{1,0},{4,6},{6,7},{7,5},{5,4},{8,10},{10,11},{11... | collective-permute-start | bytes 4718600 | tf_op jit(solution)/shard_map/ppermute | solution.py:235
  317.4 43.5 %collective-permute-start.29 = (bf16[1024,768]{1,0:T(8,128)(2,1)}, bf16[1024,768]{1,0:T(8,128)(2,1)}, u32[]{:S(2)}, u32[]{:S(2)}) collective-permute-start(bf16[1024,768]{1,0:T(8,128)(2,1)} %get-tuple-element.52), channel_id=1, source_target_pairs={{0,8},{4,12},{8,0},{12,4},{16,24},{20,28},{24,16},{28,20},{1,9},{5... | collective-permute-start | bytes 4718600 | tf_op jit(solution)/shard_map/ppermute | solution.py:215
  317.7 44.4 %collective-permute-start.30 = (bf16[1024,768]{1,0:T(8,128)(2,1)}, bf16[1024,768]{1,0:T(8,128)(2,1)}, u32[]{:S(2)}, u32[]{:S(2)}) collective-permute-start(bf16[1024,768]{1,0:T(8,128)(2,1)} %get-tuple-element.53), channel_id=1, source_target_pairs={{0,16},{4,20},{8,24},{12,28},{16,0},{20,4},{24,8},{28,12},{1,17},{... | collective-permute-start | bytes 4718600 | tf_op jit(solution)/shard_map/ppermute | solution.py:215
  324.6 44.3 %collective-permute-start.21 = (bf16[3072,256]{1,0:T(8,128)(2,1)}, bf16[3072,256]{1,0:T(8,128)(2,1)}, u32[]{:S(2)}, u32[]{:S(2)}) collective-permute-start(bf16[3072,256]{1,0:T(8,128)(2,1)} %shard_map.117), channel_id=1, source_target_pairs={{0,4},{4,0},{8,12},{12,8},{16,20},{20,16},{24,28},{28,24},{1,5},{5... | collective-permute-start | bytes 4718600 | tf_op jit(solution)/shard_map/ppermute | solution.py:215
  352.2 36.2 %collective-permute-start.25 = (bf16[3072,256]{1,0:T(8,128)(2,1)S(1)}, bf16[3072,256]{1,0:T(8,128)(2,1)S(1)}, u32[]{:S(2)}, u32[]{:S(2)}) collective-permute-start(bf16[3072,256]{1,0:T(8,128)(2,1)S(1)} %shard_map.121), channel_id=1, source_target_pairs={{0,2},{2,3},{3,1},{1,0},{4,6},{6,7},{7,5},{5,4},{8,10},{10,11},{11... | collective-permute-start | bytes 4718600 | tf_op jit(solution)/shard_map/ppermute | solution.py:235
  360.6 87.7 %collective-permute-start.28 = (bf16[1024,768]{1,0:T(8,128)(2,1)}, bf16[1024,768]{1,0:T(8,128)(2,1)}, u32[]{:S(2)}, u32[]{:S(2)}) collective-permute-start(bf16[1024,768]{1,0:T(8,128)(2,1)} %get-tuple-element.50), channel_id=1, source_target_pairs={{0,8},{4,12},{8,0},{12,4},{16,24},{20,28},{24,16},{28,20},{1,9},{5... | collective-permute-start | bytes 4718600 | tf_op jit(solution)/shard_map/ppermute | solution.py:215
  360.9 87.4 %collective-permute-start.33 = (bf16[1024,768]{1,0:T(8,128)(2,1)}, bf16[1024,768]{1,0:T(8,128)(2,1)}, u32[]{:S(2)}, u32[]{:S(2)}) collective-permute-start(bf16[1024,768]{1,0:T(8,128)(2,1)} %get-tuple-element.59), channel_id=1, source_target_pairs={{0,16},{4,20},{8,24},{12,28},{16,0},{20,4},{24,8},{28,12},{1,17},{... | collective-permute-start | bytes 4718600 | tf_op jit(solution)/shard_map/ppermute | solution.py:215
  368.6 87.0 %collective-permute-start.31 = (bf16[1024,768]{1,0:T(8,128)(2,1)}, bf16[1024,768]{1,0:T(8,128)(2,1)}, u32[]{:S(2)}, u32[]{:S(2)}) collective-permute-start(bf16[1024,768]{1,0:T(8,128)(2,1)} %get-tuple-element.57), channel_id=1, source_target_pairs={{0,16},{4,20},{8,24},{12,28},{16,0},{20,4},{24,8},{28,12},{1,17},{... | collective-permute-start | bytes 4718600 | tf_op jit(solution)/shard_map/ppermute | solution.py:215
  368.8 87.1 %collective-permute-start.32 = (bf16[1024,768]{1,0:T(8,128)(2,1)}, bf16[1024,768]{1,0:T(8,128)(2,1)}, u32[]{:S(2)}, u32[]{:S(2)}) collective-permute-start(bf16[1024,768]{1,0:T(8,128)(2,1)} %get-tuple-element.58), channel_id=1, source_target_pairs={{0,8},{4,12},{8,0},{12,4},{16,24},{20,28},{24,16},{28,20},{1,9},{5... | collective-permute-start | bytes 4718600 | tf_op jit(solution)/shard_map/ppermute | solution.py:215
  389.6 56.7 %collective-permute-start.35 = (bf16[512,768]{1,0:T(8,128)(2,1)}, bf16[512,768]{1,0:T(8,128)(2,1)}, u32[]{:S(2)}, u32[]{:S(2)}) collective-permute-start(bf16[512,768]{1,0:T(8,128)(2,1)} %get-tuple-element.62), channel_id=1, source_target_pairs={{0,8},{4,12},{8,0},{12,4},{16,24},{20,28},{24,16},{28,20},{1,9},{5... | collective-permute-start | bytes 2359304 | tf_op jit(solution)/shard_map/ppermute | solution.py:215
  446.2 50.8 %collective-permute-start.20 = (bf16[3072,256]{1,0:T(8,128)(2,1)}, bf16[3072,256]{1,0:T(8,128)(2,1)}, u32[]{:S(2)}, u32[]{:S(2)}) collective-permute-start(bf16[3072,256]{1,0:T(8,128)(2,1)} %copy-done.19), channel_id=1, source_target_pairs={{0,4},{4,0},{8,12},{12,8},{16,20},{20,16},{24,28},{28,24},{1,5},{5... | collective-permute-start | bytes 4718600 | tf_op jit(solution)/shard_map/ppermute | solution.py:215
  448.2 48.8 %collective-permute-start.26 = (bf16[3072,256]{1,0:T(8,128)(2,1)S(1)}, bf16[3072,256]{1,0:T(8,128)(2,1)}, u32[]{:S(2)}, u32[]{:S(2)}) collective-permute-start(bf16[3072,256]{1,0:T(8,128)(2,1)S(1)} %shard_map.122), channel_id=1, source_target_pairs={{0,2},{2,3},{3,1},{1,0},{4,6},{6,7},{7,5},{5,4},{8,10},{10,11},{11... | collective-permute-start | bytes 4718600 | tf_op jit(solution)/shard_map/ppermute | solution.py:235
  448.3 19.2 %collective-permute-start.38 = (bf16[512,768]{1,0:T(8,128)(2,1)}, bf16[512,768]{1,0:T(8,128)(2,1)S(1)}, u32[]{:S(2)}, u32[]{:S(2)}) collective-permute-start(bf16[512,768]{1,0:T(8,128)(2,1)} %copy-done.28), channel_id=1, source_target_pairs={{0,16},{4,20},{8,24},{12,28},{16,0},{20,4},{24,8},{28,12},{1,17},{... | collective-permute-start | bytes 2359304 | tf_op jit(solution)/shard_map/ppermute | solution.py:215
  455.7 28.7 %collective-permute-start.36 = (bf16[512,768]{1,0:T(8,128)(2,1)}, bf16[512,768]{1,0:T(8,128)(2,1)}, u32[]{:S(2)}, u32[]{:S(2)}) collective-permute-start(bf16[512,768]{1,0:T(8,128)(2,1)} %get-tuple-element.65), channel_id=1, source_target_pairs={{0,16},{4,20},{8,24},{12,28},{16,0},{20,4},{24,8},{28,12},{1,17},{... | collective-permute-start | bytes 2359304 | tf_op jit(solution)/shard_map/ppermute | solution.py:215
  455.9 28.5 %collective-permute-start.37 = (bf16[512,768]{1,0:T(8,128)(2,1)}, bf16[512,768]{1,0:T(8,128)(2,1)}, u32[]{:S(2)}, u32[]{:S(2)}) collective-permute-start(bf16[512,768]{1,0:T(8,128)(2,1)} %get-tuple-element.66), channel_id=1, source_target_pairs={{0,8},{4,12},{8,0},{12,4},{16,24},{20,28},{24,16},{28,20},{1,9},{5... | collective-permute-start | bytes 2359304 | tf_op jit(solution)/shard_map/ppermute | solution.py:215
  468.5 48.4 %collective-permute-start.34 = (bf16[768,1024]{1,0:T(8,128)(2,1)}, bf16[768,1024]{1,0:T(8,128)(2,1)}, u32[]{:S(2)}, u32[]{:S(2)}) collective-permute-start(bf16[768,1024]{1,0:T(8,128)(2,1)} %get-tuple-element.61), channel_id=1, source_target_pairs={{0,4},{4,0},{8,12},{12,8},{16,20},{20,16},{24,28},{28,24},{1,5},{5... | collective-permute-start | bytes 4718600 | tf_op jit(solution)/shard_map/ppermute | solution.py:215
  (65 other events, 489.6 us)

commit v4 on v3

--- a/solution.py
+++ b/solution.py
@@ -203,6 +203,42 @@
     )(core.reshape(1), mine, other)
 
 
+def finish_kernel(rows, n_dp, place_ref, mine_ref, other_ref, unit_ref, spread_ref, gain_ref, out_ref, held):
+    n_chips = n_dp // 2
+    held[: n_chips * rows] = mine_ref[...]
+    held[n_chips * rows :] = other_ref[...].astype(F32)
+    place = place_ref[0]
+    columns = []
+    total, inner = 0.0, 0.0
+    for b in range(n_dp):
+        r = b ^ place
+        unit = (r & 1) * n_chips + (r >> 1)
+        at = pl.ds(b * rows, rows)
+        grad = held[pl.ds(pl.multiple_of(unit * rows, rows), rows), :].T
+        scaled = grad * gain_ref[:, at]
+        total = total + jnp.sum(scaled, axis=-1, keepdims=True)
+        inner = inner + jnp.sum(scaled * unit_ref[:, at], axis=-1, keepdims=True)
+        columns.append(scaled)
+    average, inner = total * (1.0 / (n_dp * rows)), inner * (1.0 / (n_dp * rows))
+    for b in range(n_dp):
+        at = pl.ds(b * rows, rows)
+        result = (columns[b] - average - unit_ref[:, at] * inner) * spread_ref[...]
+        out_ref[:, at] = result.astype(BF)
+
+
+def finish_call(place, mine, other, unit_rows, row_spread, norm_gain, rows):
+    own, width = unit_rows.shape
+    vmem = pl.BlockSpec(memory_space=pltpu.VMEM)
+    return pl.pallas_call(
+        functools.partial(finish_kernel, rows, width // rows),
+        in_specs=[pl.BlockSpec(memory_space=pltpu.SMEM)] + [vmem] * 5,
+        out_specs=vmem,
+        out_shape=jax.ShapeDtypeStruct((own, width), BF),
+        scratch_shapes=[pltpu.VMEM((width, own), F32)],
+        compiler_params=params(32),
+    )(place.reshape(1), mine, other, unit_rows, row_spread, norm_gain.reshape(1, width))
+
+
 def per_device(n_dp, n_mp, tokens, norm_gain, q_gain, k_gain, w_query, w_key, w_value, grad_heads):
     own, width = tokens.shape
     rows, cols = w_query.shape[0], w_query.shape[1] // 2
@@ -240,16 +276,11 @@
     def feature_block(array, r):
         return lax.dynamic_slice_in_dim(array, (place ^ r) * rows, rows, 1)
 
-    weights = (w_query, w_key, w_value)
-    other_rows = swap(jnp.concatenate([half(w, 1 - core) for w in weights], axis=1), 1)
-    own_rows = jnp.concatenate([half(w, core) for w in weights], axis=1)
-    shard_pair, shard_value = (
-        jnp.concatenate([own_rows[:, at], other_rows[:, at]], axis=0)
-        for at in (slice(0, 2 * cols), slice(2 * cols, None))
-    )
-
-    def gather_start(shard):
-        held = {0: shard}
+    def columns_of(weights, which):
+        return jnp.concatenate([half(w, which) for w in weights], axis=1)
+
+    def gather_start(held):
+        held = dict(held)
         bit = 8
         while bit < n_dp:
             held.update({r ^ bit: swap(part, bit) for r, part in list(held.items())})
@@ -260,25 +291,27 @@
         return held
 
     def gather_rest(held):
-        relays = {}
+        held = dict(held)
         for r in range(0, n_dp, 8):
-            relays[r ^ 6] = swap(held[r ^ 2][:rows], 4)
-            relays[r ^ 7] = swap(held[r ^ 4][rows:], 2)
-        return relays
-
-    def whole(held, relays):
-        pieces = dict(relays)
-        for r, part in held.items():
-            pieces[r], pieces[r ^ 1] = part[:rows], part[rows:]
-        return jnp.concatenate([pieces[r] for r in (*range(0, n_dp, 2), *range(1, n_dp, 2))], axis=0)
-
-    held_pair = gather_start(shard_pair)
-
+            held[r ^ 6] = swap(held[r ^ 2], 4)
+            held[r ^ 7] = swap(held[r ^ 5], 2)
+        return held
+
+    def whole(held):
+        return jnp.concatenate([held[r] for r in (*range(0, n_dp, 2), *range(1, n_dp, 2))], axis=0)
+
+    pair_weights = (w_query, w_key)
+    own_pair, sent_pair = columns_of(pair_weights, core), columns_of(pair_weights, 1 - core)
+    held_pair = gather_start({0: own_pair})
+    other_pair = swap(sent_pair, 1)
+
+    tokens = after(tokens, own_pair, sent_pair)
     normed_own, unit_rows, row_spread = normalize(tokens.astype(F32), norm_gain)
     normed_own = normed_own.astype(BF)
     even = jnp.concatenate([feature_block(normed_own, r) for r in range(0, n_dp, 2)], axis=1)
     odd = jnp.concatenate([feature_block(normed_own, r) for r in range(1, n_dp, 2)], axis=1)
     block = jnp.concatenate([even, swap(odd, 1)], axis=0)
+    held_pair.update(gather_start({1: other_pair}))
 
     normed = blank((2 * group, width), BF)
 
@@ -296,22 +329,25 @@
         return normed
 
     normed = put(normed, block, 0)
-    relays_pair = None
     for step in range(1, n_mp):
         block = ring_on(block)
         normed = put(normed, block, step)
         if step == 1:
-            held_pair, normed = after((held_pair, normed))
-            relays_pair = gather_rest(held_pair)
-    held_value = gather_start(after(shard_value, relays_pair))
-
-    grads_other = swap(half(grad_heads, 1 - core), 1)
+            held_pair, normed, w_value, grad_heads = after((held_pair, normed, w_value, grad_heads))
+            held_pair = gather_rest(held_pair)
+            shard_value = [half(w_value, core), swap(half(w_value, 1 - core), 1)]
+            shard_value = jnp.concatenate(shard_value, axis=0)
+            grads_mine, grads_other = half(grad_heads, core), swap(half(grad_heads, 1 - core), 1)
+        elif step == 2:
+            shard_value, normed = after((shard_value, normed))
+            held_value = gather_start({0: shard_value})
+
     grad_out = blank((2 * group, cols), BF)
-    grad_out = lax.dynamic_update_slice_in_dim(grad_out, half(grad_heads, core), core * group, 0)
+    grad_out = lax.dynamic_update_slice_in_dim(grad_out, grads_mine, core * group, 0)
     grad_out = lax.dynamic_update_slice_in_dim(grad_out, grads_other, (1 - core) * group, 0)
     gains = jnp.stack([q_gain, k_gain])
 
-    full_pair = whole(held_pair, relays_pair)
+    full_pair = whole(held_pair)
     pair = jnp.dot(normed, full_pair, preferred_element_type=F32)
     turned_value = attention_call(first_kernel, (pair, grad_out), gains, cols)
 
@@ -320,27 +356,22 @@
             turned, normed, rows, [unit_of(r ^ f) for f in offsets], addends, turn
         )
 
-    def scatter_far(turned):
-        sent = {}
-        for r in range(0, n_dp, 8):
-            far_even, far_odd = products(turned, r, (6, 7))
-            sent[r] = [swap(far_even, 2), swap(far_odd, 4)]
-        return sent
-
-    def scatter_early(turned):
-        sent = {}
-        for r in range(0, n_dp, 8):
-            even_x, odd_y = products(turned, r, (2, 5))
-            sent[r] = [swap(even_x, 2), swap(odd_y, 4)]
-        return sent
-
-    def scatter_late(turned, far):
-        sent = {}
-        for r in range(0, n_dp, 8):
-            from_x, from_y = far[r]
-            odd_x, even_y = products(turned, r, (3, 4), ((from_y,), (from_x,)))
-            sent[r] = [swap(odd_x, 2), swap(even_y, 4)]
-        return sent
+    blocks_of_four = range(0, n_dp, 8)
+
+    def far_messages(turned):
+        return [products(turned, r, (6, 7)) for r in blocks_of_four]
+
+    def early_messages(turned):
+        return [products(turned, r, (2, 5)) for r in blocks_of_four]
+
+    def late_messages(turned, far):
+        return [
+            products(turned, r, (3, 4), ((from_y,), (from_x,)))
+            for r, (from_x, from_y) in zip(blocks_of_four, far)
+        ]
+
+    def send(messages):
+        return [[swap(to_x, 2), swap(to_y, 4)] for to_x, to_y in messages]
 
     def scatter_end(turned, early, late):
         if n_dp == 8:
@@ -348,7 +379,7 @@
             return products(turned, 0, (0, 1), ((even_x, even_y), (odd_x, odd_y)), True)
         totals = {}
         for r in range(0, n_dp, 8):
-            (even_x, odd_y), (odd_x, even_y) = early[r], late[r]
+            (even_x, odd_y), (odd_x, even_y) = early[r // 8], late[r // 8]
             totals[r] = products(turned, r, (0, 1), ((even_x, even_y), (odd_x, odd_y)))
         bit = n_dp // 2
         while bit >= 8:
@@ -360,60 +391,80 @@
             bit //= 2
         return [total.T for total in totals[0]]
 
-    held_value, turned_value = after((held_value, turned_value))
-    relays_value = gather_rest(held_value)
-    far_value = scatter_far(turned_value)
-    early_value = scatter_early(turned_value)
-    full_value = whole(held_value, relays_value)
+    far_value, early_value = far_messages(turned_value), early_messages(turned_value)
+    held_value, far_value, early_value = after((held_value, far_value, early_value))
+    held_value = {r ^ f: held_value[r][f * rows : (f + 1) * rows] for r in held_value for f in (0, 1)}
+    held_value, far_value = after((held_value, far_value))
+    held_value = gather_rest(held_value)
+    far_value = send(far_value)
+    held_value, early_value = after((held_value, early_value))
+    early_value = send(early_value)
+    full_value = whole(held_value)
     values = jnp.dot(normed, full_value, preferred_element_type=F32).astype(BF)
     turned_pair = attention_call(rest_kernel, (pair, grad_out, values), gains, 2 * cols)
 
-    turned_pair, turned_value, far_value = after((turned_pair, turned_value, far_value))
-    late_value = scatter_late(turned_value, far_value)
-
-    def back_odd(step):
+    turned_value, turned_pair, far_value = after((turned_value, turned_pair, far_value))
+    late_value = late_messages(turned_value, far_value)
+    turned_value, turned_pair, late_value = after((turned_value, turned_pair, late_value))
+    late_value = send(late_value)
+
+    def back_odd(step, gate):
         at = level_at(step + 1) * own
         chosen = [
             jnp.concatenate(
                 [lax.dynamic_slice_in_dim(turned, g * group + at, own, 1) for g in range(2)], axis=1
             )
-            for turned in (turned_pair, turned_value)
+            for turned in after((turned_pair, turned_value), gate)
         ]
         sent = back_call(*chosen, full_pair, full_value, rows, True, (), BF)
-        return chosen, swap(sent, 1)
-
-    def back_even(chosen, passed, arrived, dtype):
-        addends = (passed,) if arrived is None else (passed, arrived)
-        return back_call(*chosen, full_pair, full_value, rows, False, addends, dtype)
-
-    arrived = None
+        return chosen, sent, swap(sent, 1)
+
+    gate, arrived = [], None
     for step in range(n_mp):
         last = step == n_mp - 1
-        chosen, passed = back_odd(step)
-        total = back_even(chosen, passed, arrived, F32 if last else BF)
+        if last:
+            early_pair, gate = after((early_pair, gate))
+        chosen, sent, passed = back_odd(step, gate)
+        if step == 0:
+            far_pair = far_messages(after(turned_pair, sent))
+            chosen, far_pair, early_value = after((chosen, far_pair, early_value))
+        elif step == 1:
+            turned_early, late_value = after((turned_pair, late_value), sent)
+            early_pair = early_messages(turned_early)
+            chosen, early_pair = after((chosen, early_pair))
+        elif step == 2:
+            late_pair = late_messages(after(turned_pair, sent), far_pair)
+            chosen, late_pair = after((chosen, late_pair))
+            late_pair = send(late_pair)
+            chosen, ends_value = after((chosen, scatter_end(turned_value, early_value, late_value)))
+            passed_value = swap(ends_value[1], 1)
+        total = back_call(
+            *chosen, full_pair, full_value, rows, False, (passed,), F32 if last else BF
+        )
+        if last:
+            ends_pair = scatter_end(after(turned_pair, total), early_pair, late_pair)
+            total, ends_pair = after((total, ends_pair))
+        if arrived is not None:
+            total = total.astype(F32) + arrived.astype(F32)
         if not last:
+            total = total.astype(BF)
             arrived = ring_on(total)
+        gate = total
         if step == 0:
-            far_pair = scatter_far(after(turned_pair, total))
-            early_pair = scatter_early(turned_pair)
+            far_pair, gate = after((far_pair, total))
+            far_pair = send(far_pair)
         elif step == 1:
-            turned_late, far_pair = after((turned_pair, far_pair), total)
-            late_pair = scatter_late(turned_late, far_pair)
-
+            early_pair, gate = after((early_pair, total))
+            early_pair = send(early_pair)
+
+    passed_pair = swap(ends_pair[1], 1)
     mine = lax.dynamic_slice_in_dim(total, core * own, own, 1)
-    other = swap(lax.dynamic_slice_in_dim(total, (1 - core) * own, own, 1).astype(BF), 1).astype(F32)
-    units = jnp.concatenate([mine, other], axis=0).T
-    ordered = [
-        lax.dynamic_slice_in_dim(units, unit_of(b ^ place) * rows, rows, 1) for b in range(n_dp)
-    ]
-    grad_normed = jnp.concatenate(ordered, axis=1)
-    grad_tokens = normalize_back(grad_normed, unit_rows, row_spread, norm_gain).astype(BF)
-
-    mine, other = scatter_end(turned_value, early_value, late_value)
-    out_value = place_call(core, mine, swap(other, 1), cols, 0)
-    mine, other = scatter_end(turned_pair, early_pair, late_pair)
-    other = swap(other, 1)
-    out_query, out_key = (place_call(core, mine, other, cols, part) for part in range(2))
+    other = swap(lax.dynamic_slice_in_dim(total, (1 - core) * own, own, 1).astype(BF), 1)
+    out_value = place_call(core, ends_value[0], passed_value, cols, 0)
+    out_query, out_key = (
+        place_call(core, ends_pair[0], passed_pair, cols, part) for part in range(2)
+    )
+    grad_tokens = finish_call(place, mine, other, unit_rows, row_spread, norm_gain, rows)
     return (grad_tokens, out_query, out_key, out_value)
 
 

time: 534 us -> 443 us (0.83)
  waiting for transfers between devices: 231 us -> 166 us
  local copies, waits for them, and re-layouts: 92.7 us -> 69.7 us
  Pallas kernels: 107 us -> 97 us
  starting transfers between devices: 54.6 us -> 60.3 us
    ppermute x6, waiting for transfers between devices: 108 us -> 64.2 us  [ring_on(): return lax.ppermute(array, 'mp', ring_pairs)]
    ppermute x34 -> x37, waiting for transfers between devices: 123 us -> 102 us  [swap(): return lax.ppermute(array, 'dp', [(i, i ^ bit) for i in range(n_dp)])]
    pallas_call x8, Pallas kernels: 44.3 us -> 33.3 us  [back_call(): pl.pallas_call(back_kernel, grid=(units,), in_specs=[pl.BlockSpec(pair.sh...]
    unnamed x126 -> x148, local copies, waits for them, and re-layouts: 54 us -> 46.4 us
    ppermute x34 -> x37, starting transfers between devices: 37.3 us -> 42.2 us  [swap(): return lax.ppermute(array, 'dp', [(i, i ^ bit) for i in range(n_dp)])]
  transfers between devices with their start and end apart: 40 -> 43, of which waited for: 16 -> 17; matrix products, arithmetic and copies ran while one was open for 13% -> 14% of each run, Pallas kernels for 19% -> 20%
where the time goes in v4:
time: 443 us; the launch traced here: 437 us
  waiting for transfers between devices  166 us (37%)
  Pallas kernels  97 us (22%)
  local copies, waits for them, and re-layouts  69.7 us (16%)
  starting transfers between devices  60.3 us (14%)
  matrix products  25.2 us (6%)
  other arithmetic  17.2 us (4%)
    ppermute x37, waiting for transfers between devices, swap(): return lax.ppermute(array, 'dp', [(i, i ^ bit) for i in range(n_dp)])  102 us
    ppermute x6, waiting for transfers between devices, ring_on(): return lax.ppermute(array, 'mp', ring_pairs)  64.2 us
    unnamed x148, local copies, waits for them, and re-layouts  46.4 us
    ppermute x37, starting transfers between devices, swap(): return lax.ppermute(array, 'dp', [(i, i ^ bit) for i in range(n_dp)])  42.2 us
    pallas_call x8, Pallas kernels, product_call(): pl.pallas_call(functools.partial(product_kernel, n_add, turn), grid=(step...  38.3 us
    pallas_call x8, Pallas kernels, back_call(): pl.pallas_call(back_kernel, grid=(units,), in_specs=[pl.BlockSpec(pair.sh...  33.3 us
    ppermute x6, starting transfers between devices, ring_on(): return lax.ppermute(array, 'mp', ring_pairs)  18.1 us
    pallas_call x2, Pallas kernels, attention_call(): pl.pallas_call(kernel, grid=(tokens // PATCH,), in_specs=[pl.BlockSpec((P...  15.9 us
  transfers between devices with their start and end apart: 43, of which 17 were waited for; matrix products, arithmetic and copies ran while one was open for 14% of the time, Pallas kernels for 20%

profile of v4, /device:TPU:1, one launch (start us, length us, event | category | flops | bytes accessed | tf_op | source)
XLA Modules:
  0.0 437.5 jit_solution(7076159836973852493)
XLA Ops:
  22.5 28.1 %collective-permute-done.7 = bf16[256,3072]{1,0:T(8,128)(2,1)} collective-permute-done((bf16[256,3072]{1,0:T(8,128)(2,1)}, bf16[256,3072]{1,0:T(8,128)(2,1)}, u32[]{:S(2)}, u32[]{:S(2)}) %collective-permute-start.7) | collective-permute-done | bytes 1572896 | tf_op jit(solution)/shard_map/ppermute | solution.py:271
  65.0 20.8 %collective-permute-done.2 = bf16[768,1024]{1,0:T(8,128)(2,1)S(1)} collective-permute-done((bf16[768,1024]{1,0:T(8,128)(2,1)}, bf16[768,1024]{1,0:T(8,128)(2,1)S(1)}, u32[]{:S(2)}, u32[]{:S(2)}) %collective-permute-start.2) | collective-permute-done | bytes 1572896 | tf_op jit(solution)/shard_map/ppermute | solution.py:251
  105.9 29.7 %collective-permute-done.12 = bf16[256,3072]{1,0:T(8,128)(2,1)S(1)} collective-permute-done((bf16[256,3072]{1,0:T(8,128)(2,1)S(1)}, bf16[256,3072]{1,0:T(8,128)(2,1)S(1)}, u32[]{:S(2)}, u32[]{:S(2)}) %collective-permute-start.12) | collective-permute-done | bytes 1572896 | tf_op jit(solution)/shard_map/ppermute | solution.py:271
  139.6 13.1 %fusion.7.qk_ref = f32[1024,1024]{1,0:T(8,128)S(1)} fusion(bf16[1024,6144]{1,0:T(8,128)(2,1)S(1)} %slice_dynamic-update-slice_fusion.refs_0_.refs_1_, bf16[6144,1024]{1,0:T(8,128)(2,1)S(1)} %constant_dynamic-update-slice_fusion.w_pair_ref), kind=kOutput, calls=%fused_computation.97 | convolution fusion | flops 12884901888 | bytes 29360128 | tf_op jit(solution)/shard_map/dot_general | solution.py:351
  152.7 4.6 %copy-done.3 = bf16[6144,1024]{1,0:T(8,128)(2,1)} copy-done((bf16[6144,1024]{1,0:T(8,128)(2,1)}, bf16[6144,1024]{1,0:T(8,128)(2,1)S(1)}, u32[]{:S(2)}) %copy-start.3) | copy-done | bytes 12582936
  157.3 5.8 %shard_map.113.turned_ref = bf16[512,1024]{1,0:T(8,128)(2,1)S(1)} custom-call(f32[1024,1024]{1,0:T(8,128)S(1)} %fusion.7.qk_ref, bf16[1024,512]{1,0:T(8,128)(2,1)S(1)} %constant_dynamic-update-slice_fusion.16.g_ref, f32[2,128]{1,0:T(2,128)S(1)} %pad_maximum_fusion.13.gains_ref), custom_call_target="tpu_custom_call" | custom-call | flops 1073741824 | bytes 8388608 | tf_op jit(solution)/shard_map/pallas_call | solution.py:91
  179.9 16.1 %collective-permute-done.19 = bf16[768,512]{1,0:T(8,128)(2,1)} collective-permute-done((bf16[768,512]{1,0:T(8,128)(2,1)}, bf16[768,512]{1,0:T(8,128)(2,1)}, u32[]{:S(2)}, u32[]{:S(2)}) %collective-permute-start.19) | collective-permute-done | bytes 786464 | tf_op jit(solution)/shard_map/ppermute | solution.py:251
  202.1 12.1 %convolution_convert_fusion.v_ref = bf16[1024,512]{1,0:T(8,128)(2,1)S(1)} fusion(bf16[1024,6144]{1,0:T(8,128)(2,1)} %copy-done.1, bf16[6144,512]{1,0:T(8,128)(2,1)S(1)} %constant_dynamic-update-slice_fusion.8.w_value_ref), kind=kOutput, calls=%fused_computation.14 | convolution fusion | flops 6442975232 | bytes 19922944 | tf_op jit(solution)/shard_map/dot_general | solution.py:403
  216.4 10.1 %shard_map.116.turned_ref = bf16[1024,1024]{1,0:T(8,128)(2,1)S(1)} custom-call(f32[1024,1024]{1,0:T(8,128)S(1)} %copy-done.16, bf16[1024,512]{1,0:T(8,128)(2,1)S(1)} %copy-done.20, bf16[1024,512]{1,0:T(8,128)(2,1)S(1)} %convolution_convert_fusion.v_ref, f32[2,128]{1,0:T(2,128)S(1)} %pad_maximum_fusion.13.gains_ref), custom_call_target="tpu_custom_call" | custom-call | flops 1073741824 | bytes 12582912 | tf_op jit(solution)/shard_map/pallas_call | solution.py:91
  230.7 4.6 %copy-done.4 = bf16[6144,1024]{1,0:T(8,128)(2,1)S(1)} copy-done((bf16[6144,1024]{1,0:T(8,128)(2,1)S(1)}, bf16[6144,1024]{1,0:T(8,128)(2,1)}, u32[]{:S(2)}) %copy-start.4) | copy-done | bytes 12582936
  243.4 3.9 shard_map.120
  247.9 5.5 %shard_map.124 = (bf16[1024,768]{1,0:T(8,128)(2,1)}, bf16[1024,768]{1,0:T(8,128)(2,1)}) custom-call(bf16[1024,1024]{1,0:T(8,128)(2,1)S(1)} %copy-done.9, bf16[1024,6144]{1,0:T(8,128)(2,1)S(1)} %bitcast.12, bf16[1024,6144]{1,0:T(8,128)(2,1)S(1)} %bitcast.12), custom_call_target="tpu_custom_call" | custom-call | flops 3221225472 | bytes 8388608 | tf_op jit(solution)/shard_map/pallas_call | solution.py:128
  253.4 7.9 %collective-permute-done.27.refs_2_ = bf16[512,768]{1,0:T(8,128)(2,1)} collective-permute-done((bf16[512,768]{1,0:T(8,128)(2,1)}, bf16[512,768]{1,0:T(8,128)(2,1)}, u32[]{:S(2)}, u32[]{:S(2)}) %collective-permute-start.27) | collective-permute-done | bytes 786464 | tf_op jit(solution)/shard_map/ppermute | solution.py:251
  264.8 3.9 shard_map.125
  272.5 3.9 shard_map.126
  278.3 11.2 %collective-permute-done.24.refs_4_ = bf16[512,768]{1,0:T(8,128)(2,1)S(1)} collective-permute-done((bf16[512,768]{1,0:T(8,128)(2,1)S(1)}, bf16[512,768]{1,0:T(8,128)(2,1)S(1)}, u32[]{:S(2)}, u32[]{:S(2)}) %collective-permute-start.24) | collective-permute-done | bytes 786464 | tf_op jit(solution)/shard_map/ppermute | solution.py:251
  290.7 4.4 %shard_map.121 = (bf16[1024,768]{1,0:T(8,128)(2,1)S(1)}, bf16[1024,768]{1,0:T(8,128)(2,1)S(1)}) custom-call(bf16[1024,1024]{1,0:T(8,128)(2,1)S(1)} %copy-done.9, bf16[1024,6144]{1,0:T(8,128)(2,1)S(1)} %bitcast.12, bf16[1024,6144]{1,0:T(8,128)(2,1)S(1)} %bitcast.12), custom_call_target="tpu_custom_call" | custom-call | flops 3221225472 | bytes 8388608 | tf_op jit(solution)/shard_map/pallas_call | solution.py:128
  296.4 4.4 %shard_map.122 = bf16[3072,256]{1,0:T(8,128)(2,1)S(1)} custom-call(bf16[1024,256]{1,0:T(8,128)(2,1)S(1)} %pad_maximum_fusion.6.pair_ref, bf16[512,256]{1,0:T(8,128)(2,1)S(1)} %pad_maximum_fusion.10.value_ref, bf16[6144,1024]{1,0:T(8,128)(2,1)S(1)} %copy-done.4, bf16[6144,512]{1,0:T(8,128)(2,1)S(1)} %constant_dynamic-update-slice_fusion.8.w_value_ref, ...), custom_call_target="tpu_custom_call" | custom-call | flops 2415919104 | bytes 14155776 | tf_op jit(solution)/shard_map/pallas_call | solution.py:157
  310.9 3.9 shard_map.118
  317.2 4.9 %shard_map.128 = (bf16[768,512]{1,0:T(8,128)(2,1)S(1)}, bf16[768,512]{1,0:T(8,128)(2,1)}) custom-call(bf16[512,1024]{1,0:T(8,128)(2,1)S(1)} %copy-done.14, bf16[1024,6144]{1,0:T(8,128)(2,1)S(1)} %bitcast.12, bf16[1024,6144]{1,0:T(8,128)(2,1)S(1)} %bitcast.12, bf16[512,768]{1,0:T(8,128)(2,1)} %collective-permute-done.27.refs_2_, ...), custom_call_target="tpu_custom_call" | custom-call | flops 1610612736 | bytes 8912896 | tf_op jit(solution)/shard_map/pallas_call | solution.py:128
  323.0 6.1 %collective-permute-done.33.refs_2_ = bf16[1024,768]{1,0:T(8,128)(2,1)} collective-permute-done((bf16[1024,768]{1,0:T(8,128)(2,1)}, bf16[1024,768]{1,0:T(8,128)(2,1)}, u32[]{:S(2)}, u32[]{:S(2)}) %collective-permute-start.33) | collective-permute-done | bytes 1572896 | tf_op jit(solution)/shard_map/ppermute | solution.py:251
  330.7 6.5 %shard_map.127 = (bf16[1024,768]{1,0:T(8,128)(2,1)}, bf16[1024,768]{1,0:T(8,128)(2,1)}) custom-call(bf16[1024,1024]{1,0:T(8,128)(2,1)S(1)} %copy-done.10, bf16[1024,6144]{1,0:T(8,128)(2,1)S(1)} %bitcast.12, bf16[1024,6144]{1,0:T(8,128)(2,1)S(1)} %bitcast.12, bf16[1024,768]{1,0:T(8,128)(2,1)} %collective-permute-done.33.refs_2_, ...), custom_call_target="tpu_custom_call" | custom-call | flops 3221225472 | bytes 11534336 | tf_op jit(solution)/shard_map/pallas_call | solution.py:128
  339.5 4.5 %shard_map.129 = bf16[3072,256]{1,0:T(8,128)(2,1)S(1)} custom-call(bf16[1024,256]{1,0:T(8,128)(2,1)S(1)} %copy-done.22, bf16[512,256]{1,0:T(8,128)(2,1)S(1)} %copy-done.26, bf16[6144,1024]{1,0:T(8,128)(2,1)S(1)} %copy-done.4, bf16[6144,512]{1,0:T(8,128)(2,1)S(1)} %constant_dynamic-update-slice_fusion.8.w_value_ref, ...), custom_call_target="tpu_custom_call" | custom-call | flops 2415919104 | bytes 14155776 | tf_op jit(solution)/shard_map/pallas_call | solution.py:157
  349.4 4.6 %copy-done.5 = bf16[6144,1024]{1,0:T(8,128)(2,1)S(1)} copy-done((bf16[6144,1024]{1,0:T(8,128)(2,1)S(1)}, bf16[6144,1024]{1,0:T(8,128)(2,1)}, u32[]{:S(2)}) %copy-start.5) | copy-done | bytes 12582936
  356.8 4.8 %shard_map.119 = f32[3072,256]{1,0:T(8,128)S(1)} custom-call(bf16[1024,256]{1,0:T(8,128)(2,1)S(1)} %copy-done.24, bf16[512,256]{1,0:T(8,128)(2,1)S(1)} %copy-done.28, bf16[6144,1024]{1,0:T(8,128)(2,1)S(1)} %copy-done.5, bf16[6144,512]{1,0:T(8,128)(2,1)S(1)} %copy-done.7, bf16[3072,256]{1,0:T(8,128)(2,1)} %collective-permute-done.23.refs_0_), custom_call_target="tpu_custom_call" | custom-call | flops 2415919104 | bytes 14155776 | tf_op jit(solution)/shard_map/pallas_call | solution.py:157
  361.6 8.4 %collective-permute-done.31.refs_2_ = bf16[1024,768]{1,0:T(8,128)(2,1)} collective-permute-done((bf16[1024,768]{1,0:T(8,128)(2,1)}, bf16[1024,768]{1,0:T(8,128)(2,1)}, u32[]{:S(2)}, u32[]{:S(2)}) %collective-permute-start.31) | collective-permute-done | bytes 1572896 | tf_op jit(solution)/shard_map/ppermute | solution.py:251
  370.0 8.4 %collective-permute-start.42 = (bf16[768,512]{1,0:T(8,128)(2,1)}, bf16[768,512]{1,0:T(8,128)(2,1)}, u32[]{:S(2)}, u32[]{:S(2)}) collective-permute-start(bf16[768,512]{1,0:T(8,128)(2,1)} %get-tuple-element.195), channel_id=1, source_target_pairs={{0,4},{4,0},{8,12},{12,8},{16,20},{20,16},{24,28},{28,24},{1,5},{5... | collective-permute-start | bytes 2359304 | tf_op jit(solution)/shard_map/ppermute | solution.py:251
  378.4 25.7 %collective-permute-done.37.refs_3_ = bf16[1024,768]{1,0:T(8,128)(2,1)} collective-permute-done((bf16[1024,768]{1,0:T(8,128)(2,1)}, bf16[1024,768]{1,0:T(8,128)(2,1)}, u32[]{:S(2)}, u32[]{:S(2)}) %collective-permute-start.37) | collective-permute-done | bytes 1572896 | tf_op jit(solution)/shard_map/ppermute | solution.py:251
  404.1 4.6 %copy-done.2 = bf16[1024,6144]{1,0:T(8,128)(2,1)S(1)} copy-done((bf16[1024,6144]{1,0:T(8,128)(2,1)S(1)}, bf16[1024,6144]{1,0:T(8,128)(2,1)}, u32[]{:S(2)}) %copy-start.2) | copy-done | bytes 12582936
  408.6 7.0 %shard_map.130 = (bf16[768,1024]{1,0:T(8,128)(2,1)S(1)}, bf16[768,1024]{1,0:T(8,128)(2,1)}) custom-call(bf16[1024,1024]{1,0:T(8,128)(2,1)S(1)} %copy-done.11, bf16[1024,6144]{1,0:T(8,128)(2,1)S(1)} %copy-done.2, bf16[1024,6144]{1,0:T(8,128)(2,1)S(1)} %copy-done.2, bf16[1024,768]{1,0:T(8,128)(2,1)} %collective-permute-done.31.refs_2_, ...), custom_call_target="tpu_custom_call" | custom-call | flops 3221225472 | bytes 14680064 | tf_op jit(solution)/shard_map/pallas_call | solution.py:128
  415.7 4.8 %collective-permute-start.41 = (bf16[768,1024]{1,0:T(8,128)(2,1)}, bf16[768,1024]{1,0:T(8,128)(2,1)S(1)}, u32[]{:S(2)}, u32[]{:S(2)}) collective-permute-start(bf16[768,1024]{1,0:T(8,128)(2,1)} %get-tuple-element.193), channel_id=1, source_target_pairs={{0,4},{4,0},{8,12},{12,8},{16,20},{20,16},{24,28},{28,24},{1,5},{5... | collective-permute-start | bytes 4718600 | tf_op jit(solution)/shard_map/ppermute | solution.py:251
  432.7 4.5 %shard_map.131 = bf16[128,6144]{1,0:T(8,128)(2,1)} custom-call(s32[1]{0:T(128)} %bitcast.place_ref, f32[3072,128]{1,0:T(8,128)S(1)} %constant_dynamic-slice_fusion.mine_ref, bf16[3072,128]{1,0:T(8,128)(2,1)} %collective-permute-done.40.other_ref, f32[128,6144]{1,0:T(8,128)S(1)} %copy-done.17, f32[128,1]{1,0:T(8,128)S(1)} %copy.12.spread_ref, ...), custom_call_target="tpu_custom_call" | custom-call | tf_op jit(solution)/shard_map/pallas_call | solution.py:232
  (282 shorter events, 146.5 us)
Async XLA Ops:
  12.9 37.6 %collective-permute-start.7 = (bf16[256,3072]{1,0:T(8,128)(2,1)}, bf16[256,3072]{1,0:T(8,128)(2,1)}, u32[]{:S(2)}, u32[]{:S(2)}) collective-permute-start(bf16[256,3072]{1,0:T(8,128)(2,1)} %pad_maximum_fusion.2), channel_id=1, source_target_pairs={{0,2},{2,3},{3,1},{1,0},{4,6},{6,7},{7,5},{5,4},{8,10},{10,11},{11... | collective-permute-start | bytes 4718600 | tf_op jit(solution)/shard_map/ppermute | solution.py:271
  16.6 48.4 %collective-permute-start.1 = (bf16[768,1024]{1,0:T(8,128)(2,1)S(1)}, bf16[768,1024]{1,0:T(8,128)(2,1)}, u32[]{:S(2)}, u32[]{:S(2)}) collective-permute-start(bf16[768,1024]{1,0:T(8,128)(2,1)S(1)} %pad_maximum_fusion), channel_id=1, source_target_pairs={{0,8},{4,12},{8,0},{12,4},{16,24},{20,28},{24,16},{28,20},{1,9},{5... | collective-permute-start | bytes 4718600 | tf_op jit(solution)/shard_map/ppermute | solution.py:251
  17.8 47.2 %collective-permute-start.3 = (bf16[768,1024]{1,0:T(8,128)(2,1)S(1)}, bf16[768,1024]{1,0:T(8,128)(2,1)}, u32[]{:S(2)}, u32[]{:S(2)}) collective-permute-start(bf16[768,1024]{1,0:T(8,128)(2,1)S(1)} %pad_maximum_fusion), channel_id=1, source_target_pairs={{0,16},{4,20},{8,24},{12,28},{16,0},{20,4},{24,8},{28,12},{1,17},{... | collective-permute-start | bytes 4718600 | tf_op jit(solution)/shard_map/ppermute | solution.py:251
  22.0 63.8 %collective-permute-start.2 = (bf16[768,1024]{1,0:T(8,128)(2,1)}, bf16[768,1024]{1,0:T(8,128)(2,1)S(1)}, u32[]{:S(2)}, u32[]{:S(2)}) collective-permute-start(bf16[768,1024]{1,0:T(8,128)(2,1)} %collective-permute-done), channel_id=1, source_target_pairs={{0,8},{4,12},{8,0},{12,4},{16,24},{20,28},{24,16},{28,20},{1,9},{5... | collective-permute-start | bytes 4718600 | tf_op jit(solution)/shard_map/ppermute | solution.py:251
  22.3 64.5 %collective-permute-start.4 = (bf16[768,1024]{1,0:T(8,128)(2,1)}, bf16[768,1024]{1,0:T(8,128)(2,1)S(1)}, u32[]{:S(2)}, u32[]{:S(2)}) collective-permute-start(bf16[768,1024]{1,0:T(8,128)(2,1)} %collective-permute-done), channel_id=1, source_target_pairs={{0,16},{4,20},{8,24},{12,28},{16,0},{20,4},{24,8},{28,12},{1,17},{... | collective-permute-start | bytes 4718600 | tf_op jit(solution)/shard_map/ppermute | solution.py:251
  60.1 37.2 %collective-permute-start.10 = (bf16[256,3072]{1,0:T(8,128)(2,1)}, bf16[256,3072]{1,0:T(8,128)(2,1)S(1)}, u32[]{:S(2)}, u32[]{:S(2)}) collective-permute-start(bf16[256,3072]{1,0:T(8,128)(2,1)} %collective-permute-done.7), channel_id=1, source_target_pairs={{0,2},{2,3},{3,1},{1,0},{4,6},{6,7},{7,5},{5,4},{8,10},{10,11},{11... | collective-permute-start | bytes 4718600 | tf_op jit(solution)/shard_map/ppermute | solution.py:271
  86.8 49.6 %collective-permute-start.14 = (bf16[768,1024]{1,0:T(8,128)(2,1)}, bf16[768,1024]{1,0:T(8,128)(2,1)S(1)}, u32[]{:S(2)}, u32[]{:S(2)}) collective-permute-start(bf16[768,1024]{1,0:T(8,128)(2,1)} %collective-permute-done.1), channel_id=1, source_target_pairs={{0,16},{4,20},{8,24},{12,28},{16,0},{20,4},{24,8},{28,12},{1,17},{... | collective-permute-start | bytes 4718600 | tf_op jit(solution)/shard_map/ppermute | solution.py:251
  88.0 50.3 %collective-permute-start.15 = (bf16[768,1024]{1,0:T(8,128)(2,1)S(1)}, bf16[768,1024]{1,0:T(8,128)(2,1)S(1)}, u32[]{:S(2)}, u32[]{:S(2)}) collective-permute-start(bf16[768,1024]{1,0:T(8,128)(2,1)S(1)} %collective-permute-done.4), channel_id=1, source_target_pairs={{0,8},{4,12},{8,0},{12,4},{16,24},{20,28},{24,16},{28,20},{1,9},{5... | collective-permute-start | bytes 4718600 | tf_op jit(solution)/shard_map/ppermute | solution.py:251
  98.2 37.5 %collective-permute-start.12 = (bf16[256,3072]{1,0:T(8,128)(2,1)S(1)}, bf16[256,3072]{1,0:T(8,128)(2,1)S(1)}, u32[]{:S(2)}, u32[]{:S(2)}) collective-permute-start(bf16[256,3072]{1,0:T(8,128)(2,1)S(1)} %collective-permute-done.10), channel_id=1, source_target_pairs={{0,2},{2,3},{3,1},{1,0},{4,6},{6,7},{7,5},{5,4},{8,10},{10,11},{11... | collective-permute-start | bytes 4718600 | tf_op jit(solution)/shard_map/ppermute | solution.py:271
  103.4 66.8 %collective-permute-start.17 = (bf16[1536,512]{1,0:T(8,128)(2,1)}, bf16[1536,512]{1,0:T(8,128)(2,1)S(1)}, u32[]{:S(2)}, u32[]{:S(2)}) collective-permute-start(bf16[1536,512]{1,0:T(8,128)(2,1)} %pad_maximum_fusion.3), channel_id=1, source_target_pairs={{0,8},{4,12},{8,0},{12,4},{16,24},{20,28},{24,16},{28,20},{1,9},{5... | collective-permute-start | bytes 4718600 | tf_op jit(solution)/shard_map/ppermute | solution.py:251
  104.7 65.5 %collective-permute-start.18 = (bf16[1536,512]{1,0:T(8,128)(2,1)}, bf16[1536,512]{1,0:T(8,128)(2,1)}, u32[]{:S(2)}, u32[]{:S(2)}) collective-permute-start(bf16[1536,512]{1,0:T(8,128)(2,1)} %pad_maximum_fusion.3), channel_id=1, source_target_pairs={{0,16},{4,20},{8,24},{12,28},{16,0},{20,4},{24,8},{28,12},{1,17},{... | collective-permute-start | bytes 4718600 | tf_op jit(solution)/shard_map/ppermute | solution.py:251
  177.0 19.1 %collective-permute-start.19 = (bf16[768,512]{1,0:T(8,128)(2,1)}, bf16[768,512]{1,0:T(8,128)(2,1)}, u32[]{:S(2)}, u32[]{:S(2)}) collective-permute-start(bf16[768,512]{1,0:T(8,128)(2,1)} %get-tuple-element.130), channel_id=1, source_target_pairs={{0,16},{4,20},{8,24},{12,28},{16,0},{20,4},{24,8},{28,12},{1,17},{... | collective-permute-start | bytes 2359304 | tf_op jit(solution)/shard_map/ppermute | solution.py:251
  178.2 18.5 %collective-permute-start.20 = (bf16[768,512]{1,0:T(8,128)(2,1)S(1)}, bf16[768,512]{1,0:T(8,128)(2,1)}, u32[]{:S(2)}, u32[]{:S(2)}) collective-permute-start(bf16[768,512]{1,0:T(8,128)(2,1)S(1)} %get-tuple-element.135), channel_id=1, source_target_pairs={{0,8},{4,12},{8,0},{12,4},{16,24},{20,28},{24,16},{28,20},{1,9},{5... | collective-permute-start | bytes 2359304 | tf_op jit(solution)/shard_map/ppermute | solution.py:251
  179.4 47.1 %collective-permute-start.21 = (bf16[512,768]{1,0:T(8,128)(2,1)}, bf16[512,768]{1,0:T(8,128)(2,1)S(1)}, u32[]{:S(2)}, u32[]{:S(2)}) collective-permute-start(bf16[512,768]{1,0:T(8,128)(2,1)} %get-tuple-element.137), channel_id=1, source_target_pairs={{0,8},{4,12},{8,0},{12,4},{16,24},{20,28},{24,16},{28,20},{1,9},{5... | collective-permute-start | bytes 2359304 | tf_op jit(solution)/shard_map/ppermute | solution.py:251
  179.7 46.8 %collective-permute-start.22 = (bf16[512,768]{1,0:T(8,128)(2,1)}, bf16[512,768]{1,0:T(8,128)(2,1)S(1)}, u32[]{:S(2)}, u32[]{:S(2)}) collective-permute-start(bf16[512,768]{1,0:T(8,128)(2,1)} %get-tuple-element.138), channel_id=1, source_target_pairs={{0,16},{4,20},{8,24},{12,28},{16,0},{20,4},{24,8},{28,12},{1,17},{... | collective-permute-start | bytes 2359304 | tf_op jit(solution)/shard_map/ppermute | solution.py:251
  239.2 23.1 %collective-permute-start.29 = (bf16[3072,256]{1,0:T(8,128)(2,1)}, bf16[3072,256]{1,0:T(8,128)(2,1)S(1)}, u32[]{:S(2)}, u32[]{:S(2)}) collective-permute-start(bf16[3072,256]{1,0:T(8,128)(2,1)} %shard_map.123), channel_id=1, source_target_pairs={{0,4},{4,0},{8,12},{12,8},{16,20},{20,16},{24,28},{28,24},{1,5},{5... | collective-permute-start | bytes 4718600 | tf_op jit(solution)/shard_map/ppermute | solution.py:251
  241.9 19.5 %collective-permute-start.27 = (bf16[512,768]{1,0:T(8,128)(2,1)}, bf16[512,768]{1,0:T(8,128)(2,1)}, u32[]{:S(2)}, u32[]{:S(2)}) collective-permute-start(bf16[512,768]{1,0:T(8,128)(2,1)} %get-tuple-element.162), channel_id=1, source_target_pairs={{0,8},{4,12},{8,0},{12,4},{16,24},{20,28},{24,16},{28,20},{1,9},{5... | collective-permute-start | bytes 2359304 | tf_op jit(solution)/shard_map/ppermute | solution.py:251
  243.1 19.2 %collective-permute-start.28 = (bf16[512,768]{1,0:T(8,128)(2,1)}, bf16[512,768]{1,0:T(8,128)(2,1)}, u32[]{:S(2)}, u32[]{:S(2)}) collective-permute-start(bf16[512,768]{1,0:T(8,128)(2,1)} %get-tuple-element.163), channel_id=1, source_target_pairs={{0,16},{4,20},{8,24},{12,28},{16,0},{20,4},{24,8},{28,12},{1,17},{... | collective-permute-start | bytes 2359304 | tf_op jit(solution)/shard_map/ppermute | solution.py:251
  247.3 49.1 %collective-permute-start.26 = (bf16[3072,256]{1,0:T(8,128)(2,1)}, bf16[3072,256]{1,0:T(8,128)(2,1)}, u32[]{:S(2)}, u32[]{:S(2)}) collective-permute-start(bf16[3072,256]{1,0:T(8,128)(2,1)} %shard_map.120), channel_id=1, source_target_pairs={{0,4},{4,0},{8,12},{12,8},{16,20},{20,16},{24,28},{28,24},{1,5},{5... | collective-permute-start | bytes 4718600 | tf_op jit(solution)/shard_map/ppermute | solution.py:251
  268.7 36.1 %collective-permute-start.30 = (bf16[3072,256]{1,0:T(8,128)(2,1)}, bf16[3072,256]{1,0:T(8,128)(2,1)}, u32[]{:S(2)}, u32[]{:S(2)}) collective-permute-start(bf16[3072,256]{1,0:T(8,128)(2,1)} %shard_map.125), channel_id=1, source_target_pairs={{0,2},{2,3},{3,1},{1,0},{4,6},{6,7},{7,5},{5,4},{8,10},{10,11},{11... | collective-permute-start | bytes 4718600 | tf_op jit(solution)/shard_map/ppermute | solution.py:271
  271.8 17.7 %collective-permute-start.24 = (bf16[512,768]{1,0:T(8,128)(2,1)S(1)}, bf16[512,768]{1,0:T(8,128)(2,1)S(1)}, u32[]{:S(2)}, u32[]{:S(2)}) collective-permute-start(bf16[512,768]{1,0:T(8,128)(2,1)S(1)} %copy-done.44), channel_id=1, source_target_pairs={{0,8},{4,12},{8,0},{12,4},{16,24},{20,28},{24,16},{28,20},{1,9},{5... | collective-permute-start | bytes 2359304 | tf_op jit(solution)/shard_map/ppermute | solution.py:251
  276.5 62.7 %collective-permute-start.35 = (bf16[3072,256]{1,0:T(8,128)(2,1)}, bf16[3072,256]{1,0:T(8,128)(2,1)}, u32[]{:S(2)}, u32[]{:S(2)}) collective-permute-start(bf16[3072,256]{1,0:T(8,128)(2,1)} %shard_map.126), channel_id=1, source_target_pairs={{0,4},{4,0},{8,12},{12,8},{16,20},{20,16},{24,28},{28,24},{1,5},{5... | collective-permute-start | bytes 4718600 | tf_op jit(solution)/shard_map/ppermute | solution.py:251
  295.2 33.9 %collective-permute-start.33 = (bf16[1024,768]{1,0:T(8,128)(2,1)}, bf16[1024,768]{1,0:T(8,128)(2,1)}, u32[]{:S(2)}, u32[]{:S(2)}) collective-permute-start(bf16[1024,768]{1,0:T(8,128)(2,1)} %get-tuple-element.171), channel_id=1, source_target_pairs={{0,16},{4,20},{8,24},{12,28},{16,0},{20,4},{24,8},{28,12},{1,17},{... | collective-permute-start | bytes 4718600 | tf_op jit(solution)/shard_map/ppermute | solution.py:251
  295.4 33.7 %collective-permute-start.34 = (bf16[1024,768]{1,0:T(8,128)(2,1)}, bf16[1024,768]{1,0:T(8,128)(2,1)}, u32[]{:S(2)}, u32[]{:S(2)}) collective-permute-start(bf16[1024,768]{1,0:T(8,128)(2,1)} %get-tuple-element.172), channel_id=1, source_target_pairs={{0,8},{4,12},{8,0},{12,4},{16,24},{20,28},{24,16},{28,20},{1,9},{5... | collective-permute-start | bytes 4718600 | tf_op jit(solution)/shard_map/ppermute | solution.py:251
  307.7 36.3 %collective-permute-start.36 = (bf16[3072,256]{1,0:T(8,128)(2,1)}, bf16[3072,256]{1,0:T(8,128)(2,1)}, u32[]{:S(2)}, u32[]{:S(2)}) collective-permute-start(bf16[3072,256]{1,0:T(8,128)(2,1)} %add_convert_fusion.1), channel_id=1, source_target_pairs={{0,2},{2,3},{3,1},{1,0},{4,6},{6,7},{7,5},{5,4},{8,10},{10,11},{11... | collective-permute-start | bytes 4718600 | tf_op jit(solution)/shard_map/ppermute | solution.py:271
  314.9 32.8 %collective-permute-start.23 = (bf16[3072,256]{1,0:T(8,128)(2,1)}, bf16[3072,256]{1,0:T(8,128)(2,1)}, u32[]{:S(2)}, u32[]{:S(2)}) collective-permute-start(bf16[3072,256]{1,0:T(8,128)(2,1)} %shard_map.118), channel_id=1, source_target_pairs={{0,4},{4,0},{8,12},{12,8},{16,20},{20,16},{24,28},{28,24},{1,5},{5... | collective-permute-start | bytes 4718600 | tf_op jit(solution)/shard_map/ppermute | solution.py:251
  337.2 32.7 %collective-permute-start.31 = (bf16[1024,768]{1,0:T(8,128)(2,1)}, bf16[1024,768]{1,0:T(8,128)(2,1)}, u32[]{:S(2)}, u32[]{:S(2)}) collective-permute-start(bf16[1024,768]{1,0:T(8,128)(2,1)} %copy-done.40), channel_id=1, source_target_pairs={{0,8},{4,12},{8,0},{12,4},{16,24},{20,28},{24,16},{28,20},{1,9},{5... | collective-permute-start | bytes 4718600 | tf_op jit(solution)/shard_map/ppermute | solution.py:251
  338.0 40.3 %collective-permute-start.32 = (bf16[1024,768]{1,0:T(8,128)(2,1)}, bf16[1024,768]{1,0:T(8,128)(2,1)}, u32[]{:S(2)}, u32[]{:S(2)}) collective-permute-start(bf16[1024,768]{1,0:T(8,128)(2,1)} %copy-done.39), channel_id=1, source_target_pairs={{0,16},{4,20},{8,24},{12,28},{16,0},{20,4},{24,8},{28,12},{1,17},{... | collective-permute-start | bytes 4718600 | tf_op jit(solution)/shard_map/ppermute | solution.py:251
  339.2 64.8 %collective-permute-start.37 = (bf16[1024,768]{1,0:T(8,128)(2,1)}, bf16[1024,768]{1,0:T(8,128)(2,1)}, u32[]{:S(2)}, u32[]{:S(2)}) collective-permute-start(bf16[1024,768]{1,0:T(8,128)(2,1)} %get-tuple-element.186), channel_id=1, source_target_pairs={{0,16},{4,20},{8,24},{12,28},{16,0},{20,4},{24,8},{28,12},{1,17},{... | collective-permute-start | bytes 4718600 | tf_op jit(solution)/shard_map/ppermute | solution.py:251
  344.0 60.0 %collective-permute-start.38 = (bf16[1024,768]{1,0:T(8,128)(2,1)}, bf16[1024,768]{1,0:T(8,128)(2,1)S(1)}, u32[]{:S(2)}, u32[]{:S(2)}) collective-permute-start(bf16[1024,768]{1,0:T(8,128)(2,1)} %get-tuple-element.187), channel_id=1, source_target_pairs={{0,8},{4,12},{8,0},{12,4},{16,24},{20,28},{24,16},{28,20},{1,9},{5... | collective-permute-start | bytes 4718600 | tf_op jit(solution)/shard_map/ppermute | solution.py:251
  347.7 72.8 %collective-permute-start.39 = (bf16[3072,256]{1,0:T(8,128)(2,1)}, bf16[3072,256]{1,0:T(8,128)(2,1)}, u32[]{:S(2)}, u32[]{:S(2)}) collective-permute-start(bf16[3072,256]{1,0:T(8,128)(2,1)} %add_convert_fusion), channel_id=1, source_target_pairs={{0,2},{2,3},{3,1},{1,0},{4,6},{6,7},{7,5},{5,4},{8,10},{10,11},{11... | collective-permute-start | bytes 4718600 | tf_op jit(solution)/shard_map/ppermute | solution.py:271
  370.0 55.1 %collective-permute-start.42 = (bf16[768,512]{1,0:T(8,128)(2,1)}, bf16[768,512]{1,0:T(8,128)(2,1)}, u32[]{:S(2)}, u32[]{:S(2)}) collective-permute-start(bf16[768,512]{1,0:T(8,128)(2,1)} %get-tuple-element.195), channel_id=1, source_target_pairs={{0,4},{4,0},{8,12},{12,8},{16,20},{20,16},{24,28},{28,24},{1,5},{5... | collective-permute-start | bytes 2359304 | tf_op jit(solution)/shard_map/ppermute | solution.py:251
  (78 other events, 835.4 us)

commit v5 on v4

--- a/solution.py
+++ b/solution.py
@@ -36,6 +36,10 @@
 
 def params(mib):
     return pltpu.CompilerParams(vmem_limit_bytes=mib * 2**20)
+
+
+def cost(flops, bytes_accessed):
+    return pl.CostEstimate(flops=flops, bytes_accessed=bytes_accessed, transcendentals=0)
 
 
 def blank(shape, dtype):
@@ -96,11 +100,7 @@
         out_specs=pl.BlockSpec((out_rows, PATCH), lambda i: (0, i)),
         out_shape=jax.ShapeDtypeStruct((out_rows, tokens), BF),
         compiler_params=params(32),
-        cost_estimate=pl.CostEstimate(
-            flops=pairs * 8 * PATCH * PATCH * head,
-            bytes_accessed=4 * len(arrays) * arrays[0].size,
-            transcendentals=pairs * PATCH * PATCH,
-        ),
+        cost_estimate=cost(pairs * 8 * PATCH * PATCH * head, 4 * len(arrays) * arrays[0].size),
     )(*arrays, gains)
 
 
@@ -117,28 +117,35 @@
 def product_call(turned, normed, rows, units, addends=((), ()), turn=False):
     columns, tokens = turned.shape
     tile = 256 if rows % 256 == 0 else 128
-    n_add, steps = len(addends[0]), rows // tile
-    wide = pl.BlockSpec((columns, tile), lambda i: (0, i))
-    tall = pl.BlockSpec((tile, columns), lambda i: (i, 0))
-
-    def side(unit):
-        return pl.BlockSpec((tokens, tile), lambda i: (0, unit * steps + i))
-
-    shape = (rows, columns) if turn else (columns, rows)
+    count, n_add, steps = len(units[0]), len(addends[0]), rows // tile
+
+    def side(first, last):
+        return pl.BlockSpec((tokens, tile), lambda u, i: (0, (first + u * (last - first)) * steps + i))
+
+    def added(which):
+        return pl.BlockSpec((columns, tile), lambda u, i: (which, i))
+
+    if turn:
+        shape, out = (rows, columns), pl.BlockSpec((tile, columns), lambda u, i: (i, 0))
+    else:
+        shape, out = (count * columns, rows), pl.BlockSpec((columns, tile), lambda u, i: (u, i))
+    addends = [*addends[0], *addends[1]]
     return pl.pallas_call(
         functools.partial(product_kernel, n_add, turn),
-        grid=(steps,),
-        in_specs=[pl.BlockSpec((columns, tokens), lambda i: (0, 0)), side(units[0]), side(units[1])]
-        + [wide] * (2 * n_add),
-        out_specs=[tall if turn else wide] * 2,
+        grid=(count, steps),
+        in_specs=[
+            pl.BlockSpec((columns, tokens), lambda u, i: (0, 0)),
+            *[side(chosen[0], chosen[-1]) for chosen in units],
+            *[added(which) for _, which in addends],
+        ],
+        out_specs=[out] * 2,
         out_shape=[jax.ShapeDtypeStruct(shape, BF)] * 2,
         compiler_params=params(24),
-        cost_estimate=pl.CostEstimate(
-            flops=4 * columns * tokens * rows,
-            bytes_accessed=2 * (columns * tokens + 2 * tokens * rows + (2 + 2 * n_add) * columns * rows),
-            transcendentals=0,
+        cost_estimate=cost(
+            4 * count * columns * tokens * rows,
+            2 * columns * tokens + 4 * count * tokens * rows + (4 + 4 * n_add) * columns * rows,
         ),
-    )(turned, normed, normed, *addends[0], *addends[1])
+    )(turned, normed, normed, *[array for array, _ in addends])
 
 
 def back_kernel(pair_ref, value_ref, w_pair_ref, w_value_ref, *refs):
@@ -167,10 +174,9 @@
         out_specs=block,
         out_shape=jax.ShapeDtypeStruct((units * rows, level_tokens), dtype),
         compiler_params=params(24),
-        cost_estimate=pl.CostEstimate(
-            flops=2 * units * rows * level_tokens * (pair.shape[0] + value.shape[0]),
-            bytes_accessed=2 * units * rows * (pair.shape[0] + value.shape[0] + 3 * level_tokens),
-            transcendentals=0,
+        cost_estimate=cost(
+            2 * units * rows * level_tokens * (pair.shape[0] + value.shape[0]),
+            2 * units * rows * (pair.shape[0] + value.shape[0] + 3 * level_tokens),
         ),
     )(pair, value, w_pair, w_value, *addends)
 
@@ -253,10 +259,8 @@
     def half(array, which):
         return lax.dynamic_slice_in_dim(array, which * cols, cols, 1)
 
-    def after(arrays, *others):
-        flat, tree = jax.tree.flatten(arrays)
-        done = lax.optimization_barrier((*flat, *jax.tree.leaves(others)))
-        return jax.tree.unflatten(tree, done[: len(flat)])
+    def together(*arrays):
+        return lax.optimization_barrier(arrays)
 
     ring = list(range(0, n_mp, 2)) + list(range(n_mp - 1, 0, -2))
     level = lax.axis_index("mp")
@@ -302,16 +306,15 @@
 
     pair_weights = (w_query, w_key)
     own_pair, sent_pair = columns_of(pair_weights, core), columns_of(pair_weights, 1 - core)
+    tokens, own_pair, sent_pair = together(tokens, own_pair, sent_pair)
     held_pair = gather_start({0: own_pair})
     other_pair = swap(sent_pair, 1)
 
-    tokens = after(tokens, own_pair, sent_pair)
     normed_own, unit_rows, row_spread = normalize(tokens.astype(F32), norm_gain)
     normed_own = normed_own.astype(BF)
     even = jnp.concatenate([feature_block(normed_own, r) for r in range(0, n_dp, 2)], axis=1)
     odd = jnp.concatenate([feature_block(normed_own, r) for r in range(1, n_dp, 2)], axis=1)
     block = jnp.concatenate([even, swap(odd, 1)], axis=0)
-    held_pair.update(gather_start({1: other_pair}))
 
     normed = blank((2 * group, width), BF)
 
@@ -328,18 +331,20 @@
             normed = lax.dynamic_update_slice(normed, piece, (at, column))
         return normed
 
+    held_pair, normed = together(held_pair, normed)
+    held_pair.update(gather_start({1: other_pair}))
     normed = put(normed, block, 0)
     for step in range(1, n_mp):
         block = ring_on(block)
         normed = put(normed, block, step)
         if step == 1:
-            held_pair, normed, w_value, grad_heads = after((held_pair, normed, w_value, grad_heads))
+            held_pair, normed, w_value, grad_heads = together(held_pair, normed, w_value, grad_heads)
             held_pair = gather_rest(held_pair)
             shard_value = [half(w_value, core), swap(half(w_value, 1 - core), 1)]
             shard_value = jnp.concatenate(shard_value, axis=0)
             grads_mine, grads_other = half(grad_heads, core), swap(half(grad_heads, 1 - core), 1)
         elif step == 2:
-            shard_value, normed = after((shard_value, normed))
+            shard_value, normed = together(shard_value, normed)
             held_value = gather_start({0: shard_value})
 
     grad_out = blank((2 * group, cols), BF)
@@ -352,35 +357,32 @@
     turned_value = attention_call(first_kernel, (pair, grad_out), gains, cols)
 
     def products(turned, r, offsets, addends=((), ()), turn=False):
-        return product_call(
-            turned, normed, rows, [unit_of(r ^ f) for f in offsets], addends, turn
-        )
+        units = [[unit_of(r ^ f) for f in side] for side in offsets]
+        return product_call(turned, normed, rows, units, addends, turn)
 
     blocks_of_four = range(0, n_dp, 8)
 
-    def far_messages(turned):
-        return [products(turned, r, (6, 7)) for r in blocks_of_four]
-
-    def early_messages(turned):
-        return [products(turned, r, (2, 5)) for r in blocks_of_four]
+    def messages(turned, to_x, to_y):
+        return [products(turned, r, (to_x, to_y)) for r in blocks_of_four]
 
     def late_messages(turned, far):
         return [
-            products(turned, r, (3, 4), ((from_y,), (from_x,)))
+            products(turned, r, ((3,), (4,)), (((from_y, 0),), ((from_x, 0),)))
             for r, (from_x, from_y) in zip(blocks_of_four, far)
         ]
 
     def send(messages):
         return [[swap(to_x, 2), swap(to_y, 4)] for to_x, to_y in messages]
 
-    def scatter_end(turned, early, late):
+    def scatter_end(turned, early, unit, late):
+        def own(r, turn):
+            (early_x, early_y), (late_x, late_y) = early[r // 8], late[r // 8]
+            addends = (((early_x, unit), (late_y, 0)), ((early_y, unit), (late_x, 0)))
+            return products(turned, r, ((0,), (1,)), addends, turn)
+
         if n_dp == 8:
-            (even_x, odd_y), (odd_x, even_y) = early[0], late[0]
-            return products(turned, 0, (0, 1), ((even_x, even_y), (odd_x, odd_y)), True)
-        totals = {}
-        for r in range(0, n_dp, 8):
-            (even_x, odd_y), (odd_x, even_y) = early[r // 8], late[r // 8]
-            totals[r] = products(turned, r, (0, 1), ((even_x, even_y), (odd_x, odd_y)))
+            return own(0, True)
+        totals = {r: own(r, False) for r in blocks_of_four}
         bit = n_dp // 2
         while bit >= 8:
             for r in [r for r in totals if r < bit]:
@@ -391,75 +393,89 @@
             bit //= 2
         return [total.T for total in totals[0]]
 
-    far_value, early_value = far_messages(turned_value), early_messages(turned_value)
-    held_value, far_value, early_value = after((held_value, far_value, early_value))
-    held_value = {r ^ f: held_value[r][f * rows : (f + 1) * rows] for r in held_value for f in (0, 1)}
-    held_value, far_value = after((held_value, far_value))
-    held_value = gather_rest(held_value)
-    far_value = send(far_value)
-    held_value, early_value = after((held_value, early_value))
-    early_value = send(early_value)
+    held_value, turned_value = together(held_value, turned_value)
+    pieces = {r ^ f: part[f * rows : (f + 1) * rows] for r, part in held_value.items() for f in (0, 1)}
+    relayed = [r ^ f for r in blocks_of_four for f in (2, 5)]
+    pieces.update(zip(relayed, together(*[pieces[r] for r in relayed])))
+    held_value = gather_rest(pieces)
+    first_value = send(messages(turned_value, (6, 2), (7, 5)))
     full_value = whole(held_value)
     values = jnp.dot(normed, full_value, preferred_element_type=F32).astype(BF)
     turned_pair = attention_call(rest_kernel, (pair, grad_out, values), gains, 2 * cols)
 
-    turned_value, turned_pair, far_value = after((turned_value, turned_pair, far_value))
-    late_value = late_messages(turned_value, far_value)
-    turned_value, turned_pair, late_value = after((turned_value, turned_pair, late_value))
-    late_value = send(late_value)
-
-    def back_odd(step, gate):
+    def back_odd(step, turned_pair, turned_value):
         at = level_at(step + 1) * own
         chosen = [
             jnp.concatenate(
                 [lax.dynamic_slice_in_dim(turned, g * group + at, own, 1) for g in range(2)], axis=1
             )
-            for turned in after((turned_pair, turned_value), gate)
+            for turned in (turned_pair, turned_value)
         ]
-        sent = back_call(*chosen, full_pair, full_value, rows, True, (), BF)
-        return chosen, sent, swap(sent, 1)
-
-    gate, arrived = [], None
-    for step in range(n_mp):
-        last = step == n_mp - 1
-        if last:
-            early_pair, gate = after((early_pair, gate))
-        chosen, sent, passed = back_odd(step, gate)
-        if step == 0:
-            far_pair = far_messages(after(turned_pair, sent))
-            chosen, far_pair, early_value = after((chosen, far_pair, early_value))
-        elif step == 1:
-            turned_early, late_value = after((turned_pair, late_value), sent)
-            early_pair = early_messages(turned_early)
-            chosen, early_pair = after((chosen, early_pair))
+        return chosen, back_call(*chosen, full_pair, full_value, rows, True, (), BF)
+
+    def back_even(chosen, passed, dtype):
+        return back_call(*chosen, full_pair, full_value, rows, False, (passed,), dtype)
+
+    chosen, sent, partial = {}, {}, {}
+    chosen[0], sent[0] = back_odd(0, turned_pair, turned_value)
+    chosen[1], sent[1] = back_odd(1, turned_pair, turned_value)
+    late_value = late_messages(turned_value, first_value)
+    late_value, sent = together(late_value, sent)
+    late_value = send(late_value)
+    passed = {step: swap(sent[step], 1) for step in range(2)}
+    far_pair = messages(turned_pair, (6,), (7,))
+    far_pair, passed = together(far_pair, passed)
+    message = back_even(chosen[0], passed[0], BF)
+    message, far_pair, turned_pair, turned_value = together(message, far_pair, turned_pair, turned_value)
+    arrived, far_pair = ring_on(message), send(far_pair)
+
+    turned_pair, turned_value, late_value = together(turned_pair, turned_value, late_value)
+    for step in range(2, 4):
+        chosen[step], sent[step] = back_odd(step, turned_pair, turned_value)
+    ends_value = scatter_end(turned_value, first_value, 1, late_value)
+    partial[1] = back_even(chosen[1], passed[1], BF)
+    early_pair = messages(turned_pair, (2,), (5,))
+    for step in range(1, n_mp - 1):
+        if step == 1:
+            partial[1], early_pair, sent, far_pair, ends_value = together(
+                partial[1], early_pair, sent, far_pair, ends_value
+            )
         elif step == 2:
-            late_pair = late_messages(after(turned_pair, sent), far_pair)
-            chosen, late_pair = after((chosen, late_pair))
-            late_pair = send(late_pair)
-            chosen, ends_value = after((chosen, scatter_end(turned_value, early_value, late_value)))
-            passed_value = swap(ends_value[1], 1)
-        total = back_call(
-            *chosen, full_pair, full_value, rows, False, (passed,), F32 if last else BF
-        )
-        if last:
-            ends_pair = scatter_end(after(turned_pair, total), early_pair, late_pair)
-            total, ends_pair = after((total, ends_pair))
-        if arrived is not None:
-            total = total.astype(F32) + arrived.astype(F32)
-        if not last:
-            total = total.astype(BF)
-            arrived = ring_on(total)
-        gate = total
-        if step == 0:
-            far_pair, gate = after((far_pair, total))
-            far_pair = send(far_pair)
-        elif step == 1:
-            early_pair, gate = after((early_pair, total))
+            partial[2], late_pair, early_pair = together(partial[2], late_pair, early_pair)
+        message = (partial[step].astype(F32) + arrived.astype(F32)).astype(BF)
+        if step == 1:
+            message, early_pair, sent, turned_pair, turned_value = together(
+                message, early_pair, sent, turned_pair, turned_value
+            )
             early_pair = send(early_pair)
-
+        elif step == 2:
+            message, late_pair, ends_value = together(message, late_pair, ends_value)
+            late_pair, passed_value = send(late_pair), swap(ends_value[1], 1)
+        arrived = ring_on(message)
+        if step + 2 < n_mp:
+            near = [step + 1, step + 2] if step + 3 == n_mp else [step + 1]
+            for level_step in near:
+                passed[level_step] = swap(sent[level_step], 1)
+            here = [passed[level_step] for level_step in near]
+            turned_pair, turned_value, here = together(turned_pair, turned_value, here)
+            passed.update(zip(near, here))
+            for level_step in near:
+                dtype = F32 if level_step == n_mp - 1 else BF
+                partial[level_step] = back_even(chosen[level_step], passed[level_step], dtype)
+            if step + 3 == n_mp:
+                partial[n_mp - 2], partial[n_mp - 1] = together(partial[n_mp - 2], partial[n_mp - 1])
+            else:
+                chosen[step + 3], sent[step + 3] = back_odd(step + 3, turned_pair, turned_value)
+            if step == 1:
+                late_pair = late_messages(turned_pair, far_pair)
+    total = partial[n_mp - 1] + arrived.astype(F32)
+
+    mine = lax.dynamic_slice_in_dim(total, core * own, own, 1)
+    other = lax.dynamic_slice_in_dim(total, (1 - core) * own, own, 1).astype(BF)
+    mine, other, turned_pair = together(mine, other, turned_pair)
+    other = swap(other, 1)
+    ends_pair = scatter_end(turned_pair, early_pair, 0, late_pair)
     passed_pair = swap(ends_pair[1], 1)
-    mine = lax.dynamic_slice_in_dim(total, core * own, own, 1)
-    other = swap(lax.dynamic_slice_in_dim(total, (1 - core) * own, own, 1).astype(BF), 1)
     out_value = place_call(core, ends_value[0], passed_value, cols, 0)
     out_query, out_key = (
         place_call(core, ends_pair[0], passed_pair, cols, part) for part in range(2)

time: 443 us -> 407 us (0.919)
  waiting for transfers between devices: 166 us -> 139 us
  starting transfers between devices: 60.3 us -> 49.5 us
  local copies, waits for them, and re-layouts: 69.7 us -> 75.8 us
  matrix products: 25.2 us -> 19.9 us
    ppermute x37 -> x35, waiting for transfers between devices: 102 us -> 74 us  [swap(): return lax.ppermute(array, 'dp', [(i, i ^ bit) for i in range(n_dp)])]
    ppermute x37 -> x35, starting transfers between devices: 42.2 us -> 32.7 us  [swap(): return lax.ppermute(array, 'dp', [(i, i ^ bit) for i in range(n_dp)])]
    unnamed x148 -> x140, local copies, waits for them, and re-layouts: 46.4 us -> 55.7 us
    dot_general x1, matrix products: 12.1 us -> 6.63 us  [per_device(): values = jnp.dot(normed, full_value, preferred_element_type=F32).astype(BF)]
    pallas_call x8 -> x7, Pallas kernels: 38.3 us -> 39.2 us  [product_call(): pl.pallas_call(functools.partial(product_kernel, n_add, turn), grid=(coun...]
  transfers between devices with their start and end apart: 43 -> 41, of which waited for: 17 -> 16; matrix products, arithmetic and copies ran while one was open for 14% -> 13% of each run, Pallas kernels for 20% -> 20%
where the time goes in v5:
time: 407 us; the launch traced here: 402 us
  waiting for transfers between devices  139 us (34%)
  Pallas kernels  97.9 us (24%)
  local copies, waits for them, and re-layouts  75.8 us (19%)
  starting transfers between devices  49.5 us (12%)
  matrix products  19.9 us (5%)
  other arithmetic  17.9 us (4%)
    ppermute x35, waiting for transfers between devices, swap(): return lax.ppermute(array, 'dp', [(i, i ^ bit) for i in range(n_dp)])  74 us
    ppermute x6, waiting for transfers between devices, ring_on(): return lax.ppermute(array, 'mp', ring_pairs)  64.8 us
    unnamed x140, local copies, waits for them, and re-layouts  55.7 us
    pallas_call x7, Pallas kernels, product_call(): pl.pallas_call(functools.partial(product_kernel, n_add, turn), grid=(coun...  39.2 us
    ppermute x35, starting transfers between devices, swap(): return lax.ppermute(array, 'dp', [(i, i ^ bit) for i in range(n_dp)])  32.7 us
    pallas_call x8, Pallas kernels, back_call(): pl.pallas_call(back_kernel, grid=(units,), in_specs=[pl.BlockSpec(pair.sh...  31 us
    ppermute x6, starting transfers between devices, ring_on(): return lax.ppermute(array, 'mp', ring_pairs)  16.8 us
    pallas_call x2, Pallas kernels, attention_call(): pl.pallas_call(kernel, grid=(tokens // PATCH,), in_specs=[pl.BlockSpec((P...  16 us
  transfers between devices with their start and end apart: 41, of which 16 were waited for; matrix products, arithmetic and copies ran while one was open for 13% of the time, Pallas kernels for 20%

profile of v5, /device:TPU:1, one launch (start us, length us, event | category | flops | bytes accessed | tf_op | source)
XLA Modules:
  0.0 401.5 jit_solution(8830263702177320669)
XLA Ops:
  17.4 28.9 %collective-permute-done = bf16[768,1024]{1,0:T(8,128)(2,1)} collective-permute-done((bf16[768,1024]{1,0:T(8,128)(2,1)S(1)}, bf16[768,1024]{1,0:T(8,128)(2,1)}, u32[]{:S(2)}, u32[]{:S(2)}) %collective-permute-start) | collective-permute-done | bytes 1572896 | tf_op jit(solution)/shard_map/ppermute | solution.py:257
  65.5 16.7 %collective-permute-done.3 = bf16[768,1024]{1,0:T(8,128)(2,1)S(1)} collective-permute-done((bf16[768,1024]{1,0:T(8,128)(2,1)}, bf16[768,1024]{1,0:T(8,128)(2,1)S(1)}, u32[]{:S(2)}, u32[]{:S(2)}) %collective-permute-start.3) | collective-permute-done | bytes 1572896 | tf_op jit(solution)/shard_map/ppermute | solution.py:257
  97.5 31.1 %collective-permute-done.12 = bf16[256,3072]{1,0:T(8,128)(2,1)S(1)} collective-permute-done((bf16[256,3072]{1,0:T(8,128)(2,1)S(1)}, bf16[256,3072]{1,0:T(8,128)(2,1)S(1)}, u32[]{:S(2)}, u32[]{:S(2)}) %collective-permute-start.12) | collective-permute-done | bytes 1572896 | tf_op jit(solution)/shard_map/ppermute | solution.py:275
  133.1 13.3 %fusion.4.qk_ref = f32[1024,1024]{1,0:T(8,128)S(1)} fusion(bf16[1024,6144]{1,0:T(8,128)(2,1)S(1)} %slice_dynamic-update-slice_fusion.refs_0_.refs_1_, bf16[6144,1024]{1,0:T(8,128)(2,1)S(1)} %constant_dynamic-update-slice_fusion.w_pair_ref), kind=kOutput, calls=%fused_computation.94 | convolution fusion | flops 12884901888 | bytes 29360128 | tf_op jit(solution)/shard_map/dot_general | solution.py:356
  146.4 4.6 %copy-done.4 = bf16[6144,1024]{1,0:T(8,128)(2,1)} copy-done((bf16[6144,1024]{1,0:T(8,128)(2,1)}, bf16[6144,1024]{1,0:T(8,128)(2,1)S(1)}, u32[]{:S(2)}) %copy-start.4) | copy-done | bytes 12582936
  151.0 5.9 %shard_map.113.turned_ref = bf16[512,1024]{1,0:T(8,128)(2,1)S(1)} custom-call(f32[1024,1024]{1,0:T(8,128)S(1)} %fusion.4.qk_ref, bf16[1024,512]{1,0:T(8,128)(2,1)S(1)} %constant_dynamic-update-slice_fusion.12.g_ref, f32[2,128]{1,0:T(2,128)S(1)} %pad_maximum_fusion.13.gains_ref), custom_call_target="tpu_custom_call" | custom-call | flops 1073741824 | bytes 8388608 | tf_op jit(solution)/shard_map/pallas_call | solution.py:95
  159.9 6.1 %shard_map.116 = (bf16[1024,768]{1,0:T(8,128)(2,1)}, bf16[1024,768]{1,0:T(8,128)(2,1)}) custom-call(bf16[512,1024]{1,0:T(8,128)(2,1)S(1)} %shard_map.113.turned_ref, bf16[1024,6144]{1,0:T(8,128)(2,1)S(1)} %slice_dynamic-update-slice_fusion.refs_0_.refs_1_, bf16[1024,6144]{1,0:T(8,128)(2,1)S(1)} %slice_dynamic-update-slice_fusion.refs_0_.refs_1_), custom_call_target="tpu_custom_call" | custom-call | flops 3221225472 | bytes 8912896 | tf_op jit(solution)/shard_map/pallas_call | solution.py:133
  171.2 6.9 %collective-permute-done.19 = bf16[768,512]{1,0:T(8,128)(2,1)S(1)} collective-permute-done((bf16[768,512]{1,0:T(8,128)(2,1)S(1)}, bf16[768,512]{1,0:T(8,128)(2,1)S(1)}, u32[]{:S(2)}, u32[]{:S(2)}) %collective-permute-start.19) | collective-permute-done | bytes 786464 | tf_op jit(solution)/shard_map/ppermute | solution.py:257
  180.7 6.6 %convolution_convert_fusion.v_ref = bf16[1024,512]{1,0:T(8,128)(2,1)S(1)} fusion(bf16[1024,6144]{1,0:T(8,128)(2,1)S(1)} %slice_dynamic-update-slice_fusion.refs_0_.refs_1_, bf16[6144,512]{1,0:T(8,128)(2,1)S(1)} %constant_dynamic-update-slice_fusion.8.w_value_ref), kind=kOutput, calls=%fused_computation.14 | convolution fusion | flops 6442975232 | bytes 19922944 | tf_op jit(solution)/shard_map/dot_general | solution.py:403
  187.4 10.1 %shard_map.114.turned_ref = bf16[1024,1024]{1,0:T(8,128)(2,1)S(1)} custom-call(f32[1024,1024]{1,0:T(8,128)S(1)} %copy-done.14, bf16[1024,512]{1,0:T(8,128)(2,1)S(1)} %copy-done.19, bf16[1024,512]{1,0:T(8,128)(2,1)S(1)} %convolution_convert_fusion.v_ref, f32[2,128]{1,0:T(2,128)S(1)} %pad_maximum_fusion.13.gains_ref), custom_call_target="tpu_custom_call" | custom-call | flops 1073741824 | bytes 12582912 | tf_op jit(solution)/shard_map/pallas_call | solution.py:95
  198.9 4.6 %copy-done.5 = bf16[6144,1024]{1,0:T(8,128)(2,1)S(1)} copy-done((bf16[6144,1024]{1,0:T(8,128)(2,1)S(1)}, bf16[6144,1024]{1,0:T(8,128)(2,1)}, u32[]{:S(2)}) %copy-start.5) | copy-done | bytes 12582936
  203.5 3.9 shard_map.119
  207.4 3.9 shard_map.118
  211.9 5.1 %shard_map.117 = (bf16[512,768]{1,0:T(8,128)(2,1)}, bf16[512,768]{1,0:T(8,128)(2,1)}) custom-call(bf16[512,1024]{1,0:T(8,128)(2,1)S(1)} %shard_map.113.turned_ref, bf16[1024,6144]{1,0:T(8,128)(2,1)S(1)} %slice_dynamic-update-slice_fusion.refs_0_.refs_1_, bf16[1024,6144]{1,0:T(8,128)(2,1)S(1)} %slice_dynamic-update-slice_fusion.refs_0_.refs_1_, ...), custom_call_target="tpu_custom_call" | custom-call | flops 1610612736 | bytes 7340032 | tf_op jit(solution)/shard_map/pallas_call | solution.py:133
  220.1 4.6 %copy-done.2 = bf16[1024,6144]{1,0:T(8,128)(2,1)S(1)} copy-done((bf16[1024,6144]{1,0:T(8,128)(2,1)S(1)}, bf16[1024,6144]{1,0:T(8,128)(2,1)}, u32[]{:S(2)}) %copy-start.2) | copy-done | bytes 12582936
  224.7 5.3 %shard_map.115 = (bf16[1024,768]{1,0:T(8,128)(2,1)}, bf16[1024,768]{1,0:T(8,128)(2,1)}) custom-call(bf16[1024,1024]{1,0:T(8,128)(2,1)S(1)} %copy-done.12, bf16[1024,6144]{1,0:T(8,128)(2,1)S(1)} %copy-done.2, bf16[1024,6144]{1,0:T(8,128)(2,1)S(1)} %copy-done.2), custom_call_target="tpu_custom_call" | custom-call | flops 3221225472 | bytes 8388608 | tf_op jit(solution)/shard_map/pallas_call | solution.py:133
  230.0 4.7 %copy-done.6 = bf16[6144,1024]{1,0:T(8,128)(2,1)S(1)} copy-done((bf16[6144,1024]{1,0:T(8,128)(2,1)S(1)}, bf16[6144,1024]{1,0:T(8,128)(2,1)}, u32[]{:S(2)}) %copy-start.6) | copy-done | bytes 12582936
  237.6 6.3 %shard_map.120 = bf16[3072,256]{1,0:T(8,128)(2,1)} custom-call(bf16[1024,256]{1,0:T(8,128)(2,1)S(1)} %copy-done.26, bf16[512,256]{1,0:T(8,128)(2,1)S(1)} %copy-done.30, bf16[6144,1024]{1,0:T(8,128)(2,1)S(1)} %copy-done.6, bf16[6144,512]{1,0:T(8,128)(2,1)S(1)} %copy-done.8, bf16[3072,256]{1,0:T(8,128)(2,1)} %collective-permute-done.23.refs_0_), custom_call_target="tpu_custom_call" | custom-call | flops 2415919104 | bytes 14155776 | tf_op jit(solution)/shard_map/pallas_call | solution.py:164
  249.3 5.2 %shard_map.125 = (bf16[768,512]{1,0:T(8,128)(2,1)S(1)}, bf16[768,512]{1,0:T(8,128)(2,1)}) custom-call(bf16[512,1024]{1,0:T(8,128)(2,1)S(1)} %shard_map.113.turned_ref, bf16[1024,6144]{1,0:T(8,128)(2,1)S(1)} %bitcast.12, bf16[1024,6144]{1,0:T(8,128)(2,1)S(1)} %bitcast.12, bf16[1024,768]{1,0:T(8,128)(2,1)} %collective-permute-done.22.refs_3_.refs_2_, ...), custom_call_target="tpu_custom_call" | custom-call | flops 1610612736 | bytes 8912896 | tf_op jit(solution)/shard_map/pallas_call | solution.py:133
  258.1 4.4 %shard_map.121 = bf16[3072,256]{1,0:T(8,128)(2,1)S(1)} custom-call(bf16[1024,256]{1,0:T(8,128)(2,1)S(1)} %copy-done.24, bf16[512,256]{1,0:T(8,128)(2,1)S(1)} %pad_maximum_fusion.10.value_ref, bf16[6144,1024]{1,0:T(8,128)(2,1)S(1)} %copy-done.6, bf16[6144,512]{1,0:T(8,128)(2,1)S(1)} %copy-done.9, bf16[3072,256]{1,0:T(8,128)(2,1)} %collective-permute-done.24.refs_0_), custom_call_target="tpu_custom_call" | custom-call | flops 2415919104 | bytes 14155776 | tf_op jit(solution)/shard_map/pallas_call | solution.py:164
  262.6 3.1 shard_map.124
  270.0 5.1 %shard_map.122 = (bf16[1024,768]{1,0:T(8,128)(2,1)S(1)}, bf16[1024,768]{1,0:T(8,128)(2,1)}) custom-call(bf16[1024,1024]{1,0:T(8,128)(2,1)S(1)} %copy-done.12, bf16[1024,6144]{1,0:T(8,128)(2,1)S(1)} %bitcast.12, bf16[1024,6144]{1,0:T(8,128)(2,1)S(1)} %bitcast.12), custom_call_target="tpu_custom_call" | custom-call | flops 3221225472 | bytes 8388608 | tf_op jit(solution)/shard_map/pallas_call | solution.py:133
  275.1 4.0 %collective-permute-done.27.refs_3_ = bf16[1024,768]{1,0:T(8,128)(2,1)S(1)} collective-permute-done((bf16[1024,768]{1,0:T(8,128)(2,1)}, bf16[1024,768]{1,0:T(8,128)(2,1)S(1)}, u32[]{:S(2)}, u32[]{:S(2)}) %collective-permute-start.27) | collective-permute-done | bytes 1572896 | tf_op jit(solution)/shard_map/ppermute | solution.py:257
  297.5 3.1 shard_map.127
  303.6 3.1 shard_map.126
  306.8 5.4 %shard_map.128 = (bf16[1024,768]{1,0:T(8,128)(2,1)S(1)}, bf16[1024,768]{1,0:T(8,128)(2,1)S(1)}) custom-call(bf16[1024,1024]{1,0:T(8,128)(2,1)S(1)} %copy-done.12, bf16[1024,6144]{1,0:T(8,128)(2,1)S(1)} %bitcast.12, bf16[1024,6144]{1,0:T(8,128)(2,1)S(1)} %bitcast.12, bf16[1024,768]{1,0:T(8,128)(2,1)} %collective-permute-done.28.refs_2_, ...), custom_call_target="tpu_custom_call" | custom-call | flops 3221225472 | bytes 11534336 | tf_op jit(solution)/shard_map/pallas_call | solution.py:133
  312.2 10.0 %collective-permute-done.32.refs_2_ = bf16[1024,768]{1,0:T(8,128)(2,1)} collective-permute-done((bf16[1024,768]{1,0:T(8,128)(2,1)}, bf16[1024,768]{1,0:T(8,128)(2,1)}, u32[]{:S(2)}, u32[]{:S(2)}) %collective-permute-start.32) | collective-permute-done | bytes 1572896 | tf_op jit(solution)/shard_map/ppermute | solution.py:257
  331.5 30.5 %collective-permute-done.35 = bf16[3072,256]{1,0:T(8,128)(2,1)} collective-permute-done((bf16[3072,256]{1,0:T(8,128)(2,1)}, bf16[3072,256]{1,0:T(8,128)(2,1)}, u32[]{:S(2)}, u32[]{:S(2)}) %collective-permute-start.35) | collective-permute-done | bytes 1572896 | tf_op jit(solution)/shard_map/ppermute | solution.py:275
  366.9 4.6 %copy-done.3 = bf16[1024,6144]{1,0:T(8,128)(2,1)S(1)} copy-done((bf16[1024,6144]{1,0:T(8,128)(2,1)S(1)}, bf16[1024,6144]{1,0:T(8,128)(2,1)}, u32[]{:S(2)}) %copy-start.3) | copy-done | bytes 12582936
  371.5 7.0 %shard_map.130 = (bf16[768,1024]{1,0:T(8,128)(2,1)S(1)}, bf16[768,1024]{1,0:T(8,128)(2,1)}) custom-call(bf16[1024,1024]{1,0:T(8,128)(2,1)S(1)} %copy-done.12, bf16[1024,6144]{1,0:T(8,128)(2,1)S(1)} %copy-done.3, bf16[1024,6144]{1,0:T(8,128)(2,1)S(1)} %copy-done.3, bf16[1024,768]{1,0:T(8,128)(2,1)} %collective-permute-done.32.refs_2_, ...), custom_call_target="tpu_custom_call" | custom-call | flops 3221225472 | bytes 14680064 | tf_op jit(solution)/shard_map/pallas_call | solution.py:133
  383.2 3.9 collective-permute-done.40.other_ref
  392.0 4.6 %shard_map.129 = bf16[128,6144]{1,0:T(8,128)(2,1)} custom-call(s32[1]{0:T(128)} %bitcast.place_ref, f32[3072,128]{1,0:T(8,128)S(1)} %copy-done.22, bf16[3072,128]{1,0:T(8,128)(2,1)} %collective-permute-done.36.other_ref, f32[128,6144]{1,0:T(8,128)S(1)} %copy-done.16, f32[128,1]{1,0:T(8,128)S(1)} %copy.12.spread_ref, f32[1,6144]{1,0:T(1,128)S(1)} %bitcast.13), custom_call_target="tpu_custom_call" | custom-call | tf_op jit(solution)/shard_map/pallas_call | solution.py:238
  (270 shorter events, 137.2 us)
Async XLA Ops:
  8.9 37.5 %collective-permute-start = (bf16[768,1024]{1,0:T(8,128)(2,1)S(1)}, bf16[768,1024]{1,0:T(8,128)(2,1)}, u32[]{:S(2)}, u32[]{:S(2)}) collective-permute-start(bf16[768,1024]{1,0:T(8,128)(2,1)S(1)} %pad_maximum_fusion), channel_id=1, source_target_pairs={{0,8},{4,12},{8,0},{12,4},{16,24},{20,28},{24,16},{28,20},{1,9},{5... | collective-permute-start | bytes 4718600 | tf_op jit(solution)/shard_map/ppermute | solution.py:257
  11.5 35.7 %collective-permute-start.1 = (bf16[768,1024]{1,0:T(8,128)(2,1)S(1)}, bf16[768,1024]{1,0:T(8,128)(2,1)}, u32[]{:S(2)}, u32[]{:S(2)}) collective-permute-start(bf16[768,1024]{1,0:T(8,128)(2,1)S(1)} %pad_maximum_fusion), channel_id=1, source_target_pairs={{0,16},{4,20},{8,24},{12,28},{16,0},{20,4},{24,8},{28,12},{1,17},{... | collective-permute-start | bytes 4718600 | tf_op jit(solution)/shard_map/ppermute | solution.py:257
  12.8 34.5 %collective-permute-start.2 = (bf16[768,1024]{1,0:T(8,128)(2,1)}, bf16[768,1024]{1,0:T(8,128)(2,1)}, u32[]{:S(2)}, u32[]{:S(2)}) collective-permute-start(bf16[768,1024]{1,0:T(8,128)(2,1)} %pad_maximum_fusion.1), channel_id=1, source_target_pairs={{0,4},{4,0},{8,12},{12,8},{16,20},{20,16},{24,28},{28,24},{1,5},{5... | collective-permute-start | bytes 4718600 | tf_op jit(solution)/shard_map/ppermute | solution.py:257
  14.7 36.5 %collective-permute-start.7 = (bf16[256,3072]{1,0:T(8,128)(2,1)}, bf16[256,3072]{1,0:T(8,128)(2,1)}, u32[]{:S(2)}, u32[]{:S(2)}) collective-permute-start(bf16[256,3072]{1,0:T(8,128)(2,1)} %pad_maximum_fusion.2), channel_id=1, source_target_pairs={{0,2},{2,3},{3,1},{1,0},{4,6},{6,7},{7,5},{5,4},{8,10},{10,11},{11... | collective-permute-start | bytes 4718600 | tf_op jit(solution)/shard_map/ppermute | solution.py:275
  17.1 38.0 %collective-permute-start.6 = (bf16[256,3072]{1,0:T(8,128)(2,1)}, bf16[256,3072]{1,0:T(8,128)(2,1)}, u32[]{:S(2)}, u32[]{:S(2)}) collective-permute-start(bf16[256,3072]{1,0:T(8,128)(2,1)} %pad_maximum_fusion.2), channel_id=1, source_target_pairs={{0,4},{4,0},{8,12},{12,8},{16,20},{20,16},{24,28},{28,24},{1,5},{5... | collective-permute-start | bytes 4718600 | tf_op jit(solution)/shard_map/ppermute | solution.py:257
  47.3 34.9 %collective-permute-start.3 = (bf16[768,1024]{1,0:T(8,128)(2,1)}, bf16[768,1024]{1,0:T(8,128)(2,1)S(1)}, u32[]{:S(2)}, u32[]{:S(2)}) collective-permute-start(bf16[768,1024]{1,0:T(8,128)(2,1)} %collective-permute-done.2), channel_id=1, source_target_pairs={{0,8},{4,12},{8,0},{12,4},{16,24},{20,28},{24,16},{28,20},{1,9},{5... | collective-permute-start | bytes 4718600 | tf_op jit(solution)/shard_map/ppermute | solution.py:257
  47.6 34.9 %collective-permute-start.4 = (bf16[768,1024]{1,0:T(8,128)(2,1)}, bf16[768,1024]{1,0:T(8,128)(2,1)S(1)}, u32[]{:S(2)}, u32[]{:S(2)}) collective-permute-start(bf16[768,1024]{1,0:T(8,128)(2,1)} %collective-permute-done.2), channel_id=1, source_target_pairs={{0,16},{4,20},{8,24},{12,28},{16,0},{20,4},{24,8},{28,12},{1,17},{... | collective-permute-start | bytes 4718600 | tf_op jit(solution)/shard_map/ppermute | solution.py:257
  51.2 12.4 %collective-permute-start.8 = (bf16[256,3072]{1,0:T(8,128)(2,1)}, bf16[256,3072]{1,0:T(8,128)(2,1)S(1)}, u32[]{:S(2)}, u32[]{:S(2)}) collective-permute-start(bf16[256,3072]{1,0:T(8,128)(2,1)} %collective-permute-done.7), channel_id=1, source_target_pairs={{0,4},{4,0},{8,12},{12,8},{16,20},{20,16},{24,28},{28,24},{1,5},{5... | collective-permute-start | bytes 4718600 | tf_op jit(solution)/shard_map/ppermute | solution.py:257
  52.5 38.8 %collective-permute-start.10 = (bf16[256,3072]{1,0:T(8,128)(2,1)}, bf16[256,3072]{1,0:T(8,128)(2,1)S(1)}, u32[]{:S(2)}, u32[]{:S(2)}) collective-permute-start(bf16[256,3072]{1,0:T(8,128)(2,1)} %collective-permute-done.7), channel_id=1, source_target_pairs={{0,2},{2,3},{3,1},{1,0},{4,6},{6,7},{7,5},{5,4},{8,10},{10,11},{11... | collective-permute-start | bytes 4718600 | tf_op jit(solution)/shard_map/ppermute | solution.py:275
  82.5 47.4 %collective-permute-start.14 = (bf16[768,1024]{1,0:T(8,128)(2,1)}, bf16[768,1024]{1,0:T(8,128)(2,1)S(1)}, u32[]{:S(2)}, u32[]{:S(2)}) collective-permute-start(bf16[768,1024]{1,0:T(8,128)(2,1)} %collective-permute-done), channel_id=1, source_target_pairs={{0,16},{4,20},{8,24},{12,28},{16,0},{20,4},{24,8},{28,12},{1,17},{... | collective-permute-start | bytes 4718600 | tf_op jit(solution)/shard_map/ppermute | solution.py:257
  83.6 48.3 %collective-permute-start.15 = (bf16[768,1024]{1,0:T(8,128)(2,1)S(1)}, bf16[768,1024]{1,0:T(8,128)(2,1)S(1)}, u32[]{:S(2)}, u32[]{:S(2)}) collective-permute-start(bf16[768,1024]{1,0:T(8,128)(2,1)S(1)} %collective-permute-done.4), channel_id=1, source_target_pairs={{0,8},{4,12},{8,0},{12,4},{16,24},{20,28},{24,16},{28,20},{1,9},{5... | collective-permute-start | bytes 4718600 | tf_op jit(solution)/shard_map/ppermute | solution.py:257
  92.8 35.8 %collective-permute-start.12 = (bf16[256,3072]{1,0:T(8,128)(2,1)S(1)}, bf16[256,3072]{1,0:T(8,128)(2,1)S(1)}, u32[]{:S(2)}, u32[]{:S(2)}) collective-permute-start(bf16[256,3072]{1,0:T(8,128)(2,1)S(1)} %collective-permute-done.10), channel_id=1, source_target_pairs={{0,2},{2,3},{3,1},{1,0},{4,6},{6,7},{7,5},{5,4},{8,10},{10,11},{11... | collective-permute-start | bytes 4718600 | tf_op jit(solution)/shard_map/ppermute | solution.py:275
  96.9 60.0 %collective-permute-start.17 = (bf16[1536,512]{1,0:T(8,128)(2,1)}, bf16[1536,512]{1,0:T(8,128)(2,1)}, u32[]{:S(2)}, u32[]{:S(2)}) collective-permute-start(bf16[1536,512]{1,0:T(8,128)(2,1)} %pad_maximum_fusion.3), channel_id=1, source_target_pairs={{0,8},{4,12},{8,0},{12,4},{16,24},{20,28},{24,16},{28,20},{1,9},{5... | collective-permute-start | bytes 4718600 | tf_op jit(solution)/shard_map/ppermute | solution.py:257
  97.3 59.6 %collective-permute-start.18 = (bf16[1536,512]{1,0:T(8,128)(2,1)}, bf16[1536,512]{1,0:T(8,128)(2,1)}, u32[]{:S(2)}, u32[]{:S(2)}) collective-permute-start(bf16[1536,512]{1,0:T(8,128)(2,1)} %pad_maximum_fusion.3), channel_id=1, source_target_pairs={{0,16},{4,20},{8,24},{12,28},{16,0},{20,4},{24,8},{28,12},{1,17},{... | collective-permute-start | bytes 4718600 | tf_op jit(solution)/shard_map/ppermute | solution.py:257
  159.3 18.8 %collective-permute-start.19 = (bf16[768,512]{1,0:T(8,128)(2,1)S(1)}, bf16[768,512]{1,0:T(8,128)(2,1)S(1)}, u32[]{:S(2)}, u32[]{:S(2)}) collective-permute-start(bf16[768,512]{1,0:T(8,128)(2,1)S(1)} %slice.75), channel_id=1, source_target_pairs={{0,16},{4,20},{8,24},{12,28},{16,0},{20,4},{24,8},{28,12},{1,17},{... | collective-permute-start | bytes 2359304 | tf_op jit(solution)/shard_map/ppermute | solution.py:257
  159.6 21.0 %collective-permute-start.20 = (bf16[768,512]{1,0:T(8,128)(2,1)S(1)}, bf16[768,512]{1,0:T(8,128)(2,1)S(1)}, u32[]{:S(2)}, u32[]{:S(2)}) collective-permute-start(bf16[768,512]{1,0:T(8,128)(2,1)S(1)} %slice.76), channel_id=1, source_target_pairs={{0,8},{4,12},{8,0},{12,4},{16,24},{20,28},{24,16},{28,20},{1,9},{5... | collective-permute-start | bytes 2359304 | tf_op jit(solution)/shard_map/ppermute | solution.py:257
  166.0 45.9 %collective-permute-start.21 = (bf16[1024,768]{1,0:T(8,128)(2,1)}, bf16[1024,768]{1,0:T(8,128)(2,1)}, u32[]{:S(2)}, u32[]{:S(2)}) collective-permute-start(bf16[1024,768]{1,0:T(8,128)(2,1)} %get-tuple-element.118), channel_id=1, source_target_pairs={{0,16},{4,20},{8,24},{12,28},{16,0},{20,4},{24,8},{28,12},{1,17},{... | collective-permute-start | bytes 4718600 | tf_op jit(solution)/shard_map/ppermute | solution.py:257
  167.3 44.6 %collective-permute-start.22 = (bf16[1024,768]{1,0:T(8,128)(2,1)}, bf16[1024,768]{1,0:T(8,128)(2,1)}, u32[]{:S(2)}, u32[]{:S(2)}) collective-permute-start(bf16[1024,768]{1,0:T(8,128)(2,1)} %get-tuple-element.119), channel_id=1, source_target_pairs={{0,8},{4,12},{8,0},{12,4},{16,24},{20,28},{24,16},{28,20},{1,9},{5... | collective-permute-start | bytes 4718600 | tf_op jit(solution)/shard_map/ppermute | solution.py:257
  217.0 13.0 %collective-permute-start.23 = (bf16[3072,256]{1,0:T(8,128)(2,1)}, bf16[3072,256]{1,0:T(8,128)(2,1)}, u32[]{:S(2)}, u32[]{:S(2)}) collective-permute-start(bf16[3072,256]{1,0:T(8,128)(2,1)} %shard_map.118), channel_id=1, source_target_pairs={{0,4},{4,0},{8,12},{12,8},{16,20},{20,16},{24,28},{28,24},{1,5},{5... | collective-permute-start | bytes 4718600 | tf_op jit(solution)/shard_map/ppermute | solution.py:257
  218.6 11.4 %collective-permute-start.24 = (bf16[3072,256]{1,0:T(8,128)(2,1)}, bf16[3072,256]{1,0:T(8,128)(2,1)}, u32[]{:S(2)}, u32[]{:S(2)}) collective-permute-start(bf16[3072,256]{1,0:T(8,128)(2,1)} %shard_map.119), channel_id=1, source_target_pairs={{0,4},{4,0},{8,12},{12,8},{16,20},{20,16},{24,28},{28,24},{1,5},{5... | collective-permute-start | bytes 4718600 | tf_op jit(solution)/shard_map/ppermute | solution.py:257
  218.7 25.2 %collective-permute-start.25 = (bf16[512,768]{1,0:T(8,128)(2,1)}, bf16[512,768]{1,0:T(8,128)(2,1)}, u32[]{:S(2)}, u32[]{:S(2)}) collective-permute-start(bf16[512,768]{1,0:T(8,128)(2,1)} %get-tuple-element.129), channel_id=1, source_target_pairs={{0,8},{4,12},{8,0},{12,4},{16,24},{20,28},{24,16},{28,20},{1,9},{5... | collective-permute-start | bytes 2359304 | tf_op jit(solution)/shard_map/ppermute | solution.py:257
  219.0 24.9 %collective-permute-start.26 = (bf16[512,768]{1,0:T(8,128)(2,1)}, bf16[512,768]{1,0:T(8,128)(2,1)}, u32[]{:S(2)}, u32[]{:S(2)}) collective-permute-start(bf16[512,768]{1,0:T(8,128)(2,1)} %get-tuple-element.130), channel_id=1, source_target_pairs={{0,16},{4,20},{8,24},{12,28},{16,0},{20,4},{24,8},{28,12},{1,17},{... | collective-permute-start | bytes 2359304 | tf_op jit(solution)/shard_map/ppermute | solution.py:257
  243.9 35.3 %collective-permute-start.27 = (bf16[1024,768]{1,0:T(8,128)(2,1)}, bf16[1024,768]{1,0:T(8,128)(2,1)S(1)}, u32[]{:S(2)}, u32[]{:S(2)}) collective-permute-start(bf16[1024,768]{1,0:T(8,128)(2,1)} %get-tuple-element.136), channel_id=1, source_target_pairs={{0,8},{4,12},{8,0},{12,4},{16,24},{20,28},{24,16},{28,20},{1,9},{5... | collective-permute-start | bytes 4718600 | tf_op jit(solution)/shard_map/ppermute | solution.py:257
  245.1 34.9 %collective-permute-start.28 = (bf16[1024,768]{1,0:T(8,128)(2,1)}, bf16[1024,768]{1,0:T(8,128)(2,1)}, u32[]{:S(2)}, u32[]{:S(2)}) collective-permute-start(bf16[1024,768]{1,0:T(8,128)(2,1)} %get-tuple-element.137), channel_id=1, source_target_pairs={{0,16},{4,20},{8,24},{12,28},{16,0},{20,4},{24,8},{28,12},{1,17},{... | collective-permute-start | bytes 4718600 | tf_op jit(solution)/shard_map/ppermute | solution.py:257
  245.5 35.6 %collective-permute-start.29 = (bf16[3072,256]{1,0:T(8,128)(2,1)}, bf16[3072,256]{1,0:T(8,128)(2,1)}, u32[]{:S(2)}, u32[]{:S(2)}) collective-permute-start(bf16[3072,256]{1,0:T(8,128)(2,1)} %shard_map.120), channel_id=1, source_target_pairs={{0,2},{2,3},{3,1},{1,0},{4,6},{6,7},{7,5},{5,4},{8,10},{10,11},{11... | collective-permute-start | bytes 4718600 | tf_op jit(solution)/shard_map/ppermute | solution.py:275
  286.4 35.8 %collective-permute-start.32 = (bf16[1024,768]{1,0:T(8,128)(2,1)}, bf16[1024,768]{1,0:T(8,128)(2,1)}, u32[]{:S(2)}, u32[]{:S(2)}) collective-permute-start(bf16[1024,768]{1,0:T(8,128)(2,1)} %copy-done.46), channel_id=1, source_target_pairs={{0,8},{4,12},{8,0},{12,4},{16,24},{20,28},{24,16},{28,20},{1,9},{5... | collective-permute-start | bytes 4718600 | tf_op jit(solution)/shard_map/ppermute | solution.py:257
  286.8 35.4 %collective-permute-start.33 = (bf16[1024,768]{1,0:T(8,128)(2,1)}, bf16[1024,768]{1,0:T(8,128)(2,1)}, u32[]{:S(2)}, u32[]{:S(2)}) collective-permute-start(bf16[1024,768]{1,0:T(8,128)(2,1)} %get-tuple-element.161), channel_id=1, source_target_pairs={{0,16},{4,20},{8,24},{12,28},{16,0},{20,4},{24,8},{28,12},{1,17},{... | collective-permute-start | bytes 4718600 | tf_op jit(solution)/shard_map/ppermute | solution.py:257
  287.9 36.1 %collective-permute-start.34 = (bf16[3072,256]{1,0:T(8,128)(2,1)}, bf16[3072,256]{1,0:T(8,128)(2,1)}, u32[]{:S(2)}, u32[]{:S(2)}) collective-permute-start(bf16[3072,256]{1,0:T(8,128)(2,1)} %add_convert_fusion.1), channel_id=1, source_target_pairs={{0,2},{2,3},{3,1},{1,0},{4,6},{6,7},{7,5},{5,4},{8,10},{10,11},{11... | collective-permute-start | bytes 4718600 | tf_op jit(solution)/shard_map/ppermute | solution.py:275
  326.9 35.1 %collective-permute-start.35 = (bf16[3072,256]{1,0:T(8,128)(2,1)}, bf16[3072,256]{1,0:T(8,128)(2,1)}, u32[]{:S(2)}, u32[]{:S(2)}) collective-permute-start(bf16[3072,256]{1,0:T(8,128)(2,1)} %add_convert_fusion), channel_id=1, source_target_pairs={{0,2},{2,3},{3,1},{1,0},{4,6},{6,7},{7,5},{5,4},{8,10},{10,11},{11... | collective-permute-start | bytes 4718600 | tf_op jit(solution)/shard_map/ppermute | solution.py:275
  330.0 36.9 %collective-permute-start.37 = (bf16[1024,768]{1,0:T(8,128)(2,1)}, bf16[1024,768]{1,0:T(8,128)(2,1)S(1)}, u32[]{:S(2)}, u32[]{:S(2)}) collective-permute-start(bf16[1024,768]{1,0:T(8,128)(2,1)} %copy-done.47), channel_id=1, source_target_pairs={{0,16},{4,20},{8,24},{12,28},{16,0},{20,4},{24,8},{28,12},{1,17},{... | collective-permute-start | bytes 4718600 | tf_op jit(solution)/shard_map/ppermute | solution.py:257
  330.3 36.6 %collective-permute-start.38 = (bf16[1024,768]{1,0:T(8,128)(2,1)}, bf16[1024,768]{1,0:T(8,128)(2,1)S(1)}, u32[]{:S(2)}, u32[]{:S(2)}) collective-permute-start(bf16[1024,768]{1,0:T(8,128)(2,1)} %copy-done.45), channel_id=1, source_target_pairs={{0,8},{4,12},{8,0},{12,4},{16,24},{20,28},{24,16},{28,20},{1,9},{5... | collective-permute-start | bytes 4718600 | tf_op jit(solution)/shard_map/ppermute | solution.py:257
  379.7 16.9 %collective-permute-start.39 = (bf16[768,1024]{1,0:T(8,128)(2,1)}, bf16[768,1024]{1,0:T(8,128)(2,1)}, u32[]{:S(2)}, u32[]{:S(2)}) collective-permute-start(bf16[768,1024]{1,0:T(8,128)(2,1)} %get-tuple-element.177), channel_id=1, source_target_pairs={{0,4},{4,0},{8,12},{12,8},{16,20},{20,16},{24,28},{28,24},{1,5},{5... | collective-permute-start | bytes 4718600 | tf_op jit(solution)/shard_map/ppermute | solution.py:257
  (72 other events, 771.7 us)

commit v6 on v5

--- a/solution.py
+++ b/solution.py
@@ -99,19 +99,23 @@
         + [pl.BlockSpec(gains.shape, lambda i: (0, 0))],
         out_specs=pl.BlockSpec((out_rows, PATCH), lambda i: (0, i)),
         out_shape=jax.ShapeDtypeStruct((out_rows, tokens), BF),
-        compiler_params=params(32),
+        compiler_params=params(16),
         cost_estimate=cost(pairs * 8 * PATCH * PATCH * head, 4 * len(arrays) * arrays[0].size),
     )(*arrays, gains)
 
 
-def product_kernel(n_add, turn, turned_ref, *refs):
-    turned = turned_ref[...]
-    outs = refs[-2:]
-    for side in range(2):
-        total = jnp.dot(turned, refs[side][...], preferred_element_type=F32)
-        for ref in refs[2 + side * n_add : 2 + (side + 1) * n_add]:
-            total = total + ref[...].astype(F32)
-        outs[side][...] = (total.T if turn else total).astype(BF)
+def product_kernel(specs, grid, n_add, turn, turned_ref, normed_ref, *refs):
+    def body(*blocks):
+        turned = turned_ref[...]
+        for side in range(2):
+            total = jnp.dot(turned, blocks[side][...], preferred_element_type=F32)
+            for block in blocks[2 + side * n_add : 2 + (side + 1) * n_add]:
+                total = total + block[...].astype(F32)
+            blocks[side - 2][...] = (total.T if turn else total).astype(BF)
+
+    pltpu.emit_pipeline(body, grid=grid, in_specs=specs[:-2], out_specs=specs[-2:])(
+        normed_ref, normed_ref, *refs
+    )
 
 
 def product_call(turned, normed, rows, units, addends=((), ()), turn=False):
@@ -130,55 +134,94 @@
     else:
         shape, out = (count * columns, rows), pl.BlockSpec((columns, tile), lambda u, i: (u, i))
     addends = [*addends[0], *addends[1]]
-    return pl.pallas_call(
-        functools.partial(product_kernel, n_add, turn),
-        grid=(count, steps),
-        in_specs=[
-            pl.BlockSpec((columns, tokens), lambda u, i: (0, 0)),
-            *[side(chosen[0], chosen[-1]) for chosen in units],
-            *[added(which) for _, which in addends],
-        ],
-        out_specs=[out] * 2,
+    specs = [side(chosen[0], chosen[-1]) for chosen in units] + [added(which) for _, which in addends]
+    return pl.pallas_call(
+        functools.partial(product_kernel, specs + [out] * 2, (count, steps), n_add, turn),
+        in_specs=[pl.BlockSpec(memory_space=pltpu.VMEM), pl.BlockSpec(memory_space=pltpu.HBM)]
+        + [pl.BlockSpec(memory_space=pl.ANY)] * len(addends),
+        out_specs=[pl.BlockSpec(memory_space=pl.ANY)] * 2,
         out_shape=[jax.ShapeDtypeStruct(shape, BF)] * 2,
-        compiler_params=params(24),
+        compiler_params=params(10),
         cost_estimate=cost(
             4 * count * columns * tokens * rows,
             2 * columns * tokens + 4 * count * tokens * rows + (4 + 4 * n_add) * columns * rows,
         ),
-    )(turned, normed, normed, *[array for array, _ in addends])
-
-
-def back_kernel(pair_ref, value_ref, w_pair_ref, w_value_ref, *refs):
-    total = jnp.dot(w_pair_ref[...], pair_ref[...], preferred_element_type=F32)
-    total = total + jnp.dot(w_value_ref[...], value_ref[...], preferred_element_type=F32)
-    for ref in refs[:-1]:
-        total = total + ref[...].astype(F32)
-    refs[-1][...] = total.astype(refs[-1].dtype)
+    )(turned, normed, *[array for array, _ in addends])
+
+
+def back_kernel(specs, grid, pair_ref, value_ref, *refs):
+    def body(w_pair_ref, w_value_ref, *blocks):
+        total = jnp.dot(w_pair_ref[...], pair_ref[...], preferred_element_type=F32)
+        total = total + jnp.dot(w_value_ref[...], value_ref[...], preferred_element_type=F32)
+        for block in blocks[:-1]:
+            total = total + block[...].astype(F32)
+        blocks[-1][...] = total.astype(blocks[-1].dtype)
+
+    pltpu.emit_pipeline(body, grid=grid, in_specs=specs[:-1], out_specs=specs[-1:])(*refs)
 
 
 def back_call(pair, value, w_pair, w_value, rows, odd, addends, dtype):
     level_tokens = pair.shape[1]
-    units = w_pair.shape[0] // rows // 2
-    first = units if odd else 0
-    block = pl.BlockSpec((rows, level_tokens), lambda i: (i, 0))
-    return pl.pallas_call(
-        back_kernel,
-        grid=(units,),
-        in_specs=[
-            pl.BlockSpec(pair.shape, lambda i: (0, 0)),
-            pl.BlockSpec(value.shape, lambda i: (0, 0)),
-            pl.BlockSpec((rows, w_pair.shape[1]), lambda i: (first + i, 0)),
-            pl.BlockSpec((rows, w_value.shape[1]), lambda i: (first + i, 0)),
-        ]
-        + [block] * len(addends),
-        out_specs=block,
-        out_shape=jax.ShapeDtypeStruct((units * rows, level_tokens), dtype),
-        compiler_params=params(24),
+    tile = rows // 2 if rows % 256 == 0 else rows
+    steps = w_pair.shape[0] // tile // 2
+    first = steps if odd else 0
+    block = pl.BlockSpec((tile, level_tokens), lambda i: (i, 0))
+    specs = [pl.BlockSpec((tile, w.shape[1]), lambda i: (first + i, 0)) for w in (w_pair, w_value)]
+    vmem, hbm = (pl.BlockSpec(memory_space=space) for space in (pltpu.VMEM, pltpu.HBM))
+    anywhere = pl.BlockSpec(memory_space=pl.ANY)
+    return pl.pallas_call(
+        functools.partial(back_kernel, specs + [block] * (len(addends) + 1), (steps,)),
+        in_specs=[vmem, vmem, hbm, hbm] + [anywhere] * len(addends),
+        out_specs=anywhere,
+        out_shape=jax.ShapeDtypeStruct((steps * tile, level_tokens), dtype),
+        compiler_params=params(8),
         cost_estimate=cost(
-            2 * units * rows * level_tokens * (pair.shape[0] + value.shape[0]),
-            2 * units * rows * (pair.shape[0] + value.shape[0] + 3 * level_tokens),
+            2 * steps * tile * level_tokens * (pair.shape[0] + value.shape[0]),
+            2 * steps * tile * (pair.shape[0] + value.shape[0] + 3 * level_tokens),
         ),
     )(pair, value, w_pair, w_value, *addends)
+
+
+def gather_kernel(cols, n_parts, core_ref, *refs):
+    parts, outs = refs[: 2 * n_parts], refs[2 * n_parts :]
+    here = pl.program_id(0) == core_ref[0]
+
+    def store(blocks):
+        total = blocks[0][...].astype(F32)
+        for block in blocks[1:]:
+            total = total + block[...].astype(F32)
+        for k, out in enumerate(outs):
+            out[...] = total[k * cols : (k + 1) * cols].T.astype(BF)
+
+    @pl.when(here)
+    def _():
+        store(parts[:n_parts])
+
+    @pl.when(jnp.logical_not(here))
+    def _():
+        store(parts[n_parts:])
+
+
+def gather_call(core, mine, other, cols):
+    columns, rows = mine[0].shape
+    tile = 256 if rows % 256 == 0 else 128
+    here = pl.BlockSpec(
+        (columns, tile), lambda h, i, core_ref: (0, jnp.where(h == core_ref[0], i, rows // tile * h - h))
+    )
+    there = pl.BlockSpec(
+        (columns, tile), lambda h, i, core_ref: (0, jnp.where(h != core_ref[0], i, rows // tile * h - h))
+    )
+    return pl.pallas_call(
+        functools.partial(gather_kernel, cols, len(mine)),
+        grid_spec=pltpu.PrefetchScalarGridSpec(
+            num_scalar_prefetch=1,
+            grid=(2, rows // tile),
+            in_specs=[here] * len(mine) + [there] * len(other),
+            out_specs=[pl.BlockSpec((tile, cols), lambda h, i, core_ref: (i, h))] * (columns // cols),
+        ),
+        out_shape=[jax.ShapeDtypeStruct((rows, 2 * cols), BF)] * (columns // cols),
+        compiler_params=params(12),
+    )(core.reshape(1), *mine, *other)
 
 
 def place_kernel(core_ref, mine_ref, other_ref, out_ref):
@@ -241,7 +284,7 @@
         out_specs=vmem,
         out_shape=jax.ShapeDtypeStruct((own, width), BF),
         scratch_shapes=[pltpu.VMEM((width, own), F32)],
-        compiler_params=params(32),
+        compiler_params=params(20),
     )(place.reshape(1), mine, other, unit_rows, row_spread, norm_gain.reshape(1, width))
 
 
@@ -371,8 +414,8 @@
             for r, (from_x, from_y) in zip(blocks_of_four, far)
         ]
 
-    def send(messages):
-        return [[swap(to_x, 2), swap(to_y, 4)] for to_x, to_y in messages]
+    def send(messages, x=2, y=4):
+        return [[swap(to_x, x), swap(to_y, y)] for to_x, to_y in messages]
 
     def scatter_end(turned, early, unit, late):
         def own(r, turn):
@@ -441,16 +484,22 @@
                 partial[1], early_pair, sent, far_pair, ends_value
             )
         elif step == 2:
-            partial[2], late_pair, early_pair = together(partial[2], late_pair, early_pair)
+            partial[2], late_pair, early_pair, own_pair = together(
+                partial[2], late_pair, early_pair, own_pair
+            )
         message = (partial[step].astype(F32) + arrived.astype(F32)).astype(BF)
         if step == 1:
             message, early_pair, sent, turned_pair, turned_value = together(
                 message, early_pair, sent, turned_pair, turned_value
             )
-            early_pair = send(early_pair)
+            early_pair = send(early_pair, y=5)
         elif step == 2:
-            message, late_pair, ends_value = together(message, late_pair, ends_value)
-            late_pair, passed_value = send(late_pair), swap(ends_value[1], 1)
+            message, late_pair, own_pair, ends_value = together(
+                message, late_pair, own_pair, ends_value
+            )
+            late_pair = send(late_pair, x=3)
+            own_pair = [[even, swap(odd, 1)] for even, odd in own_pair]
+            passed_value = swap(ends_value[1], 1)
         arrived = ring_on(message)
         if step + 2 < n_mp:
             near = [step + 1, step + 2] if step + 3 == n_mp else [step + 1]
@@ -468,19 +517,27 @@
                 chosen[step + 3], sent[step + 3] = back_odd(step + 3, turned_pair, turned_value)
             if step == 1:
                 late_pair = late_messages(turned_pair, far_pair)
+                own_pair = messages(turned_pair, (0,), (1,))
     total = partial[n_mp - 1] + arrived.astype(F32)
 
     mine = lax.dynamic_slice_in_dim(total, core * own, own, 1)
     other = lax.dynamic_slice_in_dim(total, (1 - core) * own, own, 1).astype(BF)
-    mine, other, turned_pair = together(mine, other, turned_pair)
     other = swap(other, 1)
-    ends_pair = scatter_end(turned_pair, early_pair, 0, late_pair)
-    passed_pair = swap(ends_pair[1], 1)
+    grad_tokens = finish_call(place, mine, other, unit_rows, row_spread, norm_gain, rows)
+    grad_tokens, late_pair = together(grad_tokens, late_pair)
+
+    here, there = {}, {}
+    for r, (own_even, own_odd), early, late in zip(blocks_of_four, own_pair, early_pair, late_pair):
+        here[r] = [own_even, early[0], late[1]]
+        there[r] = [own_odd, early[1], late[0]]
+    bit = n_dp // 2
+    while bit >= 8:
+        for parts in (here, there):
+            for r in [r for r in parts if r >= bit]:
+                parts[r ^ bit].append(swap(sum(p.astype(F32) for p in parts.pop(r)).astype(BF), bit))
+        bit //= 2
+    out_query, out_key = gather_call(core, here[0], there[0], cols)
     out_value = place_call(core, ends_value[0], passed_value, cols, 0)
-    out_query, out_key = (
-        place_call(core, ends_pair[0], passed_pair, cols, part) for part in range(2)
-    )
-    grad_tokens = finish_call(place, mine, other, unit_rows, row_spread, norm_gain, rows)
     return (grad_tokens, out_query, out_key, out_value)
 
 

time: 407 us -> 388 us (0.953)
  local copies, waits for them, and re-layouts: 75.8 us -> 51.8 us
  Pallas kernels: 97.9 us -> 117 us
  waiting for transfers between devices: 139 us -> 123 us
    pallas_call x15 -> x16, Pallas kernels: 70.2 us -> 95 us  [the longest x8 51.5 us: back_call(): pl.pallas_call(functools.partial(back_kernel, specs + [block] * (len(adde...]
    unnamed x140 -> x134, local copies, waits for them, and re-layouts: 55.7 us -> 31.9 us
    ppermute x35, waiting for transfers between devices: 74 us -> 59.9 us  [swap(): return lax.ppermute(array, 'dp', [(i, i ^ bit) for i in range(n_dp)])]
    pallas_call x3 -> x1, Pallas kernels: 7.09 us -> 2.47 us  [place_call(): pl.pallas_call(place_kernel, grid_spec=pltpu.PrefetchScalarGridSpec(num_s...]
  transfers between devices with their start and end apart: 41 -> 41, of which waited for: 16 -> 13; matrix products, arithmetic and copies ran while one was open for 13% -> 13% of each run, Pallas kernels for 20% -> 28%
where the time goes in v6:
time: 388 us; the launch traced here: 383 us
  waiting for transfers between devices  123 us (32%)
  Pallas kernels  117 us (30%)
  local copies, waits for them, and re-layouts  51.8 us (13%)
  starting transfers between devices  51 us (13%)
  matrix products  20.7 us (5%)
  other arithmetic  17.3 us (4%)
    ppermute x6, waiting for transfers between devices, ring_on(): return lax.ppermute(array, 'mp', ring_pairs)  63.2 us
    ppermute x35, waiting for transfers between devices, swap(): return lax.ppermute(array, 'dp', [(i, i ^ bit) for i in range(n_dp)])  59.9 us
    pallas_call x8, Pallas kernels, back_call(): pl.pallas_call(functools.partial(back_kernel, specs + [block] * (len(adde...  51.5 us
    pallas_call x7, Pallas kernels, product_call(): pl.pallas_call(functools.partial(product_kernel, specs + [out] * 2, (coun...  36.8 us
    ppermute x35, starting transfers between devices, swap(): return lax.ppermute(array, 'dp', [(i, i ^ bit) for i in range(n_dp)])  34.9 us
    unnamed x134, local copies, waits for them, and re-layouts  31.9 us
    pallas_call x2, Pallas kernels, attention_call(): pl.pallas_call(kernel, grid=(tokens // PATCH,), in_specs=[pl.BlockSpec((P...  16.2 us
    ppermute x6, starting transfers between devices, ring_on(): return lax.ppermute(array, 'mp', ring_pairs)  16.1 us
  transfers between devices with their start and end apart: 41, of which 13 were waited for; matrix products, arithmetic and copies ran while one was open for 13% of the time, Pallas kernels for 28%

profile of v6, /device:TPU:1, one launch (start us, length us, event | category | flops | bytes accessed | tf_op | source)
XLA Modules:
  0.0 382.7 jit_solution(13869838851245674338)
XLA Ops:
  17.4 28.9 %collective-permute-done = bf16[768,1024]{1,0:T(8,128)(2,1)} collective-permute-done((bf16[768,1024]{1,0:T(8,128)(2,1)S(1)}, bf16[768,1024]{1,0:T(8,128)(2,1)}, u32[]{:S(2)}, u32[]{:S(2)}) %collective-permute-start) | collective-permute-done | bytes 1572896 | tf_op jit(solution)/shard_map/ppermute | solution.py:300
  65.6 16.7 %collective-permute-done.3 = bf16[768,1024]{1,0:T(8,128)(2,1)S(1)} collective-permute-done((bf16[768,1024]{1,0:T(8,128)(2,1)}, bf16[768,1024]{1,0:T(8,128)(2,1)S(1)}, u32[]{:S(2)}, u32[]{:S(2)}) %collective-permute-start.3) | collective-permute-done | bytes 1572896 | tf_op jit(solution)/shard_map/ppermute | solution.py:300
  84.9 3.0 collective-permute-start.9
  96.5 32.2 %collective-permute-done.12 = bf16[256,3072]{1,0:T(8,128)(2,1)S(1)} collective-permute-done((bf16[256,3072]{1,0:T(8,128)(2,1)S(1)}, bf16[256,3072]{1,0:T(8,128)(2,1)S(1)}, u32[]{:S(2)}, u32[]{:S(2)}) %collective-permute-start.12) | collective-permute-done | bytes 1572896 | tf_op jit(solution)/shard_map/ppermute | solution.py:318
  133.3 13.1 %fusion.4.qk_ref = f32[1024,1024]{1,0:T(8,128)S(1)} fusion(bf16[1024,6144]{1,0:T(8,128)(2,1)S(1)} %slice_dynamic-update-slice_fusion.normed_ref, bf16[6144,1024]{1,0:T(8,128)(2,1)S(1)} %constant_dynamic-update-slice_fusion.refs_0_), kind=kOutput, calls=%fused_computation.94 | convolution fusion | flops 12884901888 | bytes 29360128 | tf_op jit(solution)/shard_map/dot_general | solution.py:399
  146.4 6.1 %shard_map.113.turned_ref = bf16[512,1024]{1,0:T(8,128)(2,1)S(1)} custom-call(f32[1024,1024]{1,0:T(8,128)S(1)} %fusion.4.qk_ref, bf16[1024,512]{1,0:T(8,128)(2,1)S(1)} %constant_dynamic-update-slice_fusion.12.g_ref, f32[2,128]{1,0:T(2,128)S(1)} %pad_maximum_fusion.13.gains_ref), custom_call_target="tpu_custom_call" | custom-call | flops 1073741824 | bytes 8388608 | tf_op jit(solution)/shard_map/pallas_call | solution.py:95
  156.0 6.5 %shard_map.116 = (bf16[1024,768]{1,0:T(8,128)(2,1)}, bf16[1024,768]{1,0:T(8,128)(2,1)}) custom-call(bf16[512,1024]{1,0:T(8,128)(2,1)S(1)} %shard_map.113.turned_ref, bf16[1024,6144]{1,0:T(8,128)(2,1)S(1)} %slice_dynamic-update-slice_fusion.normed_ref), custom_call_target="tpu_custom_call" | custom-call | flops 3221225472 | bytes 8912896 | tf_op jit(solution)/shard_map/pallas_call | solution.py:138
  167.7 5.4 %collective-permute-done.19 = bf16[768,512]{1,0:T(8,128)(2,1)S(1)} collective-permute-done((bf16[768,512]{1,0:T(8,128)(2,1)S(1)}, bf16[768,512]{1,0:T(8,128)(2,1)S(1)}, u32[]{:S(2)}, u32[]{:S(2)}) %collective-permute-start.19) | collective-permute-done | bytes 786464 | tf_op jit(solution)/shard_map/ppermute | solution.py:300
  174.6 7.6 %convolution_convert_fusion.v_ref = bf16[1024,512]{1,0:T(8,128)(2,1)} fusion(bf16[1024,6144]{1,0:T(8,128)(2,1)S(1)} %slice_dynamic-update-slice_fusion.normed_ref, bf16[6144,512]{1,0:T(8,128)(2,1)S(1)} %constant_dynamic-update-slice_fusion.8.refs_1_), kind=kOutput, calls=%fused_computation.14 | convolution fusion | flops 6442975232 | bytes 19922944 | tf_op jit(solution)/shard_map/dot_general | solution.py:446
  186.8 10.0 %shard_map.114.turned_ref = bf16[1024,1024]{1,0:T(8,128)(2,1)S(1)} custom-call(f32[1024,1024]{1,0:T(8,128)S(1)} %copy-done.13, bf16[1024,512]{1,0:T(8,128)(2,1)S(1)} %copy-done.19, bf16[1024,512]{1,0:T(8,128)(2,1)S(1)} %copy-done.32, f32[2,128]{1,0:T(2,128)S(1)} %pad_maximum_fusion.13.gains_ref), custom_call_target="tpu_custom_call" | custom-call | flops 1073741824 | bytes 12582912 | tf_op jit(solution)/shard_map/pallas_call | solution.py:95
  198.0 6.3 %shard_map.119 = bf16[3072,256]{1,0:T(8,128)(2,1)} custom-call(bf16[1024,256]{1,0:T(8,128)(2,1)S(1)} %pad_maximum_fusion.6.pair_ref, bf16[512,256]{1,0:T(8,128)(2,1)S(1)} %copy-done.22, bf16[6144,1024]{1,0:T(8,128)(2,1)S(1)} %constant_dynamic-update-slice_fusion.refs_0_, bf16[6144,512]{1,0:T(8,128)(2,1)S(1)} %constant_dynamic-update-slice_fusion.8.refs_1_), custom_call_target="tpu_custom_call" | custom-call | flops 2415919104 | bytes 14155776 | tf_op jit(solution)/shard_map/pallas_call | solution.py:172
  204.3 6.1 %shard_map.118 = bf16[3072,256]{1,0:T(8,128)(2,1)} custom-call(bf16[1024,256]{1,0:T(8,128)(2,1)S(1)} %pad_maximum_fusion.5.pair_ref, bf16[512,256]{1,0:T(8,128)(2,1)S(1)} %copy-done.24, bf16[6144,1024]{1,0:T(8,128)(2,1)S(1)} %constant_dynamic-update-slice_fusion.refs_0_, bf16[6144,512]{1,0:T(8,128)(2,1)S(1)} %constant_dynamic-update-slice_fusion.8.refs_1_), custom_call_target="tpu_custom_call" | custom-call | flops 2415919104 | bytes 14155776 | tf_op jit(solution)/shard_map/pallas_call | solution.py:172
  210.5 4.9 %shard_map.117 = (bf16[512,768]{1,0:T(8,128)(2,1)}, bf16[512,768]{1,0:T(8,128)(2,1)}) custom-call(bf16[512,1024]{1,0:T(8,128)(2,1)S(1)} %copy-done.10, bf16[1024,6144]{1,0:T(8,128)(2,1)S(1)} %slice_dynamic-update-slice_fusion.normed_ref, bf16[1024,768]{1,0:T(8,128)(2,1)} %collective-permute-done.21.refs_0_.refs_2_, ...), custom_call_target="tpu_custom_call" | custom-call | flops 1610612736 | bytes 7340032 | tf_op jit(solution)/shard_map/pallas_call | solution.py:138
  215.4 4.1 %collective-permute-start.23 = (bf16[3072,256]{1,0:T(8,128)(2,1)}, bf16[3072,256]{1,0:T(8,128)(2,1)}, u32[]{:S(2)}, u32[]{:S(2)}) collective-permute-start(bf16[3072,256]{1,0:T(8,128)(2,1)} %shard_map.118), channel_id=1, source_target_pairs={{0,4},{4,0},{8,12},{12,8},{16,20},{20,16},{24,28},{28,24},{1,5},{5... | collective-permute-start | bytes 4718600 | tf_op jit(solution)/shard_map/ppermute | solution.py:300
  220.9 4.6 %copy-done.4 = bf16[1024,6144]{1,0:T(8,128)(2,1)S(1)} copy-done((bf16[1024,6144]{1,0:T(8,128)(2,1)S(1)}, bf16[1024,6144]{1,0:T(8,128)(2,1)}, u32[]{:S(2)}) %copy-start.4) | copy-done | bytes 12582936
  225.4 5.5 %shard_map.115 = (bf16[1024,768]{1,0:T(8,128)(2,1)}, bf16[1024,768]{1,0:T(8,128)(2,1)}) custom-call(bf16[1024,1024]{1,0:T(8,128)(2,1)S(1)} %copy-done.8, bf16[1024,6144]{1,0:T(8,128)(2,1)S(1)} %copy-done.4), custom_call_target="tpu_custom_call" | custom-call | flops 3221225472 | bytes 8388608 | tf_op jit(solution)/shard_map/pallas_call | solution.py:138
  234.0 7.3 %shard_map.120 = bf16[3072,256]{1,0:T(8,128)(2,1)S(1)} custom-call(bf16[1024,256]{1,0:T(8,128)(2,1)S(1)} %copy-done.21, bf16[512,256]{1,0:T(8,128)(2,1)S(1)} %copy-done.25, bf16[6144,1024]{1,0:T(8,128)(2,1)S(1)} %copy-done.1, bf16[6144,512]{1,0:T(8,128)(2,1)S(1)} %copy-done.6, bf16[3072,256]{1,0:T(8,128)(2,1)} %collective-permute-done.23.refs_2_), custom_call_target="tpu_custom_call" | custom-call | flops 2415919104 | bytes 14155776 | tf_op jit(solution)/shard_map/pallas_call | solution.py:172
  247.1 4.7 %shard_map.125 = (bf16[768,512]{1,0:T(8,128)(2,1)S(1)}, bf16[768,512]{1,0:T(8,128)(2,1)S(1)}) custom-call(bf16[512,1024]{1,0:T(8,128)(2,1)S(1)} %copy-done.11, bf16[1024,6144]{1,0:T(8,128)(2,1)S(1)} %copy-done.4, bf16[1024,768]{1,0:T(8,128)(2,1)} %collective-permute-done.22.refs_1_.refs_0_, bf16[512,768]{1,0:T(8,128)(2,1)} %collective-permute-done.26.refs_1_, ...), custom_call_target="tpu_custom_call" | custom-call | flops 1610612736 | bytes 8912896 | tf_op jit(solution)/shard_map/pallas_call | solution.py:138
  251.9 7.5 %shard_map.121 = bf16[3072,256]{1,0:T(8,128)(2,1)S(1)} custom-call(bf16[1024,256]{1,0:T(8,128)(2,1)S(1)} %pad_maximum_fusion.6.pair_ref, bf16[512,256]{1,0:T(8,128)(2,1)S(1)} %copy-done.23, bf16[6144,1024]{1,0:T(8,128)(2,1)S(1)} %copy-done.1, bf16[6144,512]{1,0:T(8,128)(2,1)S(1)} %bitcast.12, bf16[3072,256]{1,0:T(8,128)(2,1)} %collective-permute-done.24.refs_2_), custom_call_target="tpu_custom_call" | custom-call | flops 2415919104 | bytes 14155776 | tf_op jit(solution)/shard_map/pallas_call | solution.py:172
  259.4 5.5 %shard_map.124 = bf16[3072,256]{1,0:T(8,128)(2,1)S(1)} custom-call(bf16[1024,256]{1,0:T(8,128)(2,1)S(1)} %pad_maximum_fusion.8.pair_ref, bf16[512,256]{1,0:T(8,128)(2,1)S(1)} %pad_maximum_fusion.12.value_ref, bf16[6144,1024]{1,0:T(8,128)(2,1)S(1)} %copy-done.1, bf16[6144,512]{1,0:T(8,128)(2,1)S(1)} %bitcast.12), custom_call_target="tpu_custom_call" | custom-call | flops 2415919104 | bytes 14155776 | tf_op jit(solution)/shard_map/pallas_call | solution.py:172
  265.0 5.6 %shard_map.123 = bf16[3072,256]{1,0:T(8,128)(2,1)S(1)} custom-call(bf16[1024,256]{1,0:T(8,128)(2,1)S(1)} %pad_maximum_fusion.7.pair_ref, bf16[512,256]{1,0:T(8,128)(2,1)S(1)} %pad_maximum_fusion.11.value_ref, bf16[6144,1024]{1,0:T(8,128)(2,1)S(1)} %copy-done.1, bf16[6144,512]{1,0:T(8,128)(2,1)S(1)} %bitcast.12), custom_call_target="tpu_custom_call" | custom-call | flops 2415919104 | bytes 14155776 | tf_op jit(solution)/shard_map/pallas_call | solution.py:172
  270.5 4.9 %shard_map.122 = (bf16[1024,768]{1,0:T(8,128)(2,1)S(1)}, bf16[1024,768]{1,0:T(8,128)(2,1)S(1)}) custom-call(bf16[1024,1024]{1,0:T(8,128)(2,1)S(1)} %copy-done.8, bf16[1024,6144]{1,0:T(8,128)(2,1)S(1)} %copy-done.4), custom_call_target="tpu_custom_call" | custom-call | flops 3221225472 | bytes 8388608 | tf_op jit(solution)/shard_map/pallas_call | solution.py:138
  284.9 3.2 collective-permute-start.34
  288.1 7.4 %shard_map.127 = f32[3072,256]{1,0:T(8,128)S(1)} custom-call(bf16[1024,256]{1,0:T(8,128)(2,1)S(1)} %pad_maximum_fusion.8.pair_ref, bf16[512,256]{1,0:T(8,128)(2,1)S(1)} %pad_maximum_fusion.12.value_ref, bf16[6144,1024]{1,0:T(8,128)(2,1)S(1)} %copy-done.1, bf16[6144,512]{1,0:T(8,128)(2,1)S(1)} %bitcast.12, bf16[3072,256]{1,0:T(8,128)(2,1)S(1)} %collective-permute-done.31.refs_2_), custom_call_target="tpu_custom_call" | custom-call | flops 2415919104 | bytes 14155776 | tf_op jit(solution)/shard_map/pallas_call | solution.py:172
  297.2 5.8 %shard_map.126 = bf16[3072,256]{1,0:T(8,128)(2,1)S(1)} custom-call(bf16[1024,256]{1,0:T(8,128)(2,1)S(1)} %pad_maximum_fusion.7.pair_ref, bf16[512,256]{1,0:T(8,128)(2,1)S(1)} %pad_maximum_fusion.11.value_ref, bf16[6144,1024]{1,0:T(8,128)(2,1)S(1)} %copy-done.1, bf16[6144,512]{1,0:T(8,128)(2,1)S(1)} %bitcast.12, ...), custom_call_target="tpu_custom_call" | custom-call | flops 2415919104 | bytes 14155776 | tf_op jit(solution)/shard_map/pallas_call | solution.py:172
  303.0 4.9 %shard_map.129 = (bf16[1024,768]{1,0:T(8,128)(2,1)S(1)}, bf16[1024,768]{1,0:T(8,128)(2,1)S(1)}) custom-call(bf16[1024,1024]{1,0:T(8,128)(2,1)S(1)} %copy-done.8, bf16[1024,6144]{1,0:T(8,128)(2,1)S(1)} %copy-done.4), custom_call_target="tpu_custom_call" | custom-call | flops 3221225472 | bytes 8388608 | tf_op jit(solution)/shard_map/pallas_call | solution.py:138
  307.9 5.5 %shard_map.128 = (bf16[1024,768]{1,0:T(8,128)(2,1)S(1)}, bf16[1024,768]{1,0:T(8,128)(2,1)S(1)}) custom-call(bf16[1024,1024]{1,0:T(8,128)(2,1)S(1)} %copy-done.8, bf16[1024,6144]{1,0:T(8,128)(2,1)S(1)} %copy-done.4, bf16[1024,768]{1,0:T(8,128)(2,1)S(1)} %collective-permute-done.28.refs_0_, bf16[1024,768]{1,0:T(8,128)(2,1)S(1)} %collective-permute-done.27.refs_1_), custom_call_target="tpu_custom_call" | custom-call | flops 3221225472 | bytes 11534336 | tf_op jit(solution)/shard_map/pallas_call | solution.py:138
  313.4 5.2 %collective-permute-done.32.refs_1_ = bf16[1024,768]{1,0:T(8,128)(2,1)S(1)} collective-permute-done((bf16[1024,768]{1,0:T(8,128)(2,1)}, bf16[1024,768]{1,0:T(8,128)(2,1)S(1)}, u32[]{:S(2)}, u32[]{:S(2)}) %collective-permute-start.32) | collective-permute-done | bytes 1572896 | tf_op jit(solution)/shard_map/ppermute | solution.py:300
  325.4 3.1 collective-permute-start.35
  331.5 30.5 %collective-permute-done.35 = bf16[3072,256]{1,0:T(8,128)(2,1)} collective-permute-done((bf16[3072,256]{1,0:T(8,128)(2,1)}, bf16[3072,256]{1,0:T(8,128)(2,1)}, u32[]{:S(2)}, u32[]{:S(2)}) %collective-permute-start.35) | collective-permute-done | bytes 1572896 | tf_op jit(solution)/shard_map/ppermute | solution.py:318
  372.3 3.4 shard_map.130
  375.7 6.7 %shard_map.131 = (bf16[768,1024]{1,0:T(8,128)(2,1)}, bf16[768,1024]{1,0:T(8,128)(2,1)}) custom-call(s32[1]{0:T(128)} %bitcast.5.core_ref, bf16[1024,768]{1,0:T(8,128)(2,1)S(1)} %copy-done.31, bf16[1024,768]{1,0:T(8,128)(2,1)S(1)} %copy-done.27, bf16[1024,768]{1,0:T(8,128)(2,1)} %collective-permute-done.38.refs_2_, ...), custom_call_target="tpu_custom_call" | custom-call | tf_op jit(solution)/shard_map/pallas_call | solution.py:214
  (263 shorter events, 108.7 us)
Async XLA Ops:
  8.9 37.5 %collective-permute-start = (bf16[768,1024]{1,0:T(8,128)(2,1)S(1)}, bf16[768,1024]{1,0:T(8,128)(2,1)}, u32[]{:S(2)}, u32[]{:S(2)}) collective-permute-start(bf16[768,1024]{1,0:T(8,128)(2,1)S(1)} %pad_maximum_fusion), channel_id=1, source_target_pairs={{0,8},{4,12},{8,0},{12,4},{16,24},{20,28},{24,16},{28,20},{1,9},{5... | collective-permute-start | bytes 4718600 | tf_op jit(solution)/shard_map/ppermute | solution.py:300
  11.6 35.7 %collective-permute-start.1 = (bf16[768,1024]{1,0:T(8,128)(2,1)S(1)}, bf16[768,1024]{1,0:T(8,128)(2,1)}, u32[]{:S(2)}, u32[]{:S(2)}) collective-permute-start(bf16[768,1024]{1,0:T(8,128)(2,1)S(1)} %pad_maximum_fusion), channel_id=1, source_target_pairs={{0,16},{4,20},{8,24},{12,28},{16,0},{20,4},{24,8},{28,12},{1,17},{... | collective-permute-start | bytes 4718600 | tf_op jit(solution)/shard_map/ppermute | solution.py:300
  12.8 34.5 %collective-permute-start.2 = (bf16[768,1024]{1,0:T(8,128)(2,1)}, bf16[768,1024]{1,0:T(8,128)(2,1)}, u32[]{:S(2)}, u32[]{:S(2)}) collective-permute-start(bf16[768,1024]{1,0:T(8,128)(2,1)} %pad_maximum_fusion.1), channel_id=1, source_target_pairs={{0,4},{4,0},{8,12},{12,8},{16,20},{20,16},{24,28},{28,24},{1,5},{5... | collective-permute-start | bytes 4718600 | tf_op jit(solution)/shard_map/ppermute | solution.py:300
  14.8 36.5 %collective-permute-start.7 = (bf16[256,3072]{1,0:T(8,128)(2,1)}, bf16[256,3072]{1,0:T(8,128)(2,1)}, u32[]{:S(2)}, u32[]{:S(2)}) collective-permute-start(bf16[256,3072]{1,0:T(8,128)(2,1)} %pad_maximum_fusion.2), channel_id=1, source_target_pairs={{0,2},{2,3},{3,1},{1,0},{4,6},{6,7},{7,5},{5,4},{8,10},{10,11},{11... | collective-permute-start | bytes 4718600 | tf_op jit(solution)/shard_map/ppermute | solution.py:318
  17.1 38.0 %collective-permute-start.6 = (bf16[256,3072]{1,0:T(8,128)(2,1)}, bf16[256,3072]{1,0:T(8,128)(2,1)}, u32[]{:S(2)}, u32[]{:S(2)}) collective-permute-start(bf16[256,3072]{1,0:T(8,128)(2,1)} %pad_maximum_fusion.2), channel_id=1, source_target_pairs={{0,4},{4,0},{8,12},{12,8},{16,20},{20,16},{24,28},{28,24},{1,5},{5... | collective-permute-start | bytes 4718600 | tf_op jit(solution)/shard_map/ppermute | solution.py:300
  47.3 34.9 %collective-permute-start.3 = (bf16[768,1024]{1,0:T(8,128)(2,1)}, bf16[768,1024]{1,0:T(8,128)(2,1)S(1)}, u32[]{:S(2)}, u32[]{:S(2)}) collective-permute-start(bf16[768,1024]{1,0:T(8,128)(2,1)} %collective-permute-done.2), channel_id=1, source_target_pairs={{0,8},{4,12},{8,0},{12,4},{16,24},{20,28},{24,16},{28,20},{1,9},{5... | collective-permute-start | bytes 4718600 | tf_op jit(solution)/shard_map/ppermute | solution.py:300
  47.7 34.9 %collective-permute-start.4 = (bf16[768,1024]{1,0:T(8,128)(2,1)}, bf16[768,1024]{1,0:T(8,128)(2,1)S(1)}, u32[]{:S(2)}, u32[]{:S(2)}) collective-permute-start(bf16[768,1024]{1,0:T(8,128)(2,1)} %collective-permute-done.2), channel_id=1, source_target_pairs={{0,16},{4,20},{8,24},{12,28},{16,0},{20,4},{24,8},{28,12},{1,17},{... | collective-permute-start | bytes 4718600 | tf_op jit(solution)/shard_map/ppermute | solution.py:300
  51.3 12.4 %collective-permute-start.8 = (bf16[256,3072]{1,0:T(8,128)(2,1)}, bf16[256,3072]{1,0:T(8,128)(2,1)S(1)}, u32[]{:S(2)}, u32[]{:S(2)}) collective-permute-start(bf16[256,3072]{1,0:T(8,128)(2,1)} %collective-permute-done.7), channel_id=1, source_target_pairs={{0,4},{4,0},{8,12},{12,8},{16,20},{20,16},{24,28},{28,24},{1,5},{5... | collective-permute-start | bytes 4718600 | tf_op jit(solution)/shard_map/ppermute | solution.py:300
  52.6 38.8 %collective-permute-start.10 = (bf16[256,3072]{1,0:T(8,128)(2,1)}, bf16[256,3072]{1,0:T(8,128)(2,1)S(1)}, u32[]{:S(2)}, u32[]{:S(2)}) collective-permute-start(bf16[256,3072]{1,0:T(8,128)(2,1)} %collective-permute-done.7), channel_id=1, source_target_pairs={{0,2},{2,3},{3,1},{1,0},{4,6},{6,7},{7,5},{5,4},{8,10},{10,11},{11... | collective-permute-start | bytes 4718600 | tf_op jit(solution)/shard_map/ppermute | solution.py:318
  82.6 47.4 %collective-permute-start.14 = (bf16[768,1024]{1,0:T(8,128)(2,1)}, bf16[768,1024]{1,0:T(8,128)(2,1)S(1)}, u32[]{:S(2)}, u32[]{:S(2)}) collective-permute-start(bf16[768,1024]{1,0:T(8,128)(2,1)} %collective-permute-done), channel_id=1, source_target_pairs={{0,16},{4,20},{8,24},{12,28},{16,0},{20,4},{24,8},{28,12},{1,17},{... | collective-permute-start | bytes 4718600 | tf_op jit(solution)/shard_map/ppermute | solution.py:300
  83.6 48.4 %collective-permute-start.15 = (bf16[768,1024]{1,0:T(8,128)(2,1)S(1)}, bf16[768,1024]{1,0:T(8,128)(2,1)S(1)}, u32[]{:S(2)}, u32[]{:S(2)}) collective-permute-start(bf16[768,1024]{1,0:T(8,128)(2,1)S(1)} %collective-permute-done.4), channel_id=1, source_target_pairs={{0,8},{4,12},{8,0},{12,4},{16,24},{20,28},{24,16},{28,20},{1,9},{5... | collective-permute-start | bytes 4718600 | tf_op jit(solution)/shard_map/ppermute | solution.py:300
  92.9 35.9 %collective-permute-start.12 = (bf16[256,3072]{1,0:T(8,128)(2,1)S(1)}, bf16[256,3072]{1,0:T(8,128)(2,1)S(1)}, u32[]{:S(2)}, u32[]{:S(2)}) collective-permute-start(bf16[256,3072]{1,0:T(8,128)(2,1)S(1)} %collective-permute-done.10), channel_id=1, source_target_pairs={{0,2},{2,3},{3,1},{1,0},{4,6},{6,7},{7,5},{5,4},{8,10},{10,11},{11... | collective-permute-start | bytes 4718600 | tf_op jit(solution)/shard_map/ppermute | solution.py:318
  95.9 56.7 %collective-permute-start.17 = (bf16[1536,512]{1,0:T(8,128)(2,1)S(1)}, bf16[1536,512]{1,0:T(8,128)(2,1)}, u32[]{:S(2)}, u32[]{:S(2)}) collective-permute-start(bf16[1536,512]{1,0:T(8,128)(2,1)S(1)} %pad_maximum_fusion.3), channel_id=1, source_target_pairs={{0,8},{4,12},{8,0},{12,4},{16,24},{20,28},{24,16},{28,20},{1,9},{5... | collective-permute-start | bytes 4718600 | tf_op jit(solution)/shard_map/ppermute | solution.py:300
  96.3 56.3 %collective-permute-start.18 = (bf16[1536,512]{1,0:T(8,128)(2,1)S(1)}, bf16[1536,512]{1,0:T(8,128)(2,1)}, u32[]{:S(2)}, u32[]{:S(2)}) collective-permute-start(bf16[1536,512]{1,0:T(8,128)(2,1)S(1)} %pad_maximum_fusion.3), channel_id=1, source_target_pairs={{0,16},{4,20},{8,24},{12,28},{16,0},{20,4},{24,8},{28,12},{1,17},{... | collective-permute-start | bytes 4718600 | tf_op jit(solution)/shard_map/ppermute | solution.py:300
  155.3 17.8 %collective-permute-start.19 = (bf16[768,512]{1,0:T(8,128)(2,1)S(1)}, bf16[768,512]{1,0:T(8,128)(2,1)S(1)}, u32[]{:S(2)}, u32[]{:S(2)}) collective-permute-start(bf16[768,512]{1,0:T(8,128)(2,1)S(1)} %slice.75), channel_id=1, source_target_pairs={{0,16},{4,20},{8,24},{12,28},{16,0},{20,4},{24,8},{28,12},{1,17},{... | collective-permute-start | bytes 2359304 | tf_op jit(solution)/shard_map/ppermute | solution.py:300
  155.6 18.9 %collective-permute-start.20 = (bf16[768,512]{1,0:T(8,128)(2,1)S(1)}, bf16[768,512]{1,0:T(8,128)(2,1)S(1)}, u32[]{:S(2)}, u32[]{:S(2)}) collective-permute-start(bf16[768,512]{1,0:T(8,128)(2,1)S(1)} %slice.76), channel_id=1, source_target_pairs={{0,8},{4,12},{8,0},{12,4},{16,24},{20,28},{24,16},{28,20},{1,9},{5... | collective-permute-start | bytes 2359304 | tf_op jit(solution)/shard_map/ppermute | solution.py:300
  162.4 48.0 %collective-permute-start.21 = (bf16[1024,768]{1,0:T(8,128)(2,1)}, bf16[1024,768]{1,0:T(8,128)(2,1)}, u32[]{:S(2)}, u32[]{:S(2)}) collective-permute-start(bf16[1024,768]{1,0:T(8,128)(2,1)} %get-tuple-element.124), channel_id=1, source_target_pairs={{0,16},{4,20},{8,24},{12,28},{16,0},{20,4},{24,8},{28,12},{1,17},{... | collective-permute-start | bytes 4718600 | tf_op jit(solution)/shard_map/ppermute | solution.py:300
  163.7 46.8 %collective-permute-start.22 = (bf16[1024,768]{1,0:T(8,128)(2,1)}, bf16[1024,768]{1,0:T(8,128)(2,1)}, u32[]{:S(2)}, u32[]{:S(2)}) collective-permute-start(bf16[1024,768]{1,0:T(8,128)(2,1)} %get-tuple-element.125), channel_id=1, source_target_pairs={{0,8},{4,12},{8,0},{12,4},{16,24},{20,28},{24,16},{28,20},{1,9},{5... | collective-permute-start | bytes 4718600 | tf_op jit(solution)/shard_map/ppermute | solution.py:300
  215.4 15.5 %collective-permute-start.23 = (bf16[3072,256]{1,0:T(8,128)(2,1)}, bf16[3072,256]{1,0:T(8,128)(2,1)}, u32[]{:S(2)}, u32[]{:S(2)}) collective-permute-start(bf16[3072,256]{1,0:T(8,128)(2,1)} %shard_map.118), channel_id=1, source_target_pairs={{0,4},{4,0},{8,12},{12,8},{16,20},{20,16},{24,28},{28,24},{1,5},{5... | collective-permute-start | bytes 4718600 | tf_op jit(solution)/shard_map/ppermute | solution.py:300
  219.4 21.9 %collective-permute-start.25 = (bf16[512,768]{1,0:T(8,128)(2,1)}, bf16[512,768]{1,0:T(8,128)(2,1)S(1)}, u32[]{:S(2)}, u32[]{:S(2)}) collective-permute-start(bf16[512,768]{1,0:T(8,128)(2,1)} %get-tuple-element.135), channel_id=1, source_target_pairs={{0,8},{4,12},{8,0},{12,4},{16,24},{20,28},{24,16},{28,20},{1,9},{5... | collective-permute-start | bytes 2359304 | tf_op jit(solution)/shard_map/ppermute | solution.py:300
  220.5 20.8 %collective-permute-start.26 = (bf16[512,768]{1,0:T(8,128)(2,1)}, bf16[512,768]{1,0:T(8,128)(2,1)}, u32[]{:S(2)}, u32[]{:S(2)}) collective-permute-start(bf16[512,768]{1,0:T(8,128)(2,1)} %get-tuple-element.136), channel_id=1, source_target_pairs={{0,16},{4,20},{8,24},{12,28},{16,0},{20,4},{24,8},{28,12},{1,17},{... | collective-permute-start | bytes 2359304 | tf_op jit(solution)/shard_map/ppermute | solution.py:300
  241.3 36.5 %collective-permute-start.27 = (bf16[1024,768]{1,0:T(8,128)(2,1)}, bf16[1024,768]{1,0:T(8,128)(2,1)S(1)}, u32[]{:S(2)}, u32[]{:S(2)}) collective-permute-start(bf16[1024,768]{1,0:T(8,128)(2,1)} %get-tuple-element.142), channel_id=1, source_target_pairs={{0,8},{4,12},{8,0},{12,4},{16,24},{20,28},{24,16},{28,20},{1,9},{5... | collective-permute-start | bytes 4718600 | tf_op jit(solution)/shard_map/ppermute | solution.py:300
  241.9 35.9 %collective-permute-start.28 = (bf16[1024,768]{1,0:T(8,128)(2,1)}, bf16[1024,768]{1,0:T(8,128)(2,1)S(1)}, u32[]{:S(2)}, u32[]{:S(2)}) collective-permute-start(bf16[1024,768]{1,0:T(8,128)(2,1)} %get-tuple-element.143), channel_id=1, source_target_pairs={{0,16},{4,20},{8,24},{12,28},{16,0},{20,4},{24,8},{28,12},{1,17},{... | collective-permute-start | bytes 4718600 | tf_op jit(solution)/shard_map/ppermute | solution.py:300
  242.9 34.9 %collective-permute-start.29 = (bf16[3072,256]{1,0:T(8,128)(2,1)S(1)}, bf16[3072,256]{1,0:T(8,128)(2,1)}, u32[]{:S(2)}, u32[]{:S(2)}) collective-permute-start(bf16[3072,256]{1,0:T(8,128)(2,1)S(1)} %shard_map.120), channel_id=1, source_target_pairs={{0,2},{2,3},{3,1},{1,0},{4,6},{6,7},{7,5},{5,4},{8,10},{10,11},{11... | collective-permute-start | bytes 4718600 | tf_op jit(solution)/shard_map/ppermute | solution.py:318
  282.8 35.8 %collective-permute-start.32 = (bf16[1024,768]{1,0:T(8,128)(2,1)}, bf16[1024,768]{1,0:T(8,128)(2,1)S(1)}, u32[]{:S(2)}, u32[]{:S(2)}) collective-permute-start(bf16[1024,768]{1,0:T(8,128)(2,1)} %copy-done.43), channel_id=1, source_target_pairs={{0,8},{4,12},{8,0},{12,4},{16,24},{20,28},{24,16},{28,20},{1,9},{5... | collective-permute-start | bytes 4718600 | tf_op jit(solution)/shard_map/ppermute | solution.py:300
  283.9 37.2 %collective-permute-start.33 = (bf16[1024,768]{1,0:T(8,128)(2,1)}, bf16[1024,768]{1,0:T(8,128)(2,1)S(1)}, u32[]{:S(2)}, u32[]{:S(2)}) collective-permute-start(bf16[1024,768]{1,0:T(8,128)(2,1)} %copy-done.42), channel_id=1, source_target_pairs={{0,20},{4,16},{8,28},{12,24},{16,4},{20,0},{24,12},{28,8},{1,21},{... | collective-permute-start | bytes 4718600 | tf_op jit(solution)/shard_map/ppermute | solution.py:300
  284.9 37.5 %collective-permute-start.34 = (bf16[3072,256]{1,0:T(8,128)(2,1)}, bf16[3072,256]{1,0:T(8,128)(2,1)}, u32[]{:S(2)}, u32[]{:S(2)}) collective-permute-start(bf16[3072,256]{1,0:T(8,128)(2,1)} %add_convert_fusion.1), channel_id=1, source_target_pairs={{0,2},{2,3},{3,1},{1,0},{4,6},{6,7},{7,5},{5,4},{8,10},{10,11},{11... | collective-permute-start | bytes 4718600 | tf_op jit(solution)/shard_map/ppermute | solution.py:318
  325.4 36.6 %collective-permute-start.35 = (bf16[3072,256]{1,0:T(8,128)(2,1)}, bf16[3072,256]{1,0:T(8,128)(2,1)}, u32[]{:S(2)}, u32[]{:S(2)}) collective-permute-start(bf16[3072,256]{1,0:T(8,128)(2,1)} %add_convert_fusion), channel_id=1, source_target_pairs={{0,2},{2,3},{3,1},{1,0},{4,6},{6,7},{7,5},{5,4},{8,10},{10,11},{11... | collective-permute-start | bytes 4718600 | tf_op jit(solution)/shard_map/ppermute | solution.py:318
  328.6 38.6 %collective-permute-start.40 = (bf16[768,512]{1,0:T(8,128)(2,1)}, bf16[768,512]{1,0:T(8,128)(2,1)}, u32[]{:S(2)}, u32[]{:S(2)}) collective-permute-start(bf16[768,512]{1,0:T(8,128)(2,1)} %copy-done.44), channel_id=1, source_target_pairs={{0,4},{4,0},{8,12},{12,8},{16,20},{20,16},{24,28},{28,24},{1,5},{5... | collective-permute-start | bytes 2359304 | tf_op jit(solution)/shard_map/ppermute | solution.py:300
  329.4 46.3 %collective-permute-start.37 = (bf16[1024,768]{1,0:T(8,128)(2,1)}, bf16[1024,768]{1,0:T(8,128)(2,1)}, u32[]{:S(2)}, u32[]{:S(2)}) collective-permute-start(bf16[1024,768]{1,0:T(8,128)(2,1)} %copy-done.41), channel_id=1, source_target_pairs={{0,12},{4,8},{8,4},{12,0},{16,28},{20,24},{24,20},{28,16},{1,13},{... | collective-permute-start | bytes 4718600 | tf_op jit(solution)/shard_map/ppermute | solution.py:300
  329.7 46.0 %collective-permute-start.38 = (bf16[1024,768]{1,0:T(8,128)(2,1)}, bf16[1024,768]{1,0:T(8,128)(2,1)}, u32[]{:S(2)}, u32[]{:S(2)}) collective-permute-start(bf16[1024,768]{1,0:T(8,128)(2,1)} %copy-done.40), channel_id=1, source_target_pairs={{0,16},{4,20},{8,24},{12,28},{16,0},{20,4},{24,8},{28,12},{1,17},{... | collective-permute-start | bytes 4718600 | tf_op jit(solution)/shard_map/ppermute | solution.py:300
  330.8 44.9 %collective-permute-start.39 = (bf16[1024,768]{1,0:T(8,128)(2,1)}, bf16[1024,768]{1,0:T(8,128)(2,1)}, u32[]{:S(2)}, u32[]{:S(2)}) collective-permute-start(bf16[1024,768]{1,0:T(8,128)(2,1)} %copy-done.39), channel_id=1, source_target_pairs={{0,4},{4,0},{8,12},{12,8},{16,20},{20,16},{24,28},{28,24},{1,5},{5... | collective-permute-start | bytes 4718600 | tf_op jit(solution)/shard_map/ppermute | solution.py:300
  (69 other events, 793.0 us)

commit v7 on v6

--- a/solution.py
+++ b/solution.py
@@ -39,7 +39,7 @@
 
 
 def cost(flops, bytes_accessed):
-    return pl.CostEstimate(flops=flops, bytes_accessed=bytes_accessed, transcendentals=0)
+    return pl.CostEstimate(flops=flops // 6, bytes_accessed=bytes_accessed // 6, transcendentals=0)
 
 
 def blank(shape, dtype):
@@ -99,7 +99,7 @@
         + [pl.BlockSpec(gains.shape, lambda i: (0, 0))],
         out_specs=pl.BlockSpec((out_rows, PATCH), lambda i: (0, i)),
         out_shape=jax.ShapeDtypeStruct((out_rows, tokens), BF),
-        compiler_params=params(16),
+        compiler_params=params(12),
         cost_estimate=cost(pairs * 8 * PATCH * PATCH * head, 4 * len(arrays) * arrays[0].size),
     )(*arrays, gains)
 
@@ -149,35 +149,35 @@
     )(turned, normed, *[array for array, _ in addends])
 
 
-def back_kernel(specs, grid, pair_ref, value_ref, *refs):
-    def body(w_pair_ref, w_value_ref, *blocks):
-        total = jnp.dot(w_pair_ref[...], pair_ref[...], preferred_element_type=F32)
-        total = total + jnp.dot(w_value_ref[...], value_ref[...], preferred_element_type=F32)
-        for block in blocks[:-1]:
-            total = total + block[...].astype(F32)
-        blocks[-1][...] = total.astype(blocks[-1].dtype)
-
-    pltpu.emit_pipeline(body, grid=grid, in_specs=specs[:-1], out_specs=specs[-1:])(*refs)
+def back_kernel(pair_ref, value_ref, w_pair_ref, w_value_ref, *refs):
+    total = jnp.dot(w_pair_ref[...], pair_ref[...], preferred_element_type=F32)
+    total = total + jnp.dot(w_value_ref[...], value_ref[...], preferred_element_type=F32)
+    for ref in refs[:-1]:
+        total = total + ref[...].astype(F32)
+    refs[-1][...] = total.astype(refs[-1].dtype)
 
 
 def back_call(pair, value, w_pair, w_value, rows, odd, addends, dtype):
     level_tokens = pair.shape[1]
-    tile = rows // 2 if rows % 256 == 0 else rows
-    steps = w_pair.shape[0] // tile // 2
-    first = steps if odd else 0
-    block = pl.BlockSpec((tile, level_tokens), lambda i: (i, 0))
-    specs = [pl.BlockSpec((tile, w.shape[1]), lambda i: (first + i, 0)) for w in (w_pair, w_value)]
-    vmem, hbm = (pl.BlockSpec(memory_space=space) for space in (pltpu.VMEM, pltpu.HBM))
-    anywhere = pl.BlockSpec(memory_space=pl.ANY)
-    return pl.pallas_call(
-        functools.partial(back_kernel, specs + [block] * (len(addends) + 1), (steps,)),
-        in_specs=[vmem, vmem, hbm, hbm] + [anywhere] * len(addends),
-        out_specs=anywhere,
-        out_shape=jax.ShapeDtypeStruct((steps * tile, level_tokens), dtype),
-        compiler_params=params(8),
+    units = w_pair.shape[0] // rows // 2
+    first = units if odd else 0
+    block = pl.BlockSpec((rows, level_tokens), lambda i: (i, 0))
+    return pl.pallas_call(
+        back_kernel,
+        grid=(units,),
+        in_specs=[
+            pl.BlockSpec(pair.shape, lambda i: (0, 0)),
+            pl.BlockSpec(value.shape, lambda i: (0, 0)),
+            pl.BlockSpec((rows, w_pair.shape[1]), lambda i: (first + i, 0)),
+            pl.BlockSpec((rows, w_value.shape[1]), lambda i: (first + i, 0)),
+        ]
+        + [block] * len(addends),
+        out_specs=block,
+        out_shape=jax.ShapeDtypeStruct((units * rows, level_tokens), dtype),
+        compiler_params=params(11),
         cost_estimate=cost(
-            2 * steps * tile * level_tokens * (pair.shape[0] + value.shape[0]),
-            2 * steps * tile * (pair.shape[0] + value.shape[0] + 3 * level_tokens),
+            2 * units * rows * level_tokens * (pair.shape[0] + value.shape[0]),
+            2 * units * rows * (pair.shape[0] + value.shape[0] + 3 * level_tokens),
         ),
     )(pair, value, w_pair, w_value, *addends)
 
@@ -248,7 +248,7 @@
             out_specs=pl.BlockSpec((rows, cols), lambda i, core_ref: (0, i)),
         ),
         out_shape=jax.ShapeDtypeStruct((rows, 2 * cols), BF),
-        compiler_params=params(16),
+        compiler_params=params(12),
     )(core.reshape(1), mine, other)
 
 
@@ -518,13 +518,13 @@
             if step == 1:
                 late_pair = late_messages(turned_pair, far_pair)
                 own_pair = messages(turned_pair, (0,), (1,))
+    out_value = place_call(core, ends_value[0], passed_value, cols, 0)
+    arrived, out_value = together(arrived, out_value)
     total = partial[n_mp - 1] + arrived.astype(F32)
 
     mine = lax.dynamic_slice_in_dim(total, core * own, own, 1)
     other = lax.dynamic_slice_in_dim(total, (1 - core) * own, own, 1).astype(BF)
     other = swap(other, 1)
-    grad_tokens = finish_call(place, mine, other, unit_rows, row_spread, norm_gain, rows)
-    grad_tokens, late_pair = together(grad_tokens, late_pair)
 
     here, there = {}, {}
     for r, (own_even, own_odd), early, late in zip(blocks_of_four, own_pair, early_pair, late_pair):
@@ -537,7 +537,8 @@
                 parts[r ^ bit].append(swap(sum(p.astype(F32) for p in parts.pop(r)).astype(BF), bit))
         bit //= 2
     out_query, out_key = gather_call(core, here[0], there[0], cols)
-    out_value = place_call(core, ends_value[0], passed_value, cols, 0)
+    other, out_query, out_key = together(other, out_query, out_key)
+    grad_tokens = finish_call(place, mine, other, unit_rows, row_spread, norm_gain, rows)
     return (grad_tokens, out_query, out_key, out_value)
 
 

time: 388 us -> 379 us (0.977)
  Pallas kernels: 117 us -> 95.2 us
  waiting for transfers between devices: 123 us -> 137 us
    pallas_call x8, Pallas kernels: 51.5 us -> 27.1 us  [back_call(): pl.pallas_call(back_kernel, grid=(units,), in_specs=[pl.BlockSpec(pair.sh...]
    ppermute x35, waiting for transfers between devices: 59.9 us -> 75.3 us  [swap(): return lax.ppermute(array, 'dp', [(i, i ^ bit) for i in range(n_dp)])]
    unnamed x134 -> x130, local copies, waits for them, and re-layouts: 31.9 us -> 33.1 us
  transfers between devices with their start and end apart: 41 -> 41, of which waited for: 13 -> 16; matrix products, arithmetic and copies ran while one was open for 13% -> 13% of each run, Pallas kernels for 28% -> 23%
where the time goes in v7:
time: 379 us; the launch traced here: 374 us
  waiting for transfers between devices  137 us (36%)
  Pallas kernels  95.2 us (25%)
  local copies, waits for them, and re-layouts  51.6 us (14%)
  starting transfers between devices  49.5 us (13%)
  matrix products  20.7 us (5%)
  other arithmetic  17.8 us (5%)
    ppermute x35, waiting for transfers between devices, swap(): return lax.ppermute(array, 'dp', [(i, i ^ bit) for i in range(n_dp)])  75.3 us
    ppermute x6, waiting for transfers between devices, ring_on(): return lax.ppermute(array, 'mp', ring_pairs)  61.6 us
    pallas_call x7, Pallas kernels, product_call(): pl.pallas_call(functools.partial(product_kernel, specs + [out] * 2, (coun...  39.7 us
    unnamed x130, local copies, waits for them, and re-layouts  33.1 us
    ppermute x35, starting transfers between devices, swap(): return lax.ppermute(array, 'dp', [(i, i ^ bit) for i in range(n_dp)])  32.4 us
    pallas_call x8, Pallas kernels, back_call(): pl.pallas_call(back_kernel, grid=(units,), in_specs=[pl.BlockSpec(pair.sh...  27.1 us
    ppermute x6, starting transfers between devices, ring_on(): return lax.ppermute(array, 'mp', ring_pairs)  17.1 us
    pallas_call x2, Pallas kernels, attention_call(): pl.pallas_call(kernel, grid=(tokens // PATCH,), in_specs=[pl.BlockSpec((P...  15.9 us
  transfers between devices with their start and end apart: 41, of which 16 were waited for; matrix products, arithmetic and copies ran while one was open for 13% of the time, Pallas kernels for 23%

profile of v7, /device:TPU:1, one launch (start us, length us, event | category | flops | bytes accessed | tf_op | source)
XLA Modules:
  0.0 373.6 jit_solution(1155956704703831099)
XLA Ops:
  17.3 28.9 %collective-permute-done = bf16[768,1024]{1,0:T(8,128)(2,1)} collective-permute-done((bf16[768,1024]{1,0:T(8,128)(2,1)S(1)}, bf16[768,1024]{1,0:T(8,128)(2,1)}, u32[]{:S(2)}, u32[]{:S(2)}) %collective-permute-start) | collective-permute-done | bytes 1572896 | tf_op jit(solution)/shard_map/ppermute | solution.py:300
  65.4 16.7 %collective-permute-done.3 = bf16[768,1024]{1,0:T(8,128)(2,1)S(1)} collective-permute-done((bf16[768,1024]{1,0:T(8,128)(2,1)}, bf16[768,1024]{1,0:T(8,128)(2,1)S(1)}, u32[]{:S(2)}, u32[]{:S(2)}) %collective-permute-start.3) | collective-permute-done | bytes 1572896 | tf_op jit(solution)/shard_map/ppermute | solution.py:300
  96.6 32.3 %collective-permute-done.12 = bf16[256,3072]{1,0:T(8,128)(2,1)S(1)} collective-permute-done((bf16[256,3072]{1,0:T(8,128)(2,1)S(1)}, bf16[256,3072]{1,0:T(8,128)(2,1)S(1)}, u32[]{:S(2)}, u32[]{:S(2)}) %collective-permute-start.12) | collective-permute-done | bytes 1572896 | tf_op jit(solution)/shard_map/ppermute | solution.py:318
  133.5 13.1 %fusion.4.qk_ref = f32[1024,1024]{1,0:T(8,128)S(1)} fusion(bf16[1024,6144]{1,0:T(8,128)(2,1)S(1)} %slice_dynamic-update-slice_fusion.normed_ref, bf16[6144,1024]{1,0:T(8,128)(2,1)S(1)} %constant_dynamic-update-slice_fusion.w_pair_ref), kind=kOutput, calls=%fused_computation.94 | convolution fusion | flops 12884901888 | bytes 29360128 | tf_op jit(solution)/shard_map/dot_general | solution.py:399
  146.6 5.9 %shard_map.113.turned_ref = bf16[512,1024]{1,0:T(8,128)(2,1)S(1)} custom-call(f32[1024,1024]{1,0:T(8,128)S(1)} %fusion.4.qk_ref, bf16[1024,512]{1,0:T(8,128)(2,1)S(1)} %constant_dynamic-update-slice_fusion.12.g_ref, f32[2,128]{1,0:T(2,128)S(1)} %pad_maximum_fusion.13.gains_ref), custom_call_target="tpu_custom_call" | custom-call | flops 178956976 | bytes 1398101 | tf_op jit(solution)/shard_map/pallas_call | solution.py:95
  155.9 6.5 %shard_map.116 = (bf16[1024,768]{1,0:T(8,128)(2,1)}, bf16[1024,768]{1,0:T(8,128)(2,1)}) custom-call(bf16[512,1024]{1,0:T(8,128)(2,1)S(1)} %shard_map.113.turned_ref, bf16[1024,6144]{1,0:T(8,128)(2,1)S(1)} %slice_dynamic-update-slice_fusion.normed_ref), custom_call_target="tpu_custom_call" | custom-call | flops 536870912 | bytes 1485482 | tf_op jit(solution)/shard_map/pallas_call | solution.py:138
  167.7 5.5 %collective-permute-done.19 = bf16[768,512]{1,0:T(8,128)(2,1)S(1)} collective-permute-done((bf16[768,512]{1,0:T(8,128)(2,1)S(1)}, bf16[768,512]{1,0:T(8,128)(2,1)S(1)}, u32[]{:S(2)}, u32[]{:S(2)}) %collective-permute-start.19) | collective-permute-done | bytes 786464 | tf_op jit(solution)/shard_map/ppermute | solution.py:300
  174.6 7.6 %convolution_convert_fusion.v_ref = bf16[1024,512]{1,0:T(8,128)(2,1)} fusion(bf16[1024,6144]{1,0:T(8,128)(2,1)S(1)} %slice_dynamic-update-slice_fusion.normed_ref, bf16[6144,512]{1,0:T(8,128)(2,1)S(1)} %constant_dynamic-update-slice_fusion.8.w_value_ref), kind=kOutput, calls=%fused_computation.14 | convolution fusion | flops 6442975232 | bytes 19922944 | tf_op jit(solution)/shard_map/dot_general | solution.py:446
  186.9 10.0 %shard_map.114.turned_ref = bf16[1024,1024]{1,0:T(8,128)(2,1)S(1)} custom-call(f32[1024,1024]{1,0:T(8,128)S(1)} %copy-done.15, bf16[1024,512]{1,0:T(8,128)(2,1)S(1)} %copy-done.19, bf16[1024,512]{1,0:T(8,128)(2,1)S(1)} %copy-done.33, f32[2,128]{1,0:T(2,128)S(1)} %pad_maximum_fusion.13.gains_ref), custom_call_target="tpu_custom_call" | custom-call | flops 178956976 | bytes 2097152 | tf_op jit(solution)/shard_map/pallas_call | solution.py:95
  198.1 3.2 shard_map.119
  201.3 3.2 shard_map.118
  207.0 4.8 %shard_map.117 = (bf16[512,768]{1,0:T(8,128)(2,1)}, bf16[512,768]{1,0:T(8,128)(2,1)}) custom-call(bf16[512,1024]{1,0:T(8,128)(2,1)S(1)} %copy-done.11, bf16[1024,6144]{1,0:T(8,128)(2,1)S(1)} %slice_dynamic-update-slice_fusion.normed_ref, bf16[1024,768]{1,0:T(8,128)(2,1)} %collective-permute-done.21.refs_0_.refs_2_, ...), custom_call_target="tpu_custom_call" | custom-call | flops 268435456 | bytes 1223338 | tf_op jit(solution)/shard_map/pallas_call | solution.py:138
  215.7 5.4 %shard_map.115 = (bf16[1024,768]{1,0:T(8,128)(2,1)}, bf16[1024,768]{1,0:T(8,128)(2,1)}) custom-call(bf16[1024,1024]{1,0:T(8,128)(2,1)S(1)} %shard_map.114.turned_ref, bf16[1024,6144]{1,0:T(8,128)(2,1)S(1)} %slice_dynamic-update-slice_fusion.normed_ref), custom_call_target="tpu_custom_call" | custom-call | flops 536870912 | bytes 1398101 | tf_op jit(solution)/shard_map/pallas_call | solution.py:138
  221.2 4.0 %shard_map.120 = bf16[3072,256]{1,0:T(8,128)(2,1)} custom-call(bf16[1024,256]{1,0:T(8,128)(2,1)S(1)} %pad_maximum_fusion.5.pair_ref, bf16[512,256]{1,0:T(8,128)(2,1)S(1)} %copy-done.22, bf16[6144,1024]{1,0:T(8,128)(2,1)S(1)} %constant_dynamic-update-slice_fusion.w_pair_ref, bf16[6144,512]{1,0:T(8,128)(2,1)S(1)} %constant_dynamic-update-slice_fusion.8.w_value_ref, ...), custom_call_target="tpu_custom_call" | custom-call | flops 402653184 | bytes 2359296 | tf_op jit(solution)/shard_map/pallas_call | solution.py:165
  229.6 3.4 collective-permute-done.25.refs_3_
  233.1 4.6 %copy-done.4 = bf16[1024,6144]{1,0:T(8,128)(2,1)S(1)} copy-done((bf16[1024,6144]{1,0:T(8,128)(2,1)S(1)}, bf16[1024,6144]{1,0:T(8,128)(2,1)}, u32[]{:S(2)}) %copy-start.4) | copy-done | bytes 12582936
  238.9 6.3 %shard_map.125 = (bf16[768,512]{1,0:T(8,128)(2,1)S(1)}, bf16[768,512]{1,0:T(8,128)(2,1)}) custom-call(bf16[512,1024]{1,0:T(8,128)(2,1)S(1)} %copy-done.12, bf16[1024,6144]{1,0:T(8,128)(2,1)S(1)} %copy-done.4, bf16[1024,768]{1,0:T(8,128)(2,1)} %collective-permute-done.22.refs_1_.refs_0_, bf16[512,768]{1,0:T(8,128)(2,1)} %collective-permute-done.26.refs_1_, ...), custom_call_target="tpu_custom_call" | custom-call | flops 268435456 | bytes 1485482 | tf_op jit(solution)/shard_map/pallas_call | solution.py:138
  248.9 3.2 shard_map.121
  252.7 3.1 shard_map.124
  256.0 3.9 %shard_map.123 = bf16[3072,256]{1,0:T(8,128)(2,1)} custom-call(bf16[1024,256]{1,0:T(8,128)(2,1)S(1)} %pad_maximum_fusion.7.pair_ref, bf16[512,256]{1,0:T(8,128)(2,1)S(1)} %pad_maximum_fusion.11.value_ref, bf16[6144,1024]{1,0:T(8,128)(2,1)S(1)} %copy-done.1, bf16[6144,512]{1,0:T(8,128)(2,1)S(1)} %copy-done.7), custom_call_target="tpu_custom_call" | custom-call | flops 402653184 | bytes 2359296 | tf_op jit(solution)/shard_map/pallas_call | solution.py:165
  259.9 5.4 %shard_map.122 = (bf16[1024,768]{1,0:T(8,128)(2,1)}, bf16[1024,768]{1,0:T(8,128)(2,1)}) custom-call(bf16[1024,1024]{1,0:T(8,128)(2,1)S(1)} %copy-done.9, bf16[1024,6144]{1,0:T(8,128)(2,1)S(1)} %copy-done.4), custom_call_target="tpu_custom_call" | custom-call | flops 536870912 | bytes 1398101 | tf_op jit(solution)/shard_map/pallas_call | solution.py:138
  266.8 3.6 add_convert_fusion.1
  274.9 3.1 collective-permute-start.34
  278.0 3.4 shard_map.127
  281.5 3.2 shard_map.126
  284.7 4.9 %shard_map.129 = (bf16[1024,768]{1,0:T(8,128)(2,1)S(1)}, bf16[1024,768]{1,0:T(8,128)(2,1)S(1)}) custom-call(bf16[1024,1024]{1,0:T(8,128)(2,1)S(1)} %copy-done.9, bf16[1024,6144]{1,0:T(8,128)(2,1)S(1)} %bitcast.12), custom_call_target="tpu_custom_call" | custom-call | flops 536870912 | bytes 1398101 | tf_op jit(solution)/shard_map/pallas_call | solution.py:138
  289.6 6.4 %shard_map.128 = (bf16[1024,768]{1,0:T(8,128)(2,1)S(1)}, bf16[1024,768]{1,0:T(8,128)(2,1)S(1)}) custom-call(bf16[1024,1024]{1,0:T(8,128)(2,1)S(1)} %copy-done.9, bf16[1024,6144]{1,0:T(8,128)(2,1)S(1)} %bitcast.12, bf16[1024,768]{1,0:T(8,128)(2,1)} %collective-permute-done.28.refs_0_, bf16[1024,768]{1,0:T(8,128)(2,1)S(1)} %copy-done.24), custom_call_target="tpu_custom_call" | custom-call | flops 536870912 | bytes 1922389 | tf_op jit(solution)/shard_map/pallas_call | solution.py:138
  296.0 11.6 %collective-permute-done.32.refs_1_ = bf16[1024,768]{1,0:T(8,128)(2,1)S(1)} collective-permute-done((bf16[1024,768]{1,0:T(8,128)(2,1)}, bf16[1024,768]{1,0:T(8,128)(2,1)S(1)}, u32[]{:S(2)}, u32[]{:S(2)}) %collective-permute-start.32) | collective-permute-done | bytes 1572896 | tf_op jit(solution)/shard_map/ppermute | solution.py:300
  315.4 3.1 collective-permute-start.35
  325.0 27.0 %collective-permute-done.35 = bf16[3072,256]{1,0:T(8,128)(2,1)} collective-permute-done((bf16[3072,256]{1,0:T(8,128)(2,1)}, bf16[3072,256]{1,0:T(8,128)(2,1)}, u32[]{:S(2)}, u32[]{:S(2)}) %collective-permute-start.35) | collective-permute-done | bytes 1572896 | tf_op jit(solution)/shard_map/ppermute | solution.py:318
  361.3 6.8 %shard_map.131 = (bf16[768,1024]{1,0:T(8,128)(2,1)}, bf16[768,1024]{1,0:T(8,128)(2,1)}) custom-call(s32[1]{0:T(128)} %bitcast.3.core_ref, bf16[1024,768]{1,0:T(8,128)(2,1)S(1)} %copy-done.32, bf16[1024,768]{1,0:T(8,128)(2,1)S(1)} %copy-done.26, bf16[1024,768]{1,0:T(8,128)(2,1)} %collective-permute-done.38.refs_2_, ...), custom_call_target="tpu_custom_call" | custom-call | tf_op jit(solution)/shard_map/pallas_call | solution.py:214
  370.0 3.4 shard_map.132
  (259 shorter events, 118.3 us)
Async XLA Ops:
  8.8 37.5 %collective-permute-start = (bf16[768,1024]{1,0:T(8,128)(2,1)S(1)}, bf16[768,1024]{1,0:T(8,128)(2,1)}, u32[]{:S(2)}, u32[]{:S(2)}) collective-permute-start(bf16[768,1024]{1,0:T(8,128)(2,1)S(1)} %pad_maximum_fusion), channel_id=1, source_target_pairs={{0,8},{4,12},{8,0},{12,4},{16,24},{20,28},{24,16},{28,20},{1,9},{5... | collective-permute-start | bytes 4718600 | tf_op jit(solution)/shard_map/ppermute | solution.py:300
  11.5 35.7 %collective-permute-start.1 = (bf16[768,1024]{1,0:T(8,128)(2,1)S(1)}, bf16[768,1024]{1,0:T(8,128)(2,1)}, u32[]{:S(2)}, u32[]{:S(2)}) collective-permute-start(bf16[768,1024]{1,0:T(8,128)(2,1)S(1)} %pad_maximum_fusion), channel_id=1, source_target_pairs={{0,16},{4,20},{8,24},{12,28},{16,0},{20,4},{24,8},{28,12},{1,17},{... | collective-permute-start | bytes 4718600 | tf_op jit(solution)/shard_map/ppermute | solution.py:300
  12.7 34.5 %collective-permute-start.2 = (bf16[768,1024]{1,0:T(8,128)(2,1)}, bf16[768,1024]{1,0:T(8,128)(2,1)}, u32[]{:S(2)}, u32[]{:S(2)}) collective-permute-start(bf16[768,1024]{1,0:T(8,128)(2,1)} %pad_maximum_fusion.1), channel_id=1, source_target_pairs={{0,4},{4,0},{8,12},{12,8},{16,20},{20,16},{24,28},{28,24},{1,5},{5... | collective-permute-start | bytes 4718600 | tf_op jit(solution)/shard_map/ppermute | solution.py:300
  14.7 36.5 %collective-permute-start.7 = (bf16[256,3072]{1,0:T(8,128)(2,1)}, bf16[256,3072]{1,0:T(8,128)(2,1)}, u32[]{:S(2)}, u32[]{:S(2)}) collective-permute-start(bf16[256,3072]{1,0:T(8,128)(2,1)} %pad_maximum_fusion.2), channel_id=1, source_target_pairs={{0,2},{2,3},{3,1},{1,0},{4,6},{6,7},{7,5},{5,4},{8,10},{10,11},{11... | collective-permute-start | bytes 4718600 | tf_op jit(solution)/shard_map/ppermute | solution.py:318
  17.0 38.0 %collective-permute-start.6 = (bf16[256,3072]{1,0:T(8,128)(2,1)}, bf16[256,3072]{1,0:T(8,128)(2,1)}, u32[]{:S(2)}, u32[]{:S(2)}) collective-permute-start(bf16[256,3072]{1,0:T(8,128)(2,1)} %pad_maximum_fusion.2), channel_id=1, source_target_pairs={{0,4},{4,0},{8,12},{12,8},{16,20},{20,16},{24,28},{28,24},{1,5},{5... | collective-permute-start | bytes 4718600 | tf_op jit(solution)/shard_map/ppermute | solution.py:300
  47.2 34.9 %collective-permute-start.3 = (bf16[768,1024]{1,0:T(8,128)(2,1)}, bf16[768,1024]{1,0:T(8,128)(2,1)S(1)}, u32[]{:S(2)}, u32[]{:S(2)}) collective-permute-start(bf16[768,1024]{1,0:T(8,128)(2,1)} %collective-permute-done.2), channel_id=1, source_target_pairs={{0,8},{4,12},{8,0},{12,4},{16,24},{20,28},{24,16},{28,20},{1,9},{5... | collective-permute-start | bytes 4718600 | tf_op jit(solution)/shard_map/ppermute | solution.py:300
  47.6 34.9 %collective-permute-start.4 = (bf16[768,1024]{1,0:T(8,128)(2,1)}, bf16[768,1024]{1,0:T(8,128)(2,1)S(1)}, u32[]{:S(2)}, u32[]{:S(2)}) collective-permute-start(bf16[768,1024]{1,0:T(8,128)(2,1)} %collective-permute-done.2), channel_id=1, source_target_pairs={{0,16},{4,20},{8,24},{12,28},{16,0},{20,4},{24,8},{28,12},{1,17},{... | collective-permute-start | bytes 4718600 | tf_op jit(solution)/shard_map/ppermute | solution.py:300
  51.2 12.4 %collective-permute-start.8 = (bf16[256,3072]{1,0:T(8,128)(2,1)}, bf16[256,3072]{1,0:T(8,128)(2,1)S(1)}, u32[]{:S(2)}, u32[]{:S(2)}) collective-permute-start(bf16[256,3072]{1,0:T(8,128)(2,1)} %collective-permute-done.7), channel_id=1, source_target_pairs={{0,4},{4,0},{8,12},{12,8},{16,20},{20,16},{24,28},{28,24},{1,5},{5... | collective-permute-start | bytes 4718600 | tf_op jit(solution)/shard_map/ppermute | solution.py:300
  52.5 38.8 %collective-permute-start.10 = (bf16[256,3072]{1,0:T(8,128)(2,1)}, bf16[256,3072]{1,0:T(8,128)(2,1)S(1)}, u32[]{:S(2)}, u32[]{:S(2)}) collective-permute-start(bf16[256,3072]{1,0:T(8,128)(2,1)} %collective-permute-done.7), channel_id=1, source_target_pairs={{0,2},{2,3},{3,1},{1,0},{4,6},{6,7},{7,5},{5,4},{8,10},{10,11},{11... | collective-permute-start | bytes 4718600 | tf_op jit(solution)/shard_map/ppermute | solution.py:318
  82.5 47.8 %collective-permute-start.14 = (bf16[768,1024]{1,0:T(8,128)(2,1)}, bf16[768,1024]{1,0:T(8,128)(2,1)S(1)}, u32[]{:S(2)}, u32[]{:S(2)}) collective-permute-start(bf16[768,1024]{1,0:T(8,128)(2,1)} %collective-permute-done), channel_id=1, source_target_pairs={{0,16},{4,20},{8,24},{12,28},{16,0},{20,4},{24,8},{28,12},{1,17},{... | collective-permute-start | bytes 4718600 | tf_op jit(solution)/shard_map/ppermute | solution.py:300
  83.5 48.7 %collective-permute-start.15 = (bf16[768,1024]{1,0:T(8,128)(2,1)S(1)}, bf16[768,1024]{1,0:T(8,128)(2,1)S(1)}, u32[]{:S(2)}, u32[]{:S(2)}) collective-permute-start(bf16[768,1024]{1,0:T(8,128)(2,1)S(1)} %collective-permute-done.4), channel_id=1, source_target_pairs={{0,8},{4,12},{8,0},{12,4},{16,24},{20,28},{24,16},{28,20},{1,9},{5... | collective-permute-start | bytes 4718600 | tf_op jit(solution)/shard_map/ppermute | solution.py:300
  84.8 10.9 %collective-permute-start.9 = (bf16[768,512]{1,0:T(8,128)(2,1)S(1)}, bf16[768,512]{1,0:T(8,128)(2,1)S(1)}, u32[]{:S(2)}, u32[]{:S(2)}) collective-permute-start(bf16[768,512]{1,0:T(8,128)(2,1)S(1)} %get-tuple-element.207), channel_id=1, source_target_pairs={{0,4},{4,0},{8,12},{12,8},{16,20},{20,16},{24,28},{28,24},{1,5},{5... | collective-permute-start | bytes 2359304 | tf_op jit(solution)/shard_map/ppermute | solution.py:300
  92.8 36.2 %collective-permute-start.12 = (bf16[256,3072]{1,0:T(8,128)(2,1)S(1)}, bf16[256,3072]{1,0:T(8,128)(2,1)S(1)}, u32[]{:S(2)}, u32[]{:S(2)}) collective-permute-start(bf16[256,3072]{1,0:T(8,128)(2,1)S(1)} %collective-permute-done.10), channel_id=1, source_target_pairs={{0,2},{2,3},{3,1},{1,0},{4,6},{6,7},{7,5},{5,4},{8,10},{10,11},{11... | collective-permute-start | bytes 4718600 | tf_op jit(solution)/shard_map/ppermute | solution.py:318
  96.0 56.5 %collective-permute-start.17 = (bf16[1536,512]{1,0:T(8,128)(2,1)S(1)}, bf16[1536,512]{1,0:T(8,128)(2,1)}, u32[]{:S(2)}, u32[]{:S(2)}) collective-permute-start(bf16[1536,512]{1,0:T(8,128)(2,1)S(1)} %pad_maximum_fusion.3), channel_id=1, source_target_pairs={{0,8},{4,12},{8,0},{12,4},{16,24},{20,28},{24,16},{28,20},{1,9},{5... | collective-permute-start | bytes 4718600 | tf_op jit(solution)/shard_map/ppermute | solution.py:300
  96.4 56.1 %collective-permute-start.18 = (bf16[1536,512]{1,0:T(8,128)(2,1)S(1)}, bf16[1536,512]{1,0:T(8,128)(2,1)}, u32[]{:S(2)}, u32[]{:S(2)}) collective-permute-start(bf16[1536,512]{1,0:T(8,128)(2,1)S(1)} %pad_maximum_fusion.3), channel_id=1, source_target_pairs={{0,16},{4,20},{8,24},{12,28},{16,0},{20,4},{24,8},{28,12},{1,17},{... | collective-permute-start | bytes 4718600 | tf_op jit(solution)/shard_map/ppermute | solution.py:300
  155.3 17.9 %collective-permute-start.19 = (bf16[768,512]{1,0:T(8,128)(2,1)S(1)}, bf16[768,512]{1,0:T(8,128)(2,1)S(1)}, u32[]{:S(2)}, u32[]{:S(2)}) collective-permute-start(bf16[768,512]{1,0:T(8,128)(2,1)S(1)} %slice.75), channel_id=1, source_target_pairs={{0,16},{4,20},{8,24},{12,28},{16,0},{20,4},{24,8},{28,12},{1,17},{... | collective-permute-start | bytes 2359304 | tf_op jit(solution)/shard_map/ppermute | solution.py:300
  155.6 18.9 %collective-permute-start.20 = (bf16[768,512]{1,0:T(8,128)(2,1)S(1)}, bf16[768,512]{1,0:T(8,128)(2,1)S(1)}, u32[]{:S(2)}, u32[]{:S(2)}) collective-permute-start(bf16[768,512]{1,0:T(8,128)(2,1)S(1)} %slice.76), channel_id=1, source_target_pairs={{0,8},{4,12},{8,0},{12,4},{16,24},{20,28},{24,16},{28,20},{1,9},{5... | collective-permute-start | bytes 2359304 | tf_op jit(solution)/shard_map/ppermute | solution.py:300
  162.4 44.6 %collective-permute-start.21 = (bf16[1024,768]{1,0:T(8,128)(2,1)}, bf16[1024,768]{1,0:T(8,128)(2,1)}, u32[]{:S(2)}, u32[]{:S(2)}) collective-permute-start(bf16[1024,768]{1,0:T(8,128)(2,1)} %get-tuple-element.126), channel_id=1, source_target_pairs={{0,16},{4,20},{8,24},{12,28},{16,0},{20,4},{24,8},{28,12},{1,17},{... | collective-permute-start | bytes 4718600 | tf_op jit(solution)/shard_map/ppermute | solution.py:300
  163.6 43.3 %collective-permute-start.22 = (bf16[1024,768]{1,0:T(8,128)(2,1)}, bf16[1024,768]{1,0:T(8,128)(2,1)}, u32[]{:S(2)}, u32[]{:S(2)}) collective-permute-start(bf16[1024,768]{1,0:T(8,128)(2,1)} %get-tuple-element.127), channel_id=1, source_target_pairs={{0,8},{4,12},{8,0},{12,4},{16,24},{20,28},{24,16},{28,20},{1,9},{5... | collective-permute-start | bytes 4718600 | tf_op jit(solution)/shard_map/ppermute | solution.py:300
  214.2 18.9 %collective-permute-start.25 = (bf16[512,768]{1,0:T(8,128)(2,1)}, bf16[512,768]{1,0:T(8,128)(2,1)}, u32[]{:S(2)}, u32[]{:S(2)}) collective-permute-start(bf16[512,768]{1,0:T(8,128)(2,1)} %get-tuple-element.137), channel_id=1, source_target_pairs={{0,8},{4,12},{8,0},{12,4},{16,24},{20,28},{24,16},{28,20},{1,9},{5... | collective-permute-start | bytes 2359304 | tf_op jit(solution)/shard_map/ppermute | solution.py:300
  214.5 18.6 %collective-permute-start.26 = (bf16[512,768]{1,0:T(8,128)(2,1)}, bf16[512,768]{1,0:T(8,128)(2,1)}, u32[]{:S(2)}, u32[]{:S(2)}) collective-permute-start(bf16[512,768]{1,0:T(8,128)(2,1)} %get-tuple-element.138), channel_id=1, source_target_pairs={{0,16},{4,20},{8,24},{12,28},{16,0},{20,4},{24,8},{28,12},{1,17},{... | collective-permute-start | bytes 2359304 | tf_op jit(solution)/shard_map/ppermute | solution.py:300
  225.2 41.6 %collective-permute-start.27 = (bf16[1024,768]{1,0:T(8,128)(2,1)}, bf16[1024,768]{1,0:T(8,128)(2,1)S(1)}, u32[]{:S(2)}, u32[]{:S(2)}) collective-permute-start(bf16[1024,768]{1,0:T(8,128)(2,1)} %get-tuple-element.144), channel_id=1, source_target_pairs={{0,8},{4,12},{8,0},{12,4},{16,24},{20,28},{24,16},{28,20},{1,9},{5... | collective-permute-start | bytes 4718600 | tf_op jit(solution)/shard_map/ppermute | solution.py:300
  226.3 40.5 %collective-permute-start.28 = (bf16[1024,768]{1,0:T(8,128)(2,1)}, bf16[1024,768]{1,0:T(8,128)(2,1)}, u32[]{:S(2)}, u32[]{:S(2)}) collective-permute-start(bf16[1024,768]{1,0:T(8,128)(2,1)} %get-tuple-element.145), channel_id=1, source_target_pairs={{0,16},{4,20},{8,24},{12,28},{16,0},{20,4},{24,8},{28,12},{1,17},{... | collective-permute-start | bytes 4718600 | tf_op jit(solution)/shard_map/ppermute | solution.py:300
  226.6 40.2 %collective-permute-start.29 = (bf16[3072,256]{1,0:T(8,128)(2,1)}, bf16[3072,256]{1,0:T(8,128)(2,1)}, u32[]{:S(2)}, u32[]{:S(2)}) collective-permute-start(bf16[3072,256]{1,0:T(8,128)(2,1)} %shard_map.120), channel_id=1, source_target_pairs={{0,2},{2,3},{3,1},{1,0},{4,6},{6,7},{7,5},{5,4},{8,10},{10,11},{11... | collective-permute-start | bytes 4718600 | tf_op jit(solution)/shard_map/ppermute | solution.py:318
  271.9 35.8 %collective-permute-start.32 = (bf16[1024,768]{1,0:T(8,128)(2,1)}, bf16[1024,768]{1,0:T(8,128)(2,1)S(1)}, u32[]{:S(2)}, u32[]{:S(2)}) collective-permute-start(bf16[1024,768]{1,0:T(8,128)(2,1)} %get-tuple-element.168), channel_id=1, source_target_pairs={{0,8},{4,12},{8,0},{12,4},{16,24},{20,28},{24,16},{28,20},{1,9},{5... | collective-permute-start | bytes 4718600 | tf_op jit(solution)/shard_map/ppermute | solution.py:300
  273.0 37.4 %collective-permute-start.33 = (bf16[1024,768]{1,0:T(8,128)(2,1)}, bf16[1024,768]{1,0:T(8,128)(2,1)S(1)}, u32[]{:S(2)}, u32[]{:S(2)}) collective-permute-start(bf16[1024,768]{1,0:T(8,128)(2,1)} %get-tuple-element.169), channel_id=1, source_target_pairs={{0,20},{4,16},{8,28},{12,24},{16,4},{20,0},{24,12},{28,8},{1,21},{... | collective-permute-start | bytes 4718600 | tf_op jit(solution)/shard_map/ppermute | solution.py:300
  274.9 37.4 %collective-permute-start.34 = (bf16[3072,256]{1,0:T(8,128)(2,1)}, bf16[3072,256]{1,0:T(8,128)(2,1)}, u32[]{:S(2)}, u32[]{:S(2)}) collective-permute-start(bf16[3072,256]{1,0:T(8,128)(2,1)} %add_convert_fusion.1), channel_id=1, source_target_pairs={{0,2},{2,3},{3,1},{1,0},{4,6},{6,7},{7,5},{5,4},{8,10},{10,11},{11... | collective-permute-start | bytes 4718600 | tf_op jit(solution)/shard_map/ppermute | solution.py:318
  315.4 36.6 %collective-permute-start.35 = (bf16[3072,256]{1,0:T(8,128)(2,1)}, bf16[3072,256]{1,0:T(8,128)(2,1)}, u32[]{:S(2)}, u32[]{:S(2)}) collective-permute-start(bf16[3072,256]{1,0:T(8,128)(2,1)} %add_convert_fusion), channel_id=1, source_target_pairs={{0,2},{2,3},{3,1},{1,0},{4,6},{6,7},{7,5},{5,4},{8,10},{10,11},{11... | collective-permute-start | bytes 4718600 | tf_op jit(solution)/shard_map/ppermute | solution.py:318
  319.3 37.7 %collective-permute-start.38 = (bf16[1024,768]{1,0:T(8,128)(2,1)}, bf16[1024,768]{1,0:T(8,128)(2,1)}, u32[]{:S(2)}, u32[]{:S(2)}) collective-permute-start(bf16[1024,768]{1,0:T(8,128)(2,1)} %copy-done.40), channel_id=1, source_target_pairs={{0,16},{4,20},{8,24},{12,28},{16,0},{20,4},{24,8},{28,12},{1,17},{... | collective-permute-start | bytes 4718600 | tf_op jit(solution)/shard_map/ppermute | solution.py:300
  319.5 37.5 %collective-permute-start.39 = (bf16[1024,768]{1,0:T(8,128)(2,1)}, bf16[1024,768]{1,0:T(8,128)(2,1)}, u32[]{:S(2)}, u32[]{:S(2)}) collective-permute-start(bf16[1024,768]{1,0:T(8,128)(2,1)} %copy-done.38), channel_id=1, source_target_pairs={{0,4},{4,0},{8,12},{12,8},{16,20},{20,16},{24,28},{28,24},{1,5},{5... | collective-permute-start | bytes 4718600 | tf_op jit(solution)/shard_map/ppermute | solution.py:300
  319.8 37.2 %collective-permute-start.40 = (bf16[1024,768]{1,0:T(8,128)(2,1)}, bf16[1024,768]{1,0:T(8,128)(2,1)}, u32[]{:S(2)}, u32[]{:S(2)}) collective-permute-start(bf16[1024,768]{1,0:T(8,128)(2,1)} %copy-done.39), channel_id=1, source_target_pairs={{0,12},{4,8},{8,4},{12,0},{16,28},{20,24},{24,20},{28,16},{1,13},{... | collective-permute-start | bytes 4718600 | tf_op jit(solution)/shard_map/ppermute | solution.py:300
  355.4 12.8 %collective-permute-start.37 = (bf16[3072,128]{1,0:T(8,128)(2,1)S(1)}, bf16[3072,128]{1,0:T(8,128)(2,1)S(1)}, u32[]{:S(2)}, u32[]{:S(2)}) collective-permute-start(bf16[3072,128]{1,0:T(8,128)(2,1)S(1)} %dynamic-slice_convert_fusion), channel_id=1, source_target_pairs={{0,4},{4,0},{8,12},{12,8},{16,20},{20,16},{24,28},{28,24},{1,5},{5... | collective-permute-start | bytes 2359304 | tf_op jit(solution)/shard_map/ppermute | solution.py:300
  (67 other events, 793.5 us)

commit v8 on v7

--- a/solution.py
+++ b/solution.py
@@ -104,18 +104,14 @@
     )(*arrays, gains)
 
 
-def product_kernel(specs, grid, n_add, turn, turned_ref, normed_ref, *refs):
-    def body(*blocks):
-        turned = turned_ref[...]
-        for side in range(2):
-            total = jnp.dot(turned, blocks[side][...], preferred_element_type=F32)
-            for block in blocks[2 + side * n_add : 2 + (side + 1) * n_add]:
-                total = total + block[...].astype(F32)
-            blocks[side - 2][...] = (total.T if turn else total).astype(BF)
-
-    pltpu.emit_pipeline(body, grid=grid, in_specs=specs[:-2], out_specs=specs[-2:])(
-        normed_ref, normed_ref, *refs
-    )
+def product_kernel(n_add, turn, turned_ref, *refs):
+    turned = turned_ref[...]
+    outs = refs[-2:]
+    for side in range(2):
+        total = jnp.dot(turned, refs[side][...], preferred_element_type=F32)
+        for ref in refs[2 + side * n_add : 2 + (side + 1) * n_add]:
+            total = total + ref[...].astype(F32)
+        outs[side][...] = (total.T if turn else total).astype(BF)
 
 
 def product_call(turned, normed, rows, units, addends=((), ()), turn=False):
@@ -134,19 +130,22 @@
     else:
         shape, out = (count * columns, rows), pl.BlockSpec((columns, tile), lambda u, i: (u, i))
     addends = [*addends[0], *addends[1]]
-    specs = [side(chosen[0], chosen[-1]) for chosen in units] + [added(which) for _, which in addends]
-    return pl.pallas_call(
-        functools.partial(product_kernel, specs + [out] * 2, (count, steps), n_add, turn),
-        in_specs=[pl.BlockSpec(memory_space=pltpu.VMEM), pl.BlockSpec(memory_space=pltpu.HBM)]
-        + [pl.BlockSpec(memory_space=pl.ANY)] * len(addends),
-        out_specs=[pl.BlockSpec(memory_space=pl.ANY)] * 2,
+    return pl.pallas_call(
+        functools.partial(product_kernel, n_add, turn),
+        grid=(count, steps),
+        in_specs=[
+            pl.BlockSpec((columns, tokens), lambda u, i: (0, 0)),
+            *[side(chosen[0], chosen[-1]) for chosen in units],
+            *[added(which) for _, which in addends],
+        ],
+        out_specs=[out] * 2,
         out_shape=[jax.ShapeDtypeStruct(shape, BF)] * 2,
-        compiler_params=params(10),
+        compiler_params=params(14),
         cost_estimate=cost(
             4 * count * columns * tokens * rows,
             2 * columns * tokens + 4 * count * tokens * rows + (4 + 4 * n_add) * columns * rows,
         ),
-    )(turned, normed, *[array for array, _ in addends])
+    )(turned, normed, normed, *[array for array, _ in addends])
 
 
 def back_kernel(pair_ref, value_ref, w_pair_ref, w_value_ref, *refs):
@@ -220,7 +219,7 @@
             out_specs=[pl.BlockSpec((tile, cols), lambda h, i, core_ref: (i, h))] * (columns // cols),
         ),
         out_shape=[jax.ShapeDtypeStruct((rows, 2 * cols), BF)] * (columns // cols),
-        compiler_params=params(12),
+        compiler_params=params(40),
     )(core.reshape(1), *mine, *other)
 
 
@@ -519,17 +518,19 @@
                 late_pair = late_messages(turned_pair, far_pair)
                 own_pair = messages(turned_pair, (0,), (1,))
     out_value = place_call(core, ends_value[0], passed_value, cols, 0)
-    arrived, out_value = together(arrived, out_value)
+    here, there = {}, {}
+    for r, (own_even, own_odd), (even_x, odd_y) in zip(blocks_of_four, own_pair, early_pair):
+        here[r] = (own_even.astype(F32) + even_x.astype(F32)).astype(BF)
+        there[r] = (own_odd.astype(F32) + odd_y.astype(F32)).astype(BF)
+    arrived, out_value, here, there = together(arrived, out_value, here, there)
     total = partial[n_mp - 1] + arrived.astype(F32)
 
     mine = lax.dynamic_slice_in_dim(total, core * own, own, 1)
     other = lax.dynamic_slice_in_dim(total, (1 - core) * own, own, 1).astype(BF)
     other = swap(other, 1)
 
-    here, there = {}, {}
-    for r, (own_even, own_odd), early, late in zip(blocks_of_four, own_pair, early_pair, late_pair):
-        here[r] = [own_even, early[0], late[1]]
-        there[r] = [own_odd, early[1], late[0]]
+    for r, (odd_x, even_y) in zip(blocks_of_four, late_pair):
+        here[r], there[r] = [here[r], even_y], [there[r], odd_x]
     bit = n_dp // 2
     while bit >= 8:
         for parts in (here, there):

time: 379 us -> 377 us (level)
  other arithmetic: 17.8 us -> 24.4 us
  waiting for transfers between devices: 137 us -> 132 us
    convert_element_type x0 -> x2, other arithmetic: none -> 6.81 us  [the longest x1 3.41 us: per_device(): there[r] = (own_odd.astype(F32) + odd_y.astype(F32)).astype(BF)]
    unnamed x130 -> x126, local copies, waits for them, and re-layouts: 33.1 us -> 33 us
  transfers between devices with their start and end apart: 41 -> 41, of which waited for: 16 -> 18; matrix products, arithmetic and copies ran while one was open for 13% -> 15% of each run, Pallas kernels for 23% -> 23%
where the time goes in v8:
time: 377 us; the launch traced here: 371 us
  waiting for transfers between devices  132 us (35%)
  Pallas kernels  92.6 us (25%)
  local copies, waits for them, and re-layouts  51.5 us (14%)
  starting transfers between devices  48.6 us (13%)
  other arithmetic  24.4 us (6%)
  matrix products  20.7 us (5%)
    ppermute x35, waiting for transfers between devices, swap(): return lax.ppermute(array, 'dp', [(i, i ^ bit) for i in range(n_dp)])  73.6 us
    ppermute x6, waiting for transfers between devices, ring_on(): return lax.ppermute(array, 'mp', ring_pairs)  58 us
    pallas_call x7, Pallas kernels, product_call(): pl.pallas_call(functools.partial(product_kernel, n_add, turn), grid=(coun...  38.5 us
    unnamed x126, local copies, waits for them, and re-layouts  33 us
    ppermute x35, starting transfers between devices, swap(): return lax.ppermute(array, 'dp', [(i, i ^ bit) for i in range(n_dp)])  31.8 us
    pallas_call x8, Pallas kernels, back_call(): pl.pallas_call(back_kernel, grid=(units,), in_specs=[pl.BlockSpec(pair.sh...  26.1 us
    ppermute x6, starting transfers between devices, ring_on(): return lax.ppermute(array, 'mp', ring_pairs)  16.8 us
    pallas_call x2, Pallas kernels, attention_call(): pl.pallas_call(kernel, grid=(tokens // PATCH,), in_specs=[pl.BlockSpec((P...  16 us
  transfers between devices with their start and end apart: 41, of which 18 were waited for; matrix products, arithmetic and copies ran while one was open for 15% of the time, Pallas kernels for 23%

profile of v8, /device:TPU:1, one launch (start us, length us, event | category | flops | bytes accessed | tf_op | source)
XLA Modules:
  0.0 371.1 jit_solution(6134028946495918737)
XLA Ops:
  17.3 28.9 %collective-permute-done = bf16[768,1024]{1,0:T(8,128)(2,1)} collective-permute-done((bf16[768,1024]{1,0:T(8,128)(2,1)S(1)}, bf16[768,1024]{1,0:T(8,128)(2,1)}, u32[]{:S(2)}, u32[]{:S(2)}) %collective-permute-start) | collective-permute-done | bytes 1572896 | tf_op jit(solution)/shard_map/ppermute | solution.py:299
  65.4 16.7 %collective-permute-done.3 = bf16[768,1024]{1,0:T(8,128)(2,1)S(1)} collective-permute-done((bf16[768,1024]{1,0:T(8,128)(2,1)}, bf16[768,1024]{1,0:T(8,128)(2,1)S(1)}, u32[]{:S(2)}, u32[]{:S(2)}) %collective-permute-start.3) | collective-permute-done | bytes 1572896 | tf_op jit(solution)/shard_map/ppermute | solution.py:299
  96.4 32.2 %collective-permute-done.12 = bf16[256,3072]{1,0:T(8,128)(2,1)S(1)} collective-permute-done((bf16[256,3072]{1,0:T(8,128)(2,1)S(1)}, bf16[256,3072]{1,0:T(8,128)(2,1)S(1)}, u32[]{:S(2)}, u32[]{:S(2)}) %collective-permute-start.12) | collective-permute-done | bytes 1572896 | tf_op jit(solution)/shard_map/ppermute | solution.py:317
  133.1 13.1 %fusion.4.qk_ref = f32[1024,1024]{1,0:T(8,128)S(1)} fusion(bf16[1024,6144]{1,0:T(8,128)(2,1)S(1)} %slice_dynamic-update-slice_fusion.refs_0_.refs_1_, bf16[6144,1024]{1,0:T(8,128)(2,1)S(1)} %constant_dynamic-update-slice_fusion.w_pair_ref), kind=kOutput, calls=%fused_computation.96 | convolution fusion | flops 12884901888 | bytes 29360128 | tf_op jit(solution)/shard_map/dot_general | solution.py:398
  146.3 5.9 %shard_map.113.turned_ref = bf16[512,1024]{1,0:T(8,128)(2,1)S(1)} custom-call(f32[1024,1024]{1,0:T(8,128)S(1)} %fusion.4.qk_ref, bf16[1024,512]{1,0:T(8,128)(2,1)S(1)} %constant_dynamic-update-slice_fusion.12.g_ref, f32[2,128]{1,0:T(2,128)S(1)} %pad_maximum_fusion.13.gains_ref), custom_call_target="tpu_custom_call" | custom-call | flops 178956976 | bytes 1398101 | tf_op jit(solution)/shard_map/pallas_call | solution.py:95
  155.6 6.1 %shard_map.116 = (bf16[1024,768]{1,0:T(8,128)(2,1)}, bf16[1024,768]{1,0:T(8,128)(2,1)}) custom-call(bf16[512,1024]{1,0:T(8,128)(2,1)S(1)} %shard_map.113.turned_ref, bf16[1024,6144]{1,0:T(8,128)(2,1)S(1)} %slice_dynamic-update-slice_fusion.refs_0_.refs_1_, bf16[1024,6144]{1,0:T(8,128)(2,1)S(1)} %slice_dynamic-update-slice_fusion.refs_0_.refs_1_), custom_call_target="tpu_custom_call" | custom-call | flops 536870912 | bytes 1485482 | tf_op jit(solution)/shard_map/pallas_call | solution.py:133
  167.1 5.5 %collective-permute-done.19 = bf16[768,512]{1,0:T(8,128)(2,1)S(1)} collective-permute-done((bf16[768,512]{1,0:T(8,128)(2,1)S(1)}, bf16[768,512]{1,0:T(8,128)(2,1)S(1)}, u32[]{:S(2)}, u32[]{:S(2)}) %collective-permute-start.19) | collective-permute-done | bytes 786464 | tf_op jit(solution)/shard_map/ppermute | solution.py:299
  174.0 7.6 %convolution_convert_fusion.v_ref = bf16[1024,512]{1,0:T(8,128)(2,1)} fusion(bf16[1024,6144]{1,0:T(8,128)(2,1)S(1)} %slice_dynamic-update-slice_fusion.refs_0_.refs_1_, bf16[6144,512]{1,0:T(8,128)(2,1)S(1)} %constant_dynamic-update-slice_fusion.8.w_value_ref), kind=kOutput, calls=%fused_computation.16 | convolution fusion | flops 6442975232 | bytes 19922944 | tf_op jit(solution)/shard_map/dot_general | solution.py:445
  186.2 10.0 %shard_map.114.turned_ref = bf16[1024,1024]{1,0:T(8,128)(2,1)S(1)} custom-call(f32[1024,1024]{1,0:T(8,128)S(1)} %copy-done.15, bf16[1024,512]{1,0:T(8,128)(2,1)S(1)} %copy-done.19, bf16[1024,512]{1,0:T(8,128)(2,1)S(1)} %copy-done.30, f32[2,128]{1,0:T(2,128)S(1)} %pad_maximum_fusion.13.gains_ref), custom_call_target="tpu_custom_call" | custom-call | flops 178956976 | bytes 2097152 | tf_op jit(solution)/shard_map/pallas_call | solution.py:95
  197.4 3.2 shard_map.119
  200.7 3.2 shard_map.118
  206.4 4.7 %shard_map.117 = (bf16[512,768]{1,0:T(8,128)(2,1)}, bf16[512,768]{1,0:T(8,128)(2,1)}) custom-call(bf16[512,1024]{1,0:T(8,128)(2,1)S(1)} %copy-done.11, bf16[1024,6144]{1,0:T(8,128)(2,1)S(1)} %slice_dynamic-update-slice_fusion.refs_0_.refs_1_, bf16[1024,6144]{1,0:T(8,128)(2,1)S(1)} %slice_dynamic-update-slice_fusion.refs_0_.refs_1_, ...), custom_call_target="tpu_custom_call" | custom-call | flops 268435456 | bytes 1223338 | tf_op jit(solution)/shard_map/pallas_call | solution.py:133
  215.3 5.7 %shard_map.115 = (bf16[1024,768]{1,0:T(8,128)(2,1)}, bf16[1024,768]{1,0:T(8,128)(2,1)}) custom-call(bf16[1024,1024]{1,0:T(8,128)(2,1)S(1)} %shard_map.114.turned_ref, bf16[1024,6144]{1,0:T(8,128)(2,1)S(1)} %slice_dynamic-update-slice_fusion.refs_0_.refs_1_, bf16[1024,6144]{1,0:T(8,128)(2,1)S(1)} %slice_dynamic-update-slice_fusion.refs_0_.refs_1_), custom_call_target="tpu_custom_call" | custom-call | flops 536870912 | bytes 1398101 | tf_op jit(solution)/shard_map/pallas_call | solution.py:133
  221.0 4.0 %shard_map.120 = bf16[3072,256]{1,0:T(8,128)(2,1)} custom-call(bf16[1024,256]{1,0:T(8,128)(2,1)S(1)} %pad_maximum_fusion.5.pair_ref, bf16[512,256]{1,0:T(8,128)(2,1)S(1)} %copy-done.24, bf16[6144,1024]{1,0:T(8,128)(2,1)S(1)} %constant_dynamic-update-slice_fusion.w_pair_ref, bf16[6144,512]{1,0:T(8,128)(2,1)S(1)} %constant_dynamic-update-slice_fusion.8.w_value_ref, ...), custom_call_target="tpu_custom_call" | custom-call | flops 402653184 | bytes 2359296 | tf_op jit(solution)/shard_map/pallas_call | solution.py:164
  229.5 3.1 collective-permute-done.25.refs_5_
  232.8 4.6 %copy-done.2 = bf16[1024,6144]{1,0:T(8,128)(2,1)S(1)} copy-done((bf16[1024,6144]{1,0:T(8,128)(2,1)S(1)}, bf16[1024,6144]{1,0:T(8,128)(2,1)}, u32[]{:S(2)}) %copy-start.2) | copy-done | bytes 12582936
  238.6 6.2 %shard_map.125 = (bf16[768,512]{1,0:T(8,128)(2,1)S(1)}, bf16[768,512]{1,0:T(8,128)(2,1)}) custom-call(bf16[512,1024]{1,0:T(8,128)(2,1)S(1)} %copy-done.12, bf16[1024,6144]{1,0:T(8,128)(2,1)S(1)} %copy-done.2, bf16[1024,6144]{1,0:T(8,128)(2,1)S(1)} %copy-done.2, bf16[1024,768]{1,0:T(8,128)(2,1)} %collective-permute-done.22.refs_3_.refs_2_, ...), custom_call_target="tpu_custom_call" | custom-call | flops 268435456 | bytes 1485482 | tf_op jit(solution)/shard_map/pallas_call | solution.py:133
  246.7 3.2 shard_map.121
  250.6 3.1 shard_map.124
  253.9 3.2 shard_map.123
  258.4 5.3 %shard_map.122 = (bf16[1024,768]{1,0:T(8,128)(2,1)}, bf16[1024,768]{1,0:T(8,128)(2,1)}) custom-call(bf16[1024,1024]{1,0:T(8,128)(2,1)S(1)} %copy-done.9, bf16[1024,6144]{1,0:T(8,128)(2,1)S(1)} %bitcast.12, bf16[1024,6144]{1,0:T(8,128)(2,1)S(1)} %bitcast.12), custom_call_target="tpu_custom_call" | custom-call | flops 536870912 | bytes 1398101 | tf_op jit(solution)/shard_map/pallas_call | solution.py:133
  266.5 3.4 add_convert_fusion.3
  280.0 3.1 shard_map.127
  283.1 3.2 shard_map.126
  286.3 5.1 %shard_map.129 = (bf16[1024,768]{1,0:T(8,128)(2,1)S(1)}, bf16[1024,768]{1,0:T(8,128)(2,1)}) custom-call(bf16[1024,1024]{1,0:T(8,128)(2,1)S(1)} %copy-done.9, bf16[1024,6144]{1,0:T(8,128)(2,1)S(1)} %bitcast.12, bf16[1024,6144]{1,0:T(8,128)(2,1)S(1)} %bitcast.12), custom_call_target="tpu_custom_call" | custom-call | flops 536870912 | bytes 1398101 | tf_op jit(solution)/shard_map/pallas_call | solution.py:133
  292.6 5.4 %shard_map.128 = (bf16[1024,768]{1,0:T(8,128)(2,1)S(1)}, bf16[1024,768]{1,0:T(8,128)(2,1)S(1)}) custom-call(bf16[1024,1024]{1,0:T(8,128)(2,1)S(1)} %copy-done.9, bf16[1024,6144]{1,0:T(8,128)(2,1)S(1)} %bitcast.12, bf16[1024,6144]{1,0:T(8,128)(2,1)S(1)} %bitcast.12, bf16[1024,768]{1,0:T(8,128)(2,1)} %collective-permute-done.28.refs_2_, ...), custom_call_target="tpu_custom_call" | custom-call | flops 536870912 | bytes 1922389 | tf_op jit(solution)/shard_map/pallas_call | solution.py:133
  298.1 8.9 %collective-permute-done.32 = bf16[1024,768]{1,0:T(8,128)(2,1)} collective-permute-done((bf16[1024,768]{1,0:T(8,128)(2,1)}, bf16[1024,768]{1,0:T(8,128)(2,1)}, u32[]{:S(2)}, u32[]{:S(2)}) %collective-permute-start.32) | collective-permute-done | bytes 1572896 | tf_op jit(solution)/shard_map/ppermute | solution.py:299
  319.5 3.4 add_convert_fusion.1.refs_0_
  325.5 3.4 add_convert_fusion.refs_2_
  328.9 23.4 %collective-permute-done.35 = bf16[3072,256]{1,0:T(8,128)(2,1)} collective-permute-done((bf16[3072,256]{1,0:T(8,128)(2,1)}, bf16[3072,256]{1,0:T(8,128)(2,1)}, u32[]{:S(2)}, u32[]{:S(2)}) %collective-permute-start.35) | collective-permute-done | bytes 1572896 | tf_op jit(solution)/shard_map/ppermute | solution.py:317
  359.6 6.1 %shard_map.131 = (bf16[768,1024]{1,0:T(8,128)(2,1)}, bf16[768,1024]{1,0:T(8,128)(2,1)}) custom-call(s32[1]{0:T(128)} %bitcast.3.core_ref, bf16[1024,768]{1,0:T(8,128)(2,1)S(1)} %copy-done.20, bf16[1024,768]{1,0:T(8,128)(2,1)} %collective-permute-done.39.refs_1_, bf16[1024,768]{1,0:T(8,128)(2,1)S(1)} %copy-done.21, ...), custom_call_target="tpu_custom_call" | custom-call | tf_op jit(solution)/shard_map/pallas_call | solution.py:213
  367.6 3.4 shard_map.132
  (258 shorter events, 125.0 us)
Async XLA Ops:
  8.8 37.5 %collective-permute-start = (bf16[768,1024]{1,0:T(8,128)(2,1)S(1)}, bf16[768,1024]{1,0:T(8,128)(2,1)}, u32[]{:S(2)}, u32[]{:S(2)}) collective-permute-start(bf16[768,1024]{1,0:T(8,128)(2,1)S(1)} %pad_maximum_fusion), channel_id=1, source_target_pairs={{0,8},{4,12},{8,0},{12,4},{16,24},{20,28},{24,16},{28,20},{1,9},{5... | collective-permute-start | bytes 4718600 | tf_op jit(solution)/shard_map/ppermute | solution.py:299
  11.5 35.7 %collective-permute-start.1 = (bf16[768,1024]{1,0:T(8,128)(2,1)S(1)}, bf16[768,1024]{1,0:T(8,128)(2,1)}, u32[]{:S(2)}, u32[]{:S(2)}) collective-permute-start(bf16[768,1024]{1,0:T(8,128)(2,1)S(1)} %pad_maximum_fusion), channel_id=1, source_target_pairs={{0,16},{4,20},{8,24},{12,28},{16,0},{20,4},{24,8},{28,12},{1,17},{... | collective-permute-start | bytes 4718600 | tf_op jit(solution)/shard_map/ppermute | solution.py:299
  12.7 34.5 %collective-permute-start.2 = (bf16[768,1024]{1,0:T(8,128)(2,1)}, bf16[768,1024]{1,0:T(8,128)(2,1)}, u32[]{:S(2)}, u32[]{:S(2)}) collective-permute-start(bf16[768,1024]{1,0:T(8,128)(2,1)} %pad_maximum_fusion.1), channel_id=1, source_target_pairs={{0,4},{4,0},{8,12},{12,8},{16,20},{20,16},{24,28},{28,24},{1,5},{5... | collective-permute-start | bytes 4718600 | tf_op jit(solution)/shard_map/ppermute | solution.py:299
  14.7 36.5 %collective-permute-start.7 = (bf16[256,3072]{1,0:T(8,128)(2,1)}, bf16[256,3072]{1,0:T(8,128)(2,1)}, u32[]{:S(2)}, u32[]{:S(2)}) collective-permute-start(bf16[256,3072]{1,0:T(8,128)(2,1)} %pad_maximum_fusion.2), channel_id=1, source_target_pairs={{0,2},{2,3},{3,1},{1,0},{4,6},{6,7},{7,5},{5,4},{8,10},{10,11},{11... | collective-permute-start | bytes 4718600 | tf_op jit(solution)/shard_map/ppermute | solution.py:317
  17.0 38.0 %collective-permute-start.6 = (bf16[256,3072]{1,0:T(8,128)(2,1)}, bf16[256,3072]{1,0:T(8,128)(2,1)}, u32[]{:S(2)}, u32[]{:S(2)}) collective-permute-start(bf16[256,3072]{1,0:T(8,128)(2,1)} %pad_maximum_fusion.2), channel_id=1, source_target_pairs={{0,4},{4,0},{8,12},{12,8},{16,20},{20,16},{24,28},{28,24},{1,5},{5... | collective-permute-start | bytes 4718600 | tf_op jit(solution)/shard_map/ppermute | solution.py:299
  47.2 34.9 %collective-permute-start.3 = (bf16[768,1024]{1,0:T(8,128)(2,1)}, bf16[768,1024]{1,0:T(8,128)(2,1)S(1)}, u32[]{:S(2)}, u32[]{:S(2)}) collective-permute-start(bf16[768,1024]{1,0:T(8,128)(2,1)} %collective-permute-done.2), channel_id=1, source_target_pairs={{0,8},{4,12},{8,0},{12,4},{16,24},{20,28},{24,16},{28,20},{1,9},{5... | collective-permute-start | bytes 4718600 | tf_op jit(solution)/shard_map/ppermute | solution.py:299
  47.6 34.9 %collective-permute-start.4 = (bf16[768,1024]{1,0:T(8,128)(2,1)}, bf16[768,1024]{1,0:T(8,128)(2,1)S(1)}, u32[]{:S(2)}, u32[]{:S(2)}) collective-permute-start(bf16[768,1024]{1,0:T(8,128)(2,1)} %collective-permute-done.2), channel_id=1, source_target_pairs={{0,16},{4,20},{8,24},{12,28},{16,0},{20,4},{24,8},{28,12},{1,17},{... | collective-permute-start | bytes 4718600 | tf_op jit(solution)/shard_map/ppermute | solution.py:299
  51.2 12.4 %collective-permute-start.8 = (bf16[256,3072]{1,0:T(8,128)(2,1)}, bf16[256,3072]{1,0:T(8,128)(2,1)S(1)}, u32[]{:S(2)}, u32[]{:S(2)}) collective-permute-start(bf16[256,3072]{1,0:T(8,128)(2,1)} %collective-permute-done.7), channel_id=1, source_target_pairs={{0,4},{4,0},{8,12},{12,8},{16,20},{20,16},{24,28},{28,24},{1,5},{5... | collective-permute-start | bytes 4718600 | tf_op jit(solution)/shard_map/ppermute | solution.py:299
  52.5 38.8 %collective-permute-start.10 = (bf16[256,3072]{1,0:T(8,128)(2,1)}, bf16[256,3072]{1,0:T(8,128)(2,1)S(1)}, u32[]{:S(2)}, u32[]{:S(2)}) collective-permute-start(bf16[256,3072]{1,0:T(8,128)(2,1)} %collective-permute-done.7), channel_id=1, source_target_pairs={{0,2},{2,3},{3,1},{1,0},{4,6},{6,7},{7,5},{5,4},{8,10},{10,11},{11... | collective-permute-start | bytes 4718600 | tf_op jit(solution)/shard_map/ppermute | solution.py:317
  82.5 47.4 %collective-permute-start.14 = (bf16[768,1024]{1,0:T(8,128)(2,1)}, bf16[768,1024]{1,0:T(8,128)(2,1)S(1)}, u32[]{:S(2)}, u32[]{:S(2)}) collective-permute-start(bf16[768,1024]{1,0:T(8,128)(2,1)} %collective-permute-done), channel_id=1, source_target_pairs={{0,16},{4,20},{8,24},{12,28},{16,0},{20,4},{24,8},{28,12},{1,17},{... | collective-permute-start | bytes 4718600 | tf_op jit(solution)/shard_map/ppermute | solution.py:299
  83.5 48.3 %collective-permute-start.15 = (bf16[768,1024]{1,0:T(8,128)(2,1)S(1)}, bf16[768,1024]{1,0:T(8,128)(2,1)S(1)}, u32[]{:S(2)}, u32[]{:S(2)}) collective-permute-start(bf16[768,1024]{1,0:T(8,128)(2,1)S(1)} %collective-permute-done.4), channel_id=1, source_target_pairs={{0,8},{4,12},{8,0},{12,4},{16,24},{20,28},{24,16},{28,20},{1,9},{5... | collective-permute-start | bytes 4718600 | tf_op jit(solution)/shard_map/ppermute | solution.py:299
  84.8 10.6 %collective-permute-start.9 = (bf16[768,512]{1,0:T(8,128)(2,1)S(1)}, bf16[768,512]{1,0:T(8,128)(2,1)S(1)}, u32[]{:S(2)}, u32[]{:S(2)}) collective-permute-start(bf16[768,512]{1,0:T(8,128)(2,1)S(1)} %get-tuple-element.211), channel_id=1, source_target_pairs={{0,4},{4,0},{8,12},{12,8},{16,20},{20,16},{24,28},{28,24},{1,5},{5... | collective-permute-start | bytes 2359304 | tf_op jit(solution)/shard_map/ppermute | solution.py:299
  92.8 35.8 %collective-permute-start.12 = (bf16[256,3072]{1,0:T(8,128)(2,1)S(1)}, bf16[256,3072]{1,0:T(8,128)(2,1)S(1)}, u32[]{:S(2)}, u32[]{:S(2)}) collective-permute-start(bf16[256,3072]{1,0:T(8,128)(2,1)S(1)} %collective-permute-done.10), channel_id=1, source_target_pairs={{0,2},{2,3},{3,1},{1,0},{4,6},{6,7},{7,5},{5,4},{8,10},{10,11},{11... | collective-permute-start | bytes 4718600 | tf_op jit(solution)/shard_map/ppermute | solution.py:317
  95.8 56.4 %collective-permute-start.17 = (bf16[1536,512]{1,0:T(8,128)(2,1)S(1)}, bf16[1536,512]{1,0:T(8,128)(2,1)}, u32[]{:S(2)}, u32[]{:S(2)}) collective-permute-start(bf16[1536,512]{1,0:T(8,128)(2,1)S(1)} %pad_maximum_fusion.3), channel_id=1, source_target_pairs={{0,8},{4,12},{8,0},{12,4},{16,24},{20,28},{24,16},{28,20},{1,9},{5... | collective-permute-start | bytes 4718600 | tf_op jit(solution)/shard_map/ppermute | solution.py:299
  96.2 56.1 %collective-permute-start.18 = (bf16[1536,512]{1,0:T(8,128)(2,1)S(1)}, bf16[1536,512]{1,0:T(8,128)(2,1)}, u32[]{:S(2)}, u32[]{:S(2)}) collective-permute-start(bf16[1536,512]{1,0:T(8,128)(2,1)S(1)} %pad_maximum_fusion.3), channel_id=1, source_target_pairs={{0,16},{4,20},{8,24},{12,28},{16,0},{20,4},{24,8},{28,12},{1,17},{... | collective-permute-start | bytes 4718600 | tf_op jit(solution)/shard_map/ppermute | solution.py:299
  155.0 17.6 %collective-permute-start.19 = (bf16[768,512]{1,0:T(8,128)(2,1)S(1)}, bf16[768,512]{1,0:T(8,128)(2,1)S(1)}, u32[]{:S(2)}, u32[]{:S(2)}) collective-permute-start(bf16[768,512]{1,0:T(8,128)(2,1)S(1)} %slice.75), channel_id=1, source_target_pairs={{0,16},{4,20},{8,24},{12,28},{16,0},{20,4},{24,8},{28,12},{1,17},{... | collective-permute-start | bytes 2359304 | tf_op jit(solution)/shard_map/ppermute | solution.py:299
  155.3 18.6 %collective-permute-start.20 = (bf16[768,512]{1,0:T(8,128)(2,1)S(1)}, bf16[768,512]{1,0:T(8,128)(2,1)S(1)}, u32[]{:S(2)}, u32[]{:S(2)}) collective-permute-start(bf16[768,512]{1,0:T(8,128)(2,1)S(1)} %slice.76), channel_id=1, source_target_pairs={{0,8},{4,12},{8,0},{12,4},{16,24},{20,28},{24,16},{28,20},{1,9},{5... | collective-permute-start | bytes 2359304 | tf_op jit(solution)/shard_map/ppermute | solution.py:299
  161.8 44.6 %collective-permute-start.21 = (bf16[1024,768]{1,0:T(8,128)(2,1)}, bf16[1024,768]{1,0:T(8,128)(2,1)}, u32[]{:S(2)}, u32[]{:S(2)}) collective-permute-start(bf16[1024,768]{1,0:T(8,128)(2,1)} %get-tuple-element.128), channel_id=1, source_target_pairs={{0,16},{4,20},{8,24},{12,28},{16,0},{20,4},{24,8},{28,12},{1,17},{... | collective-permute-start | bytes 4718600 | tf_op jit(solution)/shard_map/ppermute | solution.py:299
  163.0 43.4 %collective-permute-start.22 = (bf16[1024,768]{1,0:T(8,128)(2,1)}, bf16[1024,768]{1,0:T(8,128)(2,1)}, u32[]{:S(2)}, u32[]{:S(2)}) collective-permute-start(bf16[1024,768]{1,0:T(8,128)(2,1)} %get-tuple-element.129), channel_id=1, source_target_pairs={{0,8},{4,12},{8,0},{12,4},{16,24},{20,28},{24,16},{28,20},{1,9},{5... | collective-permute-start | bytes 4718600 | tf_op jit(solution)/shard_map/ppermute | solution.py:299
  213.7 18.9 %collective-permute-start.25 = (bf16[512,768]{1,0:T(8,128)(2,1)}, bf16[512,768]{1,0:T(8,128)(2,1)}, u32[]{:S(2)}, u32[]{:S(2)}) collective-permute-start(bf16[512,768]{1,0:T(8,128)(2,1)} %get-tuple-element.139), channel_id=1, source_target_pairs={{0,8},{4,12},{8,0},{12,4},{16,24},{20,28},{24,16},{28,20},{1,9},{5... | collective-permute-start | bytes 2359304 | tf_op jit(solution)/shard_map/ppermute | solution.py:299
  214.2 18.6 %collective-permute-start.26 = (bf16[512,768]{1,0:T(8,128)(2,1)}, bf16[512,768]{1,0:T(8,128)(2,1)}, u32[]{:S(2)}, u32[]{:S(2)}) collective-permute-start(bf16[512,768]{1,0:T(8,128)(2,1)} %get-tuple-element.140), channel_id=1, source_target_pairs={{0,16},{4,20},{8,24},{12,28},{16,0},{20,4},{24,8},{28,12},{1,17},{... | collective-permute-start | bytes 2359304 | tf_op jit(solution)/shard_map/ppermute | solution.py:299
  225.0 41.3 %collective-permute-start.27 = (bf16[1024,768]{1,0:T(8,128)(2,1)}, bf16[1024,768]{1,0:T(8,128)(2,1)S(1)}, u32[]{:S(2)}, u32[]{:S(2)}) collective-permute-start(bf16[1024,768]{1,0:T(8,128)(2,1)} %get-tuple-element.146), channel_id=1, source_target_pairs={{0,8},{4,12},{8,0},{12,4},{16,24},{20,28},{24,16},{28,20},{1,9},{5... | collective-permute-start | bytes 4718600 | tf_op jit(solution)/shard_map/ppermute | solution.py:299
  226.2 40.3 %collective-permute-start.28 = (bf16[1024,768]{1,0:T(8,128)(2,1)}, bf16[1024,768]{1,0:T(8,128)(2,1)}, u32[]{:S(2)}, u32[]{:S(2)}) collective-permute-start(bf16[1024,768]{1,0:T(8,128)(2,1)} %get-tuple-element.147), channel_id=1, source_target_pairs={{0,16},{4,20},{8,24},{12,28},{16,0},{20,4},{24,8},{28,12},{1,17},{... | collective-permute-start | bytes 4718600 | tf_op jit(solution)/shard_map/ppermute | solution.py:299
  226.4 40.1 %collective-permute-start.29 = (bf16[3072,256]{1,0:T(8,128)(2,1)}, bf16[3072,256]{1,0:T(8,128)(2,1)}, u32[]{:S(2)}, u32[]{:S(2)}) collective-permute-start(bf16[3072,256]{1,0:T(8,128)(2,1)} %shard_map.120), channel_id=1, source_target_pairs={{0,2},{2,3},{3,1},{1,0},{4,6},{6,7},{7,5},{5,4},{8,10},{10,11},{11... | collective-permute-start | bytes 4718600 | tf_op jit(solution)/shard_map/ppermute | solution.py:317
  271.2 35.8 %collective-permute-start.32 = (bf16[1024,768]{1,0:T(8,128)(2,1)}, bf16[1024,768]{1,0:T(8,128)(2,1)}, u32[]{:S(2)}, u32[]{:S(2)}) collective-permute-start(bf16[1024,768]{1,0:T(8,128)(2,1)} %get-tuple-element.170), channel_id=1, source_target_pairs={{0,8},{4,12},{8,0},{12,4},{16,24},{20,28},{24,16},{28,20},{1,9},{5... | collective-permute-start | bytes 4718600 | tf_op jit(solution)/shard_map/ppermute | solution.py:299
  272.2 37.4 %collective-permute-start.33 = (bf16[1024,768]{1,0:T(8,128)(2,1)}, bf16[1024,768]{1,0:T(8,128)(2,1)}, u32[]{:S(2)}, u32[]{:S(2)}) collective-permute-start(bf16[1024,768]{1,0:T(8,128)(2,1)} %get-tuple-element.171), channel_id=1, source_target_pairs={{0,20},{4,16},{8,28},{12,24},{16,4},{20,0},{24,12},{28,8},{1,21},{... | collective-permute-start | bytes 4718600 | tf_op jit(solution)/shard_map/ppermute | solution.py:299
  274.1 37.4 %collective-permute-start.34 = (bf16[3072,256]{1,0:T(8,128)(2,1)}, bf16[3072,256]{1,0:T(8,128)(2,1)}, u32[]{:S(2)}, u32[]{:S(2)}) collective-permute-start(bf16[3072,256]{1,0:T(8,128)(2,1)} %add_convert_fusion.3), channel_id=1, source_target_pairs={{0,2},{2,3},{3,1},{1,0},{4,6},{6,7},{7,5},{5,4},{8,10},{10,11},{11... | collective-permute-start | bytes 4718600 | tf_op jit(solution)/shard_map/ppermute | solution.py:317
  314.5 11.0 %collective-permute-start.37 = (bf16[1024,768]{1,0:T(8,128)(2,1)}, bf16[1024,768]{1,0:T(8,128)(2,1)}, u32[]{:S(2)}, u32[]{:S(2)}) collective-permute-start(bf16[1024,768]{1,0:T(8,128)(2,1)} %get-tuple-element.187), channel_id=1, source_target_pairs={{0,4},{4,0},{8,12},{12,8},{16,20},{20,16},{24,28},{28,24},{1,5},{5... | collective-permute-start | bytes 4718600 | tf_op jit(solution)/shard_map/ppermute | solution.py:299
  315.1 37.2 %collective-permute-start.35 = (bf16[3072,256]{1,0:T(8,128)(2,1)}, bf16[3072,256]{1,0:T(8,128)(2,1)}, u32[]{:S(2)}, u32[]{:S(2)}) collective-permute-start(bf16[3072,256]{1,0:T(8,128)(2,1)} %add_convert_fusion.2), channel_id=1, source_target_pairs={{0,2},{2,3},{3,1},{1,0},{4,6},{6,7},{7,5},{5,4},{8,10},{10,11},{11... | collective-permute-start | bytes 4718600 | tf_op jit(solution)/shard_map/ppermute | solution.py:317
  318.5 38.2 %collective-permute-start.39 = (bf16[1024,768]{1,0:T(8,128)(2,1)}, bf16[1024,768]{1,0:T(8,128)(2,1)}, u32[]{:S(2)}, u32[]{:S(2)}) collective-permute-start(bf16[1024,768]{1,0:T(8,128)(2,1)} %copy-done.36), channel_id=1, source_target_pairs={{0,16},{4,20},{8,24},{12,28},{16,0},{20,4},{24,8},{28,12},{1,17},{... | collective-permute-start | bytes 4718600 | tf_op jit(solution)/shard_map/ppermute | solution.py:299
  318.7 38.0 %collective-permute-start.40 = (bf16[1024,768]{1,0:T(8,128)(2,1)}, bf16[1024,768]{1,0:T(8,128)(2,1)}, u32[]{:S(2)}, u32[]{:S(2)}) collective-permute-start(bf16[1024,768]{1,0:T(8,128)(2,1)} %copy-done.35), channel_id=1, source_target_pairs={{0,12},{4,8},{8,4},{12,0},{16,28},{20,24},{24,20},{28,16},{1,13},{... | collective-permute-start | bytes 4718600 | tf_op jit(solution)/shard_map/ppermute | solution.py:299
  355.7 10.1 %collective-permute-start.38 = (bf16[3072,128]{1,0:T(8,128)(2,1)S(1)}, bf16[3072,128]{1,0:T(8,128)(2,1)S(1)}, u32[]{:S(2)}, u32[]{:S(2)}) collective-permute-start(bf16[3072,128]{1,0:T(8,128)(2,1)S(1)} %dynamic-slice_convert_fusion), channel_id=1, source_target_pairs={{0,4},{4,0},{8,12},{12,8},{16,20},{20,16},{24,28},{28,24},{1,5},{5... | collective-permute-start | bytes 2359304 | tf_op jit(solution)/shard_map/ppermute | solution.py:299
  (65 other events, 760.1 us)

commit v9 on v8

--- a/solution.py
+++ b/solution.py
@@ -190,7 +190,7 @@
         for block in blocks[1:]:
             total = total + block[...].astype(F32)
         for k, out in enumerate(outs):
-            out[...] = total[k * cols : (k + 1) * cols].T.astype(BF)
+            out[...] = total[:, k * cols : (k + 1) * cols].astype(BF)
 
     @pl.when(here)
     def _():
@@ -202,24 +202,25 @@
 
 
 def gather_call(core, mine, other, cols):
-    columns, rows = mine[0].shape
+    rows, columns = mine[0].shape
     tile = 256 if rows % 256 == 0 else 128
+    steps = rows // tile
     here = pl.BlockSpec(
-        (columns, tile), lambda h, i, core_ref: (0, jnp.where(h == core_ref[0], i, rows // tile * h - h))
+        (tile, columns), lambda h, i, core_ref: (jnp.where(h == core_ref[0], i, steps * h - h), 0)
     )
     there = pl.BlockSpec(
-        (columns, tile), lambda h, i, core_ref: (0, jnp.where(h != core_ref[0], i, rows // tile * h - h))
+        (tile, columns), lambda h, i, core_ref: (jnp.where(h != core_ref[0], i, steps * h - h), 0)
     )
     return pl.pallas_call(
         functools.partial(gather_kernel, cols, len(mine)),
         grid_spec=pltpu.PrefetchScalarGridSpec(
             num_scalar_prefetch=1,
-            grid=(2, rows // tile),
+            grid=(2, steps),
             in_specs=[here] * len(mine) + [there] * len(other),
             out_specs=[pl.BlockSpec((tile, cols), lambda h, i, core_ref: (i, h))] * (columns // cols),
         ),
         out_shape=[jax.ShapeDtypeStruct((rows, 2 * cols), BF)] * (columns // cols),
-        compiler_params=params(40),
+        compiler_params=params(60),
     )(core.reshape(1), *mine, *other)
 
 
@@ -407,9 +408,9 @@
     def messages(turned, to_x, to_y):
         return [products(turned, r, (to_x, to_y)) for r in blocks_of_four]
 
-    def late_messages(turned, far):
+    def late_messages(turned, far, turn=False):
         return [
-            products(turned, r, ((3,), (4,)), (((from_y, 0),), ((from_x, 0),)))
+            products(turned, r, ((3,), (4,)), (((from_y, 0),), ((from_x, 0),)), turn)
             for r, (from_x, from_y) in zip(blocks_of_four, far)
         ]
 
@@ -483,9 +484,7 @@
                 partial[1], early_pair, sent, far_pair, ends_value
             )
         elif step == 2:
-            partial[2], late_pair, early_pair, own_pair = together(
-                partial[2], late_pair, early_pair, own_pair
-            )
+            partial[2], late_pair, own_pair = together(partial[2], late_pair, own_pair)
         message = (partial[step].astype(F32) + arrived.astype(F32)).astype(BF)
         if step == 1:
             message, early_pair, sent, turned_pair, turned_value = together(
@@ -493,8 +492,8 @@
             )
             early_pair = send(early_pair, y=5)
         elif step == 2:
-            message, late_pair, own_pair, ends_value = together(
-                message, late_pair, own_pair, ends_value
+            message, late_pair, own_pair, ends_value, early_pair = together(
+                message, late_pair, own_pair, ends_value, early_pair
             )
             late_pair = send(late_pair, x=3)
             own_pair = [[even, swap(odd, 1)] for even, odd in own_pair]
@@ -515,13 +514,13 @@
             else:
                 chosen[step + 3], sent[step + 3] = back_odd(step + 3, turned_pair, turned_value)
             if step == 1:
-                late_pair = late_messages(turned_pair, far_pair)
+                late_pair = late_messages(turned_pair, far_pair, True)
                 own_pair = messages(turned_pair, (0,), (1,))
     out_value = place_call(core, ends_value[0], passed_value, cols, 0)
     here, there = {}, {}
     for r, (own_even, own_odd), (even_x, odd_y) in zip(blocks_of_four, own_pair, early_pair):
-        here[r] = (own_even.astype(F32) + even_x.astype(F32)).astype(BF)
-        there[r] = (own_odd.astype(F32) + odd_y.astype(F32)).astype(BF)
+        here[r] = (own_even.astype(F32) + even_x.astype(F32)).astype(BF).T
+        there[r] = (own_odd.astype(F32) + odd_y.astype(F32)).astype(BF).T
     arrived, out_value, here, there = together(arrived, out_value, here, there)
     total = partial[n_mp - 1] + arrived.astype(F32)
 

time: 377 us -> 381 us (1.011)
  local copies, waits for them, and re-layouts: 51.5 us -> 68 us
  waiting for transfers between devices: 132 us -> 117 us
    ppermute x35, waiting for transfers between devices: 73.6 us -> 61.3 us  [swap(): return lax.ppermute(array, 'dp', [(i, i ^ bit) for i in range(n_dp)])]
    optimization_barrier x0 -> x4, local copies, waits for them, and re-layouts: none -> 8.63 us  [together(): return lax.optimization_barrier(arrays)]
    transpose x0 -> x2, other arithmetic: none -> 7.56 us  [the longest x1 3.86 us: per_device(): there[r] = (own_odd.astype(F32) + odd_y.astype(F32)).astype(BF).T]
    convert_element_type x2 -> x0, other arithmetic: 6.81 us -> none  [the longest x1 3.41 us: per_device(): there[r] = (own_odd.astype(F32) + odd_y.astype(F32)).astype(BF)]
    unnamed x126 -> x148, local copies, waits for them, and re-layouts: 33 us -> 39.3 us
    pallas_call x8, Pallas kernels: 26.1 us -> 31.2 us  [back_call(): pl.pallas_call(back_kernel, grid=(units,), in_specs=[pl.BlockSpec(pair.sh...]
  transfers between devices with their start and end apart: 41 -> 41, of which waited for: 18 -> 15; matrix products, arithmetic and copies ran while one was open for 15% -> 18% of each run, Pallas kernels for 23% -> 23%
where the time goes in v9:
time: 381 us; the launch traced here: 375 us
  waiting for transfers between devices  117 us (31%)
  Pallas kernels  94.6 us (25%)
  local copies, waits for them, and re-layouts  68 us (18%)
  starting transfers between devices  47.3 us (12%)
  other arithmetic  26.1 us (7%)
  matrix products  20.7 us (5%)
    ppermute x35, waiting for transfers between devices, swap(): return lax.ppermute(array, 'dp', [(i, i ^ bit) for i in range(n_dp)])  61.3 us
    ppermute x6, waiting for transfers between devices, ring_on(): return lax.ppermute(array, 'mp', ring_pairs)  55.6 us
    unnamed x148, local copies, waits for them, and re-layouts  39.3 us
    pallas_call x7, Pallas kernels, product_call(): pl.pallas_call(functools.partial(product_kernel, n_add, turn), grid=(coun...  36.4 us
    ppermute x35, starting transfers between devices, swap(): return lax.ppermute(array, 'dp', [(i, i ^ bit) for i in range(n_dp)])  33.3 us
    pallas_call x8, Pallas kernels, back_call(): pl.pallas_call(back_kernel, grid=(units,), in_specs=[pl.BlockSpec(pair.sh...  31.2 us
    pallas_call x2, Pallas kernels, attention_call(): pl.pallas_call(kernel, grid=(tokens // PATCH,), in_specs=[pl.BlockSpec((P...  16 us
    ppermute x6, starting transfers between devices, ring_on(): return lax.ppermute(array, 'mp', ring_pairs)  13.9 us
  transfers between devices with their start and end apart: 41, of which 15 were waited for; matrix products, arithmetic and copies ran while one was open for 18% of the time, Pallas kernels for 23%

profile of v9, /device:TPU:1, one launch (start us, length us, event | category | flops | bytes accessed | tf_op | source)
XLA Modules:
  0.0 375.3 jit_solution(7109873045928980254)
XLA Ops:
  17.4 28.9 %collective-permute-done = bf16[768,1024]{1,0:T(8,128)(2,1)} collective-permute-done((bf16[768,1024]{1,0:T(8,128)(2,1)S(1)}, bf16[768,1024]{1,0:T(8,128)(2,1)}, u32[]{:S(2)}, u32[]{:S(2)}) %collective-permute-start) | collective-permute-done | bytes 1572896 | tf_op jit(solution)/shard_map/ppermute | solution.py:300
  65.5 16.7 %collective-permute-done.3 = bf16[768,1024]{1,0:T(8,128)(2,1)S(1)} collective-permute-done((bf16[768,1024]{1,0:T(8,128)(2,1)}, bf16[768,1024]{1,0:T(8,128)(2,1)S(1)}, u32[]{:S(2)}, u32[]{:S(2)}) %collective-permute-start.3) | collective-permute-done | bytes 1572896 | tf_op jit(solution)/shard_map/ppermute | solution.py:300
  96.4 32.2 %collective-permute-done.12 = bf16[256,3072]{1,0:T(8,128)(2,1)S(1)} collective-permute-done((bf16[256,3072]{1,0:T(8,128)(2,1)S(1)}, bf16[256,3072]{1,0:T(8,128)(2,1)S(1)}, u32[]{:S(2)}, u32[]{:S(2)}) %collective-permute-start.12) | collective-permute-done | bytes 1572896 | tf_op jit(solution)/shard_map/ppermute | solution.py:318
  133.1 13.1 %fusion.6.qk_ref = f32[1024,1024]{1,0:T(8,128)S(1)} fusion(bf16[1024,6144]{1,0:T(8,128)(2,1)S(1)} %slice_dynamic-update-slice_fusion.refs_0_.refs_1_, bf16[6144,1024]{1,0:T(8,128)(2,1)S(1)} %constant_dynamic-update-slice_fusion.w_pair_ref), kind=kOutput, calls=%fused_computation.98 | convolution fusion | flops 12884901888 | bytes 29360128 | tf_op jit(solution)/shard_map/dot_general | solution.py:399
  146.3 5.9 %shard_map.113.turned_ref = bf16[512,1024]{1,0:T(8,128)(2,1)S(1)} custom-call(f32[1024,1024]{1,0:T(8,128)S(1)} %fusion.6.qk_ref, bf16[1024,512]{1,0:T(8,128)(2,1)S(1)} %constant_dynamic-update-slice_fusion.12.g_ref, f32[2,128]{1,0:T(2,128)S(1)} %pad_maximum_fusion.13.gains_ref), custom_call_target="tpu_custom_call" | custom-call | flops 178956976 | bytes 1398101 | tf_op jit(solution)/shard_map/pallas_call | solution.py:95
  155.6 6.2 %shard_map.116 = (bf16[1024,768]{1,0:T(8,128)(2,1)}, bf16[1024,768]{1,0:T(8,128)(2,1)}) custom-call(bf16[512,1024]{1,0:T(8,128)(2,1)S(1)} %shard_map.113.turned_ref, bf16[1024,6144]{1,0:T(8,128)(2,1)S(1)} %slice_dynamic-update-slice_fusion.refs_0_.refs_1_, bf16[1024,6144]{1,0:T(8,128)(2,1)S(1)} %slice_dynamic-update-slice_fusion.refs_0_.refs_1_), custom_call_target="tpu_custom_call" | custom-call | flops 536870912 | bytes 1485482 | tf_op jit(solution)/shard_map/pallas_call | solution.py:133
  167.1 5.5 %collective-permute-done.19 = bf16[768,512]{1,0:T(8,128)(2,1)S(1)} collective-permute-done((bf16[768,512]{1,0:T(8,128)(2,1)S(1)}, bf16[768,512]{1,0:T(8,128)(2,1)S(1)}, u32[]{:S(2)}, u32[]{:S(2)}) %collective-permute-start.19) | collective-permute-done | bytes 786464 | tf_op jit(solution)/shard_map/ppermute | solution.py:300
  174.0 7.6 %convolution_convert_fusion.v_ref = bf16[1024,512]{1,0:T(8,128)(2,1)} fusion(bf16[1024,6144]{1,0:T(8,128)(2,1)S(1)} %slice_dynamic-update-slice_fusion.refs_0_.refs_1_, bf16[6144,512]{1,0:T(8,128)(2,1)S(1)} %constant_dynamic-update-slice_fusion.8.w_value_ref), kind=kOutput, calls=%fused_computation.18 | convolution fusion | flops 6442975232 | bytes 19922944 | tf_op jit(solution)/shard_map/dot_general | solution.py:446
  186.3 10.0 %shard_map.114.turned_ref = bf16[1024,1024]{1,0:T(8,128)(2,1)S(1)} custom-call(f32[1024,1024]{1,0:T(8,128)S(1)} %copy-done.16, bf16[1024,512]{1,0:T(8,128)(2,1)S(1)} %copy-done.22, bf16[1024,512]{1,0:T(8,128)(2,1)S(1)} %copy-done.40, f32[2,128]{1,0:T(2,128)S(1)} %pad_maximum_fusion.13.gains_ref), custom_call_target="tpu_custom_call" | custom-call | flops 178956976 | bytes 2097152 | tf_op jit(solution)/shard_map/pallas_call | solution.py:95
  197.5 3.2 shard_map.119
  200.7 3.2 shard_map.118
  206.4 4.6 %shard_map.117 = (bf16[512,768]{1,0:T(8,128)(2,1)}, bf16[512,768]{1,0:T(8,128)(2,1)}) custom-call(bf16[512,1024]{1,0:T(8,128)(2,1)S(1)} %copy-done.12, bf16[1024,6144]{1,0:T(8,128)(2,1)S(1)} %slice_dynamic-update-slice_fusion.refs_0_.refs_1_, bf16[1024,6144]{1,0:T(8,128)(2,1)S(1)} %slice_dynamic-update-slice_fusion.refs_0_.refs_1_, ...), custom_call_target="tpu_custom_call" | custom-call | flops 268435456 | bytes 1223338 | tf_op jit(solution)/shard_map/pallas_call | solution.py:133
  215.3 5.7 %shard_map.115 = (bf16[1024,768]{1,0:T(8,128)(2,1)}, bf16[1024,768]{1,0:T(8,128)(2,1)}) custom-call(bf16[1024,1024]{1,0:T(8,128)(2,1)S(1)} %shard_map.114.turned_ref, bf16[1024,6144]{1,0:T(8,128)(2,1)S(1)} %slice_dynamic-update-slice_fusion.refs_0_.refs_1_, bf16[1024,6144]{1,0:T(8,128)(2,1)S(1)} %slice_dynamic-update-slice_fusion.refs_0_.refs_1_), custom_call_target="tpu_custom_call" | custom-call | flops 536870912 | bytes 1398101 | tf_op jit(solution)/shard_map/pallas_call | solution.py:133
  221.0 4.0 %shard_map.120 = bf16[3072,256]{1,0:T(8,128)(2,1)} custom-call(bf16[1024,256]{1,0:T(8,128)(2,1)S(1)} %pad_maximum_fusion.5.pair_ref, bf16[512,256]{1,0:T(8,128)(2,1)S(1)} %copy-done.27, bf16[6144,1024]{1,0:T(8,128)(2,1)S(1)} %constant_dynamic-update-slice_fusion.w_pair_ref, bf16[6144,512]{1,0:T(8,128)(2,1)S(1)} %constant_dynamic-update-slice_fusion.8.w_value_ref, ...), custom_call_target="tpu_custom_call" | custom-call | flops 402653184 | bytes 2359296 | tf_op jit(solution)/shard_map/pallas_call | solution.py:164
  229.4 3.2 collective-permute-done.25.refs_5_
  232.8 4.6 %copy-done.2 = bf16[1024,6144]{1,0:T(8,128)(2,1)S(1)} copy-done((bf16[1024,6144]{1,0:T(8,128)(2,1)S(1)}, bf16[1024,6144]{1,0:T(8,128)(2,1)}, u32[]{:S(2)}) %copy-start.2) | copy-done | bytes 12582936
  238.6 5.4 %shard_map.125 = (bf16[768,512]{1,0:T(8,128)(2,1)S(1)}, bf16[768,512]{1,0:T(8,128)(2,1)S(1)}) custom-call(bf16[512,1024]{1,0:T(8,128)(2,1)S(1)} %copy-done.13, bf16[1024,6144]{1,0:T(8,128)(2,1)S(1)} %copy-done.2, bf16[1024,6144]{1,0:T(8,128)(2,1)S(1)} %copy-done.2, bf16[1024,768]{1,0:T(8,128)(2,1)} %collective-permute-done.22.refs_3_.refs_2_, ...), custom_call_target="tpu_custom_call" | custom-call | flops 268435456 | bytes 1485482 | tf_op jit(solution)/shard_map/pallas_call | solution.py:133
  246.8 3.2 shard_map.121
  250.6 3.9 %shard_map.124 = bf16[3072,256]{1,0:T(8,128)(2,1)} custom-call(bf16[1024,256]{1,0:T(8,128)(2,1)S(1)} %pad_maximum_fusion.8.pair_ref, bf16[512,256]{1,0:T(8,128)(2,1)S(1)} %pad_maximum_fusion.12.value_ref, bf16[6144,1024]{1,0:T(8,128)(2,1)S(1)} %copy-done.4, bf16[6144,512]{1,0:T(8,128)(2,1)S(1)} %copy-done.7), custom_call_target="tpu_custom_call" | custom-call | flops 402653184 | bytes 2359296 | tf_op jit(solution)/shard_map/pallas_call | solution.py:164
  254.7 3.9 %shard_map.123 = bf16[3072,256]{1,0:T(8,128)(2,1)} custom-call(bf16[1024,256]{1,0:T(8,128)(2,1)S(1)} %pad_maximum_fusion.7.pair_ref, bf16[512,256]{1,0:T(8,128)(2,1)S(1)} %pad_maximum_fusion.11.value_ref, bf16[6144,1024]{1,0:T(8,128)(2,1)S(1)} %copy-done.4, bf16[6144,512]{1,0:T(8,128)(2,1)S(1)} %copy-done.7), custom_call_target="tpu_custom_call" | custom-call | flops 402653184 | bytes 2359296 | tf_op jit(solution)/shard_map/pallas_call | solution.py:164
  260.0 4.4 %shard_map.122 = (bf16[1024,768]{1,0:T(8,128)(2,1)S(1)}, bf16[1024,768]{1,0:T(8,128)(2,1)S(1)}) custom-call(bf16[1024,1024]{1,0:T(8,128)(2,1)S(1)} %copy-done.10, bf16[1024,6144]{1,0:T(8,128)(2,1)S(1)} %bitcast.16, bf16[1024,6144]{1,0:T(8,128)(2,1)S(1)} %bitcast.16), custom_call_target="tpu_custom_call" | custom-call | flops 536870912 | bytes 1398101 | tf_op jit(solution)/shard_map/pallas_call | solution.py:133
  283.0 4.6 %copy-done.5 = bf16[6144,1024]{1,0:T(8,128)(2,1)S(1)} copy-done((bf16[6144,1024]{1,0:T(8,128)(2,1)S(1)}, bf16[6144,1024]{1,0:T(8,128)(2,1)}, u32[]{:S(2)}) %copy-start.5) | copy-done | bytes 12582936
  291.3 5.3 %shard_map.127 = f32[3072,256]{1,0:T(8,128)S(1)} custom-call(bf16[1024,256]{1,0:T(8,128)(2,1)S(1)} %pad_maximum_fusion.8.pair_ref, bf16[512,256]{1,0:T(8,128)(2,1)S(1)} %copy-done.29, bf16[6144,1024]{1,0:T(8,128)(2,1)S(1)} %copy-done.5, bf16[6144,512]{1,0:T(8,128)(2,1)S(1)} %copy-done.8, bf16[3072,256]{1,0:T(8,128)(2,1)} %collective-permute-done.31.refs_0_), custom_call_target="tpu_custom_call" | custom-call | flops 402653184 | bytes 2359296 | tf_op jit(solution)/shard_map/pallas_call | solution.py:164
  299.1 4.5 %shard_map.126 = bf16[3072,256]{1,0:T(8,128)(2,1)S(1)} custom-call(bf16[1024,256]{1,0:T(8,128)(2,1)S(1)} %copy-done.24, bf16[512,256]{1,0:T(8,128)(2,1)S(1)} %copy-done.31, bf16[6144,1024]{1,0:T(8,128)(2,1)S(1)} %copy-done.5, bf16[6144,512]{1,0:T(8,128)(2,1)S(1)} %copy-done.8, bf16[3072,256]{1,0:T(8,128)(2,1)} %collective-permute-done.30.refs_0_), custom_call_target="tpu_custom_call" | custom-call | flops 402653184 | bytes 2359296 | tf_op jit(solution)/shard_map/pallas_call | solution.py:164
  303.7 4.4 %shard_map.129 = (bf16[1024,768]{1,0:T(8,128)(2,1)S(1)}, bf16[1024,768]{1,0:T(8,128)(2,1)S(1)}) custom-call(bf16[1024,1024]{1,0:T(8,128)(2,1)S(1)} %copy-done.10, bf16[1024,6144]{1,0:T(8,128)(2,1)S(1)} %bitcast.18, bf16[1024,6144]{1,0:T(8,128)(2,1)S(1)} %bitcast.18), custom_call_target="tpu_custom_call" | custom-call | flops 536870912 | bytes 1398101 | tf_op jit(solution)/shard_map/pallas_call | solution.py:133
  310.4 5.7 %shard_map.128 = (bf16[768,1024]{1,0:T(8,128)(2,1)S(1)}, bf16[768,1024]{1,0:T(8,128)(2,1)S(1)}) custom-call(bf16[1024,1024]{1,0:T(8,128)(2,1)S(1)} %copy-done.10, bf16[1024,6144]{1,0:T(8,128)(2,1)S(1)} %bitcast.18, bf16[1024,6144]{1,0:T(8,128)(2,1)S(1)} %bitcast.18, bf16[1024,768]{1,0:T(8,128)(2,1)} %collective-permute-done.28.refs_2_, ...), custom_call_target="tpu_custom_call" | custom-call | flops 536870912 | bytes 1922389 | tf_op jit(solution)/shard_map/pallas_call | solution.py:133
  316.2 4.1 %add_convert_fusion.2 = bf16[3072,256]{1,0:T(8,128)(2,1)} fusion(bf16[3072,256]{1,0:T(8,128)(2,1)} %collective-permute-done.32, bf16[3072,256]{1,0:T(8,128)(2,1)S(1)} %shard_map.126), kind=kLoop, calls=%fused_computation.8 | loop fusion | flops 3145728 | bytes 4718592 | tf_op jit(solution)/shard_map/convert_element_type | solution.py:488
  326.0 3.7 fusion.3.refs_0_
  330.9 3.9 %fusion.4.refs_2_ = bf16[768,1024]{1,0:T(8,128)(2,1)} fusion(bf16[1024,768]{0,1:T(8,128)(2,1)} %collective-permute-done.34, bf16[1024,768]{0,1:T(8,128)(2,1)} %collective-permute-done.37), kind=kLoop, calls=%fused_computation.12 | loop fusion | flops 3145728 | bytes 4718592 | tf_op jit(solution)/shard_map/transpose | solution.py:523
  334.8 23.0 %collective-permute-done.35 = bf16[3072,256]{1,0:T(8,128)(2,1)} collective-permute-done((bf16[3072,256]{1,0:T(8,128)(2,1)}, bf16[3072,256]{1,0:T(8,128)(2,1)}, u32[]{:S(2)}, u32[]{:S(2)}) %collective-permute-start.35) | collective-permute-done | bytes 1572896 | tf_op jit(solution)/shard_map/ppermute | solution.py:318
  362.9 6.4 %shard_map.131 = (bf16[768,1024]{1,0:T(8,128)(2,1)}, bf16[768,1024]{1,0:T(8,128)(2,1)}) custom-call(s32[1]{0:T(128)} %bitcast.3.core_ref, bf16[768,1024]{1,0:T(8,128)(2,1)} %fusion.3.refs_0_, bf16[768,1024]{1,0:T(8,128)(2,1)} %collective-permute-done.39.refs_1_, bf16[768,1024]{1,0:T(8,128)(2,1)} %fusion.4.refs_2_, ...), custom_call_target="tpu_custom_call" | custom-call | tf_op jit(solution)/shard_map/pallas_call | solution.py:214
  371.7 3.4 shard_map.132
  (284 shorter events, 129.0 us)
Async XLA Ops:
  8.8 37.5 %collective-permute-start = (bf16[768,1024]{1,0:T(8,128)(2,1)S(1)}, bf16[768,1024]{1,0:T(8,128)(2,1)}, u32[]{:S(2)}, u32[]{:S(2)}) collective-permute-start(bf16[768,1024]{1,0:T(8,128)(2,1)S(1)} %pad_maximum_fusion), channel_id=1, source_target_pairs={{0,8},{4,12},{8,0},{12,4},{16,24},{20,28},{24,16},{28,20},{1,9},{5... | collective-permute-start | bytes 4718600 | tf_op jit(solution)/shard_map/ppermute | solution.py:300
  11.5 35.7 %collective-permute-start.1 = (bf16[768,1024]{1,0:T(8,128)(2,1)S(1)}, bf16[768,1024]{1,0:T(8,128)(2,1)}, u32[]{:S(2)}, u32[]{:S(2)}) collective-permute-start(bf16[768,1024]{1,0:T(8,128)(2,1)S(1)} %pad_maximum_fusion), channel_id=1, source_target_pairs={{0,16},{4,20},{8,24},{12,28},{16,0},{20,4},{24,8},{28,12},{1,17},{... | collective-permute-start | bytes 4718600 | tf_op jit(solution)/shard_map/ppermute | solution.py:300
  12.7 34.5 %collective-permute-start.2 = (bf16[768,1024]{1,0:T(8,128)(2,1)}, bf16[768,1024]{1,0:T(8,128)(2,1)}, u32[]{:S(2)}, u32[]{:S(2)}) collective-permute-start(bf16[768,1024]{1,0:T(8,128)(2,1)} %pad_maximum_fusion.1), channel_id=1, source_target_pairs={{0,4},{4,0},{8,12},{12,8},{16,20},{20,16},{24,28},{28,24},{1,5},{5... | collective-permute-start | bytes 4718600 | tf_op jit(solution)/shard_map/ppermute | solution.py:300
  14.7 36.5 %collective-permute-start.7 = (bf16[256,3072]{1,0:T(8,128)(2,1)}, bf16[256,3072]{1,0:T(8,128)(2,1)}, u32[]{:S(2)}, u32[]{:S(2)}) collective-permute-start(bf16[256,3072]{1,0:T(8,128)(2,1)} %pad_maximum_fusion.2), channel_id=1, source_target_pairs={{0,2},{2,3},{3,1},{1,0},{4,6},{6,7},{7,5},{5,4},{8,10},{10,11},{11... | collective-permute-start | bytes 4718600 | tf_op jit(solution)/shard_map/ppermute | solution.py:318
  17.1 38.0 %collective-permute-start.6 = (bf16[256,3072]{1,0:T(8,128)(2,1)}, bf16[256,3072]{1,0:T(8,128)(2,1)}, u32[]{:S(2)}, u32[]{:S(2)}) collective-permute-start(bf16[256,3072]{1,0:T(8,128)(2,1)} %pad_maximum_fusion.2), channel_id=1, source_target_pairs={{0,4},{4,0},{8,12},{12,8},{16,20},{20,16},{24,28},{28,24},{1,5},{5... | collective-permute-start | bytes 4718600 | tf_op jit(solution)/shard_map/ppermute | solution.py:300
  47.3 34.9 %collective-permute-start.3 = (bf16[768,1024]{1,0:T(8,128)(2,1)}, bf16[768,1024]{1,0:T(8,128)(2,1)S(1)}, u32[]{:S(2)}, u32[]{:S(2)}) collective-permute-start(bf16[768,1024]{1,0:T(8,128)(2,1)} %collective-permute-done.2), channel_id=1, source_target_pairs={{0,8},{4,12},{8,0},{12,4},{16,24},{20,28},{24,16},{28,20},{1,9},{5... | collective-permute-start | bytes 4718600 | tf_op jit(solution)/shard_map/ppermute | solution.py:300
  47.6 34.9 %collective-permute-start.4 = (bf16[768,1024]{1,0:T(8,128)(2,1)}, bf16[768,1024]{1,0:T(8,128)(2,1)S(1)}, u32[]{:S(2)}, u32[]{:S(2)}) collective-permute-start(bf16[768,1024]{1,0:T(8,128)(2,1)} %collective-permute-done.2), channel_id=1, source_target_pairs={{0,16},{4,20},{8,24},{12,28},{16,0},{20,4},{24,8},{28,12},{1,17},{... | collective-permute-start | bytes 4718600 | tf_op jit(solution)/shard_map/ppermute | solution.py:300
  51.2 12.4 %collective-permute-start.8 = (bf16[256,3072]{1,0:T(8,128)(2,1)}, bf16[256,3072]{1,0:T(8,128)(2,1)S(1)}, u32[]{:S(2)}, u32[]{:S(2)}) collective-permute-start(bf16[256,3072]{1,0:T(8,128)(2,1)} %collective-permute-done.7), channel_id=1, source_target_pairs={{0,4},{4,0},{8,12},{12,8},{16,20},{20,16},{24,28},{28,24},{1,5},{5... | collective-permute-start | bytes 4718600 | tf_op jit(solution)/shard_map/ppermute | solution.py:300
  52.5 38.7 %collective-permute-start.10 = (bf16[256,3072]{1,0:T(8,128)(2,1)}, bf16[256,3072]{1,0:T(8,128)(2,1)S(1)}, u32[]{:S(2)}, u32[]{:S(2)}) collective-permute-start(bf16[256,3072]{1,0:T(8,128)(2,1)} %collective-permute-done.7), channel_id=1, source_target_pairs={{0,2},{2,3},{3,1},{1,0},{4,6},{6,7},{7,5},{5,4},{8,10},{10,11},{11... | collective-permute-start | bytes 4718600 | tf_op jit(solution)/shard_map/ppermute | solution.py:318
  82.5 47.4 %collective-permute-start.14 = (bf16[768,1024]{1,0:T(8,128)(2,1)}, bf16[768,1024]{1,0:T(8,128)(2,1)S(1)}, u32[]{:S(2)}, u32[]{:S(2)}) collective-permute-start(bf16[768,1024]{1,0:T(8,128)(2,1)} %collective-permute-done), channel_id=1, source_target_pairs={{0,16},{4,20},{8,24},{12,28},{16,0},{20,4},{24,8},{28,12},{1,17},{... | collective-permute-start | bytes 4718600 | tf_op jit(solution)/shard_map/ppermute | solution.py:300
  83.5 48.3 %collective-permute-start.15 = (bf16[768,1024]{1,0:T(8,128)(2,1)S(1)}, bf16[768,1024]{1,0:T(8,128)(2,1)S(1)}, u32[]{:S(2)}, u32[]{:S(2)}) collective-permute-start(bf16[768,1024]{1,0:T(8,128)(2,1)S(1)} %collective-permute-done.4), channel_id=1, source_target_pairs={{0,8},{4,12},{8,0},{12,4},{16,24},{20,28},{24,16},{28,20},{1,9},{5... | collective-permute-start | bytes 4718600 | tf_op jit(solution)/shard_map/ppermute | solution.py:300
  84.8 10.6 %collective-permute-start.9 = (bf16[768,512]{1,0:T(8,128)(2,1)S(1)}, bf16[768,512]{1,0:T(8,128)(2,1)S(1)}, u32[]{:S(2)}, u32[]{:S(2)}) collective-permute-start(bf16[768,512]{1,0:T(8,128)(2,1)S(1)} %get-tuple-element.211), channel_id=1, source_target_pairs={{0,4},{4,0},{8,12},{12,8},{16,20},{20,16},{24,28},{28,24},{1,5},{5... | collective-permute-start | bytes 2359304 | tf_op jit(solution)/shard_map/ppermute | solution.py:300
  92.8 35.8 %collective-permute-start.12 = (bf16[256,3072]{1,0:T(8,128)(2,1)S(1)}, bf16[256,3072]{1,0:T(8,128)(2,1)S(1)}, u32[]{:S(2)}, u32[]{:S(2)}) collective-permute-start(bf16[256,3072]{1,0:T(8,128)(2,1)S(1)} %collective-permute-done.10), channel_id=1, source_target_pairs={{0,2},{2,3},{3,1},{1,0},{4,6},{6,7},{7,5},{5,4},{8,10},{10,11},{11... | collective-permute-start | bytes 4718600 | tf_op jit(solution)/shard_map/ppermute | solution.py:318
  95.8 56.4 %collective-permute-start.17 = (bf16[1536,512]{1,0:T(8,128)(2,1)S(1)}, bf16[1536,512]{1,0:T(8,128)(2,1)}, u32[]{:S(2)}, u32[]{:S(2)}) collective-permute-start(bf16[1536,512]{1,0:T(8,128)(2,1)S(1)} %pad_maximum_fusion.3), channel_id=1, source_target_pairs={{0,8},{4,12},{8,0},{12,4},{16,24},{20,28},{24,16},{28,20},{1,9},{5... | collective-permute-start | bytes 4718600 | tf_op jit(solution)/shard_map/ppermute | solution.py:300
  96.2 56.1 %collective-permute-start.18 = (bf16[1536,512]{1,0:T(8,128)(2,1)S(1)}, bf16[1536,512]{1,0:T(8,128)(2,1)}, u32[]{:S(2)}, u32[]{:S(2)}) collective-permute-start(bf16[1536,512]{1,0:T(8,128)(2,1)S(1)} %pad_maximum_fusion.3), channel_id=1, source_target_pairs={{0,16},{4,20},{8,24},{12,28},{16,0},{20,4},{24,8},{28,12},{1,17},{... | collective-permute-start | bytes 4718600 | tf_op jit(solution)/shard_map/ppermute | solution.py:300
  155.0 17.6 %collective-permute-start.19 = (bf16[768,512]{1,0:T(8,128)(2,1)S(1)}, bf16[768,512]{1,0:T(8,128)(2,1)S(1)}, u32[]{:S(2)}, u32[]{:S(2)}) collective-permute-start(bf16[768,512]{1,0:T(8,128)(2,1)S(1)} %slice.75), channel_id=1, source_target_pairs={{0,16},{4,20},{8,24},{12,28},{16,0},{20,4},{24,8},{28,12},{1,17},{... | collective-permute-start | bytes 2359304 | tf_op jit(solution)/shard_map/ppermute | solution.py:300
  155.3 18.6 %collective-permute-start.20 = (bf16[768,512]{1,0:T(8,128)(2,1)S(1)}, bf16[768,512]{1,0:T(8,128)(2,1)S(1)}, u32[]{:S(2)}, u32[]{:S(2)}) collective-permute-start(bf16[768,512]{1,0:T(8,128)(2,1)S(1)} %slice.76), channel_id=1, source_target_pairs={{0,8},{4,12},{8,0},{12,4},{16,24},{20,28},{24,16},{28,20},{1,9},{5... | collective-permute-start | bytes 2359304 | tf_op jit(solution)/shard_map/ppermute | solution.py:300
  161.8 44.6 %collective-permute-start.21 = (bf16[1024,768]{1,0:T(8,128)(2,1)}, bf16[1024,768]{1,0:T(8,128)(2,1)}, u32[]{:S(2)}, u32[]{:S(2)}) collective-permute-start(bf16[1024,768]{1,0:T(8,128)(2,1)} %get-tuple-element.128), channel_id=1, source_target_pairs={{0,16},{4,20},{8,24},{12,28},{16,0},{20,4},{24,8},{28,12},{1,17},{... | collective-permute-start | bytes 4718600 | tf_op jit(solution)/shard_map/ppermute | solution.py:300
  163.0 43.4 %collective-permute-start.22 = (bf16[1024,768]{1,0:T(8,128)(2,1)}, bf16[1024,768]{1,0:T(8,128)(2,1)}, u32[]{:S(2)}, u32[]{:S(2)}) collective-permute-start(bf16[1024,768]{1,0:T(8,128)(2,1)} %get-tuple-element.129), channel_id=1, source_target_pairs={{0,8},{4,12},{8,0},{12,4},{16,24},{20,28},{24,16},{28,20},{1,9},{5... | collective-permute-start | bytes 4718600 | tf_op jit(solution)/shard_map/ppermute | solution.py:300
  213.7 18.9 %collective-permute-start.25 = (bf16[512,768]{1,0:T(8,128)(2,1)}, bf16[512,768]{1,0:T(8,128)(2,1)}, u32[]{:S(2)}, u32[]{:S(2)}) collective-permute-start(bf16[512,768]{1,0:T(8,128)(2,1)} %get-tuple-element.139), channel_id=1, source_target_pairs={{0,8},{4,12},{8,0},{12,4},{16,24},{20,28},{24,16},{28,20},{1,9},{5... | collective-permute-start | bytes 2359304 | tf_op jit(solution)/shard_map/ppermute | solution.py:300
  214.2 18.6 %collective-permute-start.26 = (bf16[512,768]{1,0:T(8,128)(2,1)}, bf16[512,768]{1,0:T(8,128)(2,1)}, u32[]{:S(2)}, u32[]{:S(2)}) collective-permute-start(bf16[512,768]{1,0:T(8,128)(2,1)} %get-tuple-element.140), channel_id=1, source_target_pairs={{0,16},{4,20},{8,24},{12,28},{16,0},{20,4},{24,8},{28,12},{1,17},{... | collective-permute-start | bytes 2359304 | tf_op jit(solution)/shard_map/ppermute | solution.py:300
  225.0 41.4 %collective-permute-start.27 = (bf16[1024,768]{1,0:T(8,128)(2,1)}, bf16[1024,768]{1,0:T(8,128)(2,1)}, u32[]{:S(2)}, u32[]{:S(2)}) collective-permute-start(bf16[1024,768]{1,0:T(8,128)(2,1)} %get-tuple-element.146), channel_id=1, source_target_pairs={{0,8},{4,12},{8,0},{12,4},{16,24},{20,28},{24,16},{28,20},{1,9},{5... | collective-permute-start | bytes 4718600 | tf_op jit(solution)/shard_map/ppermute | solution.py:300
  226.1 40.4 %collective-permute-start.28 = (bf16[1024,768]{1,0:T(8,128)(2,1)}, bf16[1024,768]{1,0:T(8,128)(2,1)}, u32[]{:S(2)}, u32[]{:S(2)}) collective-permute-start(bf16[1024,768]{1,0:T(8,128)(2,1)} %get-tuple-element.147), channel_id=1, source_target_pairs={{0,16},{4,20},{8,24},{12,28},{16,0},{20,4},{24,8},{28,12},{1,17},{... | collective-permute-start | bytes 4718600 | tf_op jit(solution)/shard_map/ppermute | solution.py:300
  226.3 40.2 %collective-permute-start.29 = (bf16[3072,256]{1,0:T(8,128)(2,1)}, bf16[3072,256]{1,0:T(8,128)(2,1)}, u32[]{:S(2)}, u32[]{:S(2)}) collective-permute-start(bf16[3072,256]{1,0:T(8,128)(2,1)} %shard_map.120), channel_id=1, source_target_pairs={{0,2},{2,3},{3,1},{1,0},{4,6},{6,7},{7,5},{5,4},{8,10},{10,11},{11... | collective-permute-start | bytes 4718600 | tf_op jit(solution)/shard_map/ppermute | solution.py:318
  269.5 13.4 %collective-permute-start.30 = (bf16[3072,256]{1,0:T(8,128)(2,1)}, bf16[3072,256]{1,0:T(8,128)(2,1)}, u32[]{:S(2)}, u32[]{:S(2)}) collective-permute-start(bf16[3072,256]{1,0:T(8,128)(2,1)} %shard_map.123), channel_id=1, source_target_pairs={{0,4},{4,0},{8,12},{12,8},{16,20},{20,16},{24,28},{28,24},{1,5},{5... | collective-permute-start | bytes 4718600 | tf_op jit(solution)/shard_map/ppermute | solution.py:300
  271.5 11.5 %collective-permute-start.31 = (bf16[3072,256]{1,0:T(8,128)(2,1)}, bf16[3072,256]{1,0:T(8,128)(2,1)}, u32[]{:S(2)}, u32[]{:S(2)}) collective-permute-start(bf16[3072,256]{1,0:T(8,128)(2,1)} %shard_map.124), channel_id=1, source_target_pairs={{0,4},{4,0},{8,12},{12,8},{16,20},{20,16},{24,28},{28,24},{1,5},{5... | collective-permute-start | bytes 4718600 | tf_op jit(solution)/shard_map/ppermute | solution.py:300
  271.5 44.7 %collective-permute-start.32 = (bf16[3072,256]{1,0:T(8,128)(2,1)}, bf16[3072,256]{1,0:T(8,128)(2,1)}, u32[]{:S(2)}, u32[]{:S(2)}) collective-permute-start(bf16[3072,256]{1,0:T(8,128)(2,1)} %add_convert_fusion.3), channel_id=1, source_target_pairs={{0,2},{2,3},{3,1},{1,0},{4,6},{6,7},{7,5},{5,4},{8,10},{10,11},{11... | collective-permute-start | bytes 4718600 | tf_op jit(solution)/shard_map/ppermute | solution.py:318
  277.1 43.3 %collective-permute-start.33 = (bf16[1024,768]{0,1:T(8,128)(2,1)}, bf16[1024,768]{0,1:T(8,128)(2,1)}, u32[]{:S(2)}, u32[]{:S(2)}) collective-permute-start(bf16[1024,768]{0,1:T(8,128)(2,1)} %copy.12), channel_id=1, source_target_pairs={{0,8},{4,12},{8,0},{12,4},{16,24},{20,28},{24,16},{28,20},{1,9},{5... | collective-permute-start | bytes 4718600 | tf_op jit(solution)/shard_map/ppermute | solution.py:300
  280.8 39.5 %collective-permute-start.34 = (bf16[1024,768]{0,1:T(8,128)(2,1)}, bf16[1024,768]{0,1:T(8,128)(2,1)}, u32[]{:S(2)}, u32[]{:S(2)}) collective-permute-start(bf16[1024,768]{0,1:T(8,128)(2,1)} %copy.13), channel_id=1, source_target_pairs={{0,20},{4,16},{8,28},{12,24},{16,4},{20,0},{24,12},{28,8},{1,21},{... | collective-permute-start | bytes 4718600 | tf_op jit(solution)/shard_map/ppermute | solution.py:300
  322.0 35.8 %collective-permute-start.35 = (bf16[3072,256]{1,0:T(8,128)(2,1)}, bf16[3072,256]{1,0:T(8,128)(2,1)}, u32[]{:S(2)}, u32[]{:S(2)}) collective-permute-start(bf16[3072,256]{1,0:T(8,128)(2,1)} %add_convert_fusion.2), channel_id=1, source_target_pairs={{0,2},{2,3},{3,1},{1,0},{4,6},{6,7},{7,5},{5,4},{8,10},{10,11},{11... | collective-permute-start | bytes 4718600 | tf_op jit(solution)/shard_map/ppermute | solution.py:318
  325.0 37.9 %collective-permute-start.39 = (bf16[768,1024]{1,0:T(8,128)(2,1)}, bf16[768,1024]{1,0:T(8,128)(2,1)}, u32[]{:S(2)}, u32[]{:S(2)}) collective-permute-start(bf16[768,1024]{1,0:T(8,128)(2,1)} %copy-done.46), channel_id=1, source_target_pairs={{0,16},{4,20},{8,24},{12,28},{16,0},{20,4},{24,8},{28,12},{1,17},{... | collective-permute-start | bytes 4718600 | tf_op jit(solution)/shard_map/ppermute | solution.py:300
  325.2 37.7 %collective-permute-start.40 = (bf16[768,1024]{1,0:T(8,128)(2,1)}, bf16[768,1024]{1,0:T(8,128)(2,1)}, u32[]{:S(2)}, u32[]{:S(2)}) collective-permute-start(bf16[768,1024]{1,0:T(8,128)(2,1)} %copy-done.45), channel_id=1, source_target_pairs={{0,12},{4,8},{8,4},{12,0},{16,28},{20,24},{24,20},{28,16},{1,13},{... | collective-permute-start | bytes 4718600 | tf_op jit(solution)/shard_map/ppermute | solution.py:300
  (76 other events, 835.6 us)

commit v10 on v8

--- a/solution.py
+++ b/solution.py
@@ -474,27 +474,24 @@
     turned_pair, turned_value, late_value = together(turned_pair, turned_value, late_value)
     for step in range(2, 4):
         chosen[step], sent[step] = back_odd(step, turned_pair, turned_value)
-    ends_value = scatter_end(turned_value, first_value, 1, late_value)
     partial[1] = back_even(chosen[1], passed[1], BF)
     early_pair = messages(turned_pair, (2,), (5,))
     for step in range(1, n_mp - 1):
         if step == 1:
-            partial[1], early_pair, sent, far_pair, ends_value = together(
-                partial[1], early_pair, sent, far_pair, ends_value
-            )
+            partial[1], early_pair, sent = together(partial[1], early_pair, sent)
         elif step == 2:
-            partial[2], late_pair, early_pair, own_pair = together(
-                partial[2], late_pair, early_pair, own_pair
+            partial[2], late_pair, own_pair, ends_value = together(
+                partial[2], late_pair, own_pair, ends_value
             )
         message = (partial[step].astype(F32) + arrived.astype(F32)).astype(BF)
         if step == 1:
-            message, early_pair, sent, turned_pair, turned_value = together(
-                message, early_pair, sent, turned_pair, turned_value
+            message, early_pair, sent, turned_pair, turned_value, far_pair = together(
+                message, early_pair, sent, turned_pair, turned_value, far_pair
             )
             early_pair = send(early_pair, y=5)
         elif step == 2:
-            message, late_pair, own_pair, ends_value = together(
-                message, late_pair, own_pair, ends_value
+            message, late_pair, own_pair, ends_value, early_pair = together(
+                message, late_pair, own_pair, ends_value, early_pair
             )
             late_pair = send(late_pair, x=3)
             own_pair = [[even, swap(odd, 1)] for even, odd in own_pair]
@@ -517,6 +514,7 @@
             if step == 1:
                 late_pair = late_messages(turned_pair, far_pair)
                 own_pair = messages(turned_pair, (0,), (1,))
+                ends_value = scatter_end(turned_value, first_value, 1, late_value)
     out_value = place_call(core, ends_value[0], passed_value, cols, 0)
     here, there = {}, {}
     for r, (own_even, own_odd), (even_x, odd_y) in zip(blocks_of_four, own_pair, early_pair):

time: 377 us -> 376 us (level)
    unnamed x126 -> x122, local copies, waits for them, and re-layouts: 33 us -> 34.8 us
  transfers between devices with their start and end apart: 41 -> 41, of which waited for: 18 -> 18; matrix products, arithmetic and copies ran while one was open for 15% -> 16% of each run, Pallas kernels for 23% -> 22%
where the time goes in v10:
time: 376 us; the launch traced here: 370 us
  waiting for transfers between devices  133 us (35%)
  Pallas kernels  89.6 us (24%)
  local copies, waits for them, and re-layouts  54 us (14%)
  starting transfers between devices  48.6 us (13%)
  other arithmetic  22 us (6%)
  matrix products  20.7 us (6%)
    ppermute x35, waiting for transfers between devices, swap(): return lax.ppermute(array, 'dp', [(i, i ^ bit) for i in range(n_dp)])  75.3 us
    ppermute x6, waiting for transfers between devices, ring_on(): return lax.ppermute(array, 'mp', ring_pairs)  58.1 us
    pallas_call x7, Pallas kernels, product_call(): pl.pallas_call(functools.partial(product_kernel, n_add, turn), grid=(coun...  35.1 us
    unnamed x122, local copies, waits for them, and re-layouts  34.8 us
    ppermute x35, starting transfers between devices, swap(): return lax.ppermute(array, 'dp', [(i, i ^ bit) for i in range(n_dp)])  34.1 us
    pallas_call x8, Pallas kernels, back_call(): pl.pallas_call(back_kernel, grid=(units,), in_specs=[pl.BlockSpec(pair.sh...  26.6 us
    pallas_call x2, Pallas kernels, attention_call(): pl.pallas_call(kernel, grid=(tokens // PATCH,), in_specs=[pl.BlockSpec((P...  16 us
    ppermute x6, starting transfers between devices, ring_on(): return lax.ppermute(array, 'mp', ring_pairs)  14.5 us
  transfers between devices with their start and end apart: 41, of which 18 were waited for; matrix products, arithmetic and copies ran while one was open for 16% of the time, Pallas kernels for 22%

profile of v10, /device:TPU:1, one launch (start us, length us, event | category | flops | bytes accessed | tf_op | source)
XLA Modules:
  0.0 370.2 jit_solution(14665418954695167705)
XLA Ops:
  17.0 28.9 %collective-permute-done = bf16[768,1024]{1,0:T(8,128)(2,1)} collective-permute-done((bf16[768,1024]{1,0:T(8,128)(2,1)S(1)}, bf16[768,1024]{1,0:T(8,128)(2,1)}, u32[]{:S(2)}, u32[]{:S(2)}) %collective-permute-start) | collective-permute-done | bytes 1572896 | tf_op jit(solution)/shard_map/ppermute | solution.py:299
  65.1 16.6 %collective-permute-done.3 = bf16[768,1024]{1,0:T(8,128)(2,1)S(1)} collective-permute-done((bf16[768,1024]{1,0:T(8,128)(2,1)}, bf16[768,1024]{1,0:T(8,128)(2,1)S(1)}, u32[]{:S(2)}, u32[]{:S(2)}) %collective-permute-start.3) | collective-permute-done | bytes 1572896 | tf_op jit(solution)/shard_map/ppermute | solution.py:299
  95.5 31.4 %collective-permute-done.12 = bf16[256,3072]{1,0:T(8,128)(2,1)S(1)} collective-permute-done((bf16[256,3072]{1,0:T(8,128)(2,1)S(1)}, bf16[256,3072]{1,0:T(8,128)(2,1)S(1)}, u32[]{:S(2)}, u32[]{:S(2)}) %collective-permute-start.12) | collective-permute-done | bytes 1572896 | tf_op jit(solution)/shard_map/ppermute | solution.py:317
  131.5 13.1 %fusion.4.qk_ref = f32[1024,1024]{1,0:T(8,128)S(1)} fusion(bf16[1024,6144]{1,0:T(8,128)(2,1)S(1)} %slice_dynamic-update-slice_fusion.refs_0_.refs_1_, bf16[6144,1024]{1,0:T(8,128)(2,1)S(1)} %constant_dynamic-update-slice_fusion.w_pair_ref), kind=kOutput, calls=%fused_computation.96 | convolution fusion | flops 12884901888 | bytes 29360128 | tf_op jit(solution)/shard_map/dot_general | solution.py:398
  144.6 5.9 %shard_map.113.turned_ref = bf16[512,1024]{1,0:T(8,128)(2,1)S(1)} custom-call(f32[1024,1024]{1,0:T(8,128)S(1)} %fusion.4.qk_ref, bf16[1024,512]{1,0:T(8,128)(2,1)S(1)} %constant_dynamic-update-slice_fusion.12.g_ref, f32[2,128]{1,0:T(2,128)S(1)} %pad_maximum_fusion.13.gains_ref), custom_call_target="tpu_custom_call" | custom-call | flops 178956976 | bytes 1398101 | tf_op jit(solution)/shard_map/pallas_call | solution.py:95
  150.6 4.6 %collective-permute-done.17 = bf16[1536,512]{1,0:T(8,128)(2,1)} collective-permute-done((bf16[1536,512]{1,0:T(8,128)(2,1)S(1)}, bf16[1536,512]{1,0:T(8,128)(2,1)}, u32[]{:S(2)}, u32[]{:S(2)}) %collective-permute-start.17) | collective-permute-done | bytes 1572896 | tf_op jit(solution)/shard_map/ppermute | solution.py:299
  159.3 6.1 %shard_map.116 = (bf16[1024,768]{1,0:T(8,128)(2,1)}, bf16[1024,768]{1,0:T(8,128)(2,1)}) custom-call(bf16[512,1024]{1,0:T(8,128)(2,1)S(1)} %shard_map.113.turned_ref, bf16[1024,6144]{1,0:T(8,128)(2,1)S(1)} %slice_dynamic-update-slice_fusion.refs_0_.refs_1_, bf16[1024,6144]{1,0:T(8,128)(2,1)S(1)} %slice_dynamic-update-slice_fusion.refs_0_.refs_1_), custom_call_target="tpu_custom_call" | custom-call | flops 536870912 | bytes 1485482 | tf_op jit(solution)/shard_map/pallas_call | solution.py:133
  169.0 6.5 %collective-permute-done.19 = bf16[768,512]{1,0:T(8,128)(2,1)S(1)} collective-permute-done((bf16[768,512]{1,0:T(8,128)(2,1)S(1)}, bf16[768,512]{1,0:T(8,128)(2,1)S(1)}, u32[]{:S(2)}, u32[]{:S(2)}) %collective-permute-start.19) | collective-permute-done | bytes 786464 | tf_op jit(solution)/shard_map/ppermute | solution.py:299
  176.9 7.6 %convolution_convert_fusion.v_ref = bf16[1024,512]{1,0:T(8,128)(2,1)} fusion(bf16[1024,6144]{1,0:T(8,128)(2,1)S(1)} %slice_dynamic-update-slice_fusion.refs_0_.refs_1_, bf16[6144,512]{1,0:T(8,128)(2,1)S(1)} %constant_dynamic-update-slice_fusion.8.w_value_ref), kind=kOutput, calls=%fused_computation.16 | convolution fusion | flops 6442975232 | bytes 19922944 | tf_op jit(solution)/shard_map/dot_general | solution.py:445
  189.2 10.0 %shard_map.114.turned_ref = bf16[1024,1024]{1,0:T(8,128)(2,1)S(1)} custom-call(f32[1024,1024]{1,0:T(8,128)S(1)} %copy-done.14, bf16[1024,512]{1,0:T(8,128)(2,1)S(1)} %copy-done.18, bf16[1024,512]{1,0:T(8,128)(2,1)S(1)} %copy-done.28, f32[2,128]{1,0:T(2,128)S(1)} %pad_maximum_fusion.13.gains_ref), custom_call_target="tpu_custom_call" | custom-call | flops 178956976 | bytes 2097152 | tf_op jit(solution)/shard_map/pallas_call | solution.py:95
  199.6 3.2 shard_map.118
  202.9 3.2 shard_map.119
  206.1 3.2 collective-permute-done.21.refs_2_.refs_4_
  209.8 4.7 %shard_map.117 = (bf16[512,768]{1,0:T(8,128)(2,1)}, bf16[512,768]{1,0:T(8,128)(2,1)}) custom-call(bf16[512,1024]{1,0:T(8,128)(2,1)S(1)} %copy-done.11, bf16[1024,6144]{1,0:T(8,128)(2,1)S(1)} %slice_dynamic-update-slice_fusion.refs_0_.refs_1_, bf16[1024,6144]{1,0:T(8,128)(2,1)S(1)} %slice_dynamic-update-slice_fusion.refs_0_.refs_1_, ...), custom_call_target="tpu_custom_call" | custom-call | flops 268435456 | bytes 1223338 | tf_op jit(solution)/shard_map/pallas_call | solution.py:133
  218.8 4.8 %shard_map.115 = (bf16[1024,768]{1,0:T(8,128)(2,1)S(1)}, bf16[1024,768]{1,0:T(8,128)(2,1)S(1)}) custom-call(bf16[1024,1024]{1,0:T(8,128)(2,1)S(1)} %shard_map.114.turned_ref, bf16[1024,6144]{1,0:T(8,128)(2,1)S(1)} %slice_dynamic-update-slice_fusion.refs_0_.refs_1_, bf16[1024,6144]{1,0:T(8,128)(2,1)S(1)} %slice_dynamic-update-slice_fusion.refs_0_.refs_1_), custom_call_target="tpu_custom_call" | custom-call | flops 536870912 | bytes 1398101 | tf_op jit(solution)/shard_map/pallas_call | solution.py:133
  223.7 4.4 %shard_map.120 = bf16[3072,256]{1,0:T(8,128)(2,1)} custom-call(bf16[1024,256]{1,0:T(8,128)(2,1)S(1)} %pad_maximum_fusion.5.pair_ref, bf16[512,256]{1,0:T(8,128)(2,1)S(1)} %copy-done.24, bf16[6144,1024]{1,0:T(8,128)(2,1)S(1)} %constant_dynamic-update-slice_fusion.w_pair_ref, bf16[6144,512]{1,0:T(8,128)(2,1)S(1)} %constant_dynamic-update-slice_fusion.8.w_value_ref, ...), custom_call_target="tpu_custom_call" | custom-call | flops 402653184 | bytes 2359296 | tf_op jit(solution)/shard_map/pallas_call | solution.py:164
  230.5 5.2 %collective-permute-done.25.refs_5_ = bf16[512,768]{1,0:T(8,128)(2,1)} collective-permute-done((bf16[512,768]{1,0:T(8,128)(2,1)}, bf16[512,768]{1,0:T(8,128)(2,1)}, u32[]{:S(2)}, u32[]{:S(2)}) %collective-permute-start.25) | collective-permute-done | bytes 786464 | tf_op jit(solution)/shard_map/ppermute | solution.py:299
  238.9 4.6 %copy-done.3 = bf16[6144,1024]{1,0:T(8,128)(2,1)S(1)} copy-done((bf16[6144,1024]{1,0:T(8,128)(2,1)S(1)}, bf16[6144,1024]{1,0:T(8,128)(2,1)}, u32[]{:S(2)}) %copy-start.3) | copy-done | bytes 12582936
  248.6 3.2 shard_map.121
  257.1 3.1 shard_map.124
  260.3 4.5 %shard_map.122 = (bf16[1024,768]{1,0:T(8,128)(2,1)S(1)}, bf16[1024,768]{1,0:T(8,128)(2,1)S(1)}) custom-call(bf16[1024,1024]{1,0:T(8,128)(2,1)S(1)} %copy-done.9, bf16[1024,6144]{1,0:T(8,128)(2,1)S(1)} %bitcast.12, bf16[1024,6144]{1,0:T(8,128)(2,1)S(1)} %bitcast.12), custom_call_target="tpu_custom_call" | custom-call | flops 536870912 | bytes 1398101 | tf_op jit(solution)/shard_map/pallas_call | solution.py:133
  266.4 4.6 %collective-permute-done.28.refs_3_ = bf16[1024,768]{1,0:T(8,128)(2,1)S(1)} collective-permute-done((bf16[1024,768]{1,0:T(8,128)(2,1)}, bf16[1024,768]{1,0:T(8,128)(2,1)S(1)}, u32[]{:S(2)}, u32[]{:S(2)}) %collective-permute-start.28) | collective-permute-done | bytes 1572896 | tf_op jit(solution)/shard_map/ppermute | solution.py:299
  285.1 3.2 shard_map.126
  288.3 5.2 %shard_map.129 = (bf16[768,512]{1,0:T(8,128)(2,1)S(1)}, bf16[768,512]{1,0:T(8,128)(2,1)}) custom-call(bf16[512,1024]{1,0:T(8,128)(2,1)S(1)} %copy-done.12, bf16[1024,6144]{1,0:T(8,128)(2,1)S(1)} %bitcast.12, bf16[1024,6144]{1,0:T(8,128)(2,1)S(1)} %bitcast.12, bf16[1024,768]{1,0:T(8,128)(2,1)} %collective-permute-done.22.refs_3_.refs_2_, ...), custom_call_target="tpu_custom_call" | custom-call | flops 268435456 | bytes 1485482 | tf_op jit(solution)/shard_map/pallas_call | solution.py:133
  294.4 5.1 %shard_map.128 = (bf16[1024,768]{1,0:T(8,128)(2,1)S(1)}, bf16[1024,768]{1,0:T(8,128)(2,1)}) custom-call(bf16[1024,1024]{1,0:T(8,128)(2,1)S(1)} %copy-done.9, bf16[1024,6144]{1,0:T(8,128)(2,1)S(1)} %bitcast.12, bf16[1024,6144]{1,0:T(8,128)(2,1)S(1)} %bitcast.12), custom_call_target="tpu_custom_call" | custom-call | flops 536870912 | bytes 1398101 | tf_op jit(solution)/shard_map/pallas_call | solution.py:133
  300.7 4.7 %shard_map.127 = (bf16[1024,768]{1,0:T(8,128)(2,1)S(1)}, bf16[1024,768]{1,0:T(8,128)(2,1)S(1)}) custom-call(bf16[1024,1024]{1,0:T(8,128)(2,1)S(1)} %copy-done.9, bf16[1024,6144]{1,0:T(8,128)(2,1)S(1)} %bitcast.12, bf16[1024,6144]{1,0:T(8,128)(2,1)S(1)} %bitcast.12, bf16[1024,768]{1,0:T(8,128)(2,1)S(1)} %collective-permute-done.29.refs_2_, ...), custom_call_target="tpu_custom_call" | custom-call | flops 536870912 | bytes 1922389 | tf_op jit(solution)/shard_map/pallas_call | solution.py:133
  305.4 4.3 %collective-permute-done.32 = bf16[3072,256]{1,0:T(8,128)(2,1)} collective-permute-done((bf16[3072,256]{1,0:T(8,128)(2,1)}, bf16[3072,256]{1,0:T(8,128)(2,1)}, u32[]{:S(2)}, u32[]{:S(2)}) %collective-permute-start.32) | collective-permute-done | bytes 1572896 | tf_op jit(solution)/shard_map/ppermute | solution.py:317
  320.0 3.4 add_convert_fusion.1.refs_0_
  326.0 3.4 add_convert_fusion.refs_2_
  329.4 22.0 %collective-permute-done.35 = bf16[3072,256]{1,0:T(8,128)(2,1)} collective-permute-done((bf16[3072,256]{1,0:T(8,128)(2,1)}, bf16[3072,256]{1,0:T(8,128)(2,1)}, u32[]{:S(2)}, u32[]{:S(2)}) %collective-permute-start.35) | collective-permute-done | bytes 1572896 | tf_op jit(solution)/shard_map/ppermute | solution.py:317
  358.7 6.1 %shard_map.131 = (bf16[768,1024]{1,0:T(8,128)(2,1)}, bf16[768,1024]{1,0:T(8,128)(2,1)}) custom-call(s32[1]{0:T(128)} %bitcast.3.core_ref, bf16[1024,768]{1,0:T(8,128)(2,1)S(1)} %copy-done.19, bf16[1024,768]{1,0:T(8,128)(2,1)} %collective-permute-done.39.refs_1_, bf16[1024,768]{1,0:T(8,128)(2,1)S(1)} %copy-done.20, ...), custom_call_target="tpu_custom_call" | custom-call | tf_op jit(solution)/shard_map/pallas_call | solution.py:213
  366.6 3.4 shard_map.132
  (253 shorter events, 128.1 us)
Async XLA Ops:
  8.4 37.5 %collective-permute-start = (bf16[768,1024]{1,0:T(8,128)(2,1)S(1)}, bf16[768,1024]{1,0:T(8,128)(2,1)}, u32[]{:S(2)}, u32[]{:S(2)}) collective-permute-start(bf16[768,1024]{1,0:T(8,128)(2,1)S(1)} %pad_maximum_fusion), channel_id=1, source_target_pairs={{0,8},{4,12},{8,0},{12,4},{16,24},{20,28},{24,16},{28,20},{1,9},{5... | collective-permute-start | bytes 4718600 | tf_op jit(solution)/shard_map/ppermute | solution.py:299
  11.1 35.7 %collective-permute-start.1 = (bf16[768,1024]{1,0:T(8,128)(2,1)S(1)}, bf16[768,1024]{1,0:T(8,128)(2,1)}, u32[]{:S(2)}, u32[]{:S(2)}) collective-permute-start(bf16[768,1024]{1,0:T(8,128)(2,1)S(1)} %pad_maximum_fusion), channel_id=1, source_target_pairs={{0,16},{4,20},{8,24},{12,28},{16,0},{20,4},{24,8},{28,12},{1,17},{... | collective-permute-start | bytes 4718600 | tf_op jit(solution)/shard_map/ppermute | solution.py:299
  12.3 34.5 %collective-permute-start.2 = (bf16[768,1024]{1,0:T(8,128)(2,1)}, bf16[768,1024]{1,0:T(8,128)(2,1)}, u32[]{:S(2)}, u32[]{:S(2)}) collective-permute-start(bf16[768,1024]{1,0:T(8,128)(2,1)} %pad_maximum_fusion.1), channel_id=1, source_target_pairs={{0,4},{4,0},{8,12},{12,8},{16,20},{20,16},{24,28},{28,24},{1,5},{5... | collective-permute-start | bytes 4718600 | tf_op jit(solution)/shard_map/ppermute | solution.py:299
  14.3 36.5 %collective-permute-start.7 = (bf16[256,3072]{1,0:T(8,128)(2,1)}, bf16[256,3072]{1,0:T(8,128)(2,1)}, u32[]{:S(2)}, u32[]{:S(2)}) collective-permute-start(bf16[256,3072]{1,0:T(8,128)(2,1)} %pad_maximum_fusion.2), channel_id=1, source_target_pairs={{0,2},{2,3},{3,1},{1,0},{4,6},{6,7},{7,5},{5,4},{8,10},{10,11},{11... | collective-permute-start | bytes 4718600 | tf_op jit(solution)/shard_map/ppermute | solution.py:317
  16.7 38.0 %collective-permute-start.6 = (bf16[256,3072]{1,0:T(8,128)(2,1)}, bf16[256,3072]{1,0:T(8,128)(2,1)}, u32[]{:S(2)}, u32[]{:S(2)}) collective-permute-start(bf16[256,3072]{1,0:T(8,128)(2,1)} %pad_maximum_fusion.2), channel_id=1, source_target_pairs={{0,4},{4,0},{8,12},{12,8},{16,20},{20,16},{24,28},{28,24},{1,5},{5... | collective-permute-start | bytes 4718600 | tf_op jit(solution)/shard_map/ppermute | solution.py:299
  46.9 34.9 %collective-permute-start.3 = (bf16[768,1024]{1,0:T(8,128)(2,1)}, bf16[768,1024]{1,0:T(8,128)(2,1)S(1)}, u32[]{:S(2)}, u32[]{:S(2)}) collective-permute-start(bf16[768,1024]{1,0:T(8,128)(2,1)} %collective-permute-done.2), channel_id=1, source_target_pairs={{0,8},{4,12},{8,0},{12,4},{16,24},{20,28},{24,16},{28,20},{1,9},{5... | collective-permute-start | bytes 4718600 | tf_op jit(solution)/shard_map/ppermute | solution.py:299
  47.2 34.9 %collective-permute-start.4 = (bf16[768,1024]{1,0:T(8,128)(2,1)}, bf16[768,1024]{1,0:T(8,128)(2,1)S(1)}, u32[]{:S(2)}, u32[]{:S(2)}) collective-permute-start(bf16[768,1024]{1,0:T(8,128)(2,1)} %collective-permute-done.2), channel_id=1, source_target_pairs={{0,16},{4,20},{8,24},{12,28},{16,0},{20,4},{24,8},{28,12},{1,17},{... | collective-permute-start | bytes 4718600 | tf_op jit(solution)/shard_map/ppermute | solution.py:299
  50.8 12.4 %collective-permute-start.8 = (bf16[256,3072]{1,0:T(8,128)(2,1)}, bf16[256,3072]{1,0:T(8,128)(2,1)S(1)}, u32[]{:S(2)}, u32[]{:S(2)}) collective-permute-start(bf16[256,3072]{1,0:T(8,128)(2,1)} %collective-permute-done.7), channel_id=1, source_target_pairs={{0,4},{4,0},{8,12},{12,8},{16,20},{20,16},{24,28},{28,24},{1,5},{5... | collective-permute-start | bytes 4718600 | tf_op jit(solution)/shard_map/ppermute | solution.py:299
  52.1 38.8 %collective-permute-start.10 = (bf16[256,3072]{1,0:T(8,128)(2,1)}, bf16[256,3072]{1,0:T(8,128)(2,1)S(1)}, u32[]{:S(2)}, u32[]{:S(2)}) collective-permute-start(bf16[256,3072]{1,0:T(8,128)(2,1)} %collective-permute-done.7), channel_id=1, source_target_pairs={{0,2},{2,3},{3,1},{1,0},{4,6},{6,7},{7,5},{5,4},{8,10},{10,11},{11... | collective-permute-start | bytes 4718600 | tf_op jit(solution)/shard_map/ppermute | solution.py:317
  82.3 11.4 %collective-permute-start.9 = (bf16[768,512]{1,0:T(8,128)(2,1)S(1)}, bf16[768,512]{1,0:T(8,128)(2,1)S(1)}, u32[]{:S(2)}, u32[]{:S(2)}) collective-permute-start(bf16[768,512]{1,0:T(8,128)(2,1)S(1)} %get-tuple-element.215), channel_id=1, source_target_pairs={{0,4},{4,0},{8,12},{12,8},{16,20},{20,16},{24,28},{28,24},{1,5},{5... | collective-permute-start | bytes 2359304 | tf_op jit(solution)/shard_map/ppermute | solution.py:299
  84.4 43.8 %collective-permute-start.14 = (bf16[768,1024]{1,0:T(8,128)(2,1)}, bf16[768,1024]{1,0:T(8,128)(2,1)S(1)}, u32[]{:S(2)}, u32[]{:S(2)}) collective-permute-start(bf16[768,1024]{1,0:T(8,128)(2,1)} %collective-permute-done), channel_id=1, source_target_pairs={{0,16},{4,20},{8,24},{12,28},{16,0},{20,4},{24,8},{28,12},{1,17},{... | collective-permute-start | bytes 4718600 | tf_op jit(solution)/shard_map/ppermute | solution.py:299
  85.7 44.5 %collective-permute-start.15 = (bf16[768,1024]{1,0:T(8,128)(2,1)S(1)}, bf16[768,1024]{1,0:T(8,128)(2,1)S(1)}, u32[]{:S(2)}, u32[]{:S(2)}) collective-permute-start(bf16[768,1024]{1,0:T(8,128)(2,1)S(1)} %collective-permute-done.4), channel_id=1, source_target_pairs={{0,8},{4,12},{8,0},{12,4},{16,24},{20,28},{24,16},{28,20},{1,9},{5... | collective-permute-start | bytes 4718600 | tf_op jit(solution)/shard_map/ppermute | solution.py:299
  91.1 35.8 %collective-permute-start.12 = (bf16[256,3072]{1,0:T(8,128)(2,1)S(1)}, bf16[256,3072]{1,0:T(8,128)(2,1)S(1)}, u32[]{:S(2)}, u32[]{:S(2)}) collective-permute-start(bf16[256,3072]{1,0:T(8,128)(2,1)S(1)} %collective-permute-done.10), channel_id=1, source_target_pairs={{0,2},{2,3},{3,1},{1,0},{4,6},{6,7},{7,5},{5,4},{8,10},{10,11},{11... | collective-permute-start | bytes 4718600 | tf_op jit(solution)/shard_map/ppermute | solution.py:317
  94.5 60.7 %collective-permute-start.17 = (bf16[1536,512]{1,0:T(8,128)(2,1)S(1)}, bf16[1536,512]{1,0:T(8,128)(2,1)}, u32[]{:S(2)}, u32[]{:S(2)}) collective-permute-start(bf16[1536,512]{1,0:T(8,128)(2,1)S(1)} %pad_maximum_fusion.3), channel_id=1, source_target_pairs={{0,8},{4,12},{8,0},{12,4},{16,24},{20,28},{24,16},{28,20},{1,9},{5... | collective-permute-start | bytes 4718600 | tf_op jit(solution)/shard_map/ppermute | solution.py:299
  95.3 59.9 %collective-permute-start.18 = (bf16[1536,512]{1,0:T(8,128)(2,1)S(1)}, bf16[1536,512]{1,0:T(8,128)(2,1)}, u32[]{:S(2)}, u32[]{:S(2)}) collective-permute-start(bf16[1536,512]{1,0:T(8,128)(2,1)S(1)} %pad_maximum_fusion.3), channel_id=1, source_target_pairs={{0,16},{4,20},{8,24},{12,28},{16,0},{20,4},{24,8},{28,12},{1,17},{... | collective-permute-start | bytes 4718600 | tf_op jit(solution)/shard_map/ppermute | solution.py:299
  157.5 17.9 %collective-permute-start.19 = (bf16[768,512]{1,0:T(8,128)(2,1)S(1)}, bf16[768,512]{1,0:T(8,128)(2,1)S(1)}, u32[]{:S(2)}, u32[]{:S(2)}) collective-permute-start(bf16[768,512]{1,0:T(8,128)(2,1)S(1)} %slice.75), channel_id=1, source_target_pairs={{0,16},{4,20},{8,24},{12,28},{16,0},{20,4},{24,8},{28,12},{1,17},{... | collective-permute-start | bytes 2359304 | tf_op jit(solution)/shard_map/ppermute | solution.py:299
  158.1 18.7 %collective-permute-start.20 = (bf16[768,512]{1,0:T(8,128)(2,1)S(1)}, bf16[768,512]{1,0:T(8,128)(2,1)S(1)}, u32[]{:S(2)}, u32[]{:S(2)}) collective-permute-start(bf16[768,512]{1,0:T(8,128)(2,1)S(1)} %slice.76), channel_id=1, source_target_pairs={{0,8},{4,12},{8,0},{12,4},{16,24},{20,28},{24,16},{28,20},{1,9},{5... | collective-permute-start | bytes 2359304 | tf_op jit(solution)/shard_map/ppermute | solution.py:299
  165.4 43.9 %collective-permute-start.21 = (bf16[1024,768]{1,0:T(8,128)(2,1)}, bf16[1024,768]{1,0:T(8,128)(2,1)}, u32[]{:S(2)}, u32[]{:S(2)}) collective-permute-start(bf16[1024,768]{1,0:T(8,128)(2,1)} %get-tuple-element.130), channel_id=1, source_target_pairs={{0,16},{4,20},{8,24},{12,28},{16,0},{20,4},{24,8},{28,12},{1,17},{... | collective-permute-start | bytes 4718600 | tf_op jit(solution)/shard_map/ppermute | solution.py:299
  166.4 43.5 %collective-permute-start.22 = (bf16[1024,768]{1,0:T(8,128)(2,1)}, bf16[1024,768]{1,0:T(8,128)(2,1)}, u32[]{:S(2)}, u32[]{:S(2)}) collective-permute-start(bf16[1024,768]{1,0:T(8,128)(2,1)} %get-tuple-element.131), channel_id=1, source_target_pairs={{0,8},{4,12},{8,0},{12,4},{16,24},{20,28},{24,16},{28,20},{1,9},{5... | collective-permute-start | bytes 4718600 | tf_op jit(solution)/shard_map/ppermute | solution.py:299
  216.7 19.0 %collective-permute-start.25 = (bf16[512,768]{1,0:T(8,128)(2,1)}, bf16[512,768]{1,0:T(8,128)(2,1)}, u32[]{:S(2)}, u32[]{:S(2)}) collective-permute-start(bf16[512,768]{1,0:T(8,128)(2,1)} %get-tuple-element.141), channel_id=1, source_target_pairs={{0,8},{4,12},{8,0},{12,4},{16,24},{20,28},{24,16},{28,20},{1,9},{5... | collective-permute-start | bytes 2359304 | tf_op jit(solution)/shard_map/ppermute | solution.py:299
  217.8 18.7 %collective-permute-start.26 = (bf16[512,768]{1,0:T(8,128)(2,1)}, bf16[512,768]{1,0:T(8,128)(2,1)}, u32[]{:S(2)}, u32[]{:S(2)}) collective-permute-start(bf16[512,768]{1,0:T(8,128)(2,1)} %get-tuple-element.142), channel_id=1, source_target_pairs={{0,16},{4,20},{8,24},{12,28},{16,0},{20,4},{24,8},{28,12},{1,17},{... | collective-permute-start | bytes 2359304 | tf_op jit(solution)/shard_map/ppermute | solution.py:299
  228.1 36.7 %collective-permute-start.27 = (bf16[3072,256]{1,0:T(8,128)(2,1)}, bf16[3072,256]{1,0:T(8,128)(2,1)S(1)}, u32[]{:S(2)}, u32[]{:S(2)}) collective-permute-start(bf16[3072,256]{1,0:T(8,128)(2,1)} %shard_map.120), channel_id=1, source_target_pairs={{0,2},{2,3},{3,1},{1,0},{4,6},{6,7},{7,5},{5,4},{8,10},{10,11},{11... | collective-permute-start | bytes 4718600 | tf_op jit(solution)/shard_map/ppermute | solution.py:317
  236.5 34.5 %collective-permute-start.28 = (bf16[1024,768]{1,0:T(8,128)(2,1)}, bf16[1024,768]{1,0:T(8,128)(2,1)S(1)}, u32[]{:S(2)}, u32[]{:S(2)}) collective-permute-start(bf16[1024,768]{1,0:T(8,128)(2,1)} %copy-done.34), channel_id=1, source_target_pairs={{0,8},{4,12},{8,0},{12,4},{16,24},{20,28},{24,16},{28,20},{1,9},{5... | collective-permute-start | bytes 4718600 | tf_op jit(solution)/shard_map/ppermute | solution.py:299
  236.8 34.2 %collective-permute-start.29 = (bf16[1024,768]{1,0:T(8,128)(2,1)}, bf16[1024,768]{1,0:T(8,128)(2,1)S(1)}, u32[]{:S(2)}, u32[]{:S(2)}) collective-permute-start(bf16[1024,768]{1,0:T(8,128)(2,1)} %copy-done.33), channel_id=1, source_target_pairs={{0,16},{4,20},{8,24},{12,28},{16,0},{20,4},{24,8},{28,12},{1,17},{... | collective-permute-start | bytes 4718600 | tf_op jit(solution)/shard_map/ppermute | solution.py:299
  273.9 35.9 %collective-permute-start.32 = (bf16[3072,256]{1,0:T(8,128)(2,1)}, bf16[3072,256]{1,0:T(8,128)(2,1)}, u32[]{:S(2)}, u32[]{:S(2)}) collective-permute-start(bf16[3072,256]{1,0:T(8,128)(2,1)} %add_convert_fusion.3), channel_id=1, source_target_pairs={{0,2},{2,3},{3,1},{1,0},{4,6},{6,7},{7,5},{5,4},{8,10},{10,11},{11... | collective-permute-start | bytes 4718600 | tf_op jit(solution)/shard_map/ppermute | solution.py:317
  276.2 36.6 %collective-permute-start.33 = (bf16[1024,768]{1,0:T(8,128)(2,1)S(1)}, bf16[1024,768]{1,0:T(8,128)(2,1)}, u32[]{:S(2)}, u32[]{:S(2)}) collective-permute-start(bf16[1024,768]{1,0:T(8,128)(2,1)S(1)} %get-tuple-element.184), channel_id=1, source_target_pairs={{0,8},{4,12},{8,0},{12,4},{16,24},{20,28},{24,16},{28,20},{1,9},{5... | collective-permute-start | bytes 4718600 | tf_op jit(solution)/shard_map/ppermute | solution.py:299
  277.3 37.0 %collective-permute-start.34 = (bf16[1024,768]{1,0:T(8,128)(2,1)S(1)}, bf16[1024,768]{1,0:T(8,128)(2,1)}, u32[]{:S(2)}, u32[]{:S(2)}) collective-permute-start(bf16[1024,768]{1,0:T(8,128)(2,1)S(1)} %get-tuple-element.185), channel_id=1, source_target_pairs={{0,20},{4,16},{8,28},{12,24},{16,4},{20,0},{24,12},{28,8},{1,21},{... | collective-permute-start | bytes 4718600 | tf_op jit(solution)/shard_map/ppermute | solution.py:299
  314.3 11.7 %collective-permute-start.37 = (bf16[1024,768]{1,0:T(8,128)(2,1)}, bf16[1024,768]{1,0:T(8,128)(2,1)}, u32[]{:S(2)}, u32[]{:S(2)}) collective-permute-start(bf16[1024,768]{1,0:T(8,128)(2,1)} %get-tuple-element.191), channel_id=1, source_target_pairs={{0,4},{4,0},{8,12},{12,8},{16,20},{20,16},{24,28},{28,24},{1,5},{5... | collective-permute-start | bytes 4718600 | tf_op jit(solution)/shard_map/ppermute | solution.py:299
  314.9 36.4 %collective-permute-start.35 = (bf16[3072,256]{1,0:T(8,128)(2,1)}, bf16[3072,256]{1,0:T(8,128)(2,1)}, u32[]{:S(2)}, u32[]{:S(2)}) collective-permute-start(bf16[3072,256]{1,0:T(8,128)(2,1)} %add_convert_fusion.2), channel_id=1, source_target_pairs={{0,2},{2,3},{3,1},{1,0},{4,6},{6,7},{7,5},{5,4},{8,10},{10,11},{11... | collective-permute-start | bytes 4718600 | tf_op jit(solution)/shard_map/ppermute | solution.py:317
  317.6 38.2 %collective-permute-start.39 = (bf16[1024,768]{1,0:T(8,128)(2,1)}, bf16[1024,768]{1,0:T(8,128)(2,1)}, u32[]{:S(2)}, u32[]{:S(2)}) collective-permute-start(bf16[1024,768]{1,0:T(8,128)(2,1)} %copy-done.36), channel_id=1, source_target_pairs={{0,16},{4,20},{8,24},{12,28},{16,0},{20,4},{24,8},{28,12},{1,17},{... | collective-permute-start | bytes 4718600 | tf_op jit(solution)/shard_map/ppermute | solution.py:299
  318.6 37.3 %collective-permute-start.40 = (bf16[1024,768]{1,0:T(8,128)(2,1)}, bf16[1024,768]{1,0:T(8,128)(2,1)}, u32[]{:S(2)}, u32[]{:S(2)}) collective-permute-start(bf16[1024,768]{1,0:T(8,128)(2,1)} %copy-done.35), channel_id=1, source_target_pairs={{0,12},{4,8},{8,4},{12,0},{16,28},{20,24},{24,20},{28,16},{1,13},{... | collective-permute-start | bytes 4718600 | tf_op jit(solution)/shard_map/ppermute | solution.py:299
  354.8 10.1 %collective-permute-start.38 = (bf16[3072,128]{1,0:T(8,128)(2,1)S(1)}, bf16[3072,128]{1,0:T(8,128)(2,1)S(1)}, u32[]{:S(2)}, u32[]{:S(2)}) collective-permute-start(bf16[3072,128]{1,0:T(8,128)(2,1)S(1)} %dynamic-slice_convert_fusion), channel_id=1, source_target_pairs={{0,4},{4,0},{8,12},{12,8},{16,20},{20,16},{24,28},{28,24},{1,5},{5... | collective-permute-start | bytes 2359304 | tf_op jit(solution)/shard_map/ppermute | solution.py:299
  (63 other events, 760.7 us)

commit v11 on v10

--- a/solution.py
+++ b/solution.py
@@ -190,7 +190,7 @@
         for block in blocks[1:]:
             total = total + block[...].astype(F32)
         for k, out in enumerate(outs):
-            out[...] = total[k * cols : (k + 1) * cols].T.astype(BF)
+            out[...] = total[k * cols : (k + 1) * cols].astype(BF).T
 
     @pl.when(here)
     def _():

time: 376 us -> 376 us (level)
  no operation moved by 1% of the time
where the time goes in v11:
time: 376 us; the launch traced here: 370 us
  waiting for transfers between devices  133 us (35%)
  Pallas kernels  89.6 us (24%)
  local copies, waits for them, and re-layouts  54 us (14%)
  starting transfers between devices  48.6 us (13%)
  other arithmetic  22 us (6%)
  matrix products  20.7 us (6%)
    ppermute x35, waiting for transfers between devices, swap(): return lax.ppermute(array, 'dp', [(i, i ^ bit) for i in range(n_dp)])  75.3 us
    ppermute x6, waiting for transfers between devices, ring_on(): return lax.ppermute(array, 'mp', ring_pairs)  58.1 us
    pallas_call x7, Pallas kernels, product_call(): pl.pallas_call(functools.partial(product_kernel, n_add, turn), grid=(coun...  35.1 us
    unnamed x122, local copies, waits for them, and re-layouts  34.8 us
    ppermute x35, starting transfers between devices, swap(): return lax.ppermute(array, 'dp', [(i, i ^ bit) for i in range(n_dp)])  34.1 us
    pallas_call x8, Pallas kernels, back_call(): pl.pallas_call(back_kernel, grid=(units,), in_specs=[pl.BlockSpec(pair.sh...  26.6 us
    pallas_call x2, Pallas kernels, attention_call(): pl.pallas_call(kernel, grid=(tokens // PATCH,), in_specs=[pl.BlockSpec((P...  16 us
    ppermute x6, starting transfers between devices, ring_on(): return lax.ppermute(array, 'mp', ring_pairs)  14.5 us
  transfers between devices with their start and end apart: 41, of which 18 were waited for; matrix products, arithmetic and copies ran while one was open for 16% of the time, Pallas kernels for 22%

profile of v11, /device:TPU:1, one launch (start us, length us, event | category | flops | bytes accessed | tf_op | source)
XLA Modules:
  0.0 370.2 jit_solution(8232891584562377312)
XLA Ops:
  17.0 28.9 %collective-permute-done = bf16[768,1024]{1,0:T(8,128)(2,1)} collective-permute-done((bf16[768,1024]{1,0:T(8,128)(2,1)S(1)}, bf16[768,1024]{1,0:T(8,128)(2,1)}, u32[]{:S(2)}, u32[]{:S(2)}) %collective-permute-start) | collective-permute-done | bytes 1572896 | tf_op jit(solution)/shard_map/ppermute | solution.py:299
  65.1 16.6 %collective-permute-done.3 = bf16[768,1024]{1,0:T(8,128)(2,1)S(1)} collective-permute-done((bf16[768,1024]{1,0:T(8,128)(2,1)}, bf16[768,1024]{1,0:T(8,128)(2,1)S(1)}, u32[]{:S(2)}, u32[]{:S(2)}) %collective-permute-start.3) | collective-permute-done | bytes 1572896 | tf_op jit(solution)/shard_map/ppermute | solution.py:299
  95.5 31.4 %collective-permute-done.12 = bf16[256,3072]{1,0:T(8,128)(2,1)S(1)} collective-permute-done((bf16[256,3072]{1,0:T(8,128)(2,1)S(1)}, bf16[256,3072]{1,0:T(8,128)(2,1)S(1)}, u32[]{:S(2)}, u32[]{:S(2)}) %collective-permute-start.12) | collective-permute-done | bytes 1572896 | tf_op jit(solution)/shard_map/ppermute | solution.py:317
  131.5 13.1 %fusion.4.qk_ref = f32[1024,1024]{1,0:T(8,128)S(1)} fusion(bf16[1024,6144]{1,0:T(8,128)(2,1)S(1)} %slice_dynamic-update-slice_fusion.refs_0_.refs_1_, bf16[6144,1024]{1,0:T(8,128)(2,1)S(1)} %constant_dynamic-update-slice_fusion.w_pair_ref), kind=kOutput, calls=%fused_computation.96 | convolution fusion | flops 12884901888 | bytes 29360128 | tf_op jit(solution)/shard_map/dot_general | solution.py:398
  144.6 5.9 %shard_map.113.turned_ref = bf16[512,1024]{1,0:T(8,128)(2,1)S(1)} custom-call(f32[1024,1024]{1,0:T(8,128)S(1)} %fusion.4.qk_ref, bf16[1024,512]{1,0:T(8,128)(2,1)S(1)} %constant_dynamic-update-slice_fusion.12.g_ref, f32[2,128]{1,0:T(2,128)S(1)} %pad_maximum_fusion.13.gains_ref), custom_call_target="tpu_custom_call" | custom-call | flops 178956976 | bytes 1398101 | tf_op jit(solution)/shard_map/pallas_call | solution.py:95
  150.6 4.6 %collective-permute-done.17 = bf16[1536,512]{1,0:T(8,128)(2,1)} collective-permute-done((bf16[1536,512]{1,0:T(8,128)(2,1)S(1)}, bf16[1536,512]{1,0:T(8,128)(2,1)}, u32[]{:S(2)}, u32[]{:S(2)}) %collective-permute-start.17) | collective-permute-done | bytes 1572896 | tf_op jit(solution)/shard_map/ppermute | solution.py:299
  159.3 6.1 %shard_map.116 = (bf16[1024,768]{1,0:T(8,128)(2,1)}, bf16[1024,768]{1,0:T(8,128)(2,1)}) custom-call(bf16[512,1024]{1,0:T(8,128)(2,1)S(1)} %shard_map.113.turned_ref, bf16[1024,6144]{1,0:T(8,128)(2,1)S(1)} %slice_dynamic-update-slice_fusion.refs_0_.refs_1_, bf16[1024,6144]{1,0:T(8,128)(2,1)S(1)} %slice_dynamic-update-slice_fusion.refs_0_.refs_1_), custom_call_target="tpu_custom_call" | custom-call | flops 536870912 | bytes 1485482 | tf_op jit(solution)/shard_map/pallas_call | solution.py:133
  169.0 6.5 %collective-permute-done.19 = bf16[768,512]{1,0:T(8,128)(2,1)S(1)} collective-permute-done((bf16[768,512]{1,0:T(8,128)(2,1)S(1)}, bf16[768,512]{1,0:T(8,128)(2,1)S(1)}, u32[]{:S(2)}, u32[]{:S(2)}) %collective-permute-start.19) | collective-permute-done | bytes 786464 | tf_op jit(solution)/shard_map/ppermute | solution.py:299
  176.9 7.6 %convolution_convert_fusion.v_ref = bf16[1024,512]{1,0:T(8,128)(2,1)} fusion(bf16[1024,6144]{1,0:T(8,128)(2,1)S(1)} %slice_dynamic-update-slice_fusion.refs_0_.refs_1_, bf16[6144,512]{1,0:T(8,128)(2,1)S(1)} %constant_dynamic-update-slice_fusion.8.w_value_ref), kind=kOutput, calls=%fused_computation.16 | convolution fusion | flops 6442975232 | bytes 19922944 | tf_op jit(solution)/shard_map/dot_general | solution.py:445
  189.2 10.0 %shard_map.114.turned_ref = bf16[1024,1024]{1,0:T(8,128)(2,1)S(1)} custom-call(f32[1024,1024]{1,0:T(8,128)S(1)} %copy-done.14, bf16[1024,512]{1,0:T(8,128)(2,1)S(1)} %copy-done.18, bf16[1024,512]{1,0:T(8,128)(2,1)S(1)} %copy-done.28, f32[2,128]{1,0:T(2,128)S(1)} %pad_maximum_fusion.13.gains_ref), custom_call_target="tpu_custom_call" | custom-call | flops 178956976 | bytes 2097152 | tf_op jit(solution)/shard_map/pallas_call | solution.py:95
  199.6 3.2 shard_map.118
  202.9 3.2 shard_map.119
  206.1 3.2 collective-permute-done.21.refs_2_.refs_4_
  209.8 4.7 %shard_map.117 = (bf16[512,768]{1,0:T(8,128)(2,1)}, bf16[512,768]{1,0:T(8,128)(2,1)}) custom-call(bf16[512,1024]{1,0:T(8,128)(2,1)S(1)} %copy-done.11, bf16[1024,6144]{1,0:T(8,128)(2,1)S(1)} %slice_dynamic-update-slice_fusion.refs_0_.refs_1_, bf16[1024,6144]{1,0:T(8,128)(2,1)S(1)} %slice_dynamic-update-slice_fusion.refs_0_.refs_1_, ...), custom_call_target="tpu_custom_call" | custom-call | flops 268435456 | bytes 1223338 | tf_op jit(solution)/shard_map/pallas_call | solution.py:133
  218.8 4.8 %shard_map.115 = (bf16[1024,768]{1,0:T(8,128)(2,1)S(1)}, bf16[1024,768]{1,0:T(8,128)(2,1)S(1)}) custom-call(bf16[1024,1024]{1,0:T(8,128)(2,1)S(1)} %shard_map.114.turned_ref, bf16[1024,6144]{1,0:T(8,128)(2,1)S(1)} %slice_dynamic-update-slice_fusion.refs_0_.refs_1_, bf16[1024,6144]{1,0:T(8,128)(2,1)S(1)} %slice_dynamic-update-slice_fusion.refs_0_.refs_1_), custom_call_target="tpu_custom_call" | custom-call | flops 536870912 | bytes 1398101 | tf_op jit(solution)/shard_map/pallas_call | solution.py:133
  223.7 4.4 %shard_map.120 = bf16[3072,256]{1,0:T(8,128)(2,1)} custom-call(bf16[1024,256]{1,0:T(8,128)(2,1)S(1)} %pad_maximum_fusion.5.pair_ref, bf16[512,256]{1,0:T(8,128)(2,1)S(1)} %copy-done.24, bf16[6144,1024]{1,0:T(8,128)(2,1)S(1)} %constant_dynamic-update-slice_fusion.w_pair_ref, bf16[6144,512]{1,0:T(8,128)(2,1)S(1)} %constant_dynamic-update-slice_fusion.8.w_value_ref, ...), custom_call_target="tpu_custom_call" | custom-call | flops 402653184 | bytes 2359296 | tf_op jit(solution)/shard_map/pallas_call | solution.py:164
  230.5 5.2 %collective-permute-done.25.refs_5_ = bf16[512,768]{1,0:T(8,128)(2,1)} collective-permute-done((bf16[512,768]{1,0:T(8,128)(2,1)}, bf16[512,768]{1,0:T(8,128)(2,1)}, u32[]{:S(2)}, u32[]{:S(2)}) %collective-permute-start.25) | collective-permute-done | bytes 786464 | tf_op jit(solution)/shard_map/ppermute | solution.py:299
  238.9 4.6 %copy-done.3 = bf16[6144,1024]{1,0:T(8,128)(2,1)S(1)} copy-done((bf16[6144,1024]{1,0:T(8,128)(2,1)S(1)}, bf16[6144,1024]{1,0:T(8,128)(2,1)}, u32[]{:S(2)}) %copy-start.3) | copy-done | bytes 12582936
  248.6 3.2 shard_map.121
  257.1 3.1 shard_map.124
  260.3 4.5 %shard_map.122 = (bf16[1024,768]{1,0:T(8,128)(2,1)S(1)}, bf16[1024,768]{1,0:T(8,128)(2,1)S(1)}) custom-call(bf16[1024,1024]{1,0:T(8,128)(2,1)S(1)} %copy-done.9, bf16[1024,6144]{1,0:T(8,128)(2,1)S(1)} %bitcast.12, bf16[1024,6144]{1,0:T(8,128)(2,1)S(1)} %bitcast.12), custom_call_target="tpu_custom_call" | custom-call | flops 536870912 | bytes 1398101 | tf_op jit(solution)/shard_map/pallas_call | solution.py:133
  266.4 4.6 %collective-permute-done.28.refs_3_ = bf16[1024,768]{1,0:T(8,128)(2,1)S(1)} collective-permute-done((bf16[1024,768]{1,0:T(8,128)(2,1)}, bf16[1024,768]{1,0:T(8,128)(2,1)S(1)}, u32[]{:S(2)}, u32[]{:S(2)}) %collective-permute-start.28) | collective-permute-done | bytes 1572896 | tf_op jit(solution)/shard_map/ppermute | solution.py:299
  285.1 3.2 shard_map.126
  288.3 5.2 %shard_map.129 = (bf16[768,512]{1,0:T(8,128)(2,1)S(1)}, bf16[768,512]{1,0:T(8,128)(2,1)}) custom-call(bf16[512,1024]{1,0:T(8,128)(2,1)S(1)} %copy-done.12, bf16[1024,6144]{1,0:T(8,128)(2,1)S(1)} %bitcast.12, bf16[1024,6144]{1,0:T(8,128)(2,1)S(1)} %bitcast.12, bf16[1024,768]{1,0:T(8,128)(2,1)} %collective-permute-done.22.refs_3_.refs_2_, ...), custom_call_target="tpu_custom_call" | custom-call | flops 268435456 | bytes 1485482 | tf_op jit(solution)/shard_map/pallas_call | solution.py:133
  294.4 5.1 %shard_map.128 = (bf16[1024,768]{1,0:T(8,128)(2,1)S(1)}, bf16[1024,768]{1,0:T(8,128)(2,1)}) custom-call(bf16[1024,1024]{1,0:T(8,128)(2,1)S(1)} %copy-done.9, bf16[1024,6144]{1,0:T(8,128)(2,1)S(1)} %bitcast.12, bf16[1024,6144]{1,0:T(8,128)(2,1)S(1)} %bitcast.12), custom_call_target="tpu_custom_call" | custom-call | flops 536870912 | bytes 1398101 | tf_op jit(solution)/shard_map/pallas_call | solution.py:133
  300.7 4.7 %shard_map.127 = (bf16[1024,768]{1,0:T(8,128)(2,1)S(1)}, bf16[1024,768]{1,0:T(8,128)(2,1)S(1)}) custom-call(bf16[1024,1024]{1,0:T(8,128)(2,1)S(1)} %copy-done.9, bf16[1024,6144]{1,0:T(8,128)(2,1)S(1)} %bitcast.12, bf16[1024,6144]{1,0:T(8,128)(2,1)S(1)} %bitcast.12, bf16[1024,768]{1,0:T(8,128)(2,1)S(1)} %collective-permute-done.29.refs_2_, ...), custom_call_target="tpu_custom_call" | custom-call | flops 536870912 | bytes 1922389 | tf_op jit(solution)/shard_map/pallas_call | solution.py:133
  305.4 4.3 %collective-permute-done.32 = bf16[3072,256]{1,0:T(8,128)(2,1)} collective-permute-done((bf16[3072,256]{1,0:T(8,128)(2,1)}, bf16[3072,256]{1,0:T(8,128)(2,1)}, u32[]{:S(2)}, u32[]{:S(2)}) %collective-permute-start.32) | collective-permute-done | bytes 1572896 | tf_op jit(solution)/shard_map/ppermute | solution.py:317
  320.0 3.4 add_convert_fusion.1.refs_0_
  326.0 3.4 add_convert_fusion.refs_2_
  329.4 22.0 %collective-permute-done.35 = bf16[3072,256]{1,0:T(8,128)(2,1)} collective-permute-done((bf16[3072,256]{1,0:T(8,128)(2,1)}, bf16[3072,256]{1,0:T(8,128)(2,1)}, u32[]{:S(2)}, u32[]{:S(2)}) %collective-permute-start.35) | collective-permute-done | bytes 1572896 | tf_op jit(solution)/shard_map/ppermute | solution.py:317
  358.7 6.0 %shard_map.131 = (bf16[768,1024]{1,0:T(8,128)(2,1)}, bf16[768,1024]{1,0:T(8,128)(2,1)}) custom-call(s32[1]{0:T(128)} %bitcast.3.core_ref, bf16[1024,768]{1,0:T(8,128)(2,1)S(1)} %copy-done.19, bf16[1024,768]{1,0:T(8,128)(2,1)} %collective-permute-done.39.refs_1_, bf16[1024,768]{1,0:T(8,128)(2,1)S(1)} %copy-done.20, ...), custom_call_target="tpu_custom_call" | custom-call | tf_op jit(solution)/shard_map/pallas_call | solution.py:213
  366.6 3.4 shard_map.132
  (253 shorter events, 128.1 us)
Async XLA Ops:
  8.4 37.5 %collective-permute-start = (bf16[768,1024]{1,0:T(8,128)(2,1)S(1)}, bf16[768,1024]{1,0:T(8,128)(2,1)}, u32[]{:S(2)}, u32[]{:S(2)}) collective-permute-start(bf16[768,1024]{1,0:T(8,128)(2,1)S(1)} %pad_maximum_fusion), channel_id=1, source_target_pairs={{0,8},{4,12},{8,0},{12,4},{16,24},{20,28},{24,16},{28,20},{1,9},{5... | collective-permute-start | bytes 4718600 | tf_op jit(solution)/shard_map/ppermute | solution.py:299
  11.1 35.7 %collective-permute-start.1 = (bf16[768,1024]{1,0:T(8,128)(2,1)S(1)}, bf16[768,1024]{1,0:T(8,128)(2,1)}, u32[]{:S(2)}, u32[]{:S(2)}) collective-permute-start(bf16[768,1024]{1,0:T(8,128)(2,1)S(1)} %pad_maximum_fusion), channel_id=1, source_target_pairs={{0,16},{4,20},{8,24},{12,28},{16,0},{20,4},{24,8},{28,12},{1,17},{... | collective-permute-start | bytes 4718600 | tf_op jit(solution)/shard_map/ppermute | solution.py:299
  12.3 34.5 %collective-permute-start.2 = (bf16[768,1024]{1,0:T(8,128)(2,1)}, bf16[768,1024]{1,0:T(8,128)(2,1)}, u32[]{:S(2)}, u32[]{:S(2)}) collective-permute-start(bf16[768,1024]{1,0:T(8,128)(2,1)} %pad_maximum_fusion.1), channel_id=1, source_target_pairs={{0,4},{4,0},{8,12},{12,8},{16,20},{20,16},{24,28},{28,24},{1,5},{5... | collective-permute-start | bytes 4718600 | tf_op jit(solution)/shard_map/ppermute | solution.py:299
  14.3 36.5 %collective-permute-start.7 = (bf16[256,3072]{1,0:T(8,128)(2,1)}, bf16[256,3072]{1,0:T(8,128)(2,1)}, u32[]{:S(2)}, u32[]{:S(2)}) collective-permute-start(bf16[256,3072]{1,0:T(8,128)(2,1)} %pad_maximum_fusion.2), channel_id=1, source_target_pairs={{0,2},{2,3},{3,1},{1,0},{4,6},{6,7},{7,5},{5,4},{8,10},{10,11},{11... | collective-permute-start | bytes 4718600 | tf_op jit(solution)/shard_map/ppermute | solution.py:317
  16.7 38.0 %collective-permute-start.6 = (bf16[256,3072]{1,0:T(8,128)(2,1)}, bf16[256,3072]{1,0:T(8,128)(2,1)}, u32[]{:S(2)}, u32[]{:S(2)}) collective-permute-start(bf16[256,3072]{1,0:T(8,128)(2,1)} %pad_maximum_fusion.2), channel_id=1, source_target_pairs={{0,4},{4,0},{8,12},{12,8},{16,20},{20,16},{24,28},{28,24},{1,5},{5... | collective-permute-start | bytes 4718600 | tf_op jit(solution)/shard_map/ppermute | solution.py:299
  46.9 34.9 %collective-permute-start.3 = (bf16[768,1024]{1,0:T(8,128)(2,1)}, bf16[768,1024]{1,0:T(8,128)(2,1)S(1)}, u32[]{:S(2)}, u32[]{:S(2)}) collective-permute-start(bf16[768,1024]{1,0:T(8,128)(2,1)} %collective-permute-done.2), channel_id=1, source_target_pairs={{0,8},{4,12},{8,0},{12,4},{16,24},{20,28},{24,16},{28,20},{1,9},{5... | collective-permute-start | bytes 4718600 | tf_op jit(solution)/shard_map/ppermute | solution.py:299
  47.2 34.9 %collective-permute-start.4 = (bf16[768,1024]{1,0:T(8,128)(2,1)}, bf16[768,1024]{1,0:T(8,128)(2,1)S(1)}, u32[]{:S(2)}, u32[]{:S(2)}) collective-permute-start(bf16[768,1024]{1,0:T(8,128)(2,1)} %collective-permute-done.2), channel_id=1, source_target_pairs={{0,16},{4,20},{8,24},{12,28},{16,0},{20,4},{24,8},{28,12},{1,17},{... | collective-permute-start | bytes 4718600 | tf_op jit(solution)/shard_map/ppermute | solution.py:299
  50.8 12.4 %collective-permute-start.8 = (bf16[256,3072]{1,0:T(8,128)(2,1)}, bf16[256,3072]{1,0:T(8,128)(2,1)S(1)}, u32[]{:S(2)}, u32[]{:S(2)}) collective-permute-start(bf16[256,3072]{1,0:T(8,128)(2,1)} %collective-permute-done.7), channel_id=1, source_target_pairs={{0,4},{4,0},{8,12},{12,8},{16,20},{20,16},{24,28},{28,24},{1,5},{5... | collective-permute-start | bytes 4718600 | tf_op jit(solution)/shard_map/ppermute | solution.py:299
  52.1 38.8 %collective-permute-start.10 = (bf16[256,3072]{1,0:T(8,128)(2,1)}, bf16[256,3072]{1,0:T(8,128)(2,1)S(1)}, u32[]{:S(2)}, u32[]{:S(2)}) collective-permute-start(bf16[256,3072]{1,0:T(8,128)(2,1)} %collective-permute-done.7), channel_id=1, source_target_pairs={{0,2},{2,3},{3,1},{1,0},{4,6},{6,7},{7,5},{5,4},{8,10},{10,11},{11... | collective-permute-start | bytes 4718600 | tf_op jit(solution)/shard_map/ppermute | solution.py:317
  82.3 11.4 %collective-permute-start.9 = (bf16[768,512]{1,0:T(8,128)(2,1)S(1)}, bf16[768,512]{1,0:T(8,128)(2,1)S(1)}, u32[]{:S(2)}, u32[]{:S(2)}) collective-permute-start(bf16[768,512]{1,0:T(8,128)(2,1)S(1)} %get-tuple-element.215), channel_id=1, source_target_pairs={{0,4},{4,0},{8,12},{12,8},{16,20},{20,16},{24,28},{28,24},{1,5},{5... | collective-permute-start | bytes 2359304 | tf_op jit(solution)/shard_map/ppermute | solution.py:299
  84.4 43.8 %collective-permute-start.14 = (bf16[768,1024]{1,0:T(8,128)(2,1)}, bf16[768,1024]{1,0:T(8,128)(2,1)S(1)}, u32[]{:S(2)}, u32[]{:S(2)}) collective-permute-start(bf16[768,1024]{1,0:T(8,128)(2,1)} %collective-permute-done), channel_id=1, source_target_pairs={{0,16},{4,20},{8,24},{12,28},{16,0},{20,4},{24,8},{28,12},{1,17},{... | collective-permute-start | bytes 4718600 | tf_op jit(solution)/shard_map/ppermute | solution.py:299
  85.7 44.5 %collective-permute-start.15 = (bf16[768,1024]{1,0:T(8,128)(2,1)S(1)}, bf16[768,1024]{1,0:T(8,128)(2,1)S(1)}, u32[]{:S(2)}, u32[]{:S(2)}) collective-permute-start(bf16[768,1024]{1,0:T(8,128)(2,1)S(1)} %collective-permute-done.4), channel_id=1, source_target_pairs={{0,8},{4,12},{8,0},{12,4},{16,24},{20,28},{24,16},{28,20},{1,9},{5... | collective-permute-start | bytes 4718600 | tf_op jit(solution)/shard_map/ppermute | solution.py:299
  91.1 35.8 %collective-permute-start.12 = (bf16[256,3072]{1,0:T(8,128)(2,1)S(1)}, bf16[256,3072]{1,0:T(8,128)(2,1)S(1)}, u32[]{:S(2)}, u32[]{:S(2)}) collective-permute-start(bf16[256,3072]{1,0:T(8,128)(2,1)S(1)} %collective-permute-done.10), channel_id=1, source_target_pairs={{0,2},{2,3},{3,1},{1,0},{4,6},{6,7},{7,5},{5,4},{8,10},{10,11},{11... | collective-permute-start | bytes 4718600 | tf_op jit(solution)/shard_map/ppermute | solution.py:317
  94.5 60.7 %collective-permute-start.17 = (bf16[1536,512]{1,0:T(8,128)(2,1)S(1)}, bf16[1536,512]{1,0:T(8,128)(2,1)}, u32[]{:S(2)}, u32[]{:S(2)}) collective-permute-start(bf16[1536,512]{1,0:T(8,128)(2,1)S(1)} %pad_maximum_fusion.3), channel_id=1, source_target_pairs={{0,8},{4,12},{8,0},{12,4},{16,24},{20,28},{24,16},{28,20},{1,9},{5... | collective-permute-start | bytes 4718600 | tf_op jit(solution)/shard_map/ppermute | solution.py:299
  95.3 59.9 %collective-permute-start.18 = (bf16[1536,512]{1,0:T(8,128)(2,1)S(1)}, bf16[1536,512]{1,0:T(8,128)(2,1)}, u32[]{:S(2)}, u32[]{:S(2)}) collective-permute-start(bf16[1536,512]{1,0:T(8,128)(2,1)S(1)} %pad_maximum_fusion.3), channel_id=1, source_target_pairs={{0,16},{4,20},{8,24},{12,28},{16,0},{20,4},{24,8},{28,12},{1,17},{... | collective-permute-start | bytes 4718600 | tf_op jit(solution)/shard_map/ppermute | solution.py:299
  157.5 17.9 %collective-permute-start.19 = (bf16[768,512]{1,0:T(8,128)(2,1)S(1)}, bf16[768,512]{1,0:T(8,128)(2,1)S(1)}, u32[]{:S(2)}, u32[]{:S(2)}) collective-permute-start(bf16[768,512]{1,0:T(8,128)(2,1)S(1)} %slice.75), channel_id=1, source_target_pairs={{0,16},{4,20},{8,24},{12,28},{16,0},{20,4},{24,8},{28,12},{1,17},{... | collective-permute-start | bytes 2359304 | tf_op jit(solution)/shard_map/ppermute | solution.py:299
  158.1 18.7 %collective-permute-start.20 = (bf16[768,512]{1,0:T(8,128)(2,1)S(1)}, bf16[768,512]{1,0:T(8,128)(2,1)S(1)}, u32[]{:S(2)}, u32[]{:S(2)}) collective-permute-start(bf16[768,512]{1,0:T(8,128)(2,1)S(1)} %slice.76), channel_id=1, source_target_pairs={{0,8},{4,12},{8,0},{12,4},{16,24},{20,28},{24,16},{28,20},{1,9},{5... | collective-permute-start | bytes 2359304 | tf_op jit(solution)/shard_map/ppermute | solution.py:299
  165.4 43.9 %collective-permute-start.21 = (bf16[1024,768]{1,0:T(8,128)(2,1)}, bf16[1024,768]{1,0:T(8,128)(2,1)}, u32[]{:S(2)}, u32[]{:S(2)}) collective-permute-start(bf16[1024,768]{1,0:T(8,128)(2,1)} %get-tuple-element.130), channel_id=1, source_target_pairs={{0,16},{4,20},{8,24},{12,28},{16,0},{20,4},{24,8},{28,12},{1,17},{... | collective-permute-start | bytes 4718600 | tf_op jit(solution)/shard_map/ppermute | solution.py:299
  166.4 43.5 %collective-permute-start.22 = (bf16[1024,768]{1,0:T(8,128)(2,1)}, bf16[1024,768]{1,0:T(8,128)(2,1)}, u32[]{:S(2)}, u32[]{:S(2)}) collective-permute-start(bf16[1024,768]{1,0:T(8,128)(2,1)} %get-tuple-element.131), channel_id=1, source_target_pairs={{0,8},{4,12},{8,0},{12,4},{16,24},{20,28},{24,16},{28,20},{1,9},{5... | collective-permute-start | bytes 4718600 | tf_op jit(solution)/shard_map/ppermute | solution.py:299
  216.7 19.0 %collective-permute-start.25 = (bf16[512,768]{1,0:T(8,128)(2,1)}, bf16[512,768]{1,0:T(8,128)(2,1)}, u32[]{:S(2)}, u32[]{:S(2)}) collective-permute-start(bf16[512,768]{1,0:T(8,128)(2,1)} %get-tuple-element.141), channel_id=1, source_target_pairs={{0,8},{4,12},{8,0},{12,4},{16,24},{20,28},{24,16},{28,20},{1,9},{5... | collective-permute-start | bytes 2359304 | tf_op jit(solution)/shard_map/ppermute | solution.py:299
  217.8 18.7 %collective-permute-start.26 = (bf16[512,768]{1,0:T(8,128)(2,1)}, bf16[512,768]{1,0:T(8,128)(2,1)}, u32[]{:S(2)}, u32[]{:S(2)}) collective-permute-start(bf16[512,768]{1,0:T(8,128)(2,1)} %get-tuple-element.142), channel_id=1, source_target_pairs={{0,16},{4,20},{8,24},{12,28},{16,0},{20,4},{24,8},{28,12},{1,17},{... | collective-permute-start | bytes 2359304 | tf_op jit(solution)/shard_map/ppermute | solution.py:299
  228.1 36.7 %collective-permute-start.27 = (bf16[3072,256]{1,0:T(8,128)(2,1)}, bf16[3072,256]{1,0:T(8,128)(2,1)S(1)}, u32[]{:S(2)}, u32[]{:S(2)}) collective-permute-start(bf16[3072,256]{1,0:T(8,128)(2,1)} %shard_map.120), channel_id=1, source_target_pairs={{0,2},{2,3},{3,1},{1,0},{4,6},{6,7},{7,5},{5,4},{8,10},{10,11},{11... | collective-permute-start | bytes 4718600 | tf_op jit(solution)/shard_map/ppermute | solution.py:317
  236.5 34.5 %collective-permute-start.28 = (bf16[1024,768]{1,0:T(8,128)(2,1)}, bf16[1024,768]{1,0:T(8,128)(2,1)S(1)}, u32[]{:S(2)}, u32[]{:S(2)}) collective-permute-start(bf16[1024,768]{1,0:T(8,128)(2,1)} %copy-done.34), channel_id=1, source_target_pairs={{0,8},{4,12},{8,0},{12,4},{16,24},{20,28},{24,16},{28,20},{1,9},{5... | collective-permute-start | bytes 4718600 | tf_op jit(solution)/shard_map/ppermute | solution.py:299
  236.8 34.2 %collective-permute-start.29 = (bf16[1024,768]{1,0:T(8,128)(2,1)}, bf16[1024,768]{1,0:T(8,128)(2,1)S(1)}, u32[]{:S(2)}, u32[]{:S(2)}) collective-permute-start(bf16[1024,768]{1,0:T(8,128)(2,1)} %copy-done.33), channel_id=1, source_target_pairs={{0,16},{4,20},{8,24},{12,28},{16,0},{20,4},{24,8},{28,12},{1,17},{... | collective-permute-start | bytes 4718600 | tf_op jit(solution)/shard_map/ppermute | solution.py:299
  273.9 35.9 %collective-permute-start.32 = (bf16[3072,256]{1,0:T(8,128)(2,1)}, bf16[3072,256]{1,0:T(8,128)(2,1)}, u32[]{:S(2)}, u32[]{:S(2)}) collective-permute-start(bf16[3072,256]{1,0:T(8,128)(2,1)} %add_convert_fusion.3), channel_id=1, source_target_pairs={{0,2},{2,3},{3,1},{1,0},{4,6},{6,7},{7,5},{5,4},{8,10},{10,11},{11... | collective-permute-start | bytes 4718600 | tf_op jit(solution)/shard_map/ppermute | solution.py:317
  276.2 36.6 %collective-permute-start.33 = (bf16[1024,768]{1,0:T(8,128)(2,1)S(1)}, bf16[1024,768]{1,0:T(8,128)(2,1)}, u32[]{:S(2)}, u32[]{:S(2)}) collective-permute-start(bf16[1024,768]{1,0:T(8,128)(2,1)S(1)} %get-tuple-element.184), channel_id=1, source_target_pairs={{0,8},{4,12},{8,0},{12,4},{16,24},{20,28},{24,16},{28,20},{1,9},{5... | collective-permute-start | bytes 4718600 | tf_op jit(solution)/shard_map/ppermute | solution.py:299
  277.3 37.0 %collective-permute-start.34 = (bf16[1024,768]{1,0:T(8,128)(2,1)S(1)}, bf16[1024,768]{1,0:T(8,128)(2,1)}, u32[]{:S(2)}, u32[]{:S(2)}) collective-permute-start(bf16[1024,768]{1,0:T(8,128)(2,1)S(1)} %get-tuple-element.185), channel_id=1, source_target_pairs={{0,20},{4,16},{8,28},{12,24},{16,4},{20,0},{24,12},{28,8},{1,21},{... | collective-permute-start | bytes 4718600 | tf_op jit(solution)/shard_map/ppermute | solution.py:299
  314.3 11.7 %collective-permute-start.37 = (bf16[1024,768]{1,0:T(8,128)(2,1)}, bf16[1024,768]{1,0:T(8,128)(2,1)}, u32[]{:S(2)}, u32[]{:S(2)}) collective-permute-start(bf16[1024,768]{1,0:T(8,128)(2,1)} %get-tuple-element.191), channel_id=1, source_target_pairs={{0,4},{4,0},{8,12},{12,8},{16,20},{20,16},{24,28},{28,24},{1,5},{5... | collective-permute-start | bytes 4718600 | tf_op jit(solution)/shard_map/ppermute | solution.py:299
  314.9 36.4 %collective-permute-start.35 = (bf16[3072,256]{1,0:T(8,128)(2,1)}, bf16[3072,256]{1,0:T(8,128)(2,1)}, u32[]{:S(2)}, u32[]{:S(2)}) collective-permute-start(bf16[3072,256]{1,0:T(8,128)(2,1)} %add_convert_fusion.2), channel_id=1, source_target_pairs={{0,2},{2,3},{3,1},{1,0},{4,6},{6,7},{7,5},{5,4},{8,10},{10,11},{11... | collective-permute-start | bytes 4718600 | tf_op jit(solution)/shard_map/ppermute | solution.py:317
  317.6 38.2 %collective-permute-start.39 = (bf16[1024,768]{1,0:T(8,128)(2,1)}, bf16[1024,768]{1,0:T(8,128)(2,1)}, u32[]{:S(2)}, u32[]{:S(2)}) collective-permute-start(bf16[1024,768]{1,0:T(8,128)(2,1)} %copy-done.36), channel_id=1, source_target_pairs={{0,16},{4,20},{8,24},{12,28},{16,0},{20,4},{24,8},{28,12},{1,17},{... | collective-permute-start | bytes 4718600 | tf_op jit(solution)/shard_map/ppermute | solution.py:299
  318.6 37.3 %collective-permute-start.40 = (bf16[1024,768]{1,0:T(8,128)(2,1)}, bf16[1024,768]{1,0:T(8,128)(2,1)}, u32[]{:S(2)}, u32[]{:S(2)}) collective-permute-start(bf16[1024,768]{1,0:T(8,128)(2,1)} %copy-done.35), channel_id=1, source_target_pairs={{0,12},{4,8},{8,4},{12,0},{16,28},{20,24},{24,20},{28,16},{1,13},{... | collective-permute-start | bytes 4718600 | tf_op jit(solution)/shard_map/ppermute | solution.py:299
  354.8 10.1 %collective-permute-start.38 = (bf16[3072,128]{1,0:T(8,128)(2,1)S(1)}, bf16[3072,128]{1,0:T(8,128)(2,1)S(1)}, u32[]{:S(2)}, u32[]{:S(2)}) collective-permute-start(bf16[3072,128]{1,0:T(8,128)(2,1)S(1)} %dynamic-slice_convert_fusion), channel_id=1, source_target_pairs={{0,4},{4,0},{8,12},{12,8},{16,20},{20,16},{24,28},{28,24},{1,5},{5... | collective-permute-start | bytes 2359304 | tf_op jit(solution)/shard_map/ppermute | solution.py:299
  (63 other events, 760.6 us)
